TPU v7x, 128 devices: a whole 4x4x4 slice. The times are simulated.
128 devices in a mesh: wide: 32 (over x_hi, y, z), narrow: 4 (over x_lo, core).
Axes of the slice: x: 4 (x_hi: 2, x_lo: 2; x = x_hi * 2 + x_lo), y: 4, z: 4, core: 2. Of those that a mesh axis runs over, the one named last changes fastest.
Arguments:
- field: bfloat16 [256, 16, 16, 400], P(('wide', 'narrow')), may hold values from -6 to 6
- cotangent: bfloat16 [256, 16, 16, 400], P(('wide', 'narrow')), may hold values from -6 to 6
- land: int32 [256, 16, 16], P(('wide', 'narrow')), may hold values from 0 to 1
- neighbours: int32 [256, 8], P(('wide', 'narrow')), may hold values from -1 to 255, as said below
- depth_weight: float32 [49, 400], replicated, may hold values from -0.875 to 0.875
- depth_bias: float32 [400], replicated, may hold values from -5 to 5
- ln_gain: float32 [400], replicated, may hold values from 0.25 to 1.75
- ln_shift: float32 [400], replicated, may hold values from -3 to 3
- up_weight: bfloat16 [400, 1600], replicated, may hold values from -0.3125 to 0.3125
- up_bias: float32 [1600], replicated, may hold values from -3 to 3
- down_weight: bfloat16 [1600, 400], replicated, may hold values from -0.15625 to 0.15625
Outputs:
- field_grad: bfloat16 [256, 16, 16, 400], P(('wide', 'narrow'))
- depth_weight_grad: float32 [49, 400], replicated
- depth_bias_grad: float32 [400], replicated
- gain_grad: float32 [400], replicated
- shift_grad: float32 [400], replicated
- up_weight_grad: float32 [400, 1600], replicated
- up_bias_grad: float32 [1600], replicated
- down_weight_grad: float32 [1600, 400], replicated
- down_bias_grad: float32 [400], replicated
Inputs may be any that keep to these rules, and one draw needn't show every extreme that they name: `neighbours`: the slots form a tile grid of 64 columns (longitude, closed into a loop) by 8 rows; the device with wide index w and narrow index n (slots (4 w + n) * 2 onward) owns the 2 x 2 positions at columns 2w, 2w+1 and rows 2n, 2n+1, holding one or two of them as wet tiles; device 0 always holds two. Neighbour entries are -1 beyond the first and last rows, toward dry positions, and on every entry of an empty slot; the relation is symmetric.
All inputs are finite; a program needn't handle non-finite values.
Results may differ from a plain program's by a relative error of at most 0.0075.
Values may be sent and summed in bfloat16 or wider, within the bound.
No kernel may reach another device: no remote copies, remote signals or barrier semaphores. Data moves between devices by JAX's collectives and lax.ppermute only.
A program may use at most 64 MiB of HBM per device.

v0:
```python
import functools

import jax
import jax.numpy as jnp
from jax import lax
from jax.experimental import pallas as pl
from jax.experimental.pallas import tpu as pltpu
from jax.sharding import PartitionSpec as P

epsilon = 1e-06
gelu_root = 0.7978845608028654
gelu_cubic = 0.044715

C = 400
CP = 512
HID = 1600
TE = 16
CELLS = 512
GROUPS = 4
HT = 13
PITCH = 32
TILES = 696
EXTRA = 650
AXES = ("wide", "narrow")
f32 = jnp.float32
bf16 = jnp.bfloat16
VMEM = pl.BlockSpec(memory_space=pltpu.VMEM)
SMEM = pl.BlockSpec(memory_space=pltpu.SMEM)


def group_width(g):
    return min(128, C - 128 * g)


def lanes(g):
    return slice(128 * g, 128 * g + group_width(g))


def land_mask(land):
    spread = jnp.broadcast_to(land.astype(f32)[:, :, None], (2 * TE, TE, C))
    return spread.reshape(CELLS, C)


def zero_lanes(ref):
    ref[...] = jnp.zeros(ref.shape, ref.dtype)


def pack_narrow(tile_rows, even, first_ref, second_ref):
    for ref in (first_ref, second_ref):
        zero_lanes(ref)
    for s in range(2):
        north = tile_rows(s, 0)
        south = tile_rows(s, TE - 3)
        first_ref[s, :, 0:C] = jnp.where(even, south, north).astype(bf16)
        second_ref[s, :, 0:C] = jnp.where(even, north, south).astype(bf16)


def narrow_kernel(field_ref, land_ref, first_ref, second_ref, mask_ref):
    mask_ref[...] = land_mask(land_ref[...].reshape(2 * TE, TE))

    def tile_rows(s, row):
        cells = field_ref[s, row : row + 3].reshape(3 * TE, C).astype(f32)
        at = s * TE * TE + row * TE
        return cells * mask_ref[at : at + 3 * TE, :]

    pack_narrow(tile_rows, lax.axis_index("narrow") % 2 == 0, first_ref, second_ref)


def wide_kernel(masked, *refs):
    if masked:
        tiles_ref, land_ref, n1_ref, n2_ref, first_ref, second_ref, m_ref, r_ref, o_ref = refs
        mask = land_mask(land_ref[...].reshape(2 * TE, TE))
    else:
        tiles_ref, n1_ref, n2_ref, first_ref, second_ref, m_ref, r_ref, o_ref = refs
    n_even = lax.axis_index("narrow") % 2 == 0
    w_even = lax.axis_index("wide") % 2 == 0
    zero_lanes(o_ref)
    for s in range(2):
        cells = tiles_ref[s].reshape(TE * TE, C).astype(f32)
        if masked:
            cells = cells * mask[s * TE * TE : (s + 1) * TE * TE]
        one = n1_ref[s].astype(f32)
        two = n2_ref[s].astype(f32)
        from_north = jnp.where(n_even, two, one)
        from_south = jnp.where(n_even, one, two)
        for g in range(GROUPS):
            m_ref[s, g, :, 0 : group_width(g)] = cells[:, lanes(g)]
            r_ref[0, s, g] = from_north[:, 128 * g : 128 * g + 128]
            r_ref[1, s, g] = from_south[:, 128 * g : 128 * g + 128]
    for s in range(2):
        for g in range(GROUPS):
            w = group_width(g)
            for side in range(2):
                for c in range(3):
                    col = c + side * (TE - 3)
                    at = c * 22
                    o_ref[side, s, g, at : at + 3, :] = r_ref[0, s, g, pl.ds(col, 3, stride=TE), :]
                    o_ref[side, s, g, at + 3 : at + 19, 0:w] = m_ref[s, g, pl.ds(col, TE, stride=TE), 0:w]
                    o_ref[side, s, g, at + 19 : at + 22, :] = r_ref[1, s, g, pl.ds(col, 3, stride=TE), :]
            west = o_ref[0, s, g]
            east = o_ref[1, s, g]
            first_ref[s, :, 128 * g : 128 * g + 128] = jnp.where(w_even, east, west).astype(bf16)
            second_ref[s, :, 128 * g : 128 * g + 128] = jnp.where(w_even, west, east).astype(bf16)


def place_centre(cells, s, p_ref):
    for g in range(GROUPS):
        w = group_width(g)
        for r in range(TE):
            at = (r + 3) * PITCH + 8
            p_ref[s, g, at : at + TE, 0:w] = cells[r * TE : (r + 1) * TE, lanes(g)]


def place_borders(neighbours_ref, n1_ref, n2_ref, w1_ref, w2_ref, p_ref, rn_ref, rw_ref):
    here_w = lax.axis_index("wide")
    here_n = lax.axis_index("narrow")
    here = here_w * lax.axis_size("narrow") + here_n
    n_even = here_n % 2 == 0
    w_even = here_w % 2 == 0
    for s in range(2):
        one = n1_ref[s].astype(f32)
        two = n2_ref[s].astype(f32)
        north = jnp.where(n_even, two, one)
        south = jnp.where(n_even, one, two)
        one = w1_ref[s].astype(f32)
        two = w2_ref[s].astype(f32)
        west = jnp.where(w_even, two, one)
        east = jnp.where(w_even, one, two)
        for g in range(GROUPS):
            at = slice(128 * g, 128 * g + 128)
            rn_ref[0, s, g] = north[:, at]
            rn_ref[1, s, g] = south[:, at]
            rw_ref[0, s, g] = west[:, at]
            rw_ref[1, s, g] = east[:, at]

    def column(t, g):
        def entry(d):
            e = neighbours_ref[t, d]
            near = jnp.maximum(e, 0)
            return e >= 0, near // 2, near % 2

        def chosen(options, present):
            value = options[-1][1]
            for test, other in reversed(options[:-1]):
                value = jnp.where(test, other, value)
            return jnp.where(present, value, 0.0)

        for d in range(2):
            present, device, slot = entry(d)
            from_row = 3 + TE - 3 if d == 0 else 3
            to_row = 0 if d == 0 else 3 + TE
            for i in range(3):
                own = p_ref[slot, g, pl.ds((from_row + i) * PITCH + 8, TE), :]
                other = rn_ref[d, slot, g, pl.ds(i * TE, TE), :]
                p_ref[t, g, pl.ds((to_row + i) * PITCH + 8, TE), :] = chosen(
                    [(device == here, own), (None, other)], present
                )
        for d in range(2):
            present, device, slot = entry(2 + d)
            from_col = 8 + TE - 3 if d == 0 else 8
            to_col = 5 if d == 0 else 8 + TE
            for c in range(3):
                own = p_ref[slot, g, pl.ds(3 * PITCH + from_col + c, TE, stride=PITCH), :]
                other = rw_ref[d, slot, g, pl.ds(c * 22 + 3, TE), :]
                p_ref[t, g, pl.ds(3 * PITCH + to_col + c, TE, stride=PITCH), :] = chosen(
                    [(device == here, own), (None, other)], present
                )
        for d in range(4):
            south, east = d // 2, d % 2
            present, device, slot = entry(4 + d)
            same_w = device // lax.axis_size("narrow") == here_w
            same_n = device % lax.axis_size("narrow") == here_n
            from_row = 3 if south else 3 + TE - 3
            to_row = 3 + TE if south else 0
            from_col = 8 if east else 8 + TE - 3
            to_col = 8 + TE if east else 5
            for c in range(3):
                own = p_ref[slot, g, pl.ds(from_row * PITCH + from_col + c, 3, stride=PITCH), :]
                beyond = rn_ref[south, slot, g, pl.ds(from_col - 8 + c, 3, stride=TE), :]
                beside = rw_ref[east, slot, g, pl.ds(c * 22 + from_row, 3), :]
                across = rw_ref[east, slot, g, pl.ds(c * 22 + (19 if south else 0), 3), :]
                p_ref[t, g, pl.ds(to_row * PITCH + to_col + c, 3, stride=PITCH), :] = chosen(
                    [(device == here, own), (same_w, beyond), (same_n, beside), (None, across)], present
                )

    def step(i, _):
        column(i // GROUPS, i % GROUPS)
        return _

    lax.fori_loop(0, 2 * GROUPS, step, 0)


def weight_rows(weight_ref, g, taps):
    at = pl.ds(pl.multiple_of(g * 128, 128), 128)
    return [jnp.broadcast_to(weight_ref[pl.ds(k, 1), at], (8, 128)) for k in taps]


def convolve(p_ref, weight_ref, start, finish, flip):
    def step(i, _):
        t, g = i // GROUPS, i % GROUPS
        for h in range(2):
            total = start(t, g, h)
            for b in range(7):
                taps = [48 - (7 * a + b) if flip else 7 * a + b for a in range(7)]
                weights = weight_rows(weight_ref, g, taps)
                for row in range(22):
                    x = p_ref[t, g, pl.ds(row * PITCH + 5 + b + 8 * h, 8), :]
                    for a in range(7):
                        r = row - a
                        if 0 <= r < TE:
                            total[r] = total[r] + weights[a] * x
            finish(t, g, h, total)
        return _

    lax.fori_loop(0, 2 * GROUPS, step, 0)


def gelu_pair(hidden):
    square = hidden * hidden
    bent = jnp.tanh(gelu_root * hidden * (1.0 + gelu_cubic * square))
    half = 0.5 * (1.0 + bent)
    slope = half + 0.5 * hidden * (1.0 - bent * bent) * (gelu_root * (1.0 + 3.0 * gelu_cubic * square))
    return hidden * half, slope


def front_kernel(
    neighbours_ref,
    field_ref,
    land_ref,
    cot_ref,
    n1_ref,
    n2_ref,
    w1_ref,
    w2_ref,
    depth_weight_ref,
    depth_bias_ref,
    gain_ref,
    shift_ref,
    up_ref,
    up_bias_ref,
    down_ref,
    cg_ref,
    keep_ref,
    send_ref,
    g1_ref,
    g2_ref,
    p_ref,
    rn_ref,
    rw_ref,
    weight_ref,
    y_ref,
    z_ref,
    r_ref,
    normed_ref,
    normed_t_ref,
    gated_ref,
    gated_t_ref,
    ng_ref,
    dw_ref,
    up_bias_sum_ref,
):
    core0 = lax.axis_index("narrow") % 2 == 0
    p_ref[...] = jnp.zeros(p_ref.shape, f32)
    mask = land_mask(land_ref[...].reshape(2 * TE, TE))
    for s in range(2):
        cells = field_ref[s].reshape(TE * TE, C).astype(f32)
        place_centre(cells * mask[s * TE * TE : (s + 1) * TE * TE], s, p_ref)
    gated = cot_ref[...].reshape(CELLS, C).astype(f32) * mask
    gated_ref[...] = jnp.zeros(gated_ref.shape, bf16)
    gated_ref[:, 0:C] = gated.astype(bf16)
    gated_t_ref[...] = gated_ref[...].T
    down_bias = jnp.sum(gated, axis=0, keepdims=True)
    place_borders(neighbours_ref, n1_ref, n2_ref, w1_ref, w2_ref, p_ref, rn_ref, rw_ref)

    weight_ref[...] = jnp.zeros(weight_ref.shape, f32)
    weight_ref[0:49, 0:C] = depth_weight_ref[...]
    weight_ref[49:50, 0:C] = depth_bias_ref[...]

    def start(t, g, h):
        return weight_rows(weight_ref, g, [49]) * TE

    def finish(t, g, h, rows):
        for r in range(TE):
            at = pl.ds(t * TE * TE + r * TE + 8 * h, 8)
            y_ref[at, pl.ds(pl.multiple_of(g * 128, 128), 128)] = rows[r]

    convolve(p_ref, weight_ref, start, finish, False)

    normed_ref[...] = jnp.zeros(normed_ref.shape, bf16)
    step_rows = 64

    def norm(i, _):
        at = pl.ds(pl.multiple_of(i * step_rows, step_rows), step_rows)
        conv = y_ref[at, 0:C]
        mean = jnp.sum(conv, axis=1, keepdims=True) * (1.0 / C)
        dev = conv - mean
        var = jnp.sum(dev * dev, axis=1, keepdims=True) * (1.0 / C)
        rstd = lax.rsqrt(var + epsilon)
        zhat = dev * rstd
        z_ref[at, :] = zhat
        r_ref[at, :] = jnp.broadcast_to(rstd, (step_rows, 128))
        normed_ref[at, 0:C] = (zhat * gain_ref[...] + shift_ref[...]).astype(bf16)
        return _

    lax.fori_loop(0, CELLS // step_rows, norm, 0)
    normed_t_ref[...] = normed_ref[...].T

    for l in range(EXTRA, TILES):
        keep_ref[l] = jnp.zeros((8, 128), f32)
        send_ref[l] = jnp.zeros((8, 128), bf16)

    def hidden_chunk(lo, width, lane_tile, first):
        at = pl.ds(lo, width)
        up = up_ref[:, at]
        h = jnp.dot(normed_ref[:, 0:C], up, preferred_element_type=f32) + up_bias_ref[:, at]
        act, slope = gelu_pair(h)
        ag = jnp.dot(gated_ref[:, 0:C], down_ref[:, at], preferred_element_type=f32)
        hg = ag * slope
        hgb = hg.astype(bf16)
        dg = jnp.dot(gated_t_ref[0:C, :], act.astype(bf16), preferred_element_type=f32)
        ug = jnp.dot(normed_t_ref[0:C, :], hgb, preferred_element_type=f32)
        ng = lax.dot_general(hgb, up, (((1,), (1,)), ((), ())), preferred_element_type=f32)
        if first:
            ng_ref[...] = ng
        else:
            ng_ref[...] += ng
        up_bias_sum_ref[:, at] = jnp.sum(hgb.astype(f32), axis=0, keepdims=True)
        keep = jnp.where(core0, ug, dg)
        send = jnp.where(core0, dg, ug).astype(bf16)
        for k in range((width + 127) // 128):
            w = min(128, width - 128 * k)
            for i in range(C // 8):
                kt = keep[8 * i : 8 * i + 8, 128 * k : 128 * k + w]
                st = send[8 * i : 8 * i + 8, 128 * k : 128 * k + w]
                l = (lane_tile + k) * (C // 8) + i
                if w < 128:
                    keep_ref[l] = jnp.zeros((8, 128), f32)
                    send_ref[l] = jnp.zeros((8, 128), bf16)
                keep_ref[l, :, 0:w] = kt
                send_ref[l, :, 0:w] = st

    ng_ref[...] = jnp.zeros(ng_ref.shape, f32)

    def more(i, _):
        hidden_chunk(pl.multiple_of(i * 256, 256), 256, 2 * i, False)
        return _

    lax.fori_loop(0, 6, more, 0)
    hidden_chunk(1536, 64, 12, False)

    y_ref[...] = jnp.zeros(y_ref.shape, f32)

    def back(i, sums):
        at = pl.ds(pl.multiple_of(i * step_rows, step_rows), step_rows)
        ng = ng_ref[at, :]
        zhat = z_ref[at, :]
        rstd = r_ref[at, 0:1]
        q = ng * gain_ref[...]
        a = jnp.sum(q, axis=1, keepdims=True) * (1.0 / C)
        b = jnp.sum(q * zhat, axis=1, keepdims=True) * (1.0 / C)
        cg = (rstd * (q - a - zhat * b)).astype(bf16)
        t = i // 4
        cg_ref[t, pl.ds((i % 4) * 4, 4)] = cg.reshape(4, TE, C)
        wide = cg.astype(f32)
        y_ref[at, 0:C] = wide
        return (
            sums[0] + jnp.sum(ng * zhat, axis=0, keepdims=True),
            sums[1] + jnp.sum(ng, axis=0, keepdims=True),
            sums[2] + jnp.sum(wide, axis=0, keepdims=True),
        )

    zero = jnp.zeros((1, C), f32)
    gain_sum, shift_sum, bias_sum = lax.fori_loop(0, CELLS // step_rows, back, (zero, zero, zero))

    def tile_rows(s, row):
        at = s * TE * TE + row * TE
        return y_ref[at : at + 3 * TE, 0:C]

    pack_narrow(tile_rows, core0, g1_ref, g2_ref)

    dw_ref[...] = jnp.zeros(dw_ref.shape, f32)

    def taps(i, _):
        t, g = i // GROUPS, i % GROUPS
        for h in range(2):
            cg = [
                y_ref[
                    pl.ds(t * TE * TE + r * TE + 8 * h, 8),
                    pl.ds(pl.multiple_of(g * 128, 128), 128),
                ]
                for r in range(TE)
            ]
            for b in range(7):
                total = [None] * 7
                for row in range(22):
                    x = p_ref[t, g, pl.ds(row * PITCH + 5 + b + 8 * h, 8), :]
                    for a in range(7):
                        r = row - a
                        if 0 <= r < TE:
                            term = x * cg[r]
                            total[a] = term if total[a] is None else total[a] + term
                for a in range(7):
                    dw_ref[g, 7 * a + b] += total[a]
        return _

    lax.fori_loop(0, 2 * GROUPS, taps, 0)

    for g in range(GROUPS):
        w = group_width(g)
        tap_sums = jnp.sum(dw_ref[g], axis=1)
        for k in range(0, 48, 8):
            keep_ref[EXTRA + g * 8 + k // 8] = tap_sums[k : k + 8]
        tail = EXTRA + g * 8 + 6
        keep_ref[tail, 0:1, :] = tap_sums[48:49]
        keep_ref[tail, 1:2, 0:w] = bias_sum[:, lanes(g)]
        keep_ref[tail, 2:3, 0:w] = gain_sum[:, lanes(g)]
        keep_ref[tail, 3:4, 0:w] = shift_sum[:, lanes(g)]
        keep_ref[tail, 4:5, 0:w] = down_bias[:, lanes(g)]
    for l in range(HT):
        w = min(128, HID - 128 * l)
        keep_ref[EXTRA + 32 + l // 8, l % 8 : l % 8 + 1, 0:w] = up_bias_sum_ref[:, 128 * l : 128 * l + w]


def back_kernel(
    neighbours_ref,
    cg_ref,
    land_ref,
    cot_ref,
    n1_ref,
    n2_ref,
    w1_ref,
    w2_ref,
    depth_weight_ref,
    out_ref,
    p_ref,
    rn_ref,
    rw_ref,
    weight_ref,
    y_ref,
):
    p_ref[...] = jnp.zeros(p_ref.shape, f32)
    for s in range(2):
        place_centre(cg_ref[s].reshape(TE * TE, C).astype(f32), s, p_ref)
    mask = land_mask(land_ref[...].reshape(2 * TE, TE))
    place_borders(neighbours_ref, n1_ref, n2_ref, w1_ref, w2_ref, p_ref, rn_ref, rw_ref)
    weight_ref[...] = jnp.zeros(weight_ref.shape, f32)
    weight_ref[0:49, 0:C] = depth_weight_ref[...]
    y_ref[...] = jnp.zeros(y_ref.shape, f32)
    y_ref[:, 0:C] = cot_ref[...].reshape(CELLS, C).astype(f32) * mask

    def place(t, g, h, r):
        return (
            pl.ds(t * TE * TE + r * TE + 8 * h, 8),
            pl.ds(pl.multiple_of(g * 128, 128), 128),
        )

    def start(t, g, h):
        return [y_ref[place(t, g, h, r)] for r in range(TE)]

    def finish(t, g, h, rows):
        for r in range(TE):
            y_ref[place(t, g, h, r)] = rows[r]

    convolve(p_ref, weight_ref, start, finish, True)
    out_ref[...] = (y_ref[:, 0:C] * mask).astype(bf16).reshape(2, TE, TE, C)


def params():
    return pltpu.CompilerParams(vmem_limit_bytes=48 * 1024 * 1024)


P_SCRATCH = pltpu.VMEM((2, GROUPS, 22 * PITCH, 128), f32)
RN_SCRATCH = pltpu.VMEM((2, 2, GROUPS, 48, 128), f32)
RW_SCRATCH = pltpu.VMEM((2, 2, GROUPS, 80, 128), f32)
W_SCRATCH = pltpu.VMEM((56, CP), f32)
Y_SCRATCH = pltpu.VMEM((CELLS, CP), f32)


def swap_pairs(kind):
    axis, offset = kind
    pairs = []
    for w in range(32):
        for n in range(4):
            if axis == "narrow":
                up = (n - offset) % 2 == 0
                other = (w, (n + (1 if up else -1)) % 4)
            else:
                up = (w - offset) % 2 == 0
                other = ((w + (1 if up else -1)) % 32, n)
            pairs.append((w * 4 + n, other[0] * 4 + other[1]))
    return pairs


def swap(x, kind):
    return lax.ppermute(x, AXES, swap_pairs(kind))


def flip(x, mask):
    return lax.ppermute(x, AXES, [(i, i ^ mask) for i in range(128)])


STAGES = {
    "x1": (2, (1, 6)),
    "x2": (66, (6,)),
    "z1": (4, (2, 3)),
    "z2": (12, (3,)),
    "y1": (16, (4, 5)),
    "y2": (48, (5,)),
}
ORDERS = (
    ("x1", "y1", "z1", "x2", "y2", "z2"),
    ("y1", "z1", "x1", "y2", "z2", "x2"),
    ("z1", "x1", "y1", "z2", "x2", "y2"),
)
DEPTH = 2


def parity(me, bits):
    return sum((me >> bit) & 1 for bit in bits) & 1


def sum_over_chips(total, me, orders):
    size = total.shape[0] // len(orders)
    parts = [total[i * size : (i + 1) * size] for i in range(len(orders))]
    for stage in range(DEPTH):
        steps = []
        for order, part in zip(orders, parts):
            mask, bits = STAGES[order[stage]]
            high = parity(me, bits)
            half = part.shape[0] // 2
            send = lax.dynamic_slice_in_dim(part, (1 - high) * half, half, 0).astype(bf16)
            keep = lax.dynamic_slice_in_dim(part, high * half, half, 0)
            steps.append((keep, flip(send, mask)))
        parts = [keep + got.astype(f32) for keep, got in steps]
    for stage in range(DEPTH, 6):
        steps = []
        for order, part in zip(orders, parts):
            mine = part.astype(bf16)
            steps.append((mine, flip(mine, STAGES[order[stage]][0])))
        parts = [mine.astype(f32) + got.astype(f32) for mine, got in steps]
    parts = [part.astype(bf16) for part in parts]
    for stage in reversed(range(DEPTH)):
        steps = []
        for order, part in zip(orders, parts):
            mask, bits = STAGES[order[stage]]
            low = parity(me, bits) == 0
            got = flip(part, mask)
            steps.append(
                jnp.concatenate([jnp.where(low, part, got), jnp.where(low, got, part)], axis=0)
            )
        parts = steps
    return jnp.concatenate(parts, axis=0)


def local(
    field,
    cotangent,
    land,
    neighbours,
    depth_weight,
    depth_bias,
    ln_gain,
    ln_shift,
    up_weight,
    up_bias,
    down_weight,
):
    me = lax.axis_index("wide") * 4 + lax.axis_index("narrow")
    core = lax.axis_index("narrow") % 2
    narrow_shape = jax.ShapeDtypeStruct((2, 48, CP), bf16)
    wide_shape = jax.ShapeDtypeStruct((2, 80, CP), bf16)
    wide_scratch = [
        pltpu.VMEM((2, GROUPS, TE * TE, 128), f32),
        RN_SCRATCH,
        RW_SCRATCH,
    ]

    s1, s2 = pl.pallas_call(
        narrow_kernel,
        out_shape=(narrow_shape, narrow_shape),
        in_specs=[VMEM] * 2,
        out_specs=(VMEM, VMEM),
        scratch_shapes=[pltpu.VMEM((CELLS, C), f32)],
        compiler_params=params(),
        name="pack_rows",
    )(field, land)
    n1, n2 = swap(s1, ("narrow", 0)), swap(s2, ("narrow", 1))
    s1, s2 = pl.pallas_call(
        functools.partial(wide_kernel, True),
        out_shape=(wide_shape, wide_shape),
        in_specs=[VMEM] * 4,
        out_specs=(VMEM, VMEM),
        scratch_shapes=wide_scratch,
        compiler_params=params(),
        name="pack_columns",
    )(field, land, n1, n2)
    w1, w2 = swap(s1, ("wide", 0)), swap(s2, ("wide", 1))

    row = lambda v: v.reshape(1, -1)
    cg, keep, send, g1, g2 = pl.pallas_call(
        front_kernel,
        out_shape=(
            jax.ShapeDtypeStruct((2, TE, TE, C), bf16),
            jax.ShapeDtypeStruct((TILES, 8, 128), f32),
            jax.ShapeDtypeStruct((TILES, 8, 128), bf16),
            narrow_shape,
            narrow_shape,
        ),
        in_specs=[SMEM] + [VMEM] * 14,
        out_specs=(VMEM,) * 5,
        scratch_shapes=[
            P_SCRATCH,
            RN_SCRATCH,
            RW_SCRATCH,
            W_SCRATCH,
            Y_SCRATCH,
            pltpu.VMEM((CELLS, C), f32),
            pltpu.VMEM((CELLS, 128), f32),
            pltpu.VMEM((CELLS, CP), bf16),
            pltpu.VMEM((CP, CELLS), bf16),
            pltpu.VMEM((CELLS, CP), bf16),
            pltpu.VMEM((CP, CELLS), bf16),
            pltpu.VMEM((CELLS, C), f32),
            pltpu.VMEM((GROUPS, 49, 8, 128), f32),
            pltpu.VMEM((1, HID), f32),
        ],
        compiler_params=params(),
        name="front",
    )(
        neighbours,
        field,
        land,
        cotangent,
        n1,
        n2,
        w1,
        w2,
        depth_weight,
        row(depth_bias),
        row(ln_gain),
        row(ln_shift),
        up_weight,
        row(up_bias),
        down_weight.T,
    )

    got = flip(send, 1)
    n1, n2 = swap(g1, ("narrow", 0)), swap(g2, ("narrow", 1))
    s1, s2 = pl.pallas_call(
        functools.partial(wide_kernel, False),
        out_shape=(wide_shape, wide_shape),
        in_specs=[VMEM] * 3,
        out_specs=(VMEM, VMEM),
        scratch_shapes=wide_scratch,
        compiler_params=params(),
        name="pack_columns_back",
    )(cg, n1, n2)
    w1, w2 = swap(s1, ("wide", 0)), swap(s2, ("wide", 1))
    field_grad = pl.pallas_call(
        back_kernel,
        out_shape=jax.ShapeDtypeStruct((2, TE, TE, C), bf16),
        in_specs=[SMEM] + [VMEM] * 8,
        out_specs=VMEM,
        scratch_shapes=[P_SCRATCH, RN_SCRATCH, RW_SCRATCH, W_SCRATCH, Y_SCRATCH],
        compiler_params=params(),
        name="back",
    )(neighbours, cg, land, cotangent, n1, n2, w1, w2, depth_weight)

    mine = sum_over_chips(keep + got.astype(f32), me, ORDERS)
    theirs = flip(mine, 1)
    up_part = jnp.where(core == 0, mine, theirs)[0:EXTRA].astype(f32)
    down_part = jnp.where(core == 0, theirs, mine)[0:EXTRA].astype(f32)
    extra = mine[EXTRA:].astype(f32) + theirs[EXTRA:].astype(f32)

    def weight_grad(part):
        return jnp.transpose(part.reshape(HT, C, 128), (1, 0, 2)).reshape(C, HT * 128)[:, 0:HID]

    channel = jnp.transpose(extra[0:32].reshape(GROUPS, 64, 128), (1, 0, 2)).reshape(64, CP)[:, 0:C]
    up_bias_grad = extra[32:34].reshape(-1)[0:HID]
    return (
        field_grad,
        channel[0:49],
        channel[49],
        channel[50],
        channel[51],
        weight_grad(up_part),
        up_bias_grad,
        weight_grad(down_part).T,
        channel[52],
    )


def solution(mesh):
    return jax.shard_map(
        local,
        mesh=mesh,
        in_specs=(
            P(("wide", "narrow"), None, None, None),
            P(("wide", "narrow"), None, None, None),
            P(("wide", "narrow"), None, None),
            P(("wide", "narrow"), None),
            P(),
            P(),
            P(),
            P(),
            P(),
            P(),
            P(),
        ),
        out_specs=(P(("wide", "narrow"), None, None, None), P(), P(), P(), P(), P(), P(), P(), P()),
        check_vma=False,
    )
```

profile of v0, /device:TPU:1, one launch (start us, length us, event | category | flops | bytes accessed | tf_op | source)
XLA Modules:
  0.0 147.5 jit_solution(4525794262391154794)
XLA Ops:
  2.6 1.5 %collective-permute-start = (bf16[2,48,512]{2,1,0:T(8,128)(2,1)S(1)}, bf16[2,48,512]{2,1,0:T(8,128)(2,1)S(1)}, u32[]{:S(2)}, u32[]{:S(2)}) collective-permute-start(bf16[2,48,512]{2,1,0:T(8,128)(2,1)S(1)} %get-tuple-element.20), channel_id=1, source_target_pairs={{0,1},{1,0},{2,3},{3,2},{4,5},{5,4},{6,7},{7,6},{8,9},{9,8},{10,11... | collective-permute-start | bytes 294920 | tf_op jit(solution)/shard_map/ppermute | solution.py:495
  5.3 3.2 %collective-permute-done.1.refs_3_.n2_ref = bf16[2,48,512]{2,1,0:T(8,128)(2,1)S(1)} collective-permute-done((bf16[2,48,512]{2,1,0:T(8,128)(2,1)S(1)}, bf16[2,48,512]{2,1,0:T(8,128)(2,1)S(1)}, u32[]{:S(2)}, u32[]{:S(2)}) %collective-permute-start.1) | collective-permute-done | bytes 98336 | tf_op jit(solution)/shard_map/ppermute | solution.py:495
  9.0 1.8 %collective-permute-start.2 = (bf16[2,80,512]{2,1,0:T(8,128)(2,1)S(1)}, bf16[2,80,512]{2,1,0:T(8,128)(2,1)S(1)}, u32[]{:S(2)}, u32[]{:S(2)}) collective-permute-start(bf16[2,80,512]{2,1,0:T(8,128)(2,1)S(1)} %get-tuple-element.22), channel_id=1, source_target_pairs={{0,4},{1,5},{2,6},{3,7},{4,0},{5,1},{6,2},{7,3},{8,12},{9,13},{10,... | collective-permute-start | bytes 491528 | tf_op jit(solution)/shard_map/ppermute | solution.py:495
  10.8 7.2 %collective-permute-start.3 = (bf16[2,80,512]{2,1,0:T(8,128)(2,1)S(1)}, bf16[2,80,512]{2,1,0:T(8,128)(2,1)S(1)}, u32[]{:S(2)}, u32[]{:S(2)}) collective-permute-start(bf16[2,80,512]{2,1,0:T(8,128)(2,1)S(1)} %get-tuple-element.23), channel_id=1, source_target_pairs={{0,124},{1,125},{2,126},{3,127},{4,8},{5,9},{6,10},{7,11},{8,4},{9... | collective-permute-start | bytes 491528 | tf_op jit(solution)/shard_map/ppermute | solution.py:495
  18.6 3.2 %collective-permute-done.3.w2_ref = bf16[2,80,512]{2,1,0:T(8,128)(2,1)S(1)} collective-permute-done((bf16[2,80,512]{2,1,0:T(8,128)(2,1)S(1)}, bf16[2,80,512]{2,1,0:T(8,128)(2,1)S(1)}, u32[]{:S(2)}, u32[]{:S(2)}) %collective-permute-start.3) | collective-permute-done | bytes 163872 | tf_op jit(solution)/shard_map/ppermute | solution.py:495
  21.8 1.3 copy-done.2
  23.2 1.3 copy-done.3
  28.1 22.9 %front.1 = (bf16[2,16,16,400]{3,2,1,0:T(8,128)(2,1)S(1)}, f32[696,8,128]{2,1,0:T(8,128)}, bf16[696,8,128]{2,1,0:T(8,128)(2,1)}, bf16[2,48,512]{2,1,0:T(8,128)(2,1)S(1)}, bf16[2,48,512]{2,1,0:T(8,128)(2,1)S(1)}) custom-call(s32[2,8]{1,0:T(2,128)S(1)} %copy-done.8, bf16[2,16,16,400]{3,2,1,0:T(8,128)(2,1)S(1)} %copy-done, s32[2,16,16]{2,1,0:T(8,128)S(1)} %copy-done.6, ...), custom_call_target="tpu_custom_call" | custom-call | tf_op jit(solution)/shard_map/front/pallas_call | solution.py:600
  52.3 3.0 %collective-permute-done.8 = bf16[696,8,128]{2,1,0:T(8,128)(2,1)S(1)} collective-permute-done((bf16[696,8,128]{2,1,0:T(8,128)(2,1)}, bf16[696,8,128]{2,1,0:T(8,128)(2,1)S(1)}, u32[]{:S(2)}, u32[]{:S(2)}) %collective-permute-start.8) | collective-permute-done | bytes 1425440 | tf_op jit(solution)/shard_map/ppermute | solution.py:499
  55.3 2.0 %convert_add_fusion = f32[696,8,128]{2,1,0:T(8,128)S(1)} fusion(f32[696,8,128]{2,1,0:T(8,128)} %get-tuple-element.29, bf16[696,8,128]{2,1,0:T(8,128)(2,1)S(1)} %collective-permute-done.8), kind=kLoop, calls=%fused_computation | loop fusion | flops 1425408 | bytes 7127040 | tf_op jit(solution)/shard_map/add | solution.py:669
  60.1 5.6 %collective-permute-done.17 = bf16[116,8,128]{2,1,0:T(8,128)(2,1)} collective-permute-done((bf16[116,8,128]{2,1,0:T(8,128)(2,1)S(1)}, bf16[116,8,128]{2,1,0:T(8,128)(2,1)}, u32[]{:S(2)}, u32[]{:S(2)}) %collective-permute-start.17) | collective-permute-done | bytes 237600 | tf_op jit(solution)/shard_map/ppermute | solution.py:499
  68.6 2.1 %collective-permute-done.18 = bf16[58,8,128]{2,1,0:T(8,128)(2,1)S(1)} collective-permute-done((bf16[58,8,128]{2,1,0:T(8,128)(2,1)S(1)}, bf16[58,8,128]{2,1,0:T(8,128)(2,1)S(1)}, u32[]{:S(2)}, u32[]{:S(2)}) %collective-permute-start.18) | collective-permute-done | bytes 118816 | tf_op jit(solution)/shard_map/ppermute | solution.py:499
  70.9 1.3 collective-permute-start.27
  72.2 1.6 %collective-permute-start.11 = (bf16[58,8,128]{2,1,0:T(8,128)(2,1)S(1)}, bf16[58,8,128]{2,1,0:T(8,128)(2,1)S(1)}, u32[]{:S(2)}, u32[]{:S(2)}) collective-permute-start(bf16[58,8,128]{2,1,0:T(8,128)(2,1)S(1)} %add_convert_fusion.14), channel_id=1, source_target_pairs={{0,16},{1,17},{2,18},{3,19},{4,20},{5,21},{6,22},{7,23},{8,24},{9,... | collective-permute-start | bytes 356360 | tf_op jit(solution)/shard_map/ppermute | solution.py:499
  74.5 2.6 %collective-permute-start.20 = (bf16[58,8,128]{2,1,0:T(8,128)(2,1)S(1)}, bf16[58,8,128]{2,1,0:T(8,128)(2,1)S(1)}, u32[]{:S(2)}, u32[]{:S(2)}) collective-permute-start(bf16[58,8,128]{2,1,0:T(8,128)(2,1)S(1)} %add_convert_fusion.8), channel_id=1, source_target_pairs={{0,66},{1,67},{2,64},{3,65},{4,70},{5,71},{6,68},{7,69},{8,74},{9,... | collective-permute-start | bytes 356360 | tf_op jit(solution)/shard_map/ppermute | solution.py:499
  77.3 5.0 %collective-permute-start.12 = (bf16[58,8,128]{2,1,0:T(8,128)(2,1)S(1)}, bf16[58,8,128]{2,1,0:T(8,128)(2,1)S(1)}, u32[]{:S(2)}, u32[]{:S(2)}) collective-permute-start(bf16[58,8,128]{2,1,0:T(8,128)(2,1)S(1)} %add_convert_fusion.13), channel_id=1, source_target_pairs={{0,12},{1,13},{2,14},{3,15},{4,8},{5,9},{6,10},{7,11},{8,4},{9,5},... | collective-permute-start | bytes 356360 | tf_op jit(solution)/shard_map/ppermute | solution.py:499
  82.5 2.2 %collective-permute-start.29 = (bf16[58,8,128]{2,1,0:T(8,128)(2,1)S(1)}, bf16[58,8,128]{2,1,0:T(8,128)(2,1)S(1)}, u32[]{:S(2)}, u32[]{:S(2)}) collective-permute-start(bf16[58,8,128]{2,1,0:T(8,128)(2,1)S(1)} %add_convert_fusion.2), channel_id=1, source_target_pairs={{0,12},{1,13},{2,14},{3,15},{4,8},{5,9},{6,10},{7,11},{8,4},{9,5},... | collective-permute-start | bytes 356360 | tf_op jit(solution)/shard_map/ppermute | solution.py:499
  84.8 2.6 %collective-permute-start.13 = (bf16[58,8,128]{2,1,0:T(8,128)(2,1)S(1)}, bf16[58,8,128]{2,1,0:T(8,128)(2,1)S(1)}, u32[]{:S(2)}, u32[]{:S(2)}) collective-permute-start(bf16[58,8,128]{2,1,0:T(8,128)(2,1)S(1)} %add_convert_fusion.12), channel_id=1, source_target_pairs={{0,66},{1,67},{2,64},{3,65},{4,70},{5,71},{6,68},{7,69},{8,74},{9,... | collective-permute-start | bytes 356360 | tf_op jit(solution)/shard_map/ppermute | solution.py:499
  88.1 2.6 %collective-permute-start.30 = (bf16[58,8,128]{2,1,0:T(8,128)(2,1)S(1)}, bf16[58,8,128]{2,1,0:T(8,128)(2,1)S(1)}, u32[]{:S(2)}, u32[]{:S(2)}) collective-permute-start(bf16[58,8,128]{2,1,0:T(8,128)(2,1)S(1)} %add_convert_fusion.1), channel_id=1, source_target_pairs={{0,66},{1,67},{2,64},{3,65},{4,70},{5,71},{6,68},{7,69},{8,74},{9,... | collective-permute-start | bytes 356360 | tf_op jit(solution)/shard_map/ppermute | solution.py:499
  90.7 2.9 %collective-permute-start.14 = (bf16[58,8,128]{2,1,0:T(8,128)(2,1)S(1)}, bf16[58,8,128]{2,1,0:T(8,128)(2,1)S(1)}, u32[]{:S(2)}, u32[]{:S(2)}) collective-permute-start(bf16[58,8,128]{2,1,0:T(8,128)(2,1)S(1)} %add_convert_fusion.11), channel_id=1, source_target_pairs={{0,48},{1,49},{2,50},{3,51},{4,52},{5,53},{6,54},{7,55},{8,56},{9,... | collective-permute-start | bytes 356360 | tf_op jit(solution)/shard_map/ppermute | solution.py:499
  94.5 1.3 collective-permute-done.14
  96.0 2.4 %collective-permute-done.23 = bf16[58,8,128]{2,1,0:T(8,128)(2,1)S(1)} collective-permute-done((bf16[58,8,128]{2,1,0:T(8,128)(2,1)S(1)}, bf16[58,8,128]{2,1,0:T(8,128)(2,1)S(1)}, u32[]{:S(2)}, u32[]{:S(2)}) %collective-permute-start.23) | collective-permute-done | bytes 118816 | tf_op jit(solution)/shard_map/ppermute | solution.py:499
  98.6 1.5 %collective-permute-start.32 = (bf16[116,8,128]{2,1,0:T(8,128)(2,1)S(1)}, bf16[116,8,128]{2,1,0:T(8,128)(2,1)S(1)}, u32[]{:S(2)}, u32[]{:S(2)}) collective-permute-start(bf16[116,8,128]{2,1,0:T(8,128)(2,1)S(1)} %pad_maximum_fusion.2), channel_id=1, source_target_pairs={{0,16},{1,17},{2,18},{3,19},{4,20},{5,21},{6,22},{7,23},{8,24},{9,... | collective-permute-start | bytes 712712 | tf_op jit(solution)/shard_map/ppermute | solution.py:499
  100.2 3.5 %collective-permute-done.24 = bf16[116,8,128]{2,1,0:T(8,128)(2,1)S(1)} collective-permute-done((bf16[116,8,128]{2,1,0:T(8,128)(2,1)S(1)}, bf16[116,8,128]{2,1,0:T(8,128)(2,1)S(1)}, u32[]{:S(2)}, u32[]{:S(2)}) %collective-permute-start.24) | collective-permute-done | bytes 237600 | tf_op jit(solution)/shard_map/ppermute | solution.py:499
  107.5 7.2 %collective-permute-start.33 = (bf16[696,8,128]{2,1,0:T(8,128)(2,1)S(1)}, bf16[696,8,128]{2,1,0:T(8,128)(2,1)}, u32[]{:S(2)}, u32[]{:S(2)}) collective-permute-start(bf16[696,8,128]{2,1,0:T(8,128)(2,1)S(1)} %get-tuple-element.31), channel_id=1, source_target_pairs={{0,1},{1,0},{2,3},{3,2},{4,5},{5,4},{6,7},{7,6},{8,9},{9,8},{10,11... | collective-permute-start | bytes 4276232 | tf_op jit(solution)/shard_map/ppermute | solution.py:499
  115.0 2.6 %collective-permute-done.4.refs_1_.n1_ref = bf16[2,48,512]{2,1,0:T(8,128)(2,1)S(1)} collective-permute-done((bf16[2,48,512]{2,1,0:T(8,128)(2,1)S(1)}, bf16[2,48,512]{2,1,0:T(8,128)(2,1)S(1)}, u32[]{:S(2)}, u32[]{:S(2)}) %collective-permute-start.4) | collective-permute-done | bytes 98336 | tf_op jit(solution)/shard_map/ppermute | solution.py:495
  117.6 2.2 %collective-permute-done.5.refs_2_.n2_ref = bf16[2,48,512]{2,1,0:T(8,128)(2,1)S(1)} collective-permute-done((bf16[2,48,512]{2,1,0:T(8,128)(2,1)S(1)}, bf16[2,48,512]{2,1,0:T(8,128)(2,1)S(1)}, u32[]{:S(2)}, u32[]{:S(2)}) %collective-permute-start.5) | collective-permute-done | bytes 98336 | tf_op jit(solution)/shard_map/ppermute | solution.py:495
  120.7 4.0 %collective-permute-start.7 = (bf16[2,80,512]{2,1,0:T(8,128)(2,1)S(1)}, bf16[2,80,512]{2,1,0:T(8,128)(2,1)S(1)}, u32[]{:S(2)}, u32[]{:S(2)}) collective-permute-start(bf16[2,80,512]{2,1,0:T(8,128)(2,1)S(1)} %get-tuple-element.28), channel_id=1, source_target_pairs={{0,124},{1,125},{2,126},{3,127},{4,8},{5,9},{6,10},{7,11},{8,4},{9... | collective-permute-start | bytes 491528 | tf_op jit(solution)/shard_map/ppermute | solution.py:495
  125.6 5.8 %collective-permute-done.7.w2_ref = bf16[2,80,512]{2,1,0:T(8,128)(2,1)S(1)} collective-permute-done((bf16[2,80,512]{2,1,0:T(8,128)(2,1)S(1)}, bf16[2,80,512]{2,1,0:T(8,128)(2,1)S(1)}, u32[]{:S(2)}, u32[]{:S(2)}) %collective-permute-start.7) | collective-permute-done | bytes 163872 | tf_op jit(solution)/shard_map/ppermute | solution.py:495
  131.5 7.1 %back.1 = bf16[2,16,16,400]{3,2,1,0:T(8,128)(2,1)} custom-call(s32[2,8]{1,0:T(2,128)S(1)} %copy-done.9, bf16[2,16,16,400]{3,2,1,0:T(8,128)(2,1)S(1)} %get-tuple-element.24.refs_0_.cg_ref, s32[2,16,16]{2,1,0:T(8,128)S(1)} %copy-done.7, bf16[2,16,16,400]{3,2,1,0:T(8,128)(2,1)S(1)} %copy-done.1, bf16[2,48,512]{2,1,0:T(8,128)(2,1)S(1)} %collective-permute-done.4.refs_1_.n1_ref, ...), custom_call_target="tpu_custom_call" | custom-call | tf_op jit(solution)/shard_map/back/pallas_call | solution.py:659
  141.5 1.7 %broadcast_select_fusion = (bf16[650,8,128]{2,1,0:T(8,128)(2,1)S(1)}, bf16[650,8,128]{2,1,0:T(8,128)(2,1)S(1)}) fusion(pred[]{:T(512)S(6)} %eq.21, bf16[696,8,128]{2,1,0:T(8,128)(2,1)} %collective-permute-done.33, bf16[696,8,128]{2,1,0:T(8,128)(2,1)S(1)} %get-tuple-element.31), kind=kLoop, calls=%fused_computation.5 | loop fusion | flops 1331200 | bytes 5324801 | tf_op jit(solution)/shard_map/jit(_where)/select_n | solution.py:672
  144.7 2.7 %convert_bitcast_fusion = (f32[1600,400]{0,1:T(8,128)}, f32[400,1600]{1,0:T(8,128)}) fusion(bf16[400,1664]{1,0:T(8,128)(2,1)S(1)} %bitcast.39, bf16[400,1664]{1,0:T(8,128)(2,1)S(1)} %bitcast.38), kind=kLoop, calls=%fused_computation.1 | loop fusion | flops 1280000 | bytes 7680000 | tf_op jit(solution)/shard_map/transpose | solution.py:688
  (120 shorter events, 28.4 us)
Async XLA Ops:
  4.1 4.5 %collective-permute-start.1 = (bf16[2,48,512]{2,1,0:T(8,128)(2,1)S(1)}, bf16[2,48,512]{2,1,0:T(8,128)(2,1)S(1)}, u32[]{:S(2)}, u32[]{:S(2)}) collective-permute-start(bf16[2,48,512]{2,1,0:T(8,128)(2,1)S(1)} %get-tuple-element.21), channel_id=1, source_target_pairs={{0,3},{1,2},{2,1},{3,0},{4,7},{5,6},{6,5},{7,4},{8,11},{9,10},{10,... | collective-permute-start | bytes 294920 | tf_op jit(solution)/shard_map/ppermute | solution.py:495
  9.0 9.7 %collective-permute-start.2 = (bf16[2,80,512]{2,1,0:T(8,128)(2,1)S(1)}, bf16[2,80,512]{2,1,0:T(8,128)(2,1)S(1)}, u32[]{:S(2)}, u32[]{:S(2)}) collective-permute-start(bf16[2,80,512]{2,1,0:T(8,128)(2,1)S(1)} %get-tuple-element.22), channel_id=1, source_target_pairs={{0,4},{1,5},{2,6},{3,7},{4,0},{5,1},{6,2},{7,3},{8,12},{9,13},{10,... | collective-permute-start | bytes 491528 | tf_op jit(solution)/shard_map/ppermute | solution.py:495
  10.8 11.1 %collective-permute-start.3 = (bf16[2,80,512]{2,1,0:T(8,128)(2,1)S(1)}, bf16[2,80,512]{2,1,0:T(8,128)(2,1)S(1)}, u32[]{:S(2)}, u32[]{:S(2)}) collective-permute-start(bf16[2,80,512]{2,1,0:T(8,128)(2,1)S(1)} %get-tuple-element.23), channel_id=1, source_target_pairs={{0,124},{1,125},{2,126},{3,127},{4,8},{5,9},{6,10},{7,11},{8,4},{9... | collective-permute-start | bytes 491528 | tf_op jit(solution)/shard_map/ppermute | solution.py:495
  51.0 4.3 %collective-permute-start.8 = (bf16[696,8,128]{2,1,0:T(8,128)(2,1)}, bf16[696,8,128]{2,1,0:T(8,128)(2,1)S(1)}, u32[]{:S(2)}, u32[]{:S(2)}) collective-permute-start(bf16[696,8,128]{2,1,0:T(8,128)(2,1)} %get-tuple-element.30), channel_id=1, source_target_pairs={{0,1},{1,0},{2,3},{3,2},{4,5},{5,4},{6,7},{7,6},{8,9},{9,8},{10,11... | collective-permute-start | bytes 4276232 | tf_op jit(solution)/shard_map/ppermute | solution.py:499
  58.5 7.2 %collective-permute-start.17 = (bf16[116,8,128]{2,1,0:T(8,128)(2,1)S(1)}, bf16[116,8,128]{2,1,0:T(8,128)(2,1)}, u32[]{:S(2)}, u32[]{:S(2)}) collective-permute-start(bf16[116,8,128]{2,1,0:T(8,128)(2,1)S(1)} %dynamic-slice_convert_fusion.1), channel_id=1, source_target_pairs={{0,2},{1,3},{2,0},{3,1},{4,6},{5,7},{6,4},{7,5},{8,10},{9,11},{10,... | collective-permute-start | bytes 712712 | tf_op jit(solution)/shard_map/ppermute | solution.py:499
  59.8 7.2 %collective-permute-start.25 = (bf16[116,8,128]{2,1,0:T(8,128)(2,1)S(1)}, bf16[116,8,128]{2,1,0:T(8,128)(2,1)S(1)}, u32[]{:S(2)}, u32[]{:S(2)}) collective-permute-start(bf16[116,8,128]{2,1,0:T(8,128)(2,1)S(1)} %dynamic-slice_convert_fusion), channel_id=1, source_target_pairs={{0,16},{1,17},{2,18},{3,19},{4,20},{5,21},{6,22},{7,23},{8,24},{9,... | collective-permute-start | bytes 712712 | tf_op jit(solution)/shard_map/ppermute | solution.py:499
  60.0 7.2 %collective-permute-start.9 = (bf16[116,8,128]{2,1,0:T(8,128)(2,1)S(1)}, bf16[116,8,128]{2,1,0:T(8,128)(2,1)S(1)}, u32[]{:S(2)}, u32[]{:S(2)}) collective-permute-start(bf16[116,8,128]{2,1,0:T(8,128)(2,1)S(1)} %dynamic-slice_convert_fusion.2), channel_id=1, source_target_pairs={{0,4},{1,5},{2,6},{3,7},{4,0},{5,1},{6,2},{7,3},{8,12},{9,13},{10,... | collective-permute-start | bytes 712712 | tf_op jit(solution)/shard_map/ppermute | solution.py:499
  66.9 3.8 %collective-permute-start.18 = (bf16[58,8,128]{2,1,0:T(8,128)(2,1)S(1)}, bf16[58,8,128]{2,1,0:T(8,128)(2,1)S(1)}, u32[]{:S(2)}, u32[]{:S(2)}) collective-permute-start(bf16[58,8,128]{2,1,0:T(8,128)(2,1)S(1)} %dynamic-slice_convert_fusion.4), channel_id=1, source_target_pairs={{0,16},{1,17},{2,18},{3,19},{4,20},{5,21},{6,22},{7,23},{8,24},{9,... | collective-permute-start | bytes 356360 | tf_op jit(solution)/shard_map/ppermute | solution.py:499
  67.1 3.8 %collective-permute-start.26 = (bf16[58,8,128]{2,1,0:T(8,128)(2,1)S(1)}, bf16[58,8,128]{2,1,0:T(8,128)(2,1)S(1)}, u32[]{:S(2)}, u32[]{:S(2)}) collective-permute-start(bf16[58,8,128]{2,1,0:T(8,128)(2,1)S(1)} %dynamic-slice_convert_fusion.3), channel_id=1, source_target_pairs={{0,4},{1,5},{2,6},{3,7},{4,0},{5,1},{6,2},{7,3},{8,12},{9,13},{10,... | collective-permute-start | bytes 356360 | tf_op jit(solution)/shard_map/ppermute | solution.py:499
  67.3 4.9 %collective-permute-start.10 = (bf16[58,8,128]{2,1,0:T(8,128)(2,1)S(1)}, bf16[58,8,128]{2,1,0:T(8,128)(2,1)S(1)}, u32[]{:S(2)}, u32[]{:S(2)}) collective-permute-start(bf16[58,8,128]{2,1,0:T(8,128)(2,1)S(1)} %dynamic-slice_convert_fusion.5), channel_id=1, source_target_pairs={{0,2},{1,3},{2,0},{3,1},{4,6},{5,7},{6,4},{7,5},{8,10},{9,11},{10,... | collective-permute-start | bytes 356360 | tf_op jit(solution)/shard_map/ppermute | solution.py:499
  70.7 3.8 %collective-permute-start.19 = (bf16[58,8,128]{2,1,0:T(8,128)(2,1)S(1)}, bf16[58,8,128]{2,1,0:T(8,128)(2,1)S(1)}, u32[]{:S(2)}, u32[]{:S(2)}) collective-permute-start(bf16[58,8,128]{2,1,0:T(8,128)(2,1)S(1)} %add_convert_fusion.9), channel_id=1, source_target_pairs={{0,4},{1,5},{2,6},{3,7},{4,0},{5,1},{6,2},{7,3},{8,12},{9,13},{10,... | collective-permute-start | bytes 356360 | tf_op jit(solution)/shard_map/ppermute | solution.py:499
  70.9 6.2 %collective-permute-start.27 = (bf16[58,8,128]{2,1,0:T(8,128)(2,1)S(1)}, bf16[58,8,128]{2,1,0:T(8,128)(2,1)S(1)}, u32[]{:S(2)}, u32[]{:S(2)}) collective-permute-start(bf16[58,8,128]{2,1,0:T(8,128)(2,1)S(1)} %add_convert_fusion.4), channel_id=1, source_target_pairs={{0,2},{1,3},{2,0},{3,1},{4,6},{5,7},{6,4},{7,5},{8,10},{9,11},{10,... | collective-permute-start | bytes 356360 | tf_op jit(solution)/shard_map/ppermute | solution.py:499
  72.2 5.0 %collective-permute-start.11 = (bf16[58,8,128]{2,1,0:T(8,128)(2,1)S(1)}, bf16[58,8,128]{2,1,0:T(8,128)(2,1)S(1)}, u32[]{:S(2)}, u32[]{:S(2)}) collective-permute-start(bf16[58,8,128]{2,1,0:T(8,128)(2,1)S(1)} %add_convert_fusion.14), channel_id=1, source_target_pairs={{0,16},{1,17},{2,18},{3,19},{4,20},{5,21},{6,22},{7,23},{8,24},{9,... | collective-permute-start | bytes 356360 | tf_op jit(solution)/shard_map/ppermute | solution.py:499
  74.5 7.8 %collective-permute-start.20 = (bf16[58,8,128]{2,1,0:T(8,128)(2,1)S(1)}, bf16[58,8,128]{2,1,0:T(8,128)(2,1)S(1)}, u32[]{:S(2)}, u32[]{:S(2)}) collective-permute-start(bf16[58,8,128]{2,1,0:T(8,128)(2,1)S(1)} %add_convert_fusion.8), channel_id=1, source_target_pairs={{0,66},{1,67},{2,64},{3,65},{4,70},{5,71},{6,68},{7,69},{8,74},{9,... | collective-permute-start | bytes 356360 | tf_op jit(solution)/shard_map/ppermute | solution.py:499
  77.1 5.3 %collective-permute-start.28 = (bf16[58,8,128]{2,1,0:T(8,128)(2,1)S(1)}, bf16[58,8,128]{2,1,0:T(8,128)(2,1)S(1)}, u32[]{:S(2)}, u32[]{:S(2)}) collective-permute-start(bf16[58,8,128]{2,1,0:T(8,128)(2,1)S(1)} %add_convert_fusion.3), channel_id=1, source_target_pairs={{0,48},{1,49},{2,50},{3,51},{4,52},{5,53},{6,54},{7,55},{8,56},{9,... | collective-permute-start | bytes 356360 | tf_op jit(solution)/shard_map/ppermute | solution.py:499
  77.3 7.4 %collective-permute-start.12 = (bf16[58,8,128]{2,1,0:T(8,128)(2,1)S(1)}, bf16[58,8,128]{2,1,0:T(8,128)(2,1)S(1)}, u32[]{:S(2)}, u32[]{:S(2)}) collective-permute-start(bf16[58,8,128]{2,1,0:T(8,128)(2,1)S(1)} %add_convert_fusion.13), channel_id=1, source_target_pairs={{0,12},{1,13},{2,14},{3,15},{4,8},{5,9},{6,10},{7,11},{8,4},{9,5},... | collective-permute-start | bytes 356360 | tf_op jit(solution)/shard_map/ppermute | solution.py:499
  82.3 5.6 %collective-permute-start.21 = (bf16[58,8,128]{2,1,0:T(8,128)(2,1)S(1)}, bf16[58,8,128]{2,1,0:T(8,128)(2,1)S(1)}, u32[]{:S(2)}, u32[]{:S(2)}) collective-permute-start(bf16[58,8,128]{2,1,0:T(8,128)(2,1)S(1)} %add_convert_fusion.7), channel_id=1, source_target_pairs={{0,48},{1,49},{2,50},{3,51},{4,52},{5,53},{6,54},{7,55},{8,56},{9,... | collective-permute-start | bytes 356360 | tf_op jit(solution)/shard_map/ppermute | solution.py:499
  82.5 5.6 %collective-permute-start.29 = (bf16[58,8,128]{2,1,0:T(8,128)(2,1)S(1)}, bf16[58,8,128]{2,1,0:T(8,128)(2,1)S(1)}, u32[]{:S(2)}, u32[]{:S(2)}) collective-permute-start(bf16[58,8,128]{2,1,0:T(8,128)(2,1)S(1)} %add_convert_fusion.2), channel_id=1, source_target_pairs={{0,12},{1,13},{2,14},{3,15},{4,8},{5,9},{6,10},{7,11},{8,4},{9,5},... | collective-permute-start | bytes 356360 | tf_op jit(solution)/shard_map/ppermute | solution.py:499
  84.8 5.9 %collective-permute-start.13 = (bf16[58,8,128]{2,1,0:T(8,128)(2,1)S(1)}, bf16[58,8,128]{2,1,0:T(8,128)(2,1)S(1)}, u32[]{:S(2)}, u32[]{:S(2)}) collective-permute-start(bf16[58,8,128]{2,1,0:T(8,128)(2,1)S(1)} %add_convert_fusion.12), channel_id=1, source_target_pairs={{0,66},{1,67},{2,64},{3,65},{4,70},{5,71},{6,68},{7,69},{8,74},{9,... | collective-permute-start | bytes 356360 | tf_op jit(solution)/shard_map/ppermute | solution.py:499
  88.0 6.3 %collective-permute-start.22 = (bf16[58,8,128]{2,1,0:T(8,128)(2,1)S(1)}, bf16[58,8,128]{2,1,0:T(8,128)(2,1)S(1)}, u32[]{:S(2)}, u32[]{:S(2)}) collective-permute-start(bf16[58,8,128]{2,1,0:T(8,128)(2,1)S(1)} %add_convert_fusion.6), channel_id=1, source_target_pairs={{0,12},{1,13},{2,14},{3,15},{4,8},{5,9},{6,10},{7,11},{8,4},{9,5},... | collective-permute-start | bytes 356360 | tf_op jit(solution)/shard_map/ppermute | solution.py:499
  88.1 6.3 %collective-permute-start.30 = (bf16[58,8,128]{2,1,0:T(8,128)(2,1)S(1)}, bf16[58,8,128]{2,1,0:T(8,128)(2,1)S(1)}, u32[]{:S(2)}, u32[]{:S(2)}) collective-permute-start(bf16[58,8,128]{2,1,0:T(8,128)(2,1)S(1)} %add_convert_fusion.1), channel_id=1, source_target_pairs={{0,66},{1,67},{2,64},{3,65},{4,70},{5,71},{6,68},{7,69},{8,74},{9,... | collective-permute-start | bytes 356360 | tf_op jit(solution)/shard_map/ppermute | solution.py:499
  90.7 5.1 %collective-permute-start.14 = (bf16[58,8,128]{2,1,0:T(8,128)(2,1)S(1)}, bf16[58,8,128]{2,1,0:T(8,128)(2,1)S(1)}, u32[]{:S(2)}, u32[]{:S(2)}) collective-permute-start(bf16[58,8,128]{2,1,0:T(8,128)(2,1)S(1)} %add_convert_fusion.11), channel_id=1, source_target_pairs={{0,48},{1,49},{2,50},{3,51},{4,52},{5,53},{6,54},{7,55},{8,56},{9,... | collective-permute-start | bytes 356360 | tf_op jit(solution)/shard_map/ppermute | solution.py:499
  94.3 4.1 %collective-permute-start.23 = (bf16[58,8,128]{2,1,0:T(8,128)(2,1)S(1)}, bf16[58,8,128]{2,1,0:T(8,128)(2,1)S(1)}, u32[]{:S(2)}, u32[]{:S(2)}) collective-permute-start(bf16[58,8,128]{2,1,0:T(8,128)(2,1)S(1)} %add_convert_fusion.5), channel_id=1, source_target_pairs={{0,16},{1,17},{2,18},{3,19},{4,20},{5,21},{6,22},{7,23},{8,24},{9,... | collective-permute-start | bytes 356360 | tf_op jit(solution)/shard_map/ppermute | solution.py:499
  94.4 4.1 %collective-permute-start.31 = (bf16[58,8,128]{2,1,0:T(8,128)(2,1)S(1)}, bf16[58,8,128]{2,1,0:T(8,128)(2,1)S(1)}, u32[]{:S(2)}, u32[]{:S(2)}) collective-permute-start(bf16[58,8,128]{2,1,0:T(8,128)(2,1)S(1)} %add_convert_fusion), channel_id=1, source_target_pairs={{0,4},{1,5},{2,6},{3,7},{4,0},{5,1},{6,2},{7,3},{8,12},{9,13},{10,... | collective-permute-start | bytes 356360 | tf_op jit(solution)/shard_map/ppermute | solution.py:499
  95.9 4.2 %collective-permute-start.15 = (bf16[58,8,128]{2,1,0:T(8,128)(2,1)S(1)}, bf16[58,8,128]{2,1,0:T(8,128)(2,1)S(1)}, u32[]{:S(2)}, u32[]{:S(2)}) collective-permute-start(bf16[58,8,128]{2,1,0:T(8,128)(2,1)S(1)} %add_convert_fusion.10), channel_id=1, source_target_pairs={{0,2},{1,3},{2,0},{3,1},{4,6},{5,7},{6,4},{7,5},{8,10},{9,11},{10,... | collective-permute-start | bytes 356360 | tf_op jit(solution)/shard_map/ppermute | solution.py:499
  98.4 5.3 %collective-permute-start.24 = (bf16[116,8,128]{2,1,0:T(8,128)(2,1)S(1)}, bf16[116,8,128]{2,1,0:T(8,128)(2,1)S(1)}, u32[]{:S(2)}, u32[]{:S(2)}) collective-permute-start(bf16[116,8,128]{2,1,0:T(8,128)(2,1)S(1)} %pad_maximum_fusion.1), channel_id=1, source_target_pairs={{0,2},{1,3},{2,0},{3,1},{4,6},{5,7},{6,4},{7,5},{8,10},{9,11},{10,... | collective-permute-start | bytes 712712 | tf_op jit(solution)/shard_map/ppermute | solution.py:499
  98.6 6.6 %collective-permute-start.32 = (bf16[116,8,128]{2,1,0:T(8,128)(2,1)S(1)}, bf16[116,8,128]{2,1,0:T(8,128)(2,1)S(1)}, u32[]{:S(2)}, u32[]{:S(2)}) collective-permute-start(bf16[116,8,128]{2,1,0:T(8,128)(2,1)S(1)} %pad_maximum_fusion.2), channel_id=1, source_target_pairs={{0,16},{1,17},{2,18},{3,19},{4,20},{5,21},{6,22},{7,23},{8,24},{9,... | collective-permute-start | bytes 712712 | tf_op jit(solution)/shard_map/ppermute | solution.py:499
  100.2 6.5 %collective-permute-start.16 = (bf16[116,8,128]{2,1,0:T(8,128)(2,1)S(1)}, bf16[116,8,128]{2,1,0:T(8,128)(2,1)S(1)}, u32[]{:S(2)}, u32[]{:S(2)}) collective-permute-start(bf16[116,8,128]{2,1,0:T(8,128)(2,1)S(1)} %pad_maximum_fusion), channel_id=1, source_target_pairs={{0,4},{1,5},{2,6},{3,7},{4,0},{5,1},{6,2},{7,3},{8,12},{9,13},{10,... | collective-permute-start | bytes 712712 | tf_op jit(solution)/shard_map/ppermute | solution.py:499
  107.5 31.1 %collective-permute-start.33 = (bf16[696,8,128]{2,1,0:T(8,128)(2,1)S(1)}, bf16[696,8,128]{2,1,0:T(8,128)(2,1)}, u32[]{:S(2)}, u32[]{:S(2)}) collective-permute-start(bf16[696,8,128]{2,1,0:T(8,128)(2,1)S(1)} %get-tuple-element.31), channel_id=1, source_target_pairs={{0,1},{1,0},{2,3},{3,2},{4,5},{5,4},{6,7},{7,6},{8,9},{9,8},{10,11... | collective-permute-start | bytes 4276232 | tf_op jit(solution)/shard_map/ppermute | solution.py:499
  114.8 5.0 %collective-permute-start.5 = (bf16[2,48,512]{2,1,0:T(8,128)(2,1)S(1)}, bf16[2,48,512]{2,1,0:T(8,128)(2,1)S(1)}, u32[]{:S(2)}, u32[]{:S(2)}) collective-permute-start(bf16[2,48,512]{2,1,0:T(8,128)(2,1)S(1)} %get-tuple-element.26), channel_id=1, source_target_pairs={{0,3},{1,2},{2,1},{3,0},{4,7},{5,6},{6,5},{7,4},{8,11},{9,10},{10,... | collective-permute-start | bytes 294920 | tf_op jit(solution)/shard_map/ppermute | solution.py:495
  120.2 5.5 %collective-permute-start.6 = (bf16[2,80,512]{2,1,0:T(8,128)(2,1)S(1)}, bf16[2,80,512]{2,1,0:T(8,128)(2,1)S(1)}, u32[]{:S(2)}, u32[]{:S(2)}) collective-permute-start(bf16[2,80,512]{2,1,0:T(8,128)(2,1)S(1)} %get-tuple-element.27), channel_id=1, source_target_pairs={{0,4},{1,5},{2,6},{3,7},{4,0},{5,1},{6,2},{7,3},{8,12},{9,13},{10,... | collective-permute-start | bytes 491528 | tf_op jit(solution)/shard_map/ppermute | solution.py:495
  120.7 10.8 %collective-permute-start.7 = (bf16[2,80,512]{2,1,0:T(8,128)(2,1)S(1)}, bf16[2,80,512]{2,1,0:T(8,128)(2,1)S(1)}, u32[]{:S(2)}, u32[]{:S(2)}) collective-permute-start(bf16[2,80,512]{2,1,0:T(8,128)(2,1)S(1)} %get-tuple-element.28), channel_id=1, source_target_pairs={{0,124},{1,125},{2,126},{3,127},{4,8},{5,9},{6,10},{7,11},{8,4},{9... | collective-permute-start | bytes 491528 | tf_op jit(solution)/shard_map/ppermute | solution.py:495
  (16 other events, 112.5 us)
where the time goes:
time: 148 us; the launch traced here: 147 us
  starting transfers between devices  50.9 us (34%)
  waiting for transfers between devices  40.5 us (27%)
  Pallas kernels  31 us (21%)
  local copies, waits for them, and re-layouts  13.5 us (9%)
  other arithmetic  10.6 us (7%)
    ppermute x26, starting transfers between devices, flip(): return lax.ppermute(x, AXES, [(i, i ^ mask) for i in range(128)])  34.4 us
    pallas_call x1, Pallas kernels, local(): pl.pallas_call(front_kernel, out_shape=(jax.ShapeDtypeStruct((2, TE, TE,...  22.9 us
    ppermute x26, waiting for transfers between devices, flip(): return lax.ppermute(x, AXES, [(i, i ^ mask) for i in range(128)])  22.5 us
    ppermute x8, waiting for transfers between devices, swap(): return lax.ppermute(x, AXES, swap_pairs(kind))  18 us
    ppermute x8, starting transfers between devices, swap(): return lax.ppermute(x, AXES, swap_pairs(kind))  16.5 us
    unnamed x30, local copies, waits for them, and re-layouts  9.71 us
    pallas_call x1, Pallas kernels, local(): pl.pallas_call(back_kernel, out_shape=jax.ShapeDtypeStruct((2, TE, TE, C)...  7.15 us
  transfers between devices with their start and end apart: 34, of which 18 were waited for; matrix products, arithmetic and copies ran while one was open for 2% of the time, Pallas kernels for 5%

commit v1 on v0

v1 whole, which is shorter than its diff:
```python
import functools

import jax
import jax.numpy as jnp
from jax import lax
from jax.experimental import pallas as pl
from jax.experimental.pallas import tpu as pltpu
from jax.sharding import PartitionSpec as P

epsilon = 1e-06
gelu_root = 0.7978845608028654
gelu_cubic = 0.044715

C = 400
CP = 512
HID = 1600
TE = 16
CELLS = 512
GROUPS = 4
HT = 13
PITCH = 32
ROWS = HT * C
EXTRA = 368
PARTS = 3
AXES = ("wide", "narrow")
f32 = jnp.float32
bf16 = jnp.bfloat16
VMEM = pl.BlockSpec(memory_space=pltpu.VMEM)
SMEM = pl.BlockSpec(memory_space=pltpu.SMEM)
ANY = pl.BlockSpec(memory_space=pl.ANY)


def group_width(g):
    return min(128, C - 128 * g)


def lanes(g):
    return slice(128 * g, 128 * g + group_width(g))


def land_mask(land):
    spread = jnp.broadcast_to(land.astype(f32)[:, :, None], (2 * TE, TE, C))
    return spread.reshape(CELLS, C)


def zero_lanes(ref):
    ref[...] = jnp.zeros(ref.shape, ref.dtype)


def pack_narrow(tile_rows, even, first_ref, second_ref):
    for ref in (first_ref, second_ref):
        zero_lanes(ref)
    for s in range(2):
        north = tile_rows(s, 0)
        south = tile_rows(s, TE - 3)
        first_ref[s, :, 0:C] = jnp.where(even, south, north).astype(bf16)
        second_ref[s, :, 0:C] = jnp.where(even, north, south).astype(bf16)


def narrow_kernel(field_ref, land_ref, first_ref, second_ref, rows_ref, cells_ref, sems):
    copies = [pltpu.make_async_copy(land_ref, cells_ref, sems.at[4])]
    for s in range(2):
        for k, row in enumerate((0, TE - 3)):
            copies.append(
                pltpu.make_async_copy(field_ref.at[s, pl.ds(row, 3)], rows_ref.at[s, k], sems.at[2 * s + k])
            )
    for copy in copies:
        copy.start()
    for copy in copies:
        copy.wait()

    def tile_rows(s, row):
        cells = rows_ref[s, 1 if row else 0].reshape(3 * TE, C).astype(f32)
        land = cells_ref[s, row : row + 3].astype(f32)
        return cells * jnp.broadcast_to(land[:, :, None], (3, TE, C)).reshape(3 * TE, C)

    pack_narrow(tile_rows, lax.axis_index("narrow") % 2 == 0, first_ref, second_ref)


def wide_kernel(masked, *refs):
    if masked:
        tiles_ref, land_ref, n1_ref, n2_ref, first_ref, second_ref, m_ref, r_ref, o_ref = refs
        mask = land_mask(land_ref[...].reshape(2 * TE, TE))
    else:
        tiles_ref, n1_ref, n2_ref, first_ref, second_ref, m_ref, r_ref, o_ref = refs
    n_even = lax.axis_index("narrow") % 2 == 0
    w_even = lax.axis_index("wide") % 2 == 0
    zero_lanes(o_ref)
    for s in range(2):
        cells = tiles_ref[s].reshape(TE * TE, C).astype(f32)
        if masked:
            cells = cells * mask[s * TE * TE : (s + 1) * TE * TE]
        one = n1_ref[s].astype(f32)
        two = n2_ref[s].astype(f32)
        from_north = jnp.where(n_even, two, one)
        from_south = jnp.where(n_even, one, two)
        for g in range(GROUPS):
            m_ref[s, g, :, 0 : group_width(g)] = cells[:, lanes(g)]
            r_ref[0, s, g] = from_north[:, 128 * g : 128 * g + 128]
            r_ref[1, s, g] = from_south[:, 128 * g : 128 * g + 128]
    for s in range(2):
        for g in range(GROUPS):
            w = group_width(g)
            for side in range(2):
                for c in range(3):
                    col = c + side * (TE - 3)
                    at = c * 22
                    o_ref[side, s, g, at : at + 3, :] = r_ref[0, s, g, pl.ds(col, 3, stride=TE), :]
                    o_ref[side, s, g, at + 3 : at + 19, 0:w] = m_ref[s, g, pl.ds(col, TE, stride=TE), 0:w]
                    o_ref[side, s, g, at + 19 : at + 22, :] = r_ref[1, s, g, pl.ds(col, 3, stride=TE), :]
            west = o_ref[0, s, g]
            east = o_ref[1, s, g]
            first_ref[s, :, 128 * g : 128 * g + 128] = jnp.where(w_even, east, west).astype(bf16)
            second_ref[s, :, 128 * g : 128 * g + 128] = jnp.where(w_even, west, east).astype(bf16)


def place_centre(cells, s, p_ref):
    for g in range(GROUPS):
        w = group_width(g)
        for r in range(TE):
            at = (r + 3) * PITCH + 8
            p_ref[s, g, at : at + TE, 0:w] = cells[r * TE : (r + 1) * TE, lanes(g)]


def place_rows(n1_ref, n2_ref, rn_ref):
    n_even = lax.axis_index("narrow") % 2 == 0
    for s in range(2):
        one = n1_ref[s].astype(f32)
        two = n2_ref[s].astype(f32)
        north = jnp.where(n_even, two, one)
        south = jnp.where(n_even, one, two)
        for g in range(GROUPS):
            at = slice(128 * g, 128 * g + 128)
            rn_ref[0, s, g] = north[:, at]
            rn_ref[1, s, g] = south[:, at]


def place_columns(w1_ref, w2_ref, rw_ref):
    w_even = lax.axis_index("wide") % 2 == 0
    for s in range(2):
        one = w1_ref[s].astype(f32)
        two = w2_ref[s].astype(f32)
        west = jnp.where(w_even, two, one)
        east = jnp.where(w_even, one, two)
        for g in range(GROUPS):
            at = slice(128 * g, 128 * g + 128)
            rw_ref[0, s, g] = west[:, at]
            rw_ref[1, s, g] = east[:, at]


def entry_of(neighbours_ref, t, d):
    e = neighbours_ref[t, d]
    near = jnp.maximum(e, 0)
    return e >= 0, near // 2, near % 2


def chosen(options, present):
    value = options[-1][1]
    for test, other in reversed(options[:-1]):
        value = jnp.where(test, other, value)
    return jnp.where(present, value, 0.0)


def here():
    return lax.axis_index("wide") * lax.axis_size("narrow") + lax.axis_index("narrow")


def border_rows(neighbours_ref, p_ref, rn_ref, t, g):
    for d in range(2):
        present, device, slot = entry_of(neighbours_ref, t, d)
        from_row = 3 + TE - 3 if d == 0 else 3
        to_row = 0 if d == 0 else 3 + TE
        for i in range(3):
            own = p_ref[slot, g, pl.ds((from_row + i) * PITCH + 8, TE), :]
            other = rn_ref[d, slot, g, pl.ds(i * TE, TE), :]
            p_ref[t, g, pl.ds((to_row + i) * PITCH + 8, TE), :] = chosen(
                [(device == here(), own), (None, other)], present
            )


def border_columns(neighbours_ref, p_ref, rn_ref, rw_ref, t, g, put):
    narrow = lax.axis_size("narrow")
    for d in range(2):
        present, device, slot = entry_of(neighbours_ref, t, 2 + d)
        from_col = 8 + TE - 3 if d == 0 else 8
        for c in range(3):
            own = p_ref[slot, g, pl.ds(3 * PITCH + from_col + c, TE, stride=PITCH), :]
            other = rw_ref[d, slot, g, pl.ds(c * 22 + 3, TE), :]
            put(d, c, 3, TE, chosen([(device == here(), own), (None, other)], present))
    for d in range(4):
        south, east = d // 2, d % 2
        present, device, slot = entry_of(neighbours_ref, t, 4 + d)
        same_w = device // narrow == lax.axis_index("wide")
        same_n = device % narrow == lax.axis_index("narrow")
        from_row = 3 if south else 3 + TE - 3
        to_row = 3 + TE if south else 0
        from_col = 8 if east else 8 + TE - 3
        for c in range(3):
            own = p_ref[slot, g, pl.ds(from_row * PITCH + from_col + c, 3, stride=PITCH), :]
            beyond = rn_ref[south, slot, g, pl.ds(from_col - 8 + c, 3, stride=TE), :]
            beside = rw_ref[east, slot, g, pl.ds(c * 22 + from_row, 3), :]
            across = rw_ref[east, slot, g, pl.ds(c * 22 + (19 if south else 0), 3), :]
            put(
                east,
                c,
                to_row,
                3,
                chosen(
                    [(device == here(), own), (same_w, beyond), (same_n, beside), (None, across)], present
                ),
            )


def column_in(p_ref, t, g):
    def put(side, c, row, count, value):
        at = row * PITCH + (8 + TE if side else 5) + c
        p_ref[t, g, pl.ds(at, count, stride=PITCH), :] = value

    return put


def each_group(body):
    def step(i, _):
        body(i // GROUPS, i % GROUPS)
        return _

    lax.fori_loop(0, 2 * GROUPS, step, 0)


def weight_rows(weight_ref, g, taps):
    at = pl.ds(pl.multiple_of(g * 128, 128), 128)
    return [jnp.broadcast_to(weight_ref[pl.ds(k, 1), at], (8, 128)) for k in taps]


def convolve(p_ref, weight_ref, start, finish, flip):
    def body(t, g):
        for h in range(2):
            total = start(t, g, h)
            for b in range(7):
                taps = [48 - (7 * a + b) if flip else 7 * a + b for a in range(7)]
                weights = weight_rows(weight_ref, g, taps)
                for row in range(22):
                    x = p_ref[t, g, pl.ds(row * PITCH + 5 + b + 8 * h, 8), :]
                    for a in range(7):
                        r = row - a
                        if 0 <= r < TE:
                            total[r] = total[r] + weights[a] * x
            finish(t, g, h, total)

    each_group(body)


def gelu_pair(hidden):
    square = hidden * hidden
    bent = jnp.tanh(gelu_root * hidden * (1.0 + gelu_cubic * square))
    half = 0.5 * (1.0 + bent)
    slope = half + 0.5 * hidden * (1.0 - bent * bent) * (gelu_root * (1.0 + 3.0 * gelu_cubic * square))
    return hidden * half, slope


def take_weights(weight_ref, depth_weight_ref):
    weight_ref[...] = jnp.zeros(weight_ref.shape, f32)
    weight_ref[0:49, 0:C] = depth_weight_ref[...]


def prep_kernel(
    neighbours_ref,
    field_ref,
    land_ref,
    cot_ref,
    n1_ref,
    n2_ref,
    depth_weight_ref,
    small_ref,
    up_ref,
    down_ref,
    p_ref,
    y_ref,
    gated_ref,
    gated_t_ref,
    down_bias_ref,
    up_out_ref,
    down_out_ref,
    rn_ref,
    weight_ref,
    taps_ref,
    cot_in_ref,
    sems,
):
    copies = [
        pltpu.make_async_copy(depth_weight_ref, taps_ref, sems.at[0]),
        pltpu.make_async_copy(cot_ref, cot_in_ref, sems.at[1]),
        pltpu.make_async_copy(up_ref, up_out_ref, sems.at[2]),
        pltpu.make_async_copy(down_ref, down_out_ref, sems.at[3]),
    ]
    for copy in copies:
        copy.start()
    p_ref[...] = jnp.zeros(p_ref.shape, f32)
    mask = land_mask(land_ref[...].reshape(2 * TE, TE))
    for s in range(2):
        cells = field_ref[s].reshape(TE * TE, C).astype(f32)
        place_centre(cells * mask[s * TE * TE : (s + 1) * TE * TE], s, p_ref)
    place_rows(n1_ref, n2_ref, rn_ref)
    each_group(lambda t, g: border_rows(neighbours_ref, p_ref, rn_ref, t, g))
    copies[0].wait()
    take_weights(weight_ref, taps_ref)
    weight_ref[49:50, 0:C] = small_ref[0:1, 0:C]

    def start(t, g, h):
        return weight_rows(weight_ref, g, [49]) * TE

    def finish(t, g, h, rows):
        for r in range(TE):
            y_ref[t, g, pl.ds(r * TE + 8 * h, 8), :] = rows[r]

    convolve(p_ref, weight_ref, start, finish, False)

    copies[1].wait()
    gated = cot_in_ref[...].reshape(CELLS, C).astype(f32) * mask
    gated_ref[...] = jnp.zeros(gated_ref.shape, bf16)
    gated_ref[:, 0:C] = gated.astype(bf16)
    gated_t_ref[...] = gated_ref[...].T
    down_bias_ref[...] = jnp.sum(gated, axis=0, keepdims=True)
    copies[2].wait()
    copies[3].wait()


def front_kernel(
    neighbours_ref,
    n1_ref,
    n2_ref,
    w1_ref,
    w2_ref,
    p_ref,
    y_in_ref,
    gated_ref,
    gated_t_ref,
    depth_weight_ref,
    small_ref,
    up_ref,
    down_ref,
    keep_ref,
    send_ref,
    ng_ref,
    z_ref,
    r_ref,
    up_bias_sum_ref,
    border_ref,
    rn_ref,
    rw_ref,
    weight_ref,
    y_ref,
    normed_ref,
    normed_t_ref,
):
    core0 = lax.axis_index("narrow") % 2 == 0
    place_rows(n1_ref, n2_ref, rn_ref)
    place_columns(w1_ref, w2_ref, rw_ref)
    take_weights(weight_ref, depth_weight_ref)
    y_ref[...] = y_in_ref[...]

    def sides(t, g):
        def put(side, c, row, count, value):
            border_ref[t, g, pl.ds((side * 3 + c) * 24 + row, count), :] = value

        border_columns(neighbours_ref, p_ref, rn_ref, rw_ref, t, g, put)
        at = pl.ds(pl.multiple_of(g * 128, 128), 128)
        for side in range(2):
            for out in range(3):
                col = out + side * (TE - 3)
                total = y_ref[t, g, pl.ds(col, TE, stride=TE), :]
                for c in range(3):
                    b = (19 + c if side else c) - col
                    if 0 <= b < 7:
                        for a in range(7):
                            cells = border_ref[t, g, pl.ds((side * 3 + c) * 24 + a, TE), :]
                            total = total + weight_ref[pl.ds(7 * a + b, 1), at] * cells
                y_ref[t, g, pl.ds(col, TE, stride=TE), :] = total

    each_group(sides)

    normed_ref[...] = jnp.zeros(normed_ref.shape, bf16)
    step_rows = 64

    def norm(i, _):
        at = pl.ds(pl.multiple_of(i * step_rows, step_rows), step_rows)
        inside = pl.ds(pl.multiple_of((i % 4) * step_rows, step_rows), step_rows)
        conv = jnp.concatenate([y_ref[i // 4, g, inside, :] for g in range(GROUPS)], axis=1)[:, 0:C]
        mean = jnp.sum(conv, axis=1, keepdims=True) * (1.0 / C)
        dev = conv - mean
        var = jnp.sum(dev * dev, axis=1, keepdims=True) * (1.0 / C)
        rstd = lax.rsqrt(var + epsilon)
        zhat = dev * rstd
        z_ref[at, :] = zhat
        r_ref[at, :] = jnp.broadcast_to(rstd, (step_rows, 128))
        normed_ref[at, 0:C] = (zhat * small_ref[1:2, 0:C] + small_ref[2:3, 0:C]).astype(bf16)
        return _

    lax.fori_loop(0, CELLS // step_rows, norm, 0)
    normed_t_ref[...] = normed_ref[...].T

    def hidden_chunk(lo, width, lane_tile):
        at = pl.ds(lo, width)
        up = up_ref[:, at]
        h = jnp.dot(normed_ref[:, 0:C], up, preferred_element_type=f32) + small_ref[3:4, at]
        act, slope = gelu_pair(h)
        ag = jnp.dot(gated_ref[:, 0:C], down_ref[:, at], preferred_element_type=f32)
        hg = ag * slope
        hgb = hg.astype(bf16)
        dg = jnp.dot(gated_t_ref[0:C, :], act.astype(bf16), preferred_element_type=f32)
        ug = jnp.dot(normed_t_ref[0:C, :], hgb, preferred_element_type=f32)
        ng_ref[...] += lax.dot_general(hgb, up, (((1,), (1,)), ((), ())), preferred_element_type=f32)
        up_bias_sum_ref[:, at] = jnp.sum(hgb.astype(f32), axis=0, keepdims=True)
        keep = jnp.where(core0, ug, dg)
        send = jnp.where(core0, dg, ug).astype(bf16)
        for k in range((width + 127) // 128):
            w = min(128, width - 128 * k)
            rows = pl.ds(pl.multiple_of((lane_tile + k) * C, C), C)
            if w < 128:
                keep_ref[rows, :] = jnp.zeros((C, 128), f32)
                send_ref[rows, :] = jnp.zeros((C, 128), bf16)
            keep_ref[rows, 0:w] = keep[:, 128 * k : 128 * k + w]
            send_ref[rows, 0:w] = send[:, 128 * k : 128 * k + w]

    ng_ref[...] = jnp.zeros(ng_ref.shape, f32)

    def more(i, _):
        hidden_chunk(pl.multiple_of(i * 256, 256), 256, 2 * i)
        return _

    lax.fori_loop(0, 6, more, 0)
    hidden_chunk(1536, 64, 12)


def grad_kernel(
    ng_ref,
    z_ref,
    r_ref,
    small_ref,
    p_in_ref,
    border_ref,
    up_bias_sum_ref,
    down_bias_ref,
    cg_ref,
    g1_ref,
    g2_ref,
    extra_ref,
    p_ref,
    y_ref,
    dw_ref,
):
    y_ref[...] = jnp.zeros(y_ref.shape, f32)
    step_rows = 64

    def back(i, sums):
        at = pl.ds(pl.multiple_of(i * step_rows, step_rows), step_rows)
        ng = ng_ref[at, :]
        zhat = z_ref[at, :]
        rstd = r_ref[at, 0:1]
        q = ng * small_ref[1:2, 0:C]
        a = jnp.sum(q, axis=1, keepdims=True) * (1.0 / C)
        b = jnp.sum(q * zhat, axis=1, keepdims=True) * (1.0 / C)
        cg = (rstd * (q - a - zhat * b)).astype(bf16)
        cg_ref[i // 4, pl.ds((i % 4) * 4, 4)] = cg.reshape(4, TE, C)
        wide = cg.astype(f32)
        y_ref[at, 0:C] = wide
        return (
            sums[0] + jnp.sum(ng * zhat, axis=0, keepdims=True),
            sums[1] + jnp.sum(ng, axis=0, keepdims=True),
            sums[2] + jnp.sum(wide, axis=0, keepdims=True),
        )

    zero = jnp.zeros((1, C), f32)
    gain_sum, shift_sum, bias_sum = lax.fori_loop(0, CELLS // step_rows, back, (zero, zero, zero))

    def tile_rows(s, row):
        at = s * TE * TE + row * TE
        return y_ref[at : at + 3 * TE, 0:C]

    pack_narrow(tile_rows, lax.axis_index("narrow") % 2 == 0, g1_ref, g2_ref)

    p_ref[...] = p_in_ref[...]
    dw_ref[...] = jnp.zeros(dw_ref.shape, f32)

    def taps(t, g):
        put = column_in(p_ref, t, g)
        for side in range(2):
            for c in range(3):
                put(side, c, 0, 22, border_ref[t, g, pl.ds((side * 3 + c) * 24, 22), :])
        for h in range(2):
            cg = [
                y_ref[
                    pl.ds(t * TE * TE + r * TE + 8 * h, 8),
                    pl.ds(pl.multiple_of(g * 128, 128), 128),
                ]
                for r in range(TE)
            ]
            for b in range(7):
                total = [None] * 7
                for row in range(22):
                    x = p_ref[t, g, pl.ds(row * PITCH + 5 + b + 8 * h, 8), :]
                    for a in range(7):
                        r = row - a
                        if 0 <= r < TE:
                            term = x * cg[r]
                            total[a] = term if total[a] is None else total[a] + term
                for a in range(7):
                    dw_ref[g, 7 * a + b] += total[a]

    each_group(taps)

    extra_ref[...] = jnp.zeros(extra_ref.shape, f32)
    for g in range(GROUPS):
        w = group_width(g)
        extra_ref[g * 64 : g * 64 + 49, :] = jnp.sum(dw_ref[g], axis=1)
        extra_ref[g * 64 + 49 : g * 64 + 50, 0:w] = bias_sum[:, lanes(g)]
        extra_ref[g * 64 + 50 : g * 64 + 51, 0:w] = gain_sum[:, lanes(g)]
        extra_ref[g * 64 + 51 : g * 64 + 52, 0:w] = shift_sum[:, lanes(g)]
        extra_ref[g * 64 + 52 : g * 64 + 53, 0:w] = down_bias_ref[:, lanes(g)]
    for l in range(HT):
        w = min(128, HID - 128 * l)
        extra_ref[256 + l : 257 + l, 0:w] = up_bias_sum_ref[:, 128 * l : 128 * l + w]


def split_kernel(keep_ref, got_ref, extra_ref, *refs):
    me = here()
    size = (ROWS + EXTRA) // PARTS
    half = size // 2
    for i in range(PARTS):
        send_ref, mine_ref = refs[i], refs[PARTS + i]
        high = parity(me, STAGES[ORDERS[i][0]][1])
        for j in range(2):
            lo = i * size + j * half
            inner = min(half, ROWS - lo)

            def value(a, b):
                return keep_ref[a:b, :] + got_ref[a:b, :].astype(f32)

            def store(ref):
                ref[0:inner, :] = value(lo, lo + inner).astype(ref.dtype)
                if inner < half:
                    ref[inner:half, :] = extra_ref[0 : half - inner, :].astype(ref.dtype)

            pl.when(high == j)(functools.partial(store, mine_ref))
            pl.when(high != j)(functools.partial(store, send_ref))


def unpack_kernel(mine_ref, theirs_ref, up_ref, down_ref, channel_ref, up_bias_ref):
    core0 = lax.axis_index("narrow") % 2 == 0
    for l in range(HT):
        w = min(128, HID - 128 * l)
        rows = slice(l * C, l * C + C)
        one = mine_ref[rows, :].astype(f32)
        two = theirs_ref[rows, :].astype(f32)
        up_ref[:, 128 * l : 128 * l + w] = jnp.where(core0, one, two)[:, 0:w]
        down_ref[:, 128 * l : 128 * l + w] = jnp.where(core0, two, one)[:, 0:w]
    extra = mine_ref[ROWS:, :].astype(f32) + theirs_ref[ROWS:, :].astype(f32)
    for g in range(GROUPS):
        channel_ref[:, lanes(g)] = extra[g * 64 : g * 64 + 56, 0 : group_width(g)]
    up_bias_ref[...] = extra[256:272]


def back_kernel(
    neighbours_ref,
    cg_ref,
    land_ref,
    cot_ref,
    n1_ref,
    n2_ref,
    w1_ref,
    w2_ref,
    depth_weight_ref,
    out_ref,
    p_ref,
    rn_ref,
    rw_ref,
    weight_ref,
    y_ref,
):
    p_ref[...] = jnp.zeros(p_ref.shape, f32)
    for s in range(2):
        place_centre(cg_ref[s].reshape(TE * TE, C).astype(f32), s, p_ref)
    mask = land_mask(land_ref[...].reshape(2 * TE, TE))
    place_rows(n1_ref, n2_ref, rn_ref)
    place_columns(w1_ref, w2_ref, rw_ref)

    def borders(t, g):
        border_rows(neighbours_ref, p_ref, rn_ref, t, g)
        border_columns(neighbours_ref, p_ref, rn_ref, rw_ref, t, g, column_in(p_ref, t, g))

    each_group(borders)
    take_weights(weight_ref, depth_weight_ref)
    y_ref[...] = jnp.zeros(y_ref.shape, f32)
    y_ref[:, 0:C] = cot_ref[...].reshape(CELLS, C).astype(f32) * mask

    def place(t, g, h, r):
        return (
            pl.ds(t * TE * TE + r * TE + 8 * h, 8),
            pl.ds(pl.multiple_of(g * 128, 128), 128),
        )

    def start(t, g, h):
        return [y_ref[place(t, g, h, r)] for r in range(TE)]

    def finish(t, g, h, rows):
        for r in range(TE):
            y_ref[place(t, g, h, r)] = rows[r]

    convolve(p_ref, weight_ref, start, finish, True)
    out_ref[...] = (y_ref[:, 0:C] * mask).astype(bf16).reshape(2, TE, TE, C)


def params(size=16):
    return pltpu.CompilerParams(vmem_limit_bytes=size * 1024 * 1024)


P_SCRATCH = pltpu.VMEM((2, GROUPS, 22 * PITCH, 128), f32)
RN_SCRATCH = pltpu.VMEM((2, 2, GROUPS, 48, 128), f32)
RW_SCRATCH = pltpu.VMEM((2, 2, GROUPS, 80, 128), f32)
W_SCRATCH = pltpu.VMEM((56, CP), f32)
Y_SCRATCH = pltpu.VMEM((CELLS, CP), f32)


def swap_pairs(kind):
    axis, offset = kind
    pairs = []
    for w in range(32):
        for n in range(4):
            if axis == "narrow":
                up = (n - offset) % 2 == 0
                other = (w, (n + (1 if up else -1)) % 4)
            else:
                up = (w - offset) % 2 == 0
                other = ((w + (1 if up else -1)) % 32, n)
            pairs.append((w * 4 + n, other[0] * 4 + other[1]))
    return pairs


def swap(x, kind):
    return lax.ppermute(x, AXES, swap_pairs(kind))


def flip(x, mask):
    return lax.ppermute(x, AXES, [(i, i ^ mask) for i in range(128)])


STAGES = {
    "x1": (2, (1, 6)),
    "x2": (66, (6,)),
    "z1": (4, (2, 3)),
    "z2": (12, (3,)),
    "y1": (16, (4, 5)),
    "y2": (48, (5,)),
}
ORDERS = (
    ("x1", "y1", "z1", "x2", "y2", "z2"),
    ("y1", "z1", "x1", "y2", "z2", "x2"),
    ("z1", "x1", "y1", "z2", "x2", "y2"),
)
DEPTH = 2


def parity(me, bits):
    return sum((me >> bit) & 1 for bit in bits) & 1


def halved(part, order, stage, me):
    mask, bits = STAGES[order[stage]]
    high = parity(me, bits)
    half = part.shape[0] // 2
    send = lax.dynamic_slice_in_dim(part, (1 - high) * half, half, 0).astype(bf16)
    keep = lax.dynamic_slice_in_dim(part, high * half, half, 0)
    return keep + flip(send, mask).astype(f32)


def doubled(part, order, stage):
    mine = part.astype(bf16)
    return mine.astype(f32) + flip(mine, STAGES[order[stage]][0]).astype(f32)


def joined(part, order, stage, me):
    mask, bits = STAGES[order[stage]]
    low = parity(me, bits) == 0
    got = flip(part, mask)
    return jnp.concatenate([jnp.where(low, part, got), jnp.where(low, got, part)], axis=0)


def together(*values):
    return lax.optimization_barrier(values)


def local(
    field,
    cotangent,
    land,
    neighbours,
    depth_weight,
    depth_bias,
    ln_gain,
    ln_shift,
    up_weight,
    up_bias,
    down_weight,
):
    me = here()
    shape = jax.ShapeDtypeStruct
    narrow_shape = shape((2, 48, CP), bf16)
    wide_shape = shape((2, 80, CP), bf16)
    wide_scratch = [
        pltpu.VMEM((2, GROUPS, TE * TE, 128), f32),
        RN_SCRATCH,
        RW_SCRATCH,
    ]
    p_shape = shape((2, GROUPS, 22 * PITCH, 128), f32)
    small = jnp.stack(
        [jnp.pad(v, (0, HID - C)) for v in (depth_bias, ln_gain, ln_shift)] + [up_bias]
    )

    s1, s2 = pl.pallas_call(
        narrow_kernel,
        out_shape=(narrow_shape, narrow_shape),
        in_specs=[ANY] * 2,
        out_specs=(VMEM, VMEM),
        scratch_shapes=[
            pltpu.VMEM((2, 2, 3, TE, C), bf16),
            pltpu.VMEM((2, TE, TE), jnp.int32),
            pltpu.SemaphoreType.DMA((5,)),
        ],
        compiler_params=params(),
        name="pack_rows",
    )(field, land)
    n1, n2 = swap(s1, ("narrow", 0)), swap(s2, ("narrow", 1))
    s1, s2 = pl.pallas_call(
        functools.partial(wide_kernel, True),
        out_shape=(wide_shape, wide_shape),
        in_specs=[VMEM] * 4,
        out_specs=(VMEM, VMEM),
        scratch_shapes=wide_scratch,
        compiler_params=params(),
        name="pack_columns",
    )(field, land, n1, n2)
    s1, s2, n1, n2 = together(s1, s2, n1, n2)
    w2, w1 = swap(s2, ("wide", 1)), swap(s1, ("wide", 0))
    p, y, gated, gated_t, down_bias_sum, up_held, down_held = pl.pallas_call(
        prep_kernel,
        out_shape=(
            p_shape,
            shape((2, GROUPS, TE * TE, 128), f32),
            shape((CELLS, CP), bf16),
            shape((CP, CELLS), bf16),
            shape((1, C), f32),
            shape((C, HID), bf16),
            shape((C, HID), bf16),
        ),
        in_specs=[SMEM, VMEM, VMEM, ANY, VMEM, VMEM, ANY, VMEM, ANY, ANY],
        out_specs=(VMEM,) * 7,
        scratch_shapes=[
            RN_SCRATCH,
            W_SCRATCH,
            pltpu.VMEM((49, C), f32),
            pltpu.VMEM((2, TE, TE, C), bf16),
            pltpu.SemaphoreType.DMA((4,)),
        ],
        compiler_params=params(),
        cost_estimate=pl.CostEstimate(flops=10**9, bytes_accessed=16 * 10**6, transcendentals=0),
        name="prep",
    )(neighbours, field, land, cotangent, n1, n2, depth_weight, small, up_weight, down_weight.T)

    keep, send, ng, z, r, up_bias_sum, border = pl.pallas_call(
        front_kernel,
        out_shape=(
            shape((ROWS, 128), f32),
            shape((ROWS, 128), bf16),
            shape((CELLS, C), f32),
            shape((CELLS, C), f32),
            shape((CELLS, 128), f32),
            shape((1, HID), f32),
            shape((2, GROUPS, 6 * 24, 128), f32),
        ),
        in_specs=[SMEM] + [VMEM] * 12,
        out_specs=(VMEM,) * 7,
        scratch_shapes=[
            RN_SCRATCH,
            RW_SCRATCH,
            W_SCRATCH,
            pltpu.VMEM((2, GROUPS, TE * TE, 128), f32),
            pltpu.VMEM((CELLS, CP), bf16),
            pltpu.VMEM((CP, CELLS), bf16),
        ],
        compiler_params=params(20),
        name="front",
    )(
        neighbours,
        n1,
        n2,
        w1,
        w2,
        p,
        y,
        gated,
        gated_t,
        depth_weight,
        small,
        up_held,
        down_held,
    )

    got = flip(send, 1)
    cg, g1, g2, extra = pl.pallas_call(
        grad_kernel,
        out_shape=(
            shape((2, TE, TE, C), bf16),
            narrow_shape,
            narrow_shape,
            shape((EXTRA, 128), f32),
        ),
        in_specs=[VMEM] * 8,
        out_specs=(VMEM,) * 4,
        scratch_shapes=[
            pltpu.VMEM(p_shape.shape, f32),
            Y_SCRATCH,
            pltpu.VMEM((GROUPS, 49, 8, 128), f32),
        ],
        compiler_params=params(),
        cost_estimate=pl.CostEstimate(flops=10**9, bytes_accessed=16 * 10**6, transcendentals=0),
        name="grad",
    )(ng, z, r, small, p, border, up_bias_sum, down_bias_sum)

    half = (ROWS + EXTRA) // PARTS // 2
    pieces = pl.pallas_call(
        split_kernel,
        out_shape=(shape((half, 128), bf16),) * PARTS + (shape((half, 128), f32),) * PARTS,
        in_specs=[VMEM] * 3,
        out_specs=(VMEM,) * (2 * PARTS),
        compiler_params=params(),
        name="split",
    )(keep, got, extra)

    orders = list(enumerate(ORDERS))
    n1, n2 = swap(g1, ("narrow", 0)), swap(g2, ("narrow", 1))
    parts = [
        pieces[PARTS + i] + flip(pieces[i], STAGES[order[0]][0]).astype(f32) for i, order in orders
    ]
    parts, n1, n2 = together(parts, n1, n2)
    s1, s2 = pl.pallas_call(
        functools.partial(wide_kernel, False),
        out_shape=(wide_shape, wide_shape),
        in_specs=[VMEM] * 3,
        out_specs=(VMEM, VMEM),
        scratch_shapes=wide_scratch,
        compiler_params=params(),
        name="pack_columns_back",
    )(cg, n1, n2)
    parts, s1, s2 = together(parts, s1, s2)
    w2, w1 = swap(s2, ("wide", 1)), swap(s1, ("wide", 0))
    for stage in range(1, DEPTH):
        parts = [halved(parts[i], order, stage, me) for i, order in orders]
    for stage in range(DEPTH, 6):
        parts = [doubled(parts[i], order, stage) for i, order in orders]
        if stage == 4:
            parts, w1, w2 = together(parts, w1, w2)
    parts = [part.astype(bf16) for part in parts]
    for stage in reversed(range(1, DEPTH)):
        parts = [joined(parts[i], order, stage, me) for i, order in orders]
    parts, w1, w2 = together(parts, w1, w2)
    field_grad = pl.pallas_call(
        back_kernel,
        out_shape=shape((2, TE, TE, C), bf16),
        in_specs=[SMEM] + [VMEM] * 8,
        out_specs=VMEM,
        scratch_shapes=[P_SCRATCH, RN_SCRATCH, RW_SCRATCH, W_SCRATCH, Y_SCRATCH],
        compiler_params=params(),
        cost_estimate=pl.CostEstimate(flops=10**9, bytes_accessed=16 * 10**6, transcendentals=0),
        name="back",
    )(neighbours, cg, land, cotangent, n1, n2, w1, w2, depth_weight)
    parts = [joined(parts[i], order, 0, me) for i, order in orders]
    mine = jnp.concatenate(parts, axis=0)
    theirs = flip(mine, 1)
    up_grad, down_grad, channel, up_bias_grad = pl.pallas_call(
        unpack_kernel,
        out_shape=(
            shape((C, HID), f32),
            shape((C, HID), f32),
            shape((56, C), f32),
            shape((16, 128), f32),
        ),
        in_specs=[VMEM] * 2,
        out_specs=(VMEM,) * 4,
        compiler_params=params(),
        name="unpack",
    )(mine, theirs)
    return (
        field_grad,
        channel[0:49],
        channel[49],
        channel[50],
        channel[51],
        up_grad,
        up_bias_grad.reshape(-1)[0:HID],
        down_grad.T,
        channel[52],
    )


def solution(mesh):
    return jax.shard_map(
        local,
        mesh=mesh,
        in_specs=(
            P(("wide", "narrow"), None, None, None),
            P(("wide", "narrow"), None, None, None),
            P(("wide", "narrow"), None, None),
            P(("wide", "narrow"), None),
            P(),
            P(),
            P(),
            P(),
            P(),
            P(),
            P(),
        ),
        out_specs=(P(("wide", "narrow"), None, None, None), P(), P(), P(), P(), P(), P(), P(), P()),
        check_vma=False,
    )
```

time: 148 us -> 121 us (0.82)
  waiting for transfers between devices: 40.5 us -> 29 us
  other arithmetic: 10.6 us -> 1.37 us
  starting transfers between devices: 50.9 us -> 43.8 us
  Pallas kernels: 31 us -> 35.5 us
  local copies, waits for them, and re-layouts: 13.5 us -> 9.32 us
    ppermute x8, waiting for transfers between devices: 18 us -> 0.46 us  [swap(): return lax.ppermute(x, AXES, swap_pairs(kind))]
    ppermute x26, waiting for transfers between devices: 22.5 us -> 28.5 us  [flip(): return lax.ppermute(x, AXES, [(i, i ^ mask) for i in range(128)])]
    ppermute x26, starting transfers between devices: 34.4 us -> 28.8 us  [flip(): return lax.ppermute(x, AXES, [(i, i ^ mask) for i in range(128)])]
    unnamed x30 -> x20, local copies, waits for them, and re-layouts: 9.71 us -> 5.03 us
    pallas_call x2 -> x6, Pallas kernels: 30 us -> 34.3 us  [the longest x1 11.6 us: local(): pl.pallas_call(front_kernel, out_shape=(shape((ROWS, 128), f32), shape((R...]
    add x5 -> x6, other arithmetic: 4.29 us -> 0.29 us  [the longest x3 0.19 us: local(): pieces[PARTS + i] + flip(pieces[i], STAGES[order[0]][0]).astype(f32)]
    transpose x1 -> x0, other arithmetic: 2.73 us -> none  [local(): weight_grad(down_part)]
    reshape x5 -> x0, local copies, waits for them, and re-layouts: 2.16 us -> none  [the longest x2 0.85 us: weight_grad(): part.reshape(HT, C, 128)]
  transfers between devices with their start and end apart: 34 -> 34, of which waited for: 18 -> 14; matrix products, arithmetic and copies ran while one was open for 2% -> 3% of each run, Pallas kernels for 5% -> 16%
where the time goes in v1:
time: 121 us; the launch traced here: 120 us
  starting transfers between devices  43.8 us (36%)
  Pallas kernels  35.5 us (29%)
  waiting for transfers between devices  29 us (24%)
  local copies, waits for them, and re-layouts  9.32 us (8%)
  other arithmetic  1.37 us (1%)
    ppermute x26, starting transfers between devices, flip(): return lax.ppermute(x, AXES, [(i, i ^ mask) for i in range(128)])  28.8 us
    ppermute x26, waiting for transfers between devices, flip(): return lax.ppermute(x, AXES, [(i, i ^ mask) for i in range(128)])  28.5 us
    ppermute x8, starting transfers between devices, swap(): return lax.ppermute(x, AXES, swap_pairs(kind))  15.1 us
    pallas_call x1, Pallas kernels, local(): pl.pallas_call(front_kernel, out_shape=(shape((ROWS, 128), f32), shape((R...  11.6 us
    pallas_call x1, Pallas kernels, local(): pl.pallas_call(back_kernel, out_shape=shape((2, TE, TE, C), bf16), in_spe...  7.16 us
    pallas_call x1, Pallas kernels, local(): pl.pallas_call(prep_kernel, out_shape=(p_shape, shape((2, GROUPS, TE * TE...  6.63 us
    pallas_call x1, Pallas kernels, local(): pl.pallas_call(grad_kernel, out_shape=(shape((2, TE, TE, C), bf16), narro...  5.79 us
    unnamed x20, local copies, waits for them, and re-layouts  5.03 us
  transfers between devices with their start and end apart: 34, of which 14 were waited for; matrix products, arithmetic and copies ran while one was open for 3% of the time, Pallas kernels for 16%

profile of v1, /device:TPU:1, one launch (start us, length us, event | category | flops | bytes accessed | tf_op | source)
XLA Modules:
  0.0 120.1 jit_solution(4795711443695939889)
XLA Ops:
  2.8 1.5 %collective-permute-start = (bf16[2,48,512]{2,1,0:T(8,128)(2,1)S(1)}, bf16[2,48,512]{2,1,0:T(8,128)(2,1)S(1)}, u32[]{:S(2)}, u32[]{:S(2)}) collective-permute-start(bf16[2,48,512]{2,1,0:T(8,128)(2,1)S(1)} %get-tuple-element.67), channel_id=1, source_target_pairs={{0,1},{1,0},{2,3},{3,2},{4,5},{5,4},{6,7},{7,6},{8,9},{9,8},{10,11... | collective-permute-start | bytes 294920 | tf_op jit(solution)/shard_map/ppermute | solution.py:640
  4.3 1.3 %collective-permute-start.1 = (bf16[2,48,512]{2,1,0:T(8,128)(2,1)S(1)}, bf16[2,48,512]{2,1,0:T(8,128)(2,1)S(1)}, u32[]{:S(2)}, u32[]{:S(2)}) collective-permute-start(bf16[2,48,512]{2,1,0:T(8,128)(2,1)S(1)} %get-tuple-element.68), channel_id=1, source_target_pairs={{0,3},{1,2},{2,1},{3,0},{4,7},{5,6},{6,5},{7,4},{8,11},{9,10},{10,... | collective-permute-start | bytes 294920 | tf_op jit(solution)/shard_map/ppermute | solution.py:640
  9.2 1.8 %collective-permute-start.2 = (bf16[2,80,512]{2,1,0:T(8,128)(2,1)S(1)}, bf16[2,80,512]{2,1,0:T(8,128)(2,1)S(1)}, u32[]{:S(2)}, u32[]{:S(2)}) collective-permute-start(bf16[2,80,512]{2,1,0:T(8,128)(2,1)S(1)} %get-tuple-element.73), channel_id=1, source_target_pairs={{0,4},{1,5},{2,6},{3,7},{4,0},{5,1},{6,2},{7,3},{8,12},{9,13},{10,... | collective-permute-start | bytes 491528 | tf_op jit(solution)/shard_map/ppermute | solution.py:640
  11.0 7.2 %collective-permute-start.3 = (bf16[2,80,512]{2,1,0:T(8,128)(2,1)S(1)}, bf16[2,80,512]{2,1,0:T(8,128)(2,1)S(1)}, u32[]{:S(2)}, u32[]{:S(2)}) collective-permute-start(bf16[2,80,512]{2,1,0:T(8,128)(2,1)S(1)} %get-tuple-element.74), channel_id=1, source_target_pairs={{0,124},{1,125},{2,126},{3,127},{4,8},{5,9},{6,10},{7,11},{8,4},{9... | collective-permute-start | bytes 491528 | tf_op jit(solution)/shard_map/ppermute | solution.py:640
  18.3 1.3 %copy-done.2 = bf16[1600,400]{0,1:T(8,128)(2,1)S(1)} copy-done((bf16[1600,400]{0,1:T(8,128)(2,1)S(1)}, bf16[1600,400]{0,1:T(8,128)(2,1)}, u32[]{:S(2)}) %copy-start.2) | copy-done | bytes 1280024
  19.6 1.0 copy-done.3
  21.5 6.6 %prep.1 = (f32[2,4,704,128]{3,2,1,0:T(8,128)S(1)}, f32[2,4,256,128]{3,2,1,0:T(8,128)S(1)}, bf16[512,512]{1,0:T(8,128)(2,1)S(1)}, bf16[512,512]{1,0:T(8,128)(2,1)...) custom-call(s32[2,8]{1,0:T(2,128)S(1)} %copy-done.9, ...), custom_call_target="tpu_custom_call" | custom-call | flops 1000000000 | bytes 16000000 | tf_op jit(solution)/shard_map/prep/pallas_call | solution.py:744
  28.2 11.6 %front.1 = (f32[5200,128]{1,0:T(8,128)S(1)}, bf16[5200,128]{1,0:T(8,128)(2,1)S(1)}, f32[512,400]{1,0:T(8,128)S(1)}, f32[512,400]{1,0:T(8,128)S(1)}, f32[512,128]...) custom-call(s32[2,8]{1,0:T(2,128)S(1)} %copy-done.9, ...), custom_call_target="tpu_custom_call" | custom-call | tf_op jit(solution)/shard_map/front/pallas_call | solution.py:769
  40.6 5.8 %grad.1 = (bf16[2,16,16,400]{3,2,1,0:T(8,128)(2,1)S(1)}, bf16[2,48,512]{2,1,0:T(8,128)(2,1)S(1)}, bf16[2,48,512]{2,1,0:T(8,128)(2,1)S(1)}, f32[368,128]{1,0:T(8,128)S(1)}) custom-call(f32[512,400]{1,0:T(8,128)S(1)} %get-tuple-element.81.ng_ref, f32[512,400]{1,0:T(8,128)S(1)} %get-tuple-element.82.z_ref, f32[512,128]{1,0:T(8,128)S(1)} %get-tuple-element.83.r_ref, ...), custom_call_target="tpu_custom_call" | custom-call | flops 1000000000 | bytes 16000000 | tf_op jit(solution)/shard_map/grad/pallas_call | solution.py:809
  47.6 1.2 collective-permute-start.5
  48.8 5.4 %collective-permute-done.7 = bf16[928,128]{1,0:T(8,128)(2,1)S(1)} collective-permute-done((bf16[928,128]{1,0:T(8,128)(2,1)S(1)}, bf16[928,128]{1,0:T(8,128)(2,1)S(1)}, u32[]{:S(2)}, u32[]{:S(2)}) %collective-permute-start.7) | collective-permute-done | bytes 237600 | tf_op jit(solution)/shard_map/ppermute | solution.py:644
  55.0 1.9 %collective-permute-done.5 = bf16[928,128]{1,0:T(8,128)(2,1)S(1)} collective-permute-done((bf16[928,128]{1,0:T(8,128)(2,1)S(1)}, bf16[928,128]{1,0:T(8,128)(2,1)S(1)}, u32[]{:S(2)}, u32[]{:S(2)}) %collective-permute-start.5) | collective-permute-done | bytes 237600 | tf_op jit(solution)/shard_map/ppermute | solution.py:644
  57.9 1.3 %collective-permute-start.14 = (bf16[464,128]{1,0:T(8,128)(2,1)S(1)}, bf16[464,128]{1,0:T(8,128)(2,1)S(1)}, u32[]{:S(2)}, u32[]{:S(2)}) collective-permute-start(bf16[464,128]{1,0:T(8,128)(2,1)S(1)} %dynamic-slice_convert_fusion.1), channel_id=1, source_target_pairs={{0,4},{1,5},{2,6},{3,7},{4,0},{5,1},{6,2},{7,3},{8,12},{9,13},{10,... | collective-permute-start | bytes 356360 | tf_op jit(solution)/shard_map/ppermute | solution.py:644
  59.6 2.2 %collective-permute-start.23 = (bf16[2,80,512]{2,1,0:T(8,128)(2,1)S(1)}, bf16[2,80,512]{2,1,0:T(8,128)(2,1)S(1)}, u32[]{:S(2)}, u32[]{:S(2)}) collective-permute-start(bf16[2,80,512]{2,1,0:T(8,128)(2,1)S(1)} %get-tuple-element.110), channel_id=1, source_target_pairs={{0,124},{1,125},{2,126},{3,127},{4,8},{5,9},{6,10},{7,11},{8,4},{9... | collective-permute-start | bytes 491528 | tf_op jit(solution)/shard_map/ppermute | solution.py:640
  62.0 1.2 collective-permute-start.15
  63.3 1.2 %collective-permute-start.11 = (bf16[464,128]{1,0:T(8,128)(2,1)S(1)}, bf16[464,128]{1,0:T(8,128)(2,1)S(1)}, u32[]{:S(2)}, u32[]{:S(2)}) collective-permute-start(bf16[464,128]{1,0:T(8,128)(2,1)S(1)} %add_convert_fusion.11), channel_id=1, source_target_pairs={{0,4},{1,5},{2,6},{3,7},{4,0},{5,1},{6,2},{7,3},{8,12},{9,13},{10,... | collective-permute-start | bytes 356360 | tf_op jit(solution)/shard_map/ppermute | solution.py:644
  64.5 4.2 %collective-permute-done.19 = bf16[464,128]{1,0:T(8,128)(2,1)S(1)} collective-permute-done((bf16[464,128]{1,0:T(8,128)(2,1)S(1)}, bf16[464,128]{1,0:T(8,128)(2,1)S(1)}, u32[]{:S(2)}, u32[]{:S(2)}) %collective-permute-start.19) | collective-permute-done | bytes 118816 | tf_op jit(solution)/shard_map/ppermute | solution.py:644
  68.9 1.5 %collective-permute-start.16 = (bf16[464,128]{1,0:T(8,128)(2,1)S(1)}, bf16[464,128]{1,0:T(8,128)(2,1)S(1)}, u32[]{:S(2)}, u32[]{:S(2)}) collective-permute-start(bf16[464,128]{1,0:T(8,128)(2,1)S(1)} %add_convert_fusion.7), channel_id=1, source_target_pairs={{0,48},{1,49},{2,50},{3,51},{4,52},{5,53},{6,54},{7,55},{8,56},{9,... | collective-permute-start | bytes 356360 | tf_op jit(solution)/shard_map/ppermute | solution.py:644
  70.4 2.2 %collective-permute-start.12 = (bf16[464,128]{1,0:T(8,128)(2,1)S(1)}, bf16[464,128]{1,0:T(8,128)(2,1)S(1)}, u32[]{:S(2)}, u32[]{:S(2)}) collective-permute-start(bf16[464,128]{1,0:T(8,128)(2,1)S(1)} %add_convert_fusion.10), channel_id=1, source_target_pairs={{0,66},{1,67},{2,64},{3,65},{4,70},{5,71},{6,68},{7,69},{8,74},{9,... | collective-permute-start | bytes 356360 | tf_op jit(solution)/shard_map/ppermute | solution.py:644
  72.6 1.5 %collective-permute-done.20 = bf16[464,128]{1,0:T(8,128)(2,1)S(1)} collective-permute-done((bf16[464,128]{1,0:T(8,128)(2,1)S(1)}, bf16[464,128]{1,0:T(8,128)(2,1)S(1)}, u32[]{:S(2)}, u32[]{:S(2)}) %collective-permute-start.20) | collective-permute-done | bytes 118816 | tf_op jit(solution)/shard_map/ppermute | solution.py:644
  75.1 1.7 %collective-permute-start.17 = (bf16[464,128]{1,0:T(8,128)(2,1)S(1)}, bf16[464,128]{1,0:T(8,128)(2,1)S(1)}, u32[]{:S(2)}, u32[]{:S(2)}) collective-permute-start(bf16[464,128]{1,0:T(8,128)(2,1)S(1)} %add_convert_fusion.6), channel_id=1, source_target_pairs={{0,12},{1,13},{2,14},{3,15},{4,8},{5,9},{6,10},{7,11},{8,4},{9,5},... | collective-permute-start | bytes 356360 | tf_op jit(solution)/shard_map/ppermute | solution.py:644
  77.6 2.8 %collective-permute-done.21 = bf16[464,128]{1,0:T(8,128)(2,1)S(1)} collective-permute-done((bf16[464,128]{1,0:T(8,128)(2,1)S(1)}, bf16[464,128]{1,0:T(8,128)(2,1)S(1)}, u32[]{:S(2)}, u32[]{:S(2)}) %collective-permute-start.21) | collective-permute-done | bytes 118816 | tf_op jit(solution)/shard_map/ppermute | solution.py:644
  80.5 1.6 %collective-permute-done.13 = bf16[464,128]{1,0:T(8,128)(2,1)S(1)} collective-permute-done((bf16[464,128]{1,0:T(8,128)(2,1)S(1)}, bf16[464,128]{1,0:T(8,128)(2,1)S(1)}, u32[]{:S(2)}, u32[]{:S(2)}) %collective-permute-start.13) | collective-permute-done | bytes 118816 | tf_op jit(solution)/shard_map/ppermute | solution.py:644
  83.6 2.3 %collective-permute-start.24 = (bf16[464,128]{1,0:T(8,128)(2,1)S(1)}, bf16[464,128]{1,0:T(8,128)(2,1)S(1)}, u32[]{:S(2)}, u32[]{:S(2)}) collective-permute-start(bf16[464,128]{1,0:T(8,128)(2,1)S(1)} %convert_add_fusion.5), channel_id=1, source_target_pairs={{0,12},{1,13},{2,14},{3,15},{4,8},{5,9},{6,10},{7,11},{8,4},{9,5},... | collective-permute-start | bytes 356360 | tf_op jit(solution)/shard_map/ppermute | solution.py:644
  85.9 1.9 %collective-permute-done.28 = bf16[464,128]{1,0:T(8,128)(2,1)S(1)} collective-permute-done((bf16[464,128]{1,0:T(8,128)(2,1)S(1)}, bf16[464,128]{1,0:T(8,128)(2,1)S(1)}, u32[]{:S(2)}, u32[]{:S(2)}) %collective-permute-start.28) | collective-permute-done | bytes 118816 | tf_op jit(solution)/shard_map/ppermute | solution.py:644
  89.1 2.5 %collective-permute-done.29 = bf16[464,128]{1,0:T(8,128)(2,1)S(1)} collective-permute-done((bf16[464,128]{1,0:T(8,128)(2,1)S(1)}, bf16[464,128]{1,0:T(8,128)(2,1)S(1)}, u32[]{:S(2)}, u32[]{:S(2)}) %collective-permute-start.29) | collective-permute-done | bytes 118816 | tf_op jit(solution)/shard_map/ppermute | solution.py:644
  91.6 1.3 %collective-permute-done.27 = bf16[464,128]{1,0:T(8,128)(2,1)S(1)} collective-permute-done((bf16[464,128]{1,0:T(8,128)(2,1)S(1)}, bf16[464,128]{1,0:T(8,128)(2,1)S(1)}, u32[]{:S(2)}, u32[]{:S(2)}) %collective-permute-start.27) | collective-permute-done | bytes 118816 | tf_op jit(solution)/shard_map/ppermute | solution.py:644
  94.9 4.6 %collective-permute-done.30 = bf16[928,128]{1,0:T(8,128)(2,1)S(1)} collective-permute-done((bf16[928,128]{1,0:T(8,128)(2,1)S(1)}, bf16[928,128]{1,0:T(8,128)(2,1)S(1)}, u32[]{:S(2)}, u32[]{:S(2)}) %collective-permute-start.30) | collective-permute-done | bytes 237600 | tf_op jit(solution)/shard_map/ppermute | solution.py:644
  100.1 8.6 %collective-permute-start.33 = (bf16[5568,128]{1,0:T(8,128)(2,1)S(1)}, bf16[5568,128]{1,0:T(8,128)(2,1)S(1)}, u32[]{:S(2)}, u32[]{:S(2)}) collective-permute-start(bf16[5568,128]{1,0:T(8,128)(2,1)S(1)} %select_dynamic-update-slice_fusion.mine_ref), channel_id=1, source_target_pairs={{0,1},{1,0},{2,3},{3,2},{4,5},{5,4},{6,7},{7,6},{8,9},{9,8},{10,11... | collective-permute-start | bytes 4276232 | tf_op jit(solution)/shard_map/ppermute | solution.py:644
  108.7 7.2 %back.1 = bf16[2,16,16,400]{3,2,1,0:T(8,128)(2,1)} custom-call(s32[2,8]{1,0:T(2,128)S(1)} %copy-done.9, bf16[2,16,16,400]{3,2,1,0:T(8,128)(2,1)S(1)} %get-tuple-element.87.refs_0_.cg_ref, s32[2,16,16]{2,1,0:T(8,128)S(1)} %copy-done.8, bf16[2,16,16,400]{3,2,1,0:T(8,128)(2,1)S(1)} %copy-done.4, bf16[2,48,512]{2,1,0:T(8,128)(2,1)S(1)} %collective-permute-done.8.refs_1_.n1_ref, ...), custom_call_target="tpu_custom_call" | custom-call | flops 1000000000 | bytes 16000000 | tf_op jit(solution)/shard_map/back/pallas_call | solution.py:866
  115.8 2.8 %unpack.1 = (f32[400,1600]{1,0:T(8,128)}, f32[400,1600]{1,0:T(8,128)}, f32[56,400]{1,0:T(8,128)}, f32[16,128]{1,0:T(8,128)}) custom-call(bf16[5568,128]{1,0:T(8,128)(2,1)S(1)} %select_dynamic-update-slice_fusion.mine_ref, bf16[5568,128]{1,0:T(8,128)(2,1)S(1)} %collective-permute-done.33.theirs_ref), custom_call_target="tpu_custom_call" | custom-call | tf_op jit(solution)/shard_map/unpack/pallas_call | solution.py:879
  118.7 1.5 %fusion = (f32[1,400]{1,0:T(1,128)}, f32[1,400]{1,0:T(1,128)}, f32[1,400]{1,0:T(1,128)}, f32[1,400]{1,0:T(1,128)}) fusion(f32[56,400]{1,0:T(8,128)} %get-tuple-element.121), kind=kLoop, calls=%fused_computation.37 | loop fusion | bytes 12800 | tf_op jit(solution)/shard_map/slice | solution.py:901
  (106 shorter events, 18.5 us)
Async XLA Ops:
  2.8 5.6 %collective-permute-start = (bf16[2,48,512]{2,1,0:T(8,128)(2,1)S(1)}, bf16[2,48,512]{2,1,0:T(8,128)(2,1)S(1)}, u32[]{:S(2)}, u32[]{:S(2)}) collective-permute-start(bf16[2,48,512]{2,1,0:T(8,128)(2,1)S(1)} %get-tuple-element.67), channel_id=1, source_target_pairs={{0,1},{1,0},{2,3},{3,2},{4,5},{5,4},{6,7},{7,6},{8,9},{9,8},{10,11... | collective-permute-start | bytes 294920 | tf_op jit(solution)/shard_map/ppermute | solution.py:640
  4.3 4.5 %collective-permute-start.1 = (bf16[2,48,512]{2,1,0:T(8,128)(2,1)S(1)}, bf16[2,48,512]{2,1,0:T(8,128)(2,1)S(1)}, u32[]{:S(2)}, u32[]{:S(2)}) collective-permute-start(bf16[2,48,512]{2,1,0:T(8,128)(2,1)S(1)} %get-tuple-element.68), channel_id=1, source_target_pairs={{0,3},{1,2},{2,1},{3,0},{4,7},{5,6},{6,5},{7,4},{8,11},{9,10},{10,... | collective-permute-start | bytes 294920 | tf_op jit(solution)/shard_map/ppermute | solution.py:640
  9.2 18.9 %collective-permute-start.2 = (bf16[2,80,512]{2,1,0:T(8,128)(2,1)S(1)}, bf16[2,80,512]{2,1,0:T(8,128)(2,1)S(1)}, u32[]{:S(2)}, u32[]{:S(2)}) collective-permute-start(bf16[2,80,512]{2,1,0:T(8,128)(2,1)S(1)} %get-tuple-element.73), channel_id=1, source_target_pairs={{0,4},{1,5},{2,6},{3,7},{4,0},{5,1},{6,2},{7,3},{8,12},{9,13},{10,... | collective-permute-start | bytes 491528 | tf_op jit(solution)/shard_map/ppermute | solution.py:640
  11.0 17.1 %collective-permute-start.3 = (bf16[2,80,512]{2,1,0:T(8,128)(2,1)S(1)}, bf16[2,80,512]{2,1,0:T(8,128)(2,1)S(1)}, u32[]{:S(2)}, u32[]{:S(2)}) collective-permute-start(bf16[2,80,512]{2,1,0:T(8,128)(2,1)S(1)} %get-tuple-element.74), channel_id=1, source_target_pairs={{0,124},{1,125},{2,126},{3,127},{4,8},{5,9},{6,10},{7,11},{8,4},{9... | collective-permute-start | bytes 491528 | tf_op jit(solution)/shard_map/ppermute | solution.py:640
  39.8 6.6 %collective-permute-start.4 = (bf16[5200,128]{1,0:T(8,128)(2,1)S(1)}, bf16[5200,128]{1,0:T(8,128)(2,1)S(1)}, u32[]{:S(2)}, u32[]{:S(2)}) collective-permute-start(bf16[5200,128]{1,0:T(8,128)(2,1)S(1)} %get-tuple-element.89), channel_id=1, source_target_pairs={{0,1},{1,0},{2,3},{3,2},{4,5},{5,4},{6,7},{7,6},{8,9},{9,8},{10,11... | collective-permute-start | bytes 3993608 | tf_op jit(solution)/shard_map/ppermute | solution.py:644
  46.7 7.5 %collective-permute-start.7 = (bf16[928,128]{1,0:T(8,128)(2,1)S(1)}, bf16[928,128]{1,0:T(8,128)(2,1)S(1)}, u32[]{:S(2)}, u32[]{:S(2)}) collective-permute-start(bf16[928,128]{1,0:T(8,128)(2,1)S(1)} %get-tuple-element.96), channel_id=1, source_target_pairs={{0,4},{1,5},{2,6},{3,7},{4,0},{5,1},{6,2},{7,3},{8,12},{9,13},{10,... | collective-permute-start | bytes 712712 | tf_op jit(solution)/shard_map/ppermute | solution.py:644
  46.8 10.2 %collective-permute-start.8 = (bf16[2,48,512]{2,1,0:T(8,128)(2,1)S(1)}, bf16[2,48,512]{2,1,0:T(8,128)(2,1)S(1)}, u32[]{:S(2)}, u32[]{:S(2)}) collective-permute-start(bf16[2,48,512]{2,1,0:T(8,128)(2,1)S(1)} %get-tuple-element.97), channel_id=1, source_target_pairs={{0,1},{1,0},{2,3},{3,2},{4,5},{5,4},{6,7},{7,6},{8,9},{9,8},{10,11... | collective-permute-start | bytes 294920 | tf_op jit(solution)/shard_map/ppermute | solution.py:640
  46.9 10.1 %collective-permute-start.9 = (bf16[2,48,512]{2,1,0:T(8,128)(2,1)S(1)}, bf16[2,48,512]{2,1,0:T(8,128)(2,1)S(1)}, u32[]{:S(2)}, u32[]{:S(2)}) collective-permute-start(bf16[2,48,512]{2,1,0:T(8,128)(2,1)S(1)} %get-tuple-element.98), channel_id=1, source_target_pairs={{0,3},{1,2},{2,1},{3,0},{4,7},{5,6},{6,5},{7,4},{8,11},{9,10},{10,... | collective-permute-start | bytes 294920 | tf_op jit(solution)/shard_map/ppermute | solution.py:640
  47.6 7.3 %collective-permute-start.6 = (bf16[928,128]{1,0:T(8,128)(2,1)S(1)}, bf16[928,128]{1,0:T(8,128)(2,1)S(1)}, u32[]{:S(2)}, u32[]{:S(2)}) collective-permute-start(bf16[928,128]{1,0:T(8,128)(2,1)S(1)} %get-tuple-element.94), channel_id=1, source_target_pairs={{0,16},{1,17},{2,18},{3,19},{4,20},{5,21},{6,22},{7,23},{8,24},{9,... | collective-permute-start | bytes 712712 | tf_op jit(solution)/shard_map/ppermute | solution.py:644
  47.6 9.3 %collective-permute-start.5 = (bf16[928,128]{1,0:T(8,128)(2,1)S(1)}, bf16[928,128]{1,0:T(8,128)(2,1)S(1)}, u32[]{:S(2)}, u32[]{:S(2)}) collective-permute-start(bf16[928,128]{1,0:T(8,128)(2,1)S(1)} %get-tuple-element.92), channel_id=1, source_target_pairs={{0,2},{1,3},{2,0},{3,1},{4,6},{5,7},{6,4},{7,5},{8,10},{9,11},{10,... | collective-permute-start | bytes 712712 | tf_op jit(solution)/shard_map/ppermute | solution.py:644
  57.4 4.4 %collective-permute-start.18 = (bf16[464,128]{1,0:T(8,128)(2,1)S(1)}, bf16[464,128]{1,0:T(8,128)(2,1)S(1)}, u32[]{:S(2)}, u32[]{:S(2)}) collective-permute-start(bf16[464,128]{1,0:T(8,128)(2,1)S(1)} %dynamic-slice_convert_fusion), channel_id=1, source_target_pairs={{0,2},{1,3},{2,0},{3,1},{4,6},{5,7},{6,4},{7,5},{8,10},{9,11},{10,... | collective-permute-start | bytes 356360 | tf_op jit(solution)/shard_map/ppermute | solution.py:644
  57.9 4.1 %collective-permute-start.14 = (bf16[464,128]{1,0:T(8,128)(2,1)S(1)}, bf16[464,128]{1,0:T(8,128)(2,1)S(1)}, u32[]{:S(2)}, u32[]{:S(2)}) collective-permute-start(bf16[464,128]{1,0:T(8,128)(2,1)S(1)} %dynamic-slice_convert_fusion.1), channel_id=1, source_target_pairs={{0,4},{1,5},{2,6},{3,7},{4,0},{5,1},{6,2},{7,3},{8,12},{9,13},{10,... | collective-permute-start | bytes 356360 | tf_op jit(solution)/shard_map/ppermute | solution.py:644
  59.3 22.9 %collective-permute-start.22 = (bf16[2,80,512]{2,1,0:T(8,128)(2,1)S(1)}, bf16[2,80,512]{2,1,0:T(8,128)(2,1)S(1)}, u32[]{:S(2)}, u32[]{:S(2)}) collective-permute-start(bf16[2,80,512]{2,1,0:T(8,128)(2,1)S(1)} %get-tuple-element.109), channel_id=1, source_target_pairs={{0,4},{1,5},{2,6},{3,7},{4,0},{5,1},{6,2},{7,3},{8,12},{9,13},{10,... | collective-permute-start | bytes 491528 | tf_op jit(solution)/shard_map/ppermute | solution.py:640
  59.6 22.6 %collective-permute-start.23 = (bf16[2,80,512]{2,1,0:T(8,128)(2,1)S(1)}, bf16[2,80,512]{2,1,0:T(8,128)(2,1)S(1)}, u32[]{:S(2)}, u32[]{:S(2)}) collective-permute-start(bf16[2,80,512]{2,1,0:T(8,128)(2,1)S(1)} %get-tuple-element.110), channel_id=1, source_target_pairs={{0,124},{1,125},{2,126},{3,127},{4,8},{5,9},{6,10},{7,11},{8,4},{9... | collective-permute-start | bytes 491528 | tf_op jit(solution)/shard_map/ppermute | solution.py:640
  61.9 6.8 %collective-permute-start.19 = (bf16[464,128]{1,0:T(8,128)(2,1)S(1)}, bf16[464,128]{1,0:T(8,128)(2,1)S(1)}, u32[]{:S(2)}, u32[]{:S(2)}) collective-permute-start(bf16[464,128]{1,0:T(8,128)(2,1)S(1)} %add_convert_fusion.5), channel_id=1, source_target_pairs={{0,16},{1,17},{2,18},{3,19},{4,20},{5,21},{6,22},{7,23},{8,24},{9,... | collective-permute-start | bytes 356360 | tf_op jit(solution)/shard_map/ppermute | solution.py:644
  62.0 6.8 %collective-permute-start.15 = (bf16[464,128]{1,0:T(8,128)(2,1)S(1)}, bf16[464,128]{1,0:T(8,128)(2,1)S(1)}, u32[]{:S(2)}, u32[]{:S(2)}) collective-permute-start(bf16[464,128]{1,0:T(8,128)(2,1)S(1)} %add_convert_fusion.8), channel_id=1, source_target_pairs={{0,2},{1,3},{2,0},{3,1},{4,6},{5,7},{6,4},{7,5},{8,10},{9,11},{10,... | collective-permute-start | bytes 356360 | tf_op jit(solution)/shard_map/ppermute | solution.py:644
  63.3 7.1 %collective-permute-start.11 = (bf16[464,128]{1,0:T(8,128)(2,1)S(1)}, bf16[464,128]{1,0:T(8,128)(2,1)S(1)}, u32[]{:S(2)}, u32[]{:S(2)}) collective-permute-start(bf16[464,128]{1,0:T(8,128)(2,1)S(1)} %add_convert_fusion.11), channel_id=1, source_target_pairs={{0,4},{1,5},{2,6},{3,7},{4,0},{5,1},{6,2},{7,3},{8,12},{9,13},{10,... | collective-permute-start | bytes 356360 | tf_op jit(solution)/shard_map/ppermute | solution.py:644
  68.7 5.3 %collective-permute-start.20 = (bf16[464,128]{1,0:T(8,128)(2,1)S(1)}, bf16[464,128]{1,0:T(8,128)(2,1)S(1)}, u32[]{:S(2)}, u32[]{:S(2)}) collective-permute-start(bf16[464,128]{1,0:T(8,128)(2,1)S(1)} %add_convert_fusion.4), channel_id=1, source_target_pairs={{0,12},{1,13},{2,14},{3,15},{4,8},{5,9},{6,10},{7,11},{8,4},{9,5},... | collective-permute-start | bytes 356360 | tf_op jit(solution)/shard_map/ppermute | solution.py:644
  68.9 6.1 %collective-permute-start.16 = (bf16[464,128]{1,0:T(8,128)(2,1)S(1)}, bf16[464,128]{1,0:T(8,128)(2,1)S(1)}, u32[]{:S(2)}, u32[]{:S(2)}) collective-permute-start(bf16[464,128]{1,0:T(8,128)(2,1)S(1)} %add_convert_fusion.7), channel_id=1, source_target_pairs={{0,48},{1,49},{2,50},{3,51},{4,52},{5,53},{6,54},{7,55},{8,56},{9,... | collective-permute-start | bytes 356360 | tf_op jit(solution)/shard_map/ppermute | solution.py:644
  70.4 6.4 %collective-permute-start.12 = (bf16[464,128]{1,0:T(8,128)(2,1)S(1)}, bf16[464,128]{1,0:T(8,128)(2,1)S(1)}, u32[]{:S(2)}, u32[]{:S(2)}) collective-permute-start(bf16[464,128]{1,0:T(8,128)(2,1)S(1)} %add_convert_fusion.10), channel_id=1, source_target_pairs={{0,66},{1,67},{2,64},{3,65},{4,70},{5,71},{6,68},{7,69},{8,74},{9,... | collective-permute-start | bytes 356360 | tf_op jit(solution)/shard_map/ppermute | solution.py:644
  74.1 6.3 %collective-permute-start.21 = (bf16[464,128]{1,0:T(8,128)(2,1)S(1)}, bf16[464,128]{1,0:T(8,128)(2,1)S(1)}, u32[]{:S(2)}, u32[]{:S(2)}) collective-permute-start(bf16[464,128]{1,0:T(8,128)(2,1)S(1)} %add_convert_fusion.3), channel_id=1, source_target_pairs={{0,66},{1,67},{2,64},{3,65},{4,70},{5,71},{6,68},{7,69},{8,74},{9,... | collective-permute-start | bytes 356360 | tf_op jit(solution)/shard_map/ppermute | solution.py:644
  75.1 5.4 %collective-permute-start.17 = (bf16[464,128]{1,0:T(8,128)(2,1)S(1)}, bf16[464,128]{1,0:T(8,128)(2,1)S(1)}, u32[]{:S(2)}, u32[]{:S(2)}) collective-permute-start(bf16[464,128]{1,0:T(8,128)(2,1)S(1)} %add_convert_fusion.6), channel_id=1, source_target_pairs={{0,12},{1,13},{2,14},{3,15},{4,8},{5,9},{6,10},{7,11},{8,4},{9,5},... | collective-permute-start | bytes 356360 | tf_op jit(solution)/shard_map/ppermute | solution.py:644
  76.9 5.3 %collective-permute-start.13 = (bf16[464,128]{1,0:T(8,128)(2,1)S(1)}, bf16[464,128]{1,0:T(8,128)(2,1)S(1)}, u32[]{:S(2)}, u32[]{:S(2)}) collective-permute-start(bf16[464,128]{1,0:T(8,128)(2,1)S(1)} %add_convert_fusion.9), channel_id=1, source_target_pairs={{0,48},{1,49},{2,50},{3,51},{4,52},{5,53},{6,54},{7,55},{8,56},{9,... | collective-permute-start | bytes 356360 | tf_op jit(solution)/shard_map/ppermute | solution.py:644
  82.2 5.6 %collective-permute-start.28 = (bf16[464,128]{1,0:T(8,128)(2,1)S(1)}, bf16[464,128]{1,0:T(8,128)(2,1)S(1)}, u32[]{:S(2)}, u32[]{:S(2)}) collective-permute-start(bf16[464,128]{1,0:T(8,128)(2,1)S(1)} %convert_add_fusion.3), channel_id=1, source_target_pairs={{0,48},{1,49},{2,50},{3,51},{4,52},{5,53},{6,54},{7,55},{8,56},{9,... | collective-permute-start | bytes 356360 | tf_op jit(solution)/shard_map/ppermute | solution.py:644
  82.7 6.1 %collective-permute-start.26 = (bf16[464,128]{1,0:T(8,128)(2,1)S(1)}, bf16[464,128]{1,0:T(8,128)(2,1)S(1)}, u32[]{:S(2)}, u32[]{:S(2)}) collective-permute-start(bf16[464,128]{1,0:T(8,128)(2,1)S(1)} %convert_add_fusion.4), channel_id=1, source_target_pairs={{0,66},{1,67},{2,64},{3,65},{4,70},{5,71},{6,68},{7,69},{8,74},{9,... | collective-permute-start | bytes 356360 | tf_op jit(solution)/shard_map/ppermute | solution.py:644
  83.6 5.3 %collective-permute-start.24 = (bf16[464,128]{1,0:T(8,128)(2,1)S(1)}, bf16[464,128]{1,0:T(8,128)(2,1)S(1)}, u32[]{:S(2)}, u32[]{:S(2)}) collective-permute-start(bf16[464,128]{1,0:T(8,128)(2,1)S(1)} %convert_add_fusion.5), channel_id=1, source_target_pairs={{0,12},{1,13},{2,14},{3,15},{4,8},{5,9},{6,10},{7,11},{8,4},{9,5},... | collective-permute-start | bytes 356360 | tf_op jit(solution)/shard_map/ppermute | solution.py:644
  88.8 4.1 %collective-permute-start.27 = (bf16[464,128]{1,0:T(8,128)(2,1)S(1)}, bf16[464,128]{1,0:T(8,128)(2,1)S(1)}, u32[]{:S(2)}, u32[]{:S(2)}) collective-permute-start(bf16[464,128]{1,0:T(8,128)(2,1)S(1)} %add_convert_fusion.1), channel_id=1, source_target_pairs={{0,4},{1,5},{2,6},{3,7},{4,0},{5,1},{6,2},{7,3},{8,12},{9,13},{10,... | collective-permute-start | bytes 356360 | tf_op jit(solution)/shard_map/ppermute | solution.py:644
  89.0 4.1 %collective-permute-start.25 = (bf16[464,128]{1,0:T(8,128)(2,1)S(1)}, bf16[464,128]{1,0:T(8,128)(2,1)S(1)}, u32[]{:S(2)}, u32[]{:S(2)}) collective-permute-start(bf16[464,128]{1,0:T(8,128)(2,1)S(1)} %add_convert_fusion.2), channel_id=1, source_target_pairs={{0,16},{1,17},{2,18},{3,19},{4,20},{5,21},{6,22},{7,23},{8,24},{9,... | collective-permute-start | bytes 356360 | tf_op jit(solution)/shard_map/ppermute | solution.py:644
  93.1 6.4 %collective-permute-start.30 = (bf16[928,128]{1,0:T(8,128)(2,1)S(1)}, bf16[928,128]{1,0:T(8,128)(2,1)S(1)}, u32[]{:S(2)}, u32[]{:S(2)}) collective-permute-start(bf16[928,128]{1,0:T(8,128)(2,1)S(1)} %get-tuple-element.118), channel_id=1, source_target_pairs={{0,2},{1,3},{2,0},{3,1},{4,6},{5,7},{6,4},{7,5},{8,10},{9,11},{10,... | collective-permute-start | bytes 712712 | tf_op jit(solution)/shard_map/ppermute | solution.py:644
  94.0 5.8 %collective-permute-start.31 = (bf16[928,128]{1,0:T(8,128)(2,1)S(1)}, bf16[928,128]{1,0:T(8,128)(2,1)S(1)}, u32[]{:S(2)}, u32[]{:S(2)}) collective-permute-start(bf16[928,128]{1,0:T(8,128)(2,1)S(1)} %get-tuple-element.119), channel_id=1, source_target_pairs={{0,16},{1,17},{2,18},{3,19},{4,20},{5,21},{6,22},{7,23},{8,24},{9,... | collective-permute-start | bytes 712712 | tf_op jit(solution)/shard_map/ppermute | solution.py:644
  94.0 6.0 %collective-permute-start.32 = (bf16[928,128]{1,0:T(8,128)(2,1)S(1)}, bf16[928,128]{1,0:T(8,128)(2,1)S(1)}, u32[]{:S(2)}, u32[]{:S(2)}) collective-permute-start(bf16[928,128]{1,0:T(8,128)(2,1)S(1)} %pad_maximum_fusion.2), channel_id=1, source_target_pairs={{0,4},{1,5},{2,6},{3,7},{4,0},{5,1},{6,2},{7,3},{8,12},{9,13},{10,... | collective-permute-start | bytes 712712 | tf_op jit(solution)/shard_map/ppermute | solution.py:644
  100.1 15.7 %collective-permute-start.33 = (bf16[5568,128]{1,0:T(8,128)(2,1)S(1)}, bf16[5568,128]{1,0:T(8,128)(2,1)S(1)}, u32[]{:S(2)}, u32[]{:S(2)}) collective-permute-start(bf16[5568,128]{1,0:T(8,128)(2,1)S(1)} %select_dynamic-update-slice_fusion.mine_ref), channel_id=1, source_target_pairs={{0,1},{1,0},{2,3},{3,2},{4,5},{5,4},{6,7},{7,6},{8,9},{9,8},{10,11... | collective-permute-start | bytes 4276232 | tf_op jit(solution)/shard_map/ppermute | solution.py:644
  (12 other events, 69.1 us)

commit v2 on v1

--- a/solution.py
+++ b/solution.py
@@ -19,15 +19,15 @@
 GROUPS = 4
 HT = 13
 PITCH = 32
-ROWS = HT * C
-EXTRA = 368
-PARTS = 3
+ROWS = HT * C + 16
+EXTRA = 272
+SIZES = (1856, 1856, 1504)
 AXES = ("wide", "narrow")
 f32 = jnp.float32
 bf16 = jnp.bfloat16
 VMEM = pl.BlockSpec(memory_space=pltpu.VMEM)
 SMEM = pl.BlockSpec(memory_space=pltpu.SMEM)
-ANY = pl.BlockSpec(memory_space=pl.ANY)
+HBM = pl.BlockSpec(memory_space=pltpu.HBM)
 
 
 def group_width(g):
@@ -38,9 +38,9 @@
     return slice(128 * g, 128 * g + group_width(g))
 
 
-def land_mask(land):
-    spread = jnp.broadcast_to(land.astype(f32)[:, :, None], (2 * TE, TE, C))
-    return spread.reshape(CELLS, C)
+def land_mask(land, tiles=2):
+    spread = jnp.broadcast_to(land.astype(f32)[:, :, None], (tiles * TE, TE, C))
+    return spread.reshape(tiles * TE * TE, C)
 
 
 def zero_lanes(ref):
@@ -57,20 +57,18 @@
         second_ref[s, :, 0:C] = jnp.where(even, north, south).astype(bf16)
 
 
-def narrow_kernel(field_ref, land_ref, first_ref, second_ref, rows_ref, cells_ref, sems):
-    copies = [pltpu.make_async_copy(land_ref, cells_ref, sems.at[4])]
-    for s in range(2):
-        for k, row in enumerate((0, TE - 3)):
-            copies.append(
-                pltpu.make_async_copy(field_ref.at[s, pl.ds(row, 3)], rows_ref.at[s, k], sems.at[2 * s + k])
-            )
+def narrow_kernel(field_ref, land_ref, first_ref, second_ref, held_ref, cells_ref, sems):
+    copies = [
+        pltpu.make_async_copy(field_ref, held_ref, sems.at[0]),
+        pltpu.make_async_copy(land_ref, cells_ref, sems.at[1]),
+    ]
     for copy in copies:
         copy.start()
     for copy in copies:
         copy.wait()
 
     def tile_rows(s, row):
-        cells = rows_ref[s, 1 if row else 0].reshape(3 * TE, C).astype(f32)
+        cells = held_ref[s, row : row + 3].reshape(3 * TE, C).astype(f32)
         land = cells_ref[s, row : row + 3].astype(f32)
         return cells * jnp.broadcast_to(land[:, :, None], (3, TE, C)).reshape(3 * TE, C)
 
@@ -219,12 +217,12 @@
     return put
 
 
-def each_group(body):
+def each_group(body, tiles=(0, 1)):
     def step(i, _):
-        body(i // GROUPS, i % GROUPS)
+        body(tiles[0] + i // GROUPS, i % GROUPS)
         return _
 
-    lax.fori_loop(0, 2 * GROUPS, step, 0)
+    lax.fori_loop(0, len(tiles) * GROUPS, step, 0)
 
 
 def weight_rows(weight_ref, g, taps):
@@ -232,7 +230,7 @@
     return [jnp.broadcast_to(weight_ref[pl.ds(k, 1), at], (8, 128)) for k in taps]
 
 
-def convolve(p_ref, weight_ref, start, finish, flip):
+def convolve(p_ref, weight_ref, start, finish, flip, tiles=(0, 1)):
     def body(t, g):
         for h in range(2):
             total = start(t, g, h)
@@ -247,7 +245,7 @@
                             total[r] = total[r] + weights[a] * x
             finish(t, g, h, total)
 
-    each_group(body)
+    each_group(body, tiles)
 
 
 def gelu_pair(hidden):
@@ -264,14 +262,17 @@
 
 
 def prep_kernel(
-    neighbours_ref,
+    beside_ref,
     field_ref,
     land_ref,
     cot_ref,
     n1_ref,
     n2_ref,
     depth_weight_ref,
-    small_ref,
+    depth_bias_ref,
+    gain_ref,
+    shift_ref,
+    up_bias_ref,
     up_ref,
     down_ref,
     p_ref,
@@ -281,10 +282,16 @@
     down_bias_ref,
     up_out_ref,
     down_out_ref,
+    taps_ref,
+    small_ref,
     rn_ref,
     weight_ref,
-    taps_ref,
     cot_in_ref,
+    bias_in_ref,
+    gain_in_ref,
+    shift_in_ref,
+    up_bias_in_ref,
+    neighbours_ref,
     sems,
 ):
     copies = [
@@ -292,6 +299,11 @@
         pltpu.make_async_copy(cot_ref, cot_in_ref, sems.at[1]),
         pltpu.make_async_copy(up_ref, up_out_ref, sems.at[2]),
         pltpu.make_async_copy(down_ref, down_out_ref, sems.at[3]),
+        pltpu.make_async_copy(depth_bias_ref, bias_in_ref, sems.at[4]),
+        pltpu.make_async_copy(gain_ref, gain_in_ref, sems.at[5]),
+        pltpu.make_async_copy(shift_ref, shift_in_ref, sems.at[6]),
+        pltpu.make_async_copy(up_bias_ref, up_bias_in_ref, sems.at[7]),
+        pltpu.make_async_copy(beside_ref, neighbours_ref, sems.at[8]),
     ]
     for copy in copies:
         copy.start()
@@ -301,8 +313,14 @@
         cells = field_ref[s].reshape(TE * TE, C).astype(f32)
         place_centre(cells * mask[s * TE * TE : (s + 1) * TE * TE], s, p_ref)
     place_rows(n1_ref, n2_ref, rn_ref)
+    copies[8].wait()
     each_group(lambda t, g: border_rows(neighbours_ref, p_ref, rn_ref, t, g))
-    copies[0].wait()
+    for k in (0, 4, 5, 6, 7):
+        copies[k].wait()
+    small_ref[0:1, 0:C] = bias_in_ref[...].reshape(1, C)
+    small_ref[1:2, 0:C] = gain_in_ref[...].reshape(1, C)
+    small_ref[2:3, 0:C] = shift_in_ref[...].reshape(1, C)
+    small_ref[3:4, :] = up_bias_in_ref[...].reshape(1, HID)
     take_weights(weight_ref, taps_ref)
     weight_ref[49:50, 0:C] = small_ref[0:1, 0:C]
 
@@ -326,7 +344,7 @@
 
 
 def front_kernel(
-    neighbours_ref,
+    beside_ref,
     n1_ref,
     n2_ref,
     w1_ref,
@@ -352,12 +370,17 @@
     y_ref,
     normed_ref,
     normed_t_ref,
+    neighbours_ref,
+    sem,
 ):
     core0 = lax.axis_index("narrow") % 2 == 0
+    copy = pltpu.make_async_copy(beside_ref, neighbours_ref, sem)
+    copy.start()
     place_rows(n1_ref, n2_ref, rn_ref)
     place_columns(w1_ref, w2_ref, rw_ref)
     take_weights(weight_ref, depth_weight_ref)
     y_ref[...] = y_in_ref[...]
+    copy.wait()
 
     def sides(t, g):
         def put(side, c, row, count, value):
@@ -399,37 +422,45 @@
     lax.fori_loop(0, CELLS // step_rows, norm, 0)
     normed_t_ref[...] = normed_ref[...].T
 
-    def hidden_chunk(lo, width, lane_tile):
-        at = pl.ds(lo, width)
-        up = up_ref[:, at]
-        h = jnp.dot(normed_ref[:, 0:C], up, preferred_element_type=f32) + small_ref[3:4, at]
+    def products(lo, width):
+        at = slice(lo, lo + width)
+        h = jnp.dot(normed_ref[:, 0:C], up_ref[:, at], preferred_element_type=f32) + small_ref[3:4, at]
+        ag = jnp.dot(gated_ref[:, 0:C], down_ref[:, at], preferred_element_type=f32)
+        return h, ag
+
+    def hidden_chunk(lo, width, h, ag):
+        at = slice(lo, lo + width)
         act, slope = gelu_pair(h)
-        ag = jnp.dot(gated_ref[:, 0:C], down_ref[:, at], preferred_element_type=f32)
         hg = ag * slope
         hgb = hg.astype(bf16)
         dg = jnp.dot(gated_t_ref[0:C, :], act.astype(bf16), preferred_element_type=f32)
         ug = jnp.dot(normed_t_ref[0:C, :], hgb, preferred_element_type=f32)
-        ng_ref[...] += lax.dot_general(hgb, up, (((1,), (1,)), ((), ())), preferred_element_type=f32)
+        ng = lax.dot_general(hgb, up_ref[:, at], (((1,), (1,)), ((), ())), preferred_element_type=f32)
+        if lo == 0:
+            ng_ref[...] = ng
+        else:
+            ng_ref[...] += ng
         up_bias_sum_ref[:, at] = jnp.sum(hgb.astype(f32), axis=0, keepdims=True)
         keep = jnp.where(core0, ug, dg)
         send = jnp.where(core0, dg, ug).astype(bf16)
         for k in range((width + 127) // 128):
             w = min(128, width - 128 * k)
-            rows = pl.ds(pl.multiple_of((lane_tile + k) * C, C), C)
+            rows = slice((lo // 128 + k) * C, (lo // 128 + k + 1) * C)
             if w < 128:
                 keep_ref[rows, :] = jnp.zeros((C, 128), f32)
                 send_ref[rows, :] = jnp.zeros((C, 128), bf16)
             keep_ref[rows, 0:w] = keep[:, 128 * k : 128 * k + w]
             send_ref[rows, 0:w] = send[:, 128 * k : 128 * k + w]
 
-    ng_ref[...] = jnp.zeros(ng_ref.shape, f32)
-
-    def more(i, _):
-        hidden_chunk(pl.multiple_of(i * 256, 256), 256, 2 * i)
-        return _
-
-    lax.fori_loop(0, 6, more, 0)
-    hidden_chunk(1536, 64, 12)
+    keep_ref[HT * C :, :] = jnp.zeros((16, 128), f32)
+    send_ref[HT * C :, :] = jnp.zeros((16, 128), bf16)
+    chunks = ((0, 512), (512, 512), (1024, 576))
+    ready = products(*chunks[0])
+    for i, chunk in enumerate(chunks):
+        current = ready
+        if i + 1 < len(chunks):
+            ready = products(*chunks[i + 1])
+        hidden_chunk(*chunk, *current)
 
 
 def grad_kernel(
@@ -437,17 +468,11 @@
     z_ref,
     r_ref,
     small_ref,
-    p_in_ref,
-    border_ref,
-    up_bias_sum_ref,
-    down_bias_ref,
     cg_ref,
     g1_ref,
     g2_ref,
-    extra_ref,
-    p_ref,
     y_ref,
-    dw_ref,
+    sums_ref,
 ):
     y_ref[...] = jnp.zeros(y_ref.shape, f32)
     step_rows = 64
@@ -472,6 +497,9 @@
 
     zero = jnp.zeros((1, C), f32)
     gain_sum, shift_sum, bias_sum = lax.fori_loop(0, CELLS // step_rows, back, (zero, zero, zero))
+    sums_ref[0:1, :] = bias_sum
+    sums_ref[1:2, :] = gain_sum
+    sums_ref[2:3, :] = shift_sum
 
     def tile_rows(s, row):
         at = s * TE * TE + row * TE
@@ -479,6 +507,9 @@
 
     pack_narrow(tile_rows, lax.axis_index("narrow") % 2 == 0, g1_ref, g2_ref)
 
+def taps_kernel(
+    after_ref, y_ref, p_in_ref, border_ref, sums_ref, up_bias_sum_ref, down_bias_ref, extra_ref, p_ref, dw_ref
+):
     p_ref[...] = p_in_ref[...]
     dw_ref[...] = jnp.zeros(dw_ref.shape, f32)
 
@@ -513,39 +544,35 @@
     for g in range(GROUPS):
         w = group_width(g)
         extra_ref[g * 64 : g * 64 + 49, :] = jnp.sum(dw_ref[g], axis=1)
-        extra_ref[g * 64 + 49 : g * 64 + 50, 0:w] = bias_sum[:, lanes(g)]
-        extra_ref[g * 64 + 50 : g * 64 + 51, 0:w] = gain_sum[:, lanes(g)]
-        extra_ref[g * 64 + 51 : g * 64 + 52, 0:w] = shift_sum[:, lanes(g)]
+        extra_ref[g * 64 + 49 : g * 64 + 50, 0:w] = sums_ref[0:1, lanes(g)]
+        extra_ref[g * 64 + 50 : g * 64 + 51, 0:w] = sums_ref[1:2, lanes(g)]
+        extra_ref[g * 64 + 51 : g * 64 + 52, 0:w] = sums_ref[2:3, lanes(g)]
         extra_ref[g * 64 + 52 : g * 64 + 53, 0:w] = down_bias_ref[:, lanes(g)]
     for l in range(HT):
         w = min(128, HID - 128 * l)
         extra_ref[256 + l : 257 + l, 0:w] = up_bias_sum_ref[:, 128 * l : 128 * l + w]
 
 
-def split_kernel(keep_ref, got_ref, extra_ref, *refs):
+def split_kernel(keep_ref, got_ref, after_ref, *refs):
     me = here()
-    size = (ROWS + EXTRA) // PARTS
-    half = size // 2
-    for i in range(PARTS):
-        send_ref, mine_ref = refs[i], refs[PARTS + i]
+    refs[-1][...] = jnp.zeros((8, 128), f32)
+    lo = 0
+    for i, size in enumerate(SIZES):
+        send_ref, mine_ref = refs[i], refs[len(SIZES) + i]
         high = parity(me, STAGES[ORDERS[i][0]][1])
+        half = size // 2
         for j in range(2):
-            lo = i * size + j * half
-            inner = min(half, ROWS - lo)
-
-            def value(a, b):
-                return keep_ref[a:b, :] + got_ref[a:b, :].astype(f32)
-
-            def store(ref):
-                ref[0:inner, :] = value(lo, lo + inner).astype(ref.dtype)
-                if inner < half:
-                    ref[inner:half, :] = extra_ref[0 : half - inner, :].astype(ref.dtype)
+
+            def store(ref, lo=lo):
+                total = keep_ref[lo : lo + half, :] + got_ref[lo : lo + half, :].astype(f32)
+                ref[...] = total.astype(ref.dtype)
 
             pl.when(high == j)(functools.partial(store, mine_ref))
             pl.when(high != j)(functools.partial(store, send_ref))
-
-
-def unpack_kernel(mine_ref, theirs_ref, up_ref, down_ref, channel_ref, up_bias_ref):
+            lo += half
+
+
+def unpack_kernel(mine_ref, theirs_ref, up_ref, down_ref, taps_ref, bias_ref, gain_ref, shift_ref, up_bias_ref, down_bias_ref):
     core0 = lax.axis_index("narrow") % 2 == 0
     for l in range(HT):
         w = min(128, HID - 128 * l)
@@ -556,64 +583,74 @@
         down_ref[:, 128 * l : 128 * l + w] = jnp.where(core0, two, one)[:, 0:w]
     extra = mine_ref[ROWS:, :].astype(f32) + theirs_ref[ROWS:, :].astype(f32)
     for g in range(GROUPS):
-        channel_ref[:, lanes(g)] = extra[g * 64 : g * 64 + 56, 0 : group_width(g)]
-    up_bias_ref[...] = extra[256:272]
+        taps_ref[:, lanes(g)] = extra[g * 64 : g * 64 + 49, 0 : group_width(g)]
+    for k, ref in enumerate((bias_ref, gain_ref, shift_ref, down_bias_ref)):
+        at = 49 + k
+        vector = jnp.concatenate([extra[g * 64 + at : g * 64 + at + 1] for g in range(GROUPS)], axis=1)
+        ref[...] = vector[:, 0:C].reshape(C)
+    vector = jnp.concatenate([extra[256 + l : 257 + l] for l in range(HT)], axis=1)
+    up_bias_ref[...] = vector[:, 0:HID].reshape(HID)
 
 
 def back_kernel(
-    neighbours_ref,
+    t,
+    beside_ref,
     cg_ref,
     land_ref,
-    cot_ref,
+    gated_ref,
     n1_ref,
     n2_ref,
     w1_ref,
     w2_ref,
     depth_weight_ref,
-    out_ref,
-    p_ref,
-    rn_ref,
-    rw_ref,
-    weight_ref,
-    y_ref,
+    *refs,
 ):
-    p_ref[...] = jnp.zeros(p_ref.shape, f32)
+    out_ref, p_ref, rn_ref, rw_ref, weight_ref, y_ref, tile_ref, neighbours_ref, sem = refs[-9:]
+    copy = pltpu.make_async_copy(beside_ref, neighbours_ref, sem)
+    copy.start()
+    p_ref[t] = jnp.zeros(p_ref.shape[1:], f32)
     for s in range(2):
         place_centre(cg_ref[s].reshape(TE * TE, C).astype(f32), s, p_ref)
-    mask = land_mask(land_ref[...].reshape(2 * TE, TE))
+    mask = land_mask(land_ref[t], 1)
     place_rows(n1_ref, n2_ref, rn_ref)
     place_columns(w1_ref, w2_ref, rw_ref)
-
-    def borders(t, g):
+    copy.wait()
+
+    def borders(g, _):
         border_rows(neighbours_ref, p_ref, rn_ref, t, g)
         border_columns(neighbours_ref, p_ref, rn_ref, rw_ref, t, g, column_in(p_ref, t, g))
-
-    each_group(borders)
+        return _
+
+    lax.fori_loop(0, GROUPS, borders, 0)
     take_weights(weight_ref, depth_weight_ref)
-    y_ref[...] = jnp.zeros(y_ref.shape, f32)
-    y_ref[:, 0:C] = cot_ref[...].reshape(CELLS, C).astype(f32) * mask
-
-    def place(t, g, h, r):
-        return (
-            pl.ds(t * TE * TE + r * TE + 8 * h, 8),
-            pl.ds(pl.multiple_of(g * 128, 128), 128),
-        )
+    y_ref[...] = gated_ref[t * TE * TE : (t + 1) * TE * TE, :].astype(f32)
+
+    def place(g, h, r):
+        return (pl.ds(r * TE + 8 * h, 8), pl.ds(pl.multiple_of(g * 128, 128), 128))
 
     def start(t, g, h):
-        return [y_ref[place(t, g, h, r)] for r in range(TE)]
+        return [y_ref[place(g, h, r)] for r in range(TE)]
 
     def finish(t, g, h, rows):
         for r in range(TE):
-            y_ref[place(t, g, h, r)] = rows[r]
-
-    convolve(p_ref, weight_ref, start, finish, True)
-    out_ref[...] = (y_ref[:, 0:C] * mask).astype(bf16).reshape(2, TE, TE, C)
+            y_ref[place(g, h, r)] = rows[r]
+
+    convolve(p_ref, weight_ref, start, finish, True, (t,))
+    tile_ref[...] = (y_ref[:, 0:C] * mask).astype(bf16).reshape(TE, TE, C)
+    copy = pltpu.make_async_copy(tile_ref, out_ref.at[t], sem)
+    copy.start()
+    copy.wait()
 
 
 def params(size=16):
     return pltpu.CompilerParams(vmem_limit_bytes=size * 1024 * 1024)
 
 
+def estimate():
+    return pl.CostEstimate(flops=10**9, bytes_accessed=16 * 10**6, transcendentals=0)
+
+
+NEIGHBOURS = pltpu.SMEM((2, 8), jnp.int32)
 P_SCRATCH = pltpu.VMEM((2, GROUPS, 22 * PITCH, 128), f32)
 RN_SCRATCH = pltpu.VMEM((2, 2, GROUPS, 48, 128), f32)
 RW_SCRATCH = pltpu.VMEM((2, 2, GROUPS, 80, 128), f32)
@@ -664,25 +701,22 @@
     return sum((me >> bit) & 1 for bit in bits) & 1
 
 
-def halved(part, order, stage, me):
-    mask, bits = STAGES[order[stage]]
-    high = parity(me, bits)
+def halved(part, step, high):
     half = part.shape[0] // 2
-    send = lax.dynamic_slice_in_dim(part, (1 - high) * half, half, 0).astype(bf16)
-    keep = lax.dynamic_slice_in_dim(part, high * half, half, 0)
-    return keep + flip(send, mask).astype(f32)
-
-
-def doubled(part, order, stage):
+    low_rows, high_rows = part[0:half], part[half:]
+    send = jnp.where(high, low_rows, high_rows).astype(bf16)
+    keep = jnp.where(high, high_rows, low_rows)
+    return keep + flip(send, STAGES[step][0]).astype(f32)
+
+
+def doubled(part, step):
     mine = part.astype(bf16)
-    return mine.astype(f32) + flip(mine, STAGES[order[stage]][0]).astype(f32)
-
-
-def joined(part, order, stage, me):
-    mask, bits = STAGES[order[stage]]
-    low = parity(me, bits) == 0
-    got = flip(part, mask)
-    return jnp.concatenate([jnp.where(low, part, got), jnp.where(low, got, part)], axis=0)
+    return mine.astype(f32) + flip(mine, STAGES[step][0]).astype(f32)
+
+
+def joined(part, step, high):
+    got = flip(part, STAGES[step][0])
+    return jnp.concatenate([jnp.where(high, got, part), jnp.where(high, part, got)], axis=0)
 
 
 def together(*values):
@@ -704,6 +738,12 @@
 ):
     me = here()
     shape = jax.ShapeDtypeStruct
+    stay = lambda v: pltpu.with_memory_space_constraint(v, pltpu.HBM)
+    steps = sorted({order[stage] for order in ORDERS for stage in range(DEPTH)})
+    highs = [parity(me, STAGES[step][1]) == 1 for step in steps]
+    highs, field = together(highs, field)
+    high = dict(zip(steps, highs))
+    neighbours = stay(neighbours)
     narrow_shape = shape((2, 48, CP), bf16)
     wide_shape = shape((2, 80, CP), bf16)
     wide_scratch = [
@@ -712,23 +752,21 @@
         RW_SCRATCH,
     ]
     p_shape = shape((2, GROUPS, 22 * PITCH, 128), f32)
-    small = jnp.stack(
-        [jnp.pad(v, (0, HID - C)) for v in (depth_bias, ln_gain, ln_shift)] + [up_bias]
-    )
-
-    s1, s2 = pl.pallas_call(
+
+    s1, s2, field, land = pl.pallas_call(
         narrow_kernel,
-        out_shape=(narrow_shape, narrow_shape),
-        in_specs=[ANY] * 2,
-        out_specs=(VMEM, VMEM),
-        scratch_shapes=[
-            pltpu.VMEM((2, 2, 3, TE, C), bf16),
-            pltpu.VMEM((2, TE, TE), jnp.int32),
-            pltpu.SemaphoreType.DMA((5,)),
-        ],
-        compiler_params=params(),
+        out_shape=(
+            narrow_shape,
+            narrow_shape,
+            shape((2, TE, TE, C), bf16),
+            shape((2, TE, TE), jnp.int32),
+        ),
+        in_specs=[HBM] * 2,
+        out_specs=(VMEM,) * 4,
+        scratch_shapes=[pltpu.SemaphoreType.DMA((2,))],
+        compiler_params=params(4),
         name="pack_rows",
-    )(field, land)
+    )(stay(field), stay(land))
     n1, n2 = swap(s1, ("narrow", 0)), swap(s2, ("narrow", 1))
     s1, s2 = pl.pallas_call(
         functools.partial(wide_kernel, True),
@@ -736,12 +774,12 @@
         in_specs=[VMEM] * 4,
         out_specs=(VMEM, VMEM),
         scratch_shapes=wide_scratch,
-        compiler_params=params(),
+        compiler_params=params(8),
         name="pack_columns",
     )(field, land, n1, n2)
     s1, s2, n1, n2 = together(s1, s2, n1, n2)
     w2, w1 = swap(s2, ("wide", 1)), swap(s1, ("wide", 0))
-    p, y, gated, gated_t, down_bias_sum, up_held, down_held = pl.pallas_call(
+    p, y, gated, gated_t, down_bias_sum, up_held, down_held, taps, small = pl.pallas_call(
         prep_kernel,
         out_shape=(
             p_shape,
@@ -751,20 +789,40 @@
             shape((1, C), f32),
             shape((C, HID), bf16),
             shape((C, HID), bf16),
+            shape((49, C), f32),
+            shape((4, HID), f32),
         ),
-        in_specs=[SMEM, VMEM, VMEM, ANY, VMEM, VMEM, ANY, VMEM, ANY, ANY],
-        out_specs=(VMEM,) * 7,
+        in_specs=[HBM, VMEM, VMEM, HBM, VMEM, VMEM] + [HBM] * 7,
+        out_specs=(VMEM,) * 9,
         scratch_shapes=[
             RN_SCRATCH,
             W_SCRATCH,
-            pltpu.VMEM((49, C), f32),
             pltpu.VMEM((2, TE, TE, C), bf16),
-            pltpu.SemaphoreType.DMA((4,)),
+            pltpu.VMEM((C,), f32),
+            pltpu.VMEM((C,), f32),
+            pltpu.VMEM((C,), f32),
+            pltpu.VMEM((HID,), f32),
+            NEIGHBOURS,
+            pltpu.SemaphoreType.DMA((9,)),
         ],
-        compiler_params=params(),
-        cost_estimate=pl.CostEstimate(flops=10**9, bytes_accessed=16 * 10**6, transcendentals=0),
+        compiler_params=params(8),
+        cost_estimate=estimate(),
         name="prep",
-    )(neighbours, field, land, cotangent, n1, n2, depth_weight, small, up_weight, down_weight.T)
+    )(
+        neighbours,
+        field,
+        land,
+        stay(cotangent),
+        n1,
+        n2,
+        stay(depth_weight),
+        stay(depth_bias),
+        stay(ln_gain),
+        stay(ln_shift),
+        stay(up_bias),
+        stay(up_weight),
+        stay(down_weight.T),
+    )
 
     keep, send, ng, z, r, up_bias_sum, border = pl.pallas_call(
         front_kernel,
@@ -777,7 +835,7 @@
             shape((1, HID), f32),
             shape((2, GROUPS, 6 * 24, 128), f32),
         ),
-        in_specs=[SMEM] + [VMEM] * 12,
+        in_specs=[HBM] + [VMEM] * 12,
         out_specs=(VMEM,) * 7,
         scratch_shapes=[
             RN_SCRATCH,
@@ -786,8 +844,10 @@
             pltpu.VMEM((2, GROUPS, TE * TE, 128), f32),
             pltpu.VMEM((CELLS, CP), bf16),
             pltpu.VMEM((CP, CELLS), bf16),
+            NEIGHBOURS,
+            pltpu.SemaphoreType.DMA,
         ],
-        compiler_params=params(20),
+        compiler_params=params(14),
         name="front",
     )(
         neighbours,
@@ -799,48 +859,59 @@
         y,
         gated,
         gated_t,
-        depth_weight,
+        taps,
         small,
         up_held,
         down_held,
     )
 
     got = flip(send, 1)
-    cg, g1, g2, extra = pl.pallas_call(
+    cg, g1, g2, cg_wide, sums = pl.pallas_call(
         grad_kernel,
         out_shape=(
             shape((2, TE, TE, C), bf16),
             narrow_shape,
             narrow_shape,
-            shape((EXTRA, 128), f32),
+            shape((CELLS, CP), f32),
+            shape((3, C), f32),
         ),
-        in_specs=[VMEM] * 8,
-        out_specs=(VMEM,) * 4,
+        in_specs=[VMEM] * 4,
+        out_specs=(VMEM,) * 5,
+        compiler_params=params(4),
+        cost_estimate=estimate(),
+        name="grad",
+    )(ng, z, r, small)
+
+    halves = [size // 2 for size in SIZES]
+    pieces = pl.pallas_call(
+        split_kernel,
+        out_shape=tuple(shape((half, 128), bf16) for half in halves)
+        + tuple(shape((half, 128), f32) for half in halves)
+        + (shape((8, 128), f32),),
+        in_specs=[VMEM] * 3,
+        out_specs=(VMEM,) * (2 * len(SIZES) + 1),
+        compiler_params=params(4),
+        name="split",
+    )(keep, got, sums)
+
+    orders = list(enumerate(ORDERS))
+    got = [flip(pieces[i], STAGES[order[0]][0]) for i, order in orders]
+    n1, n2 = swap(g1, ("narrow", 0)), swap(g2, ("narrow", 1))
+    extra = pl.pallas_call(
+        taps_kernel,
+        out_shape=shape((EXTRA, 128), f32),
+        in_specs=[VMEM] * 7,
+        out_specs=VMEM,
         scratch_shapes=[
             pltpu.VMEM(p_shape.shape, f32),
-            Y_SCRATCH,
             pltpu.VMEM((GROUPS, 49, 8, 128), f32),
         ],
-        compiler_params=params(),
-        cost_estimate=pl.CostEstimate(flops=10**9, bytes_accessed=16 * 10**6, transcendentals=0),
-        name="grad",
-    )(ng, z, r, small, p, border, up_bias_sum, down_bias_sum)
-
-    half = (ROWS + EXTRA) // PARTS // 2
-    pieces = pl.pallas_call(
-        split_kernel,
-        out_shape=(shape((half, 128), bf16),) * PARTS + (shape((half, 128), f32),) * PARTS,
-        in_specs=[VMEM] * 3,
-        out_specs=(VMEM,) * (2 * PARTS),
-        compiler_params=params(),
-        name="split",
-    )(keep, got, extra)
-
-    orders = list(enumerate(ORDERS))
-    n1, n2 = swap(g1, ("narrow", 0)), swap(g2, ("narrow", 1))
-    parts = [
-        pieces[PARTS + i] + flip(pieces[i], STAGES[order[0]][0]).astype(f32) for i, order in orders
-    ]
+        compiler_params=params(8),
+        cost_estimate=estimate(),
+        name="taps",
+    )(pieces[-1], cg_wide, p, border, sums, up_bias_sum, down_bias_sum)
+    parts = [pieces[len(SIZES) + i] + got[i].astype(f32) for i, order in orders]
+    parts[-1] = jnp.concatenate([parts[-1], extra], axis=0)
     parts, n1, n2 = together(parts, n1, n2)
     s1, s2 = pl.pallas_call(
         functools.partial(wide_kernel, False),
@@ -848,57 +919,88 @@
         in_specs=[VMEM] * 3,
         out_specs=(VMEM, VMEM),
         scratch_shapes=wide_scratch,
-        compiler_params=params(),
+        compiler_params=params(8),
         name="pack_columns_back",
     )(cg, n1, n2)
     parts, s1, s2 = together(parts, s1, s2)
     w2, w1 = swap(s2, ("wide", 1)), swap(s1, ("wide", 0))
     for stage in range(1, DEPTH):
-        parts = [halved(parts[i], order, stage, me) for i, order in orders]
+        parts = [halved(parts[i], order[stage], high[order[stage]]) for i, order in orders]
     for stage in range(DEPTH, 6):
-        parts = [doubled(parts[i], order, stage) for i, order in orders]
+        parts = [doubled(parts[i], order[stage]) for i, order in orders]
         if stage == 4:
             parts, w1, w2 = together(parts, w1, w2)
     parts = [part.astype(bf16) for part in parts]
     for stage in reversed(range(1, DEPTH)):
-        parts = [joined(parts[i], order, stage, me) for i, order in orders]
+        parts = [joined(parts[i], order[stage], high[order[stage]]) for i, order in orders]
     parts, w1, w2 = together(parts, w1, w2)
-    field_grad = pl.pallas_call(
-        back_kernel,
-        out_shape=shape((2, TE, TE, C), bf16),
-        in_specs=[SMEM] + [VMEM] * 8,
-        out_specs=VMEM,
-        scratch_shapes=[P_SCRATCH, RN_SCRATCH, RW_SCRATCH, W_SCRATCH, Y_SCRATCH],
-        compiler_params=params(),
-        cost_estimate=pl.CostEstimate(flops=10**9, bytes_accessed=16 * 10**6, transcendentals=0),
-        name="back",
-    )(neighbours, cg, land, cotangent, n1, n2, w1, w2, depth_weight)
-    parts = [joined(parts[i], order, 0, me) for i, order in orders]
-    mine = jnp.concatenate(parts, axis=0)
+
+    def back(t, *before):
+        operands = (neighbours, cg, land, gated, n1, n2, w1, w2, taps)
+        return pl.pallas_call(
+            functools.partial(back_kernel, t),
+            out_shape=shape((2, TE, TE, C), bf16),
+            in_specs=[HBM] + [VMEM] * 8 + [HBM] * len(before),
+            out_specs=HBM,
+            scratch_shapes=[
+                P_SCRATCH,
+                RN_SCRATCH,
+                RW_SCRATCH,
+                W_SCRATCH,
+                pltpu.VMEM((TE * TE, CP), f32),
+                pltpu.VMEM((TE, TE, C), bf16),
+                NEIGHBOURS,
+                pltpu.SemaphoreType.DMA,
+            ],
+            input_output_aliases={len(operands): 0} if before else {},
+            compiler_params=params(10),
+            cost_estimate=estimate(),
+            name=f"back_{t}",
+        )(*operands, *before)
+
+    field_grad = back(0)
+    matrix = [joined(parts[i], order[0], high[order[0]]) for i, order in orders[:-1]]
+    last = parts[-1]
+    order = ORDERS[-1]
+    got = flip(last, STAGES[order[0]][0])
+    one, two = last[0 : halves[-1]], got[0 : halves[-1]]
+    upper = high[order[0]]
+    extra = (last[halves[-1] :].astype(f32) + got[halves[-1] :].astype(f32)).astype(bf16)
+    mine = jnp.concatenate(
+        matrix + [jnp.where(upper, two, one), jnp.where(upper, one, two), extra], axis=0
+    )
+    mine, field_grad = together(mine, field_grad)
     theirs = flip(mine, 1)
-    up_grad, down_grad, channel, up_bias_grad = pl.pallas_call(
+    field_grad = back(1, field_grad)
+    theirs, field_grad = together(theirs, field_grad)
+    up_grad, down_grad, *rest = pl.pallas_call(
         unpack_kernel,
         out_shape=(
             shape((C, HID), f32),
             shape((C, HID), f32),
-            shape((56, C), f32),
-            shape((16, 128), f32),
+            shape((49, C), f32),
+            shape((C,), f32),
+            shape((C,), f32),
+            shape((C,), f32),
+            shape((HID,), f32),
+            shape((C,), f32),
         ),
         in_specs=[VMEM] * 2,
-        out_specs=(VMEM,) * 4,
-        compiler_params=params(),
+        out_specs=(VMEM,) * 8,
+        compiler_params=params(12),
         name="unpack",
     )(mine, theirs)
+    depth_grad, depth_bias_grad, gain_grad, shift_grad, up_bias_grad, down_bias_grad = rest
     return (
         field_grad,
-        channel[0:49],
-        channel[49],
-        channel[50],
-        channel[51],
+        depth_grad,
+        depth_bias_grad,
+        gain_grad,
+        shift_grad,
         up_grad,
-        up_bias_grad.reshape(-1)[0:HID],
+        up_bias_grad,
         down_grad.T,
-        channel[52],
+        down_bias_grad,
     )
 
 

time: 121 us -> 108 us (0.89)
  local copies, waits for them, and re-layouts: 9.32 us -> 0 us
  waiting for transfers between devices: 29 us -> 22.1 us
  starting transfers between devices: 43.8 us -> 46.9 us
    ppermute x26, waiting for transfers between devices: 28.5 us -> 18.9 us  [flip(): return lax.ppermute(x, AXES, [(i, i ^ mask) for i in range(128)])]
    pallas_call x3 -> x5, Pallas kernels: 7.88 us -> 14.8 us  [the longest x2 8.92 us: back(): pl.pallas_call(functools.partial(back_kernel, t), out_shape=shape((2, TE,...]
    unnamed x20 -> x0, local copies, waits for them, and re-layouts: 5.03 us -> none
    pallas_call x1, Pallas kernels: 5.79 us -> 1.34 us  [local(): pl.pallas_call(grad_kernel, out_shape=(shape((2, TE, TE, C), bf16), narro...]
    ppermute x8, starting transfers between devices: 15.1 us -> 18 us  [swap(): return lax.ppermute(x, AXES, swap_pairs(kind))]
    ppermute x8, waiting for transfers between devices: 0.46 us -> 3.24 us  [swap(): return lax.ppermute(x, AXES, swap_pairs(kind))]
    pallas_call x1, Pallas kernels: 11.6 us -> 9.41 us  [local(): pl.pallas_call(front_kernel, out_shape=(shape((ROWS, 128), f32), shape((R...]
    pad x3 -> x0, local copies, waits for them, and re-layouts: 2.05 us -> none  [local(): jnp.pad(v, (0, HID - C))]
  transfers between devices with their start and end apart: 34 -> 34, of which waited for: 14 -> 13; matrix products, arithmetic and copies ran while one was open for 3% -> 1% of each run, Pallas kernels for 16% -> 20%
where the time goes in v2:
time: 108 us
  starting transfers between devices  46.9 us (43%)
  Pallas kernels  36.1 us (33%)
  waiting for transfers between devices  22.1 us (20%)
  other arithmetic  1.46 us (1%)
  between operations  1.1 us (1%)
    ppermute x26, starting transfers between devices, flip(): return lax.ppermute(x, AXES, [(i, i ^ mask) for i in range(128)])  28.9 us
    ppermute x26, waiting for transfers between devices, flip(): return lax.ppermute(x, AXES, [(i, i ^ mask) for i in range(128)])  18.9 us
    ppermute x8, starting transfers between devices, swap(): return lax.ppermute(x, AXES, swap_pairs(kind))  18 us
    pallas_call x1, Pallas kernels, local(): pl.pallas_call(front_kernel, out_shape=(shape((ROWS, 128), f32), shape((R...  9.41 us
    pallas_call x2, Pallas kernels, back(): pl.pallas_call(functools.partial(back_kernel, t), out_shape=shape((2, TE,...  8.92 us
    pallas_call x1, Pallas kernels, local(): pl.pallas_call(prep_kernel, out_shape=(p_shape, shape((2, GROUPS, TE * TE...  6.83 us
    pallas_call x1, Pallas kernels, local(): pl.pallas_call(taps_kernel, out_shape=shape((EXTRA, 128), f32), in_specs=...  4.44 us
    ppermute x8, waiting for transfers between devices, swap(): return lax.ppermute(x, AXES, swap_pairs(kind))  3.24 us
  transfers between devices with their start and end apart: 34, of which 13 were waited for; matrix products, arithmetic and copies ran while one was open for 1% of the time, Pallas kernels for 20%

profile of v2, /device:TPU:1, one launch (start us, length us, event | category | flops | bytes accessed | tf_op | source)
XLA Modules:
  0.0 107.8 jit_solution(5265425366132668826)
XLA Ops:
  0.7 1.2 %pack_rows.1 = (bf16[2,48,512]{2,1,0:T(8,128)(2,1)S(1)}, bf16[2,48,512]{2,1,0:T(8,128)(2,1)S(1)}, bf16[2,16,16,400]{3,2,1,0:T(8,128)(2,1)S(1)}, s32[2,16,16]{2,1,0:T(8,128)S(1)}) custom-call(bf16[2,16,16,400]{3,2,1,0:T(8,128)(2,1)} %field_ref, s32[2,16,16]{2,1,0:T(8,128)} %land_ref.1), custom_call_target="tpu_custom_call" | custom-call | tf_op jit(solution)/shard_map/pack_rows/pallas_call | solution.py:756
  1.8 1.5 %collective-permute-start = (bf16[2,48,512]{2,1,0:T(8,128)(2,1)S(1)}, bf16[2,48,512]{2,1,0:T(8,128)(2,1)S(1)}, u32[]{:S(2)}, u32[]{:S(2)}) collective-permute-start(bf16[2,48,512]{2,1,0:T(8,128)(2,1)S(1)} %get-tuple-element.90), channel_id=1, source_target_pairs={{0,1},{1,0},{2,3},{3,2},{4,5},{5,4},{6,7},{7,6},{8,9},{9,8},{10,11... | collective-permute-start | bytes 294920 | tf_op jit(solution)/shard_map/ppermute | solution.py:677
  3.3 1.3 %collective-permute-start.1 = (bf16[2,48,512]{2,1,0:T(8,128)(2,1)S(1)}, bf16[2,48,512]{2,1,0:T(8,128)(2,1)S(1)}, u32[]{:S(2)}, u32[]{:S(2)}) collective-permute-start(bf16[2,48,512]{2,1,0:T(8,128)(2,1)S(1)} %get-tuple-element.91), channel_id=1, source_target_pairs={{0,3},{1,2},{2,1},{3,0},{4,7},{5,6},{6,5},{7,4},{8,11},{9,10},{10,... | collective-permute-start | bytes 294920 | tf_op jit(solution)/shard_map/ppermute | solution.py:677
  4.6 3.2 %collective-permute-done.1.refs_3_.n2_ref = bf16[2,48,512]{2,1,0:T(8,128)(2,1)S(1)} collective-permute-done((bf16[2,48,512]{2,1,0:T(8,128)(2,1)S(1)}, bf16[2,48,512]{2,1,0:T(8,128)(2,1)S(1)}, u32[]{:S(2)}, u32[]{:S(2)}) %collective-permute-start.1) | collective-permute-done | bytes 98336 | tf_op jit(solution)/shard_map/ppermute | solution.py:677
  8.2 1.8 %collective-permute-start.2 = (bf16[2,80,512]{2,1,0:T(8,128)(2,1)S(1)}, bf16[2,80,512]{2,1,0:T(8,128)(2,1)S(1)}, u32[]{:S(2)}, u32[]{:S(2)}) collective-permute-start(bf16[2,80,512]{2,1,0:T(8,128)(2,1)S(1)} %get-tuple-element.96), channel_id=1, source_target_pairs={{0,4},{1,5},{2,6},{3,7},{4,0},{5,1},{6,2},{7,3},{8,12},{9,13},{10,... | collective-permute-start | bytes 491528 | tf_op jit(solution)/shard_map/ppermute | solution.py:677
  10.0 7.2 %collective-permute-start.3 = (bf16[2,80,512]{2,1,0:T(8,128)(2,1)S(1)}, bf16[2,80,512]{2,1,0:T(8,128)(2,1)S(1)}, u32[]{:S(2)}, u32[]{:S(2)}) collective-permute-start(bf16[2,80,512]{2,1,0:T(8,128)(2,1)S(1)} %get-tuple-element.97), channel_id=1, source_target_pairs={{0,124},{1,125},{2,126},{3,127},{4,8},{5,9},{6,10},{7,11},{8,4},{9... | collective-permute-start | bytes 491528 | tf_op jit(solution)/shard_map/ppermute | solution.py:677
  17.2 6.8 %prep.1 = (f32[2,4,704,128]{3,2,1,0:T(8,128)S(1)}, f32[2,4,256,128]{3,2,1,0:T(8,128)S(1)}, bf16[512,512]{1,0:T(8,128)(2,1)S(1)}, bf16[512,512]{1,0:T(8,128)(2,1)...) custom-call(s32[2,8]{1,0:T(2,128)} %beside_ref.7, ...), custom_call_target="tpu_custom_call" | custom-call | flops 1000000000 | bytes 16000000 | tf_op jit(solution)/shard_map/prep/pallas_call | solution.py:782
  24.1 9.4 %front.1 = (f32[5216,128]{1,0:T(8,128)S(1)}, bf16[5216,128]{1,0:T(8,128)(2,1)S(1)}, f32[512,400]{1,0:T(8,128)S(1)}, f32[512,400]{1,0:T(8,128)S(1)}, f32[512,128]...) custom-call(s32[2,8]{1,0:T(2,128)} %beside_ref.7, ...), custom_call_target="tpu_custom_call" | custom-call | tf_op jit(solution)/shard_map/front/pallas_call | solution.py:827
  34.3 1.3 %grad.1 = (bf16[2,16,16,400]{3,2,1,0:T(8,128)(2,1)S(1)}, bf16[2,48,512]{2,1,0:T(8,128)(2,1)S(1)}, bf16[2,48,512]{2,1,0:T(8,128)(2,1)S(1)}, f32[512,512]{1,0:T(8,128)S(1)}, f32[3,400]{1,0:T(4,128)S(1)}) custom-call(f32[512,400]{1,0:T(8,128)S(1)} %get-tuple-element.108.ng_ref, f32[512,400]{1,0:T(8,128)S(1)} %get-tuple-element.109.z_ref, ...), custom_call_target="tpu_custom_call" | custom-call | flops 1000000000 | bytes 16000000 | tf_op jit(solution)/shard_map/grad/pallas_call | solution.py:869
  35.6 1.4 %collective-permute-done.4.got_ref = bf16[5216,128]{1,0:T(8,128)(2,1)S(1)} collective-permute-done((bf16[5216,128]{1,0:T(8,128)(2,1)S(1)}, bf16[5216,128]{1,0:T(8,128)(2,1)S(1)}, u32[]{:S(2)}, u32[]{:S(2)}) %collective-permute-start.4) | collective-permute-done | bytes 1335328 | tf_op jit(solution)/shard_map/ppermute | solution.py:681
  38.1 1.2 %collective-permute-start.5 = (bf16[928,128]{1,0:T(8,128)(2,1)S(1)}, bf16[928,128]{1,0:T(8,128)(2,1)S(1)}, u32[]{:S(2)}, u32[]{:S(2)}) collective-permute-start(bf16[928,128]{1,0:T(8,128)(2,1)S(1)} %get-tuple-element.113), channel_id=1, source_target_pairs={{0,2},{1,3},{2,0},{3,1},{4,6},{5,7},{6,4},{7,5},{8,10},{9,11},{10,... | collective-permute-start | bytes 712712 | tf_op jit(solution)/shard_map/ppermute | solution.py:681
  39.3 4.4 %taps.1 = f32[272,128]{1,0:T(8,128)S(1)} custom-call(f32[8,128]{1,0:T(8,128)S(1)} %get-tuple-element.118.after_ref, f32[512,512]{1,0:T(8,128)S(1)} %get-tuple-element.119.y_ref, f32[2,4,704,128]{3,2,1,0:T(8,128)S(1)} %get-tuple-element.98.p_ref.p_in_ref, f32[2,4,144,128]{3,2,1,0:T(8,128)S(1)} %get-tuple-element.120.border_ref, ...), custom_call_target="tpu_custom_call" | custom-call | flops 1000000000 | bytes 16000000 | tf_op jit(solution)/shard_map/taps/pallas_call | solution.py:900
  43.9 3.4 %collective-permute-done.5 = bf16[928,128]{1,0:T(8,128)(2,1)S(1)} collective-permute-done((bf16[928,128]{1,0:T(8,128)(2,1)S(1)}, bf16[928,128]{1,0:T(8,128)(2,1)S(1)}, u32[]{:S(2)}, u32[]{:S(2)}) %collective-permute-start.5) | collective-permute-done | bytes 237600 | tf_op jit(solution)/shard_map/ppermute | solution.py:681
  47.8 1.4 %collective-permute-start.14 = (bf16[464,128]{1,0:T(8,128)(2,1)S(1)}, bf16[464,128]{1,0:T(8,128)(2,1)S(1)}, u32[]{:S(2)}, u32[]{:S(2)}) collective-permute-start(bf16[464,128]{1,0:T(8,128)(2,1)S(1)} %select_convert_fusion.1), channel_id=1, source_target_pairs={{0,4},{1,5},{2,6},{3,7},{4,0},{5,1},{6,2},{7,3},{8,12},{9,13},{10,... | collective-permute-start | bytes 356360 | tf_op jit(solution)/shard_map/ppermute | solution.py:681
  49.9 5.4 %collective-permute-start.23 = (bf16[2,80,512]{2,1,0:T(8,128)(2,1)S(1)}, bf16[2,80,512]{2,1,0:T(8,128)(2,1)S(1)}, u32[]{:S(2)}, u32[]{:S(2)}) collective-permute-start(bf16[2,80,512]{2,1,0:T(8,128)(2,1)S(1)} %get-tuple-element.138), channel_id=1, source_target_pairs={{0,124},{1,125},{2,126},{3,127},{4,8},{5,9},{6,10},{7,11},{8,4},{9... | collective-permute-start | bytes 491528 | tf_op jit(solution)/shard_map/ppermute | solution.py:677
  55.7 4.2 %collective-permute-done.15 = bf16[464,128]{1,0:T(8,128)(2,1)S(1)} collective-permute-done((bf16[464,128]{1,0:T(8,128)(2,1)S(1)}, bf16[464,128]{1,0:T(8,128)(2,1)S(1)}, u32[]{:S(2)}, u32[]{:S(2)}) %collective-permute-start.15) | collective-permute-done | bytes 118816 | tf_op jit(solution)/shard_map/ppermute | solution.py:681
  60.1 1.2 %collective-permute-start.12 = (bf16[464,128]{1,0:T(8,128)(2,1)S(1)}, bf16[464,128]{1,0:T(8,128)(2,1)S(1)}, u32[]{:S(2)}, u32[]{:S(2)}) collective-permute-start(bf16[464,128]{1,0:T(8,128)(2,1)S(1)} %add_convert_fusion.10), channel_id=1, source_target_pairs={{0,66},{1,67},{2,64},{3,65},{4,70},{5,71},{6,68},{7,69},{8,74},{9,... | collective-permute-start | bytes 356360 | tf_op jit(solution)/shard_map/ppermute | solution.py:681
  61.4 4.2 %collective-permute-start.20 = (bf16[512,128]{1,0:T(8,128)(2,1)S(1)}, bf16[512,128]{1,0:T(8,128)(2,1)S(1)}, u32[]{:S(2)}, u32[]{:S(2)}) collective-permute-start(bf16[512,128]{1,0:T(8,128)(2,1)S(1)} %add_convert_fusion.2), channel_id=1, source_target_pairs={{0,12},{1,13},{2,14},{3,15},{4,8},{5,9},{6,10},{7,11},{8,4},{9,5},... | collective-permute-start | bytes 393224 | tf_op jit(solution)/shard_map/ppermute | solution.py:681
  65.8 2.4 %collective-permute-start.13 = (bf16[464,128]{1,0:T(8,128)(2,1)S(1)}, bf16[464,128]{1,0:T(8,128)(2,1)S(1)}, u32[]{:S(2)}, u32[]{:S(2)}) collective-permute-start(bf16[464,128]{1,0:T(8,128)(2,1)S(1)} %add_convert_fusion.9), channel_id=1, source_target_pairs={{0,48},{1,49},{2,50},{3,51},{4,52},{5,53},{6,54},{7,55},{8,56},{9,... | collective-permute-start | bytes 356360 | tf_op jit(solution)/shard_map/ppermute | solution.py:681
  68.3 2.3 %collective-permute-start.21 = (bf16[512,128]{1,0:T(8,128)(2,1)S(1)}, bf16[512,128]{1,0:T(8,128)(2,1)S(1)}, u32[]{:S(2)}, u32[]{:S(2)}) collective-permute-start(bf16[512,128]{1,0:T(8,128)(2,1)S(1)} %add_convert_fusion.1), channel_id=1, source_target_pairs={{0,66},{1,67},{2,64},{3,65},{4,70},{5,71},{6,68},{7,69},{8,74},{9,... | collective-permute-start | bytes 393224 | tf_op jit(solution)/shard_map/ppermute | solution.py:681
  70.6 1.1 %collective-permute-done.17 = bf16[464,128]{1,0:T(8,128)(2,1)S(1)} collective-permute-done((bf16[464,128]{1,0:T(8,128)(2,1)S(1)}, bf16[464,128]{1,0:T(8,128)(2,1)S(1)}, u32[]{:S(2)}, u32[]{:S(2)}) %collective-permute-start.17) | collective-permute-done | bytes 118816 | tf_op jit(solution)/shard_map/ppermute | solution.py:681
  71.8 1.9 %collective-permute-done.21 = bf16[512,128]{1,0:T(8,128)(2,1)S(1)} collective-permute-done((bf16[512,128]{1,0:T(8,128)(2,1)S(1)}, bf16[512,128]{1,0:T(8,128)(2,1)S(1)}, u32[]{:S(2)}, u32[]{:S(2)}) %collective-permute-start.21) | collective-permute-done | bytes 131104 | tf_op jit(solution)/shard_map/ppermute | solution.py:681
  73.7 2.2 %collective-permute-start.24 = (bf16[464,128]{1,0:T(8,128)(2,1)S(1)}, bf16[464,128]{1,0:T(8,128)(2,1)S(1)}, u32[]{:S(2)}, u32[]{:S(2)}) collective-permute-start(bf16[464,128]{1,0:T(8,128)(2,1)S(1)} %convert_add_fusion.5), channel_id=1, source_target_pairs={{0,12},{1,13},{2,14},{3,15},{4,8},{5,9},{6,10},{7,11},{8,4},{9,5},... | collective-permute-start | bytes 356360 | tf_op jit(solution)/shard_map/ppermute | solution.py:681
  76.2 2.6 %collective-permute-start.28 = (bf16[512,128]{1,0:T(8,128)(2,1)S(1)}, bf16[512,128]{1,0:T(8,128)(2,1)S(1)}, u32[]{:S(2)}, u32[]{:S(2)}) collective-permute-start(bf16[512,128]{1,0:T(8,128)(2,1)S(1)} %convert_add_fusion.3), channel_id=1, source_target_pairs={{0,48},{1,49},{2,50},{3,51},{4,52},{5,53},{6,54},{7,55},{8,56},{9,... | collective-permute-start | bytes 393224 | tf_op jit(solution)/shard_map/ppermute | solution.py:681
  78.9 1.9 %collective-permute-done.26 = bf16[464,128]{1,0:T(8,128)(2,1)S(1)} collective-permute-done((bf16[464,128]{1,0:T(8,128)(2,1)S(1)}, bf16[464,128]{1,0:T(8,128)(2,1)S(1)}, u32[]{:S(2)}, u32[]{:S(2)}) %collective-permute-start.26) | collective-permute-done | bytes 118816 | tf_op jit(solution)/shard_map/ppermute | solution.py:681
  81.3 1.2 %collective-permute-done.25 = bf16[464,128]{1,0:T(8,128)(2,1)S(1)} collective-permute-done((bf16[464,128]{1,0:T(8,128)(2,1)S(1)}, bf16[464,128]{1,0:T(8,128)(2,1)S(1)}, u32[]{:S(2)}, u32[]{:S(2)}) %collective-permute-start.25) | collective-permute-done | bytes 118816 | tf_op jit(solution)/shard_map/ppermute | solution.py:681
  82.5 2.1 %collective-permute-done.27 = bf16[464,128]{1,0:T(8,128)(2,1)S(1)} collective-permute-done((bf16[464,128]{1,0:T(8,128)(2,1)S(1)}, bf16[464,128]{1,0:T(8,128)(2,1)S(1)}, u32[]{:S(2)}, u32[]{:S(2)}) %collective-permute-start.27) | collective-permute-done | bytes 118816 | tf_op jit(solution)/shard_map/ppermute | solution.py:681
  85.7 1.3 %collective-permute-start.32 = (bf16[1024,128]{1,0:T(8,128)(2,1)S(1)}, bf16[1024,128]{1,0:T(8,128)(2,1)S(1)}, u32[]{:S(2)}, u32[]{:S(2)}) collective-permute-start(bf16[1024,128]{1,0:T(8,128)(2,1)S(1)} %pad_maximum_fusion.1), channel_id=1, source_target_pairs={{0,4},{1,5},{2,6},{3,7},{4,0},{5,1},{6,2},{7,3},{8,12},{9,13},{10,... | collective-permute-start | bytes 786440 | tf_op jit(solution)/shard_map/ppermute | solution.py:681
  86.9 4.5 %back_0.1.refs_0_ = bf16[2,16,16,400]{3,2,1,0:T(8,128)(2,1)} custom-call(s32[2,8]{1,0:T(2,128)} %beside_ref.7, bf16[2,16,16,400]{3,2,1,0:T(8,128)(2,1)S(1)} %get-tuple-element.128.refs_0_.cg_ref, s32[2,16,16]{2,1,0:T(8,128)S(1)} %get-tuple-element.89.refs_1_.land_ref, bf16[512,512]{1,0:T(8,128)(2,1)S(1)} %get-tuple-element.100.gated_ref, ...), custom_call_target="tpu_custom_call" | custom-call | flops 1000000000 | bytes 16000000 | tf_op jit(solution)/shard_map/back_0/pallas_call | solution.py:940
  92.6 7.7 %collective-permute-start.33 = (bf16[5488,128]{1,0:T(8,128)(2,1)S(1)}, bf16[5488,128]{1,0:T(8,128)(2,1)S(1)}, u32[]{:S(2)}, u32[]{:S(2)}) collective-permute-start(bf16[5488,128]{1,0:T(8,128)(2,1)S(1)} %fusion.mine_ref), channel_id=1, source_target_pairs={{0,1},{1,0},{2,3},{3,2},{4,5},{5,4},{6,7},{7,6},{8,9},{9,8},{10,11... | collective-permute-start | bytes 4214792 | tf_op jit(solution)/shard_map/ppermute | solution.py:681
  100.3 4.5 %back_1.1 = bf16[2,16,16,400]{3,2,1,0:T(8,128)(2,1)} custom-call(s32[2,8]{1,0:T(2,128)} %beside_ref.7, bf16[2,16,16,400]{3,2,1,0:T(8,128)(2,1)S(1)} %get-tuple-element.128.refs_0_.cg_ref, s32[2,16,16]{2,1,0:T(8,128)S(1)} %get-tuple-element.89.refs_1_.land_ref, bf16[512,512]{1,0:T(8,128)(2,1)S(1)} %get-tuple-element.100.gated_ref, ...), custom_call_target="tpu_custom_call", output_to_operand_aliasing={{}: (9, {})} | custom-call | flops 1000000000 | bytes 16000000 | tf_op jit(solution)/shard_map/back_1/pallas_call | solution.py:940
  104.8 3.0 %unpack.1 = (f32[400,1600]{1,0:T(8,128)}, f32[400,1600]{1,0:T(8,128)}, f32[49,400]{1,0:T(8,128)}, f32[400]{0:T(512)}, f32[400]{0:T(512)}, /*index=5*/f32[400]{0:T(512)}, f32[1600]{0:T(1024)}, f32[400]{0:T(512)}) custom-call(bf16[5488,128]{1,0:T(8,128)(2,1)S(1)} %fusion.mine_ref, bf16[5488,128]{1,0:T(8,128)(2,1)S(1)} %collective-permute-done.33.theirs_ref), custom_call_target="tpu_custom_call" | custom-call | tf_op jit(solution)/shard_map/unpack/pallas_call | solution.py:976
  (81 shorter events, 7.6 us)
Async XLA Ops:
  3.3 4.5 %collective-permute-start.1 = (bf16[2,48,512]{2,1,0:T(8,128)(2,1)S(1)}, bf16[2,48,512]{2,1,0:T(8,128)(2,1)S(1)}, u32[]{:S(2)}, u32[]{:S(2)}) collective-permute-start(bf16[2,48,512]{2,1,0:T(8,128)(2,1)S(1)} %get-tuple-element.91), channel_id=1, source_target_pairs={{0,3},{1,2},{2,1},{3,0},{4,7},{5,6},{6,5},{7,4},{8,11},{9,10},{10,... | collective-permute-start | bytes 294920 | tf_op jit(solution)/shard_map/ppermute | solution.py:677
  8.2 15.8 %collective-permute-start.2 = (bf16[2,80,512]{2,1,0:T(8,128)(2,1)S(1)}, bf16[2,80,512]{2,1,0:T(8,128)(2,1)S(1)}, u32[]{:S(2)}, u32[]{:S(2)}) collective-permute-start(bf16[2,80,512]{2,1,0:T(8,128)(2,1)S(1)} %get-tuple-element.96), channel_id=1, source_target_pairs={{0,4},{1,5},{2,6},{3,7},{4,0},{5,1},{6,2},{7,3},{8,12},{9,13},{10,... | collective-permute-start | bytes 491528 | tf_op jit(solution)/shard_map/ppermute | solution.py:677
  10.0 14.0 %collective-permute-start.3 = (bf16[2,80,512]{2,1,0:T(8,128)(2,1)S(1)}, bf16[2,80,512]{2,1,0:T(8,128)(2,1)S(1)}, u32[]{:S(2)}, u32[]{:S(2)}) collective-permute-start(bf16[2,80,512]{2,1,0:T(8,128)(2,1)S(1)} %get-tuple-element.97), channel_id=1, source_target_pairs={{0,124},{1,125},{2,126},{3,127},{4,8},{5,9},{6,10},{7,11},{8,4},{9... | collective-permute-start | bytes 491528 | tf_op jit(solution)/shard_map/ppermute | solution.py:677
  37.2 6.5 %collective-permute-start.7 = (bf16[752,128]{1,0:T(8,128)(2,1)S(1)}, bf16[752,128]{1,0:T(8,128)(2,1)S(1)}, u32[]{:S(2)}, u32[]{:S(2)}) collective-permute-start(bf16[752,128]{1,0:T(8,128)(2,1)S(1)} %get-tuple-element.117), channel_id=1, source_target_pairs={{0,4},{1,5},{2,6},{3,7},{4,0},{5,1},{6,2},{7,3},{8,12},{9,13},{10,... | collective-permute-start | bytes 577544 | tf_op jit(solution)/shard_map/ppermute | solution.py:681
  37.3 10.0 %collective-permute-start.8 = (bf16[2,48,512]{2,1,0:T(8,128)(2,1)S(1)}, bf16[2,48,512]{2,1,0:T(8,128)(2,1)S(1)}, u32[]{:S(2)}, u32[]{:S(2)}) collective-permute-start(bf16[2,48,512]{2,1,0:T(8,128)(2,1)S(1)} %get-tuple-element.123), channel_id=1, source_target_pairs={{0,1},{1,0},{2,3},{3,2},{4,5},{5,4},{6,7},{7,6},{8,9},{9,8},{10,11... | collective-permute-start | bytes 294920 | tf_op jit(solution)/shard_map/ppermute | solution.py:677
  37.8 9.6 %collective-permute-start.9 = (bf16[2,48,512]{2,1,0:T(8,128)(2,1)S(1)}, bf16[2,48,512]{2,1,0:T(8,128)(2,1)S(1)}, u32[]{:S(2)}, u32[]{:S(2)}) collective-permute-start(bf16[2,48,512]{2,1,0:T(8,128)(2,1)S(1)} %get-tuple-element.124), channel_id=1, source_target_pairs={{0,3},{1,2},{2,1},{3,0},{4,7},{5,6},{6,5},{7,4},{8,11},{9,10},{10,... | collective-permute-start | bytes 294920 | tf_op jit(solution)/shard_map/ppermute | solution.py:677
  38.1 9.1 %collective-permute-start.5 = (bf16[928,128]{1,0:T(8,128)(2,1)S(1)}, bf16[928,128]{1,0:T(8,128)(2,1)S(1)}, u32[]{:S(2)}, u32[]{:S(2)}) collective-permute-start(bf16[928,128]{1,0:T(8,128)(2,1)S(1)} %get-tuple-element.113), channel_id=1, source_target_pairs={{0,2},{1,3},{2,0},{3,1},{4,6},{5,7},{6,4},{7,5},{8,10},{9,11},{10,... | collective-permute-start | bytes 712712 | tf_op jit(solution)/shard_map/ppermute | solution.py:681
  39.3 8.0 %collective-permute-start.6 = (bf16[928,128]{1,0:T(8,128)(2,1)S(1)}, bf16[928,128]{1,0:T(8,128)(2,1)S(1)}, u32[]{:S(2)}, u32[]{:S(2)}) collective-permute-start(bf16[928,128]{1,0:T(8,128)(2,1)S(1)} %get-tuple-element.115), channel_id=1, source_target_pairs={{0,16},{1,17},{2,18},{3,19},{4,20},{5,21},{6,22},{7,23},{8,24},{9,... | collective-permute-start | bytes 712712 | tf_op jit(solution)/shard_map/ppermute | solution.py:681
  47.8 7.5 %collective-permute-start.14 = (bf16[464,128]{1,0:T(8,128)(2,1)S(1)}, bf16[464,128]{1,0:T(8,128)(2,1)S(1)}, u32[]{:S(2)}, u32[]{:S(2)}) collective-permute-start(bf16[464,128]{1,0:T(8,128)(2,1)S(1)} %select_convert_fusion.1), channel_id=1, source_target_pairs={{0,4},{1,5},{2,6},{3,7},{4,0},{5,1},{6,2},{7,3},{8,12},{9,13},{10,... | collective-permute-start | bytes 356360 | tf_op jit(solution)/shard_map/ppermute | solution.py:681
  49.2 6.2 %collective-permute-start.10 = (bf16[464,128]{1,0:T(8,128)(2,1)S(1)}, bf16[464,128]{1,0:T(8,128)(2,1)S(1)}, u32[]{:S(2)}, u32[]{:S(2)}) collective-permute-start(bf16[464,128]{1,0:T(8,128)(2,1)S(1)} %select_convert_fusion.2), channel_id=1, source_target_pairs={{0,16},{1,17},{2,18},{3,19},{4,20},{5,21},{6,22},{7,23},{8,24},{9,... | collective-permute-start | bytes 356360 | tf_op jit(solution)/shard_map/ppermute | solution.py:681
  49.4 6.2 %collective-permute-start.18 = (bf16[512,128]{1,0:T(8,128)(2,1)S(1)}, bf16[512,128]{1,0:T(8,128)(2,1)S(1)}, u32[]{:S(2)}, u32[]{:S(2)}) collective-permute-start(bf16[512,128]{1,0:T(8,128)(2,1)S(1)} %select_convert_fusion), channel_id=1, source_target_pairs={{0,2},{1,3},{2,0},{3,1},{4,6},{5,7},{6,4},{7,5},{8,10},{9,11},{10,... | collective-permute-start | bytes 393224 | tf_op jit(solution)/shard_map/ppermute | solution.py:681
  49.7 24.0 %collective-permute-start.22 = (bf16[2,80,512]{2,1,0:T(8,128)(2,1)S(1)}, bf16[2,80,512]{2,1,0:T(8,128)(2,1)S(1)}, u32[]{:S(2)}, u32[]{:S(2)}) collective-permute-start(bf16[2,80,512]{2,1,0:T(8,128)(2,1)S(1)} %get-tuple-element.137), channel_id=1, source_target_pairs={{0,4},{1,5},{2,6},{3,7},{4,0},{5,1},{6,2},{7,3},{8,12},{9,13},{10,... | collective-permute-start | bytes 491528 | tf_op jit(solution)/shard_map/ppermute | solution.py:677
  49.9 23.9 %collective-permute-start.23 = (bf16[2,80,512]{2,1,0:T(8,128)(2,1)S(1)}, bf16[2,80,512]{2,1,0:T(8,128)(2,1)S(1)}, u32[]{:S(2)}, u32[]{:S(2)}) collective-permute-start(bf16[2,80,512]{2,1,0:T(8,128)(2,1)S(1)} %get-tuple-element.138), channel_id=1, source_target_pairs={{0,124},{1,125},{2,126},{3,127},{4,8},{5,9},{6,10},{7,11},{8,4},{9... | collective-permute-start | bytes 491528 | tf_op jit(solution)/shard_map/ppermute | solution.py:677
  55.3 4.6 %collective-permute-start.15 = (bf16[464,128]{1,0:T(8,128)(2,1)S(1)}, bf16[464,128]{1,0:T(8,128)(2,1)S(1)}, u32[]{:S(2)}, u32[]{:S(2)}) collective-permute-start(bf16[464,128]{1,0:T(8,128)(2,1)S(1)} %add_convert_fusion.8), channel_id=1, source_target_pairs={{0,2},{1,3},{2,0},{3,1},{4,6},{5,7},{6,4},{7,5},{8,10},{9,11},{10,... | collective-permute-start | bytes 356360 | tf_op jit(solution)/shard_map/ppermute | solution.py:681
  55.5 4.6 %collective-permute-start.11 = (bf16[464,128]{1,0:T(8,128)(2,1)S(1)}, bf16[464,128]{1,0:T(8,128)(2,1)S(1)}, u32[]{:S(2)}, u32[]{:S(2)}) collective-permute-start(bf16[464,128]{1,0:T(8,128)(2,1)S(1)} %add_convert_fusion.11), channel_id=1, source_target_pairs={{0,4},{1,5},{2,6},{3,7},{4,0},{5,1},{6,2},{7,3},{8,12},{9,13},{10,... | collective-permute-start | bytes 356360 | tf_op jit(solution)/shard_map/ppermute | solution.py:681
  55.6 5.8 %collective-permute-start.19 = (bf16[512,128]{1,0:T(8,128)(2,1)S(1)}, bf16[512,128]{1,0:T(8,128)(2,1)S(1)}, u32[]{:S(2)}, u32[]{:S(2)}) collective-permute-start(bf16[512,128]{1,0:T(8,128)(2,1)S(1)} %add_convert_fusion.3), channel_id=1, source_target_pairs={{0,16},{1,17},{2,18},{3,19},{4,20},{5,21},{6,22},{7,23},{8,24},{9,... | collective-permute-start | bytes 393224 | tf_op jit(solution)/shard_map/ppermute | solution.py:681
  60.0 5.6 %collective-permute-start.16 = (bf16[464,128]{1,0:T(8,128)(2,1)S(1)}, bf16[464,128]{1,0:T(8,128)(2,1)S(1)}, u32[]{:S(2)}, u32[]{:S(2)}) collective-permute-start(bf16[464,128]{1,0:T(8,128)(2,1)S(1)} %add_convert_fusion.7), channel_id=1, source_target_pairs={{0,48},{1,49},{2,50},{3,51},{4,52},{5,53},{6,54},{7,55},{8,56},{9,... | collective-permute-start | bytes 356360 | tf_op jit(solution)/shard_map/ppermute | solution.py:681
  60.1 5.6 %collective-permute-start.12 = (bf16[464,128]{1,0:T(8,128)(2,1)S(1)}, bf16[464,128]{1,0:T(8,128)(2,1)S(1)}, u32[]{:S(2)}, u32[]{:S(2)}) collective-permute-start(bf16[464,128]{1,0:T(8,128)(2,1)S(1)} %add_convert_fusion.10), channel_id=1, source_target_pairs={{0,66},{1,67},{2,64},{3,65},{4,70},{5,71},{6,68},{7,69},{8,74},{9,... | collective-permute-start | bytes 356360 | tf_op jit(solution)/shard_map/ppermute | solution.py:681
  61.4 6.8 %collective-permute-start.20 = (bf16[512,128]{1,0:T(8,128)(2,1)S(1)}, bf16[512,128]{1,0:T(8,128)(2,1)S(1)}, u32[]{:S(2)}, u32[]{:S(2)}) collective-permute-start(bf16[512,128]{1,0:T(8,128)(2,1)S(1)} %add_convert_fusion.2), channel_id=1, source_target_pairs={{0,12},{1,13},{2,14},{3,15},{4,8},{5,9},{6,10},{7,11},{8,4},{9,5},... | collective-permute-start | bytes 393224 | tf_op jit(solution)/shard_map/ppermute | solution.py:681
  65.6 6.1 %collective-permute-start.17 = (bf16[464,128]{1,0:T(8,128)(2,1)S(1)}, bf16[464,128]{1,0:T(8,128)(2,1)S(1)}, u32[]{:S(2)}, u32[]{:S(2)}) collective-permute-start(bf16[464,128]{1,0:T(8,128)(2,1)S(1)} %add_convert_fusion.6), channel_id=1, source_target_pairs={{0,12},{1,13},{2,14},{3,15},{4,8},{5,9},{6,10},{7,11},{8,4},{9,5},... | collective-permute-start | bytes 356360 | tf_op jit(solution)/shard_map/ppermute | solution.py:681
  65.8 6.0 %collective-permute-start.13 = (bf16[464,128]{1,0:T(8,128)(2,1)S(1)}, bf16[464,128]{1,0:T(8,128)(2,1)S(1)}, u32[]{:S(2)}, u32[]{:S(2)}) collective-permute-start(bf16[464,128]{1,0:T(8,128)(2,1)S(1)} %add_convert_fusion.9), channel_id=1, source_target_pairs={{0,48},{1,49},{2,50},{3,51},{4,52},{5,53},{6,54},{7,55},{8,56},{9,... | collective-permute-start | bytes 356360 | tf_op jit(solution)/shard_map/ppermute | solution.py:681
  68.3 5.4 %collective-permute-start.21 = (bf16[512,128]{1,0:T(8,128)(2,1)S(1)}, bf16[512,128]{1,0:T(8,128)(2,1)S(1)}, u32[]{:S(2)}, u32[]{:S(2)}) collective-permute-start(bf16[512,128]{1,0:T(8,128)(2,1)S(1)} %add_convert_fusion.1), channel_id=1, source_target_pairs={{0,66},{1,67},{2,64},{3,65},{4,70},{5,71},{6,68},{7,69},{8,74},{9,... | collective-permute-start | bytes 393224 | tf_op jit(solution)/shard_map/ppermute | solution.py:681
  73.7 5.0 %collective-permute-start.24 = (bf16[464,128]{1,0:T(8,128)(2,1)S(1)}, bf16[464,128]{1,0:T(8,128)(2,1)S(1)}, u32[]{:S(2)}, u32[]{:S(2)}) collective-permute-start(bf16[464,128]{1,0:T(8,128)(2,1)S(1)} %convert_add_fusion.5), channel_id=1, source_target_pairs={{0,12},{1,13},{2,14},{3,15},{4,8},{5,9},{6,10},{7,11},{8,4},{9,5},... | collective-permute-start | bytes 356360 | tf_op jit(solution)/shard_map/ppermute | solution.py:681
  75.9 4.9 %collective-permute-start.26 = (bf16[464,128]{1,0:T(8,128)(2,1)S(1)}, bf16[464,128]{1,0:T(8,128)(2,1)S(1)}, u32[]{:S(2)}, u32[]{:S(2)}) collective-permute-start(bf16[464,128]{1,0:T(8,128)(2,1)S(1)} %convert_add_fusion.4), channel_id=1, source_target_pairs={{0,66},{1,67},{2,64},{3,65},{4,70},{5,71},{6,68},{7,69},{8,74},{9,... | collective-permute-start | bytes 356360 | tf_op jit(solution)/shard_map/ppermute | solution.py:681
  76.2 5.0 %collective-permute-start.28 = (bf16[512,128]{1,0:T(8,128)(2,1)S(1)}, bf16[512,128]{1,0:T(8,128)(2,1)S(1)}, u32[]{:S(2)}, u32[]{:S(2)}) collective-permute-start(bf16[512,128]{1,0:T(8,128)(2,1)S(1)} %convert_add_fusion.3), channel_id=1, source_target_pairs={{0,48},{1,49},{2,50},{3,51},{4,52},{5,53},{6,54},{7,55},{8,56},{9,... | collective-permute-start | bytes 393224 | tf_op jit(solution)/shard_map/ppermute | solution.py:681
  78.8 3.8 %collective-permute-start.25 = (bf16[464,128]{1,0:T(8,128)(2,1)S(1)}, bf16[464,128]{1,0:T(8,128)(2,1)S(1)}, u32[]{:S(2)}, u32[]{:S(2)}) collective-permute-start(bf16[464,128]{1,0:T(8,128)(2,1)S(1)} %add_convert_fusion.5), channel_id=1, source_target_pairs={{0,16},{1,17},{2,18},{3,19},{4,20},{5,21},{6,22},{7,23},{8,24},{9,... | collective-permute-start | bytes 356360 | tf_op jit(solution)/shard_map/ppermute | solution.py:681
  80.8 3.8 %collective-permute-start.27 = (bf16[464,128]{1,0:T(8,128)(2,1)S(1)}, bf16[464,128]{1,0:T(8,128)(2,1)S(1)}, u32[]{:S(2)}, u32[]{:S(2)}) collective-permute-start(bf16[464,128]{1,0:T(8,128)(2,1)S(1)} %add_convert_fusion.4), channel_id=1, source_target_pairs={{0,4},{1,5},{2,6},{3,7},{4,0},{5,1},{6,2},{7,3},{8,12},{9,13},{10,... | collective-permute-start | bytes 356360 | tf_op jit(solution)/shard_map/ppermute | solution.py:681
  81.2 4.2 %collective-permute-start.29 = (bf16[512,128]{1,0:T(8,128)(2,1)S(1)}, bf16[512,128]{1,0:T(8,128)(2,1)S(1)}, u32[]{:S(2)}, u32[]{:S(2)}) collective-permute-start(bf16[512,128]{1,0:T(8,128)(2,1)S(1)} %add_convert_fusion), channel_id=1, source_target_pairs={{0,2},{1,3},{2,0},{3,1},{4,6},{5,7},{6,4},{7,5},{8,10},{9,11},{10,... | collective-permute-start | bytes 393224 | tf_op jit(solution)/shard_map/ppermute | solution.py:681
  85.5 5.9 %collective-permute-start.30 = (bf16[928,128]{1,0:T(8,128)(2,1)S(1)}, bf16[928,128]{1,0:T(8,128)(2,1)S(1)}, u32[]{:S(2)}, u32[]{:S(2)}) collective-permute-start(bf16[928,128]{1,0:T(8,128)(2,1)S(1)} %pad_maximum_fusion.2), channel_id=1, source_target_pairs={{0,2},{1,3},{2,0},{3,1},{4,6},{5,7},{6,4},{7,5},{8,10},{9,11},{10,... | collective-permute-start | bytes 712712 | tf_op jit(solution)/shard_map/ppermute | solution.py:681
  85.6 6.6 %collective-permute-start.31 = (bf16[928,128]{1,0:T(8,128)(2,1)S(1)}, bf16[928,128]{1,0:T(8,128)(2,1)S(1)}, u32[]{:S(2)}, u32[]{:S(2)}) collective-permute-start(bf16[928,128]{1,0:T(8,128)(2,1)S(1)} %pad_maximum_fusion.3), channel_id=1, source_target_pairs={{0,16},{1,17},{2,18},{3,19},{4,20},{5,21},{6,22},{7,23},{8,24},{9,... | collective-permute-start | bytes 712712 | tf_op jit(solution)/shard_map/ppermute | solution.py:681
  85.7 6.7 %collective-permute-start.32 = (bf16[1024,128]{1,0:T(8,128)(2,1)S(1)}, bf16[1024,128]{1,0:T(8,128)(2,1)S(1)}, u32[]{:S(2)}, u32[]{:S(2)}) collective-permute-start(bf16[1024,128]{1,0:T(8,128)(2,1)S(1)} %pad_maximum_fusion.1), channel_id=1, source_target_pairs={{0,4},{1,5},{2,6},{3,7},{4,0},{5,1},{6,2},{7,3},{8,12},{9,13},{10,... | collective-permute-start | bytes 786440 | tf_op jit(solution)/shard_map/ppermute | solution.py:681
  92.6 12.2 %collective-permute-start.33 = (bf16[5488,128]{1,0:T(8,128)(2,1)S(1)}, bf16[5488,128]{1,0:T(8,128)(2,1)S(1)}, u32[]{:S(2)}, u32[]{:S(2)}) collective-permute-start(bf16[5488,128]{1,0:T(8,128)(2,1)S(1)} %fusion.mine_ref), channel_id=1, source_target_pairs={{0,1},{1,0},{2,3},{3,2},{4,5},{5,4},{6,7},{7,6},{8,9},{9,8},{10,11... | collective-permute-start | bytes 4214792 | tf_op jit(solution)/shard_map/ppermute | solution.py:681
  (2 other events, 6.3 us)

commit v3 on v2

--- a/solution.py
+++ b/solution.py
@@ -77,8 +77,7 @@
 
 def wide_kernel(masked, *refs):
     if masked:
-        tiles_ref, land_ref, n1_ref, n2_ref, first_ref, second_ref, m_ref, r_ref, o_ref = refs
-        mask = land_mask(land_ref[...].reshape(2 * TE, TE))
+        tiles_ref, mask_ref, n1_ref, n2_ref, first_ref, second_ref, m_ref, r_ref, o_ref = refs
     else:
         tiles_ref, n1_ref, n2_ref, first_ref, second_ref, m_ref, r_ref, o_ref = refs
     n_even = lax.axis_index("narrow") % 2 == 0
@@ -87,7 +86,7 @@
     for s in range(2):
         cells = tiles_ref[s].reshape(TE * TE, C).astype(f32)
         if masked:
-            cells = cells * mask[s * TE * TE : (s + 1) * TE * TE]
+            cells = cells * mask_ref[s * TE * TE : (s + 1) * TE * TE, :]
         one = n1_ref[s].astype(f32)
         two = n2_ref[s].astype(f32)
         from_north = jnp.where(n_even, two, one)
@@ -114,10 +113,13 @@
 
 def place_centre(cells, s, p_ref):
     for g in range(GROUPS):
-        w = group_width(g)
         for r in range(TE):
             at = (r + 3) * PITCH + 8
-            p_ref[s, g, at : at + TE, 0:w] = cells[r * TE : (r + 1) * TE, lanes(g)]
+            p_ref[s, g, at : at + TE, :] = cells[r * TE : (r + 1) * TE, 128 * g : 128 * g + 128]
+
+
+def padded_lanes(cells):
+    return jnp.concatenate([cells, jnp.zeros((cells.shape[0], CP - C), cells.dtype)], axis=1)
 
 
 def place_rows(n1_ref, n2_ref, rn_ref):
@@ -261,13 +263,9 @@
     weight_ref[0:49, 0:C] = depth_weight_ref[...]
 
 
-def prep_kernel(
-    beside_ref,
-    field_ref,
+def hold_kernel(
     land_ref,
     cot_ref,
-    n1_ref,
-    n2_ref,
     depth_weight_ref,
     depth_bias_ref,
     gain_ref,
@@ -275,8 +273,7 @@
     up_bias_ref,
     up_ref,
     down_ref,
-    p_ref,
-    y_ref,
+    mask_ref,
     gated_ref,
     gated_t_ref,
     down_bias_ref,
@@ -284,45 +281,66 @@
     down_out_ref,
     taps_ref,
     small_ref,
-    rn_ref,
-    weight_ref,
     cot_in_ref,
     bias_in_ref,
     gain_in_ref,
     shift_in_ref,
     up_bias_in_ref,
-    neighbours_ref,
     sems,
 ):
-    copies = [
-        pltpu.make_async_copy(depth_weight_ref, taps_ref, sems.at[0]),
-        pltpu.make_async_copy(cot_ref, cot_in_ref, sems.at[1]),
-        pltpu.make_async_copy(up_ref, up_out_ref, sems.at[2]),
-        pltpu.make_async_copy(down_ref, down_out_ref, sems.at[3]),
-        pltpu.make_async_copy(depth_bias_ref, bias_in_ref, sems.at[4]),
-        pltpu.make_async_copy(gain_ref, gain_in_ref, sems.at[5]),
-        pltpu.make_async_copy(shift_ref, shift_in_ref, sems.at[6]),
-        pltpu.make_async_copy(up_bias_ref, up_bias_in_ref, sems.at[7]),
-        pltpu.make_async_copy(beside_ref, neighbours_ref, sems.at[8]),
-    ]
+    pairs = (
+        (cot_ref, cot_in_ref),
+        (depth_weight_ref, taps_ref),
+        (depth_bias_ref, bias_in_ref),
+        (gain_ref, gain_in_ref),
+        (shift_ref, shift_in_ref),
+        (up_bias_ref, up_bias_in_ref),
+        (up_ref, up_out_ref),
+        (down_ref, down_out_ref),
+    )
+    copies = [pltpu.make_async_copy(a, b, sems.at[k]) for k, (a, b) in enumerate(pairs)]
     for copy in copies:
         copy.start()
-    p_ref[...] = jnp.zeros(p_ref.shape, f32)
-    mask = land_mask(land_ref[...].reshape(2 * TE, TE))
-    for s in range(2):
-        cells = field_ref[s].reshape(TE * TE, C).astype(f32)
-        place_centre(cells * mask[s * TE * TE : (s + 1) * TE * TE], s, p_ref)
-    place_rows(n1_ref, n2_ref, rn_ref)
-    copies[8].wait()
-    each_group(lambda t, g: border_rows(neighbours_ref, p_ref, rn_ref, t, g))
-    for k in (0, 4, 5, 6, 7):
-        copies[k].wait()
+    mask_ref[...] = land_mask(land_ref[...].reshape(2 * TE, TE))
+    copies[0].wait()
+    gated = cot_in_ref[...].reshape(CELLS, C).astype(f32) * mask_ref[...]
+    gated_ref[...] = padded_lanes(gated).astype(bf16)
+    gated_t_ref[...] = gated_ref[...].T
+    down_bias_ref[...] = jnp.sum(gated, axis=0, keepdims=True)
+    for copy in copies[1:]:
+        copy.wait()
     small_ref[0:1, 0:C] = bias_in_ref[...].reshape(1, C)
     small_ref[1:2, 0:C] = gain_in_ref[...].reshape(1, C)
     small_ref[2:3, 0:C] = shift_in_ref[...].reshape(1, C)
     small_ref[3:4, :] = up_bias_in_ref[...].reshape(1, HID)
+
+
+def prep_kernel(
+    beside_ref,
+    field_ref,
+    mask_ref,
+    n1_ref,
+    n2_ref,
+    taps_ref,
+    small_ref,
+    p_ref,
+    y_ref,
+    rn_ref,
+    weight_ref,
+    neighbours_ref,
+    sem,
+):
+    copy = pltpu.make_async_copy(beside_ref, neighbours_ref, sem)
+    copy.start()
+    p_ref[...] = jnp.zeros(p_ref.shape, f32)
+    for s in range(2):
+        cells = field_ref[s].reshape(TE * TE, C).astype(f32)
+        place_centre(padded_lanes(cells * mask_ref[s * TE * TE : (s + 1) * TE * TE, :]), s, p_ref)
+    place_rows(n1_ref, n2_ref, rn_ref)
     take_weights(weight_ref, taps_ref)
     weight_ref[49:50, 0:C] = small_ref[0:1, 0:C]
+    copy.wait()
+    each_group(lambda t, g: border_rows(neighbours_ref, p_ref, rn_ref, t, g))
 
     def start(t, g, h):
         return weight_rows(weight_ref, g, [49]) * TE
@@ -332,15 +350,6 @@
             y_ref[t, g, pl.ds(r * TE + 8 * h, 8), :] = rows[r]
 
     convolve(p_ref, weight_ref, start, finish, False)
-
-    copies[1].wait()
-    gated = cot_in_ref[...].reshape(CELLS, C).astype(f32) * mask
-    gated_ref[...] = jnp.zeros(gated_ref.shape, bf16)
-    gated_ref[:, 0:C] = gated.astype(bf16)
-    gated_t_ref[...] = gated_ref[...].T
-    down_bias_ref[...] = jnp.sum(gated, axis=0, keepdims=True)
-    copies[2].wait()
-    copies[3].wait()
 
 
 def front_kernel(
@@ -592,54 +601,69 @@
     up_bias_ref[...] = vector[:, 0:HID].reshape(HID)
 
 
-def back_kernel(
-    t,
+def back_tile(t, p_ref, weight_ref, y_ref, tile_ref, gated_ref, mask_ref, out_ref, sem):
+    at = slice(t * TE * TE, (t + 1) * TE * TE)
+    y_ref[...] = gated_ref[at, :].astype(f32)
+
+    def place(g, h, r):
+        return (pl.ds(r * TE + 8 * h, 8), pl.ds(pl.multiple_of(g * 128, 128), 128))
+
+    def start(t, g, h):
+        return [y_ref[place(g, h, r)] for r in range(TE)]
+
+    def finish(t, g, h, rows):
+        for r in range(TE):
+            y_ref[place(g, h, r)] = rows[r]
+
+    convolve(p_ref, weight_ref, start, finish, True, (t,))
+    tile_ref[...] = (y_ref[:, 0:C] * mask_ref[at, :]).astype(bf16).reshape(TE, TE, C)
+    copy = pltpu.make_async_copy(tile_ref, out_ref.at[t], sem)
+    copy.start()
+    copy.wait()
+
+
+def back_first_kernel(
     beside_ref,
     cg_ref,
-    land_ref,
+    mask_ref,
     gated_ref,
     n1_ref,
     n2_ref,
     w1_ref,
     w2_ref,
-    depth_weight_ref,
-    *refs,
+    taps_ref,
+    out_ref,
+    p_ref,
+    rn_ref,
+    rw_ref,
+    weight_ref,
+    y_ref,
+    tile_ref,
+    neighbours_ref,
+    sem,
 ):
-    out_ref, p_ref, rn_ref, rw_ref, weight_ref, y_ref, tile_ref, neighbours_ref, sem = refs[-9:]
     copy = pltpu.make_async_copy(beside_ref, neighbours_ref, sem)
     copy.start()
-    p_ref[t] = jnp.zeros(p_ref.shape[1:], f32)
     for s in range(2):
-        place_centre(cg_ref[s].reshape(TE * TE, C).astype(f32), s, p_ref)
-    mask = land_mask(land_ref[t], 1)
+        place_centre(padded_lanes(cg_ref[s].reshape(TE * TE, C).astype(f32)), s, p_ref)
     place_rows(n1_ref, n2_ref, rn_ref)
     place_columns(w1_ref, w2_ref, rw_ref)
+    take_weights(weight_ref, taps_ref)
     copy.wait()
 
-    def borders(g, _):
+    def borders(t, g):
         border_rows(neighbours_ref, p_ref, rn_ref, t, g)
         border_columns(neighbours_ref, p_ref, rn_ref, rw_ref, t, g, column_in(p_ref, t, g))
-        return _
-
-    lax.fori_loop(0, GROUPS, borders, 0)
-    take_weights(weight_ref, depth_weight_ref)
-    y_ref[...] = gated_ref[t * TE * TE : (t + 1) * TE * TE, :].astype(f32)
-
-    def place(g, h, r):
-        return (pl.ds(r * TE + 8 * h, 8), pl.ds(pl.multiple_of(g * 128, 128), 128))
-
-    def start(t, g, h):
-        return [y_ref[place(g, h, r)] for r in range(TE)]
-
-    def finish(t, g, h, rows):
-        for r in range(TE):
-            y_ref[place(g, h, r)] = rows[r]
-
-    convolve(p_ref, weight_ref, start, finish, True, (t,))
-    tile_ref[...] = (y_ref[:, 0:C] * mask).astype(bf16).reshape(TE, TE, C)
-    copy = pltpu.make_async_copy(tile_ref, out_ref.at[t], sem)
-    copy.start()
-    copy.wait()
+
+    each_group(borders)
+    back_tile(0, p_ref, weight_ref, y_ref, tile_ref, gated_ref, mask_ref, out_ref, sem)
+
+
+def back_second_kernel(
+    p_ref, mask_ref, gated_ref, taps_ref, before_ref, out_ref, weight_ref, y_ref, tile_ref, sem
+):
+    take_weights(weight_ref, taps_ref)
+    back_tile(1, p_ref, weight_ref, y_ref, tile_ref, gated_ref, mask_ref, out_ref, sem)
 
 
 def params(size=16):
@@ -768,6 +792,42 @@
         name="pack_rows",
     )(stay(field), stay(land))
     n1, n2 = swap(s1, ("narrow", 0)), swap(s2, ("narrow", 1))
+    mask, gated, gated_t, down_bias_sum, up_held, down_held, taps, small = pl.pallas_call(
+        hold_kernel,
+        out_shape=(
+            shape((CELLS, C), f32),
+            shape((CELLS, CP), bf16),
+            shape((CP, CELLS), bf16),
+            shape((1, C), f32),
+            shape((C, HID), bf16),
+            shape((C, HID), bf16),
+            shape((49, C), f32),
+            shape((4, HID), f32),
+        ),
+        in_specs=[VMEM] + [HBM] * 8,
+        out_specs=(VMEM,) * 8,
+        scratch_shapes=[
+            pltpu.VMEM((2, TE, TE, C), bf16),
+            pltpu.VMEM((C,), f32),
+            pltpu.VMEM((C,), f32),
+            pltpu.VMEM((C,), f32),
+            pltpu.VMEM((HID,), f32),
+            pltpu.SemaphoreType.DMA((8,)),
+        ],
+        compiler_params=params(8),
+        cost_estimate=estimate(),
+        name="hold",
+    )(
+        land,
+        stay(cotangent),
+        stay(depth_weight),
+        stay(depth_bias),
+        stay(ln_gain),
+        stay(ln_shift),
+        stay(up_bias),
+        stay(up_weight),
+        stay(down_weight.T),
+    )
     s1, s2 = pl.pallas_call(
         functools.partial(wide_kernel, True),
         out_shape=(wide_shape, wide_shape),
@@ -776,53 +836,19 @@
         scratch_shapes=wide_scratch,
         compiler_params=params(8),
         name="pack_columns",
-    )(field, land, n1, n2)
+    )(field, mask, n1, n2)
     s1, s2, n1, n2 = together(s1, s2, n1, n2)
     w2, w1 = swap(s2, ("wide", 1)), swap(s1, ("wide", 0))
-    p, y, gated, gated_t, down_bias_sum, up_held, down_held, taps, small = pl.pallas_call(
+    p, y = pl.pallas_call(
         prep_kernel,
-        out_shape=(
-            p_shape,
-            shape((2, GROUPS, TE * TE, 128), f32),
-            shape((CELLS, CP), bf16),
-            shape((CP, CELLS), bf16),
-            shape((1, C), f32),
-            shape((C, HID), bf16),
-            shape((C, HID), bf16),
-            shape((49, C), f32),
-            shape((4, HID), f32),
-        ),
-        in_specs=[HBM, VMEM, VMEM, HBM, VMEM, VMEM] + [HBM] * 7,
-        out_specs=(VMEM,) * 9,
-        scratch_shapes=[
-            RN_SCRATCH,
-            W_SCRATCH,
-            pltpu.VMEM((2, TE, TE, C), bf16),
-            pltpu.VMEM((C,), f32),
-            pltpu.VMEM((C,), f32),
-            pltpu.VMEM((C,), f32),
-            pltpu.VMEM((HID,), f32),
-            NEIGHBOURS,
-            pltpu.SemaphoreType.DMA((9,)),
-        ],
+        out_shape=(p_shape, shape((2, GROUPS, TE * TE, 128), f32)),
+        in_specs=[HBM] + [VMEM] * 6,
+        out_specs=(VMEM,) * 2,
+        scratch_shapes=[RN_SCRATCH, W_SCRATCH, NEIGHBOURS, pltpu.SemaphoreType.DMA],
         compiler_params=params(8),
         cost_estimate=estimate(),
         name="prep",
-    )(
-        neighbours,
-        field,
-        land,
-        stay(cotangent),
-        n1,
-        n2,
-        stay(depth_weight),
-        stay(depth_bias),
-        stay(ln_gain),
-        stay(ln_shift),
-        stay(up_bias),
-        stay(up_weight),
-        stay(down_weight.T),
-    )
+    )(neighbours, field, mask, n1, n2, taps, small)
 
     keep, send, ng, z, r, up_bias_sum, border = pl.pallas_call(
         front_kernel,
@@ -912,7 +938,7 @@
     )(pieces[-1], cg_wide, p, border, sums, up_bias_sum, down_bias_sum)
     parts = [pieces[len(SIZES) + i] + got[i].astype(f32) for i, order in orders]
     parts[-1] = jnp.concatenate([parts[-1], extra], axis=0)
-    parts, n1, n2 = together(parts, n1, n2)
+    parts[-1], n1, n2 = together(parts[-1], n1, n2)
     s1, s2 = pl.pallas_call(
         functools.partial(wide_kernel, False),
         out_shape=(wide_shape, wide_shape),
@@ -929,36 +955,29 @@
     for stage in range(DEPTH, 6):
         parts = [doubled(parts[i], order[stage]) for i, order in orders]
         if stage == 4:
-            parts, w1, w2 = together(parts, w1, w2)
+            parts[-1], w1, w2 = together(parts[-1], w1, w2)
     parts = [part.astype(bf16) for part in parts]
     for stage in reversed(range(1, DEPTH)):
         parts = [joined(parts[i], order[stage], high[order[stage]]) for i, order in orders]
-    parts, w1, w2 = together(parts, w1, w2)
-
-    def back(t, *before):
-        operands = (neighbours, cg, land, gated, n1, n2, w1, w2, taps)
-        return pl.pallas_call(
-            functools.partial(back_kernel, t),
-            out_shape=shape((2, TE, TE, C), bf16),
-            in_specs=[HBM] + [VMEM] * 8 + [HBM] * len(before),
-            out_specs=HBM,
-            scratch_shapes=[
-                P_SCRATCH,
-                RN_SCRATCH,
-                RW_SCRATCH,
-                W_SCRATCH,
-                pltpu.VMEM((TE * TE, CP), f32),
-                pltpu.VMEM((TE, TE, C), bf16),
-                NEIGHBOURS,
-                pltpu.SemaphoreType.DMA,
-            ],
-            input_output_aliases={len(operands): 0} if before else {},
-            compiler_params=params(10),
-            cost_estimate=estimate(),
-            name=f"back_{t}",
-        )(*operands, *before)
-
-    field_grad = back(0)
+    parts[-1], w1, w2 = together(parts[-1], w1, w2)
+
+    tile_scratch = [
+        W_SCRATCH,
+        pltpu.VMEM((TE * TE, CP), f32),
+        pltpu.VMEM((TE, TE, C), bf16),
+    ]
+    field_grad, grad_p = pl.pallas_call(
+        back_first_kernel,
+        out_shape=(shape((2, TE, TE, C), bf16), p_shape),
+        in_specs=[HBM] + [VMEM] * 8,
+        out_specs=(HBM, VMEM),
+        scratch_shapes=[RN_SCRATCH, RW_SCRATCH]
+        + tile_scratch
+        + [NEIGHBOURS, pltpu.SemaphoreType.DMA],
+        compiler_params=params(8),
+        cost_estimate=estimate(),
+        name="back_first",
+    )(neighbours, cg, mask, gated, n1, n2, w1, w2, taps)
     matrix = [joined(parts[i], order[0], high[order[0]]) for i, order in orders[:-1]]
     last = parts[-1]
     order = ORDERS[-1]
@@ -971,7 +990,17 @@
     )
     mine, field_grad = together(mine, field_grad)
     theirs = flip(mine, 1)
-    field_grad = back(1, field_grad)
+    field_grad = pl.pallas_call(
+        back_second_kernel,
+        out_shape=shape((2, TE, TE, C), bf16),
+        in_specs=[VMEM] * 4 + [HBM],
+        out_specs=HBM,
+        scratch_shapes=tile_scratch + [pltpu.SemaphoreType.DMA],
+        input_output_aliases={4: 0},
+        compiler_params=params(8),
+        cost_estimate=estimate(),
+        name="back_second",
+    )(grad_p, mask, gated, taps, field_grad)
     theirs, field_grad = together(theirs, field_grad)
     up_grad, down_grad, *rest = pl.pallas_call(
         unpack_kernel,

time: 108 us -> 103 us (0.954)
  waiting for transfers between devices: 22.1 us -> 17.9 us
  starting transfers between devices: 46.9 us -> 45.2 us
    ppermute x26, starting transfers between devices: 28.9 us -> 26.1 us  [flip(): return lax.ppermute(x, AXES, [(i, i ^ mask) for i in range(128)])]
    ppermute x26, waiting for transfers between devices: 18.9 us -> 16.8 us  [flip(): return lax.ppermute(x, AXES, [(i, i ^ mask) for i in range(128)])]
    pallas_call x2 -> x3, Pallas kernels: 8.92 us -> 11 us  [the longest x1 5.72 us: local(): pl.pallas_call(back_first_kernel, out_shape=(shape((2, TE, TE, C), bf16),...]
    ppermute x8, waiting for transfers between devices: 3.24 us -> 1.16 us  [swap(): return lax.ppermute(x, AXES, swap_pairs(kind))]
    pallas_call x1, Pallas kernels: 6.83 us -> 5.71 us  [local(): pl.pallas_call(prep_kernel, out_shape=(p_shape, shape((2, GROUPS, TE * TE...]
    ppermute x8, starting transfers between devices: 18 us -> 19.1 us  [swap(): return lax.ppermute(x, AXES, swap_pairs(kind))]
  transfers between devices with their start and end apart: 34 -> 34, of which waited for: 13 -> 13; matrix products, arithmetic and copies ran while one was open for 1% -> 1% of each run, Pallas kernels for 20% -> 22%
where the time goes in v3:
time: 103 us
  starting transfers between devices  45.2 us (44%)
  Pallas kernels  37.1 us (36%)
  waiting for transfers between devices  17.9 us (17%)
  other arithmetic  1.53 us (1%)
  between operations  1.09 us (1%)
    ppermute x26, starting transfers between devices, flip(): return lax.ppermute(x, AXES, [(i, i ^ mask) for i in range(128)])  26.1 us
    ppermute x8, starting transfers between devices, swap(): return lax.ppermute(x, AXES, swap_pairs(kind))  19.1 us
    ppermute x26, waiting for transfers between devices, flip(): return lax.ppermute(x, AXES, [(i, i ^ mask) for i in range(128)])  16.8 us
    pallas_call x1, Pallas kernels, local(): pl.pallas_call(front_kernel, out_shape=(shape((ROWS, 128), f32), shape((R...  9.45 us
    pallas_call x1, Pallas kernels, local(): pl.pallas_call(back_first_kernel, out_shape=(shape((2, TE, TE, C), bf16),...  5.72 us
    pallas_call x1, Pallas kernels, local(): pl.pallas_call(prep_kernel, out_shape=(p_shape, shape((2, GROUPS, TE * TE...  5.71 us
    pallas_call x1, Pallas kernels, local(): pl.pallas_call(taps_kernel, out_shape=shape((EXTRA, 128), f32), in_specs=...  4.44 us
    pallas_call x1, Pallas kernels, local(): pl.pallas_call(back_second_kernel, out_shape=shape((2, TE, TE, C), bf16),...  3.25 us
  transfers between devices with their start and end apart: 34, of which 13 were waited for; matrix products, arithmetic and copies ran while one was open for 1% of the time, Pallas kernels for 22%

profile of v3, /device:TPU:1, one launch (start us, length us, event | category | flops | bytes accessed | tf_op | source)
XLA Modules:
  0.0 102.8 jit_solution(11826114222925614449)
XLA Ops:
  0.7 1.2 %pack_rows.1 = (bf16[2,48,512]{2,1,0:T(8,128)(2,1)S(1)}, bf16[2,48,512]{2,1,0:T(8,128)(2,1)S(1)}, bf16[2,16,16,400]{3,2,1,0:T(8,128)(2,1)S(1)}, s32[2,16,16]{2,1,0:T(8,128)S(1)}) custom-call(bf16[2,16,16,400]{3,2,1,0:T(8,128)(2,1)} %field_ref, s32[2,16,16]{2,1,0:T(8,128)} %land_ref.1), custom_call_target="tpu_custom_call" | custom-call | tf_op jit(solution)/shard_map/pack_rows/pallas_call | solution.py:780
  1.8 1.5 %collective-permute-start = (bf16[2,48,512]{2,1,0:T(8,128)(2,1)S(1)}, bf16[2,48,512]{2,1,0:T(8,128)(2,1)S(1)}, u32[]{:S(2)}, u32[]{:S(2)}) collective-permute-start(bf16[2,48,512]{2,1,0:T(8,128)(2,1)S(1)} %get-tuple-element.88), channel_id=1, source_target_pairs={{0,1},{1,0},{2,3},{3,2},{4,5},{5,4},{6,7},{7,6},{8,9},{9,8},{10,11... | collective-permute-start | bytes 294920 | tf_op jit(solution)/shard_map/ppermute | solution.py:701
  3.3 1.3 %collective-permute-start.1 = (bf16[2,48,512]{2,1,0:T(8,128)(2,1)S(1)}, bf16[2,48,512]{2,1,0:T(8,128)(2,1)S(1)}, u32[]{:S(2)}, u32[]{:S(2)}) collective-permute-start(bf16[2,48,512]{2,1,0:T(8,128)(2,1)S(1)} %get-tuple-element.89), channel_id=1, source_target_pairs={{0,3},{1,2},{2,1},{3,0},{4,7},{5,6},{6,5},{7,4},{8,11},{9,10},{10,... | collective-permute-start | bytes 294920 | tf_op jit(solution)/shard_map/ppermute | solution.py:701
  4.6 2.1 %hold.1 = (f32[512,400]{1,0:T(8,128)S(1)}, bf16[512,512]{1,0:T(8,128)(2,1)S(1)}, bf16[512,512]{1,0:T(8,128)(2,1)S(1)}, f32[1,400]{1,0:T(1,128)S(1)}, bf16[400,16...) custom-call(s32[2,16,16]{2,1,0:T(8,128)S(1)} %get-tuple-element.86.land_ref, ...), custom_call_target="tpu_custom_call" | custom-call | flops 1000000000 | bytes 16000000 | tf_op jit(solution)/shard_map/hold/pallas_call | solution.py:795
  6.7 1.1 %collective-permute-done.1.refs_3_.n2_ref = bf16[2,48,512]{2,1,0:T(8,128)(2,1)S(1)} collective-permute-done((bf16[2,48,512]{2,1,0:T(8,128)(2,1)S(1)}, bf16[2,48,512]{2,1,0:T(8,128)(2,1)S(1)}, u32[]{:S(2)}, u32[]{:S(2)}) %collective-permute-start.1) | collective-permute-done | bytes 98336 | tf_op jit(solution)/shard_map/ppermute | solution.py:701
  8.3 1.8 %collective-permute-start.2 = (bf16[2,80,512]{2,1,0:T(8,128)(2,1)S(1)}, bf16[2,80,512]{2,1,0:T(8,128)(2,1)S(1)}, u32[]{:S(2)}, u32[]{:S(2)}) collective-permute-start(bf16[2,80,512]{2,1,0:T(8,128)(2,1)S(1)} %get-tuple-element.94), channel_id=1, source_target_pairs={{0,4},{1,5},{2,6},{3,7},{4,0},{5,1},{6,2},{7,3},{8,12},{9,13},{10,... | collective-permute-start | bytes 491528 | tf_op jit(solution)/shard_map/ppermute | solution.py:701
  10.1 7.2 %collective-permute-start.3 = (bf16[2,80,512]{2,1,0:T(8,128)(2,1)S(1)}, bf16[2,80,512]{2,1,0:T(8,128)(2,1)S(1)}, u32[]{:S(2)}, u32[]{:S(2)}) collective-permute-start(bf16[2,80,512]{2,1,0:T(8,128)(2,1)S(1)} %get-tuple-element.95), channel_id=1, source_target_pairs={{0,124},{1,125},{2,126},{3,127},{4,8},{5,9},{6,10},{7,11},{8,4},{9... | collective-permute-start | bytes 491528 | tf_op jit(solution)/shard_map/ppermute | solution.py:701
  17.2 5.7 %prep.1 = (f32[2,4,704,128]{3,2,1,0:T(8,128)S(1)}, f32[2,4,256,128]{3,2,1,0:T(8,128)S(1)}) custom-call(s32[2,8]{1,0:T(2,128)} %beside_ref.5, bf16[2,16,16,400]{3,2,1,0:T(8,128)(2,1)S(1)} %get-tuple-element.85.refs_0_.field_ref, f32[512,400]{1,0:T(8,128)S(1)} %get-tuple-element.87.refs_1_.mask_ref, ...), custom_call_target="tpu_custom_call" | custom-call | flops 1000000000 | bytes 16000000 | tf_op jit(solution)/shard_map/prep/pallas_call | solution.py:842
  23.0 9.5 %front.1 = (f32[5216,128]{1,0:T(8,128)S(1)}, bf16[5216,128]{1,0:T(8,128)(2,1)S(1)}, f32[512,400]{1,0:T(8,128)S(1)}, f32[512,400]{1,0:T(8,128)S(1)}, f32[512,128]...) custom-call(s32[2,8]{1,0:T(2,128)} %beside_ref.5, ...), custom_call_target="tpu_custom_call" | custom-call | tf_op jit(solution)/shard_map/front/pallas_call | solution.py:853
  33.2 1.3 %grad.1 = (bf16[2,16,16,400]{3,2,1,0:T(8,128)(2,1)S(1)}, bf16[2,48,512]{2,1,0:T(8,128)(2,1)S(1)}, bf16[2,48,512]{2,1,0:T(8,128)(2,1)S(1)}, f32[512,512]{1,0:T(8,128)S(1)}, f32[3,400]{1,0:T(4,128)S(1)}) custom-call(f32[512,400]{1,0:T(8,128)S(1)} %get-tuple-element.106.ng_ref, f32[512,400]{1,0:T(8,128)S(1)} %get-tuple-element.107.z_ref, ...), custom_call_target="tpu_custom_call" | custom-call | flops 1000000000 | bytes 16000000 | tf_op jit(solution)/shard_map/grad/pallas_call | solution.py:895
  34.6 1.4 %collective-permute-done.4.got_ref = bf16[5216,128]{1,0:T(8,128)(2,1)S(1)} collective-permute-done((bf16[5216,128]{1,0:T(8,128)(2,1)S(1)}, bf16[5216,128]{1,0:T(8,128)(2,1)S(1)}, u32[]{:S(2)}, u32[]{:S(2)}) %collective-permute-start.4) | collective-permute-done | bytes 1335328 | tf_op jit(solution)/shard_map/ppermute | solution.py:705
  37.1 1.2 %collective-permute-start.5 = (bf16[928,128]{1,0:T(8,128)(2,1)S(1)}, bf16[928,128]{1,0:T(8,128)(2,1)S(1)}, u32[]{:S(2)}, u32[]{:S(2)}) collective-permute-start(bf16[928,128]{1,0:T(8,128)(2,1)S(1)} %get-tuple-element.111), channel_id=1, source_target_pairs={{0,2},{1,3},{2,0},{3,1},{4,6},{5,7},{6,4},{7,5},{8,10},{9,11},{10,... | collective-permute-start | bytes 712712 | tf_op jit(solution)/shard_map/ppermute | solution.py:705
  38.2 4.4 %taps.1 = f32[272,128]{1,0:T(8,128)S(1)} custom-call(f32[8,128]{1,0:T(8,128)S(1)} %get-tuple-element.116.after_ref, f32[512,512]{1,0:T(8,128)S(1)} %get-tuple-element.117.y_ref, f32[2,4,704,128]{3,2,1,0:T(8,128)S(1)} %get-tuple-element.98.p_ref.p_in_ref, f32[2,4,144,128]{3,2,1,0:T(8,128)S(1)} %get-tuple-element.118.border_ref, ...), custom_call_target="tpu_custom_call" | custom-call | flops 1000000000 | bytes 16000000 | tf_op jit(solution)/shard_map/taps/pallas_call | solution.py:926
  43.2 3.0 %collective-permute-done.5 = bf16[928,128]{1,0:T(8,128)(2,1)S(1)} collective-permute-done((bf16[928,128]{1,0:T(8,128)(2,1)S(1)}, bf16[928,128]{1,0:T(8,128)(2,1)S(1)}, u32[]{:S(2)}, u32[]{:S(2)}) %collective-permute-start.5) | collective-permute-done | bytes 237600 | tf_op jit(solution)/shard_map/ppermute | solution.py:705
  46.4 1.4 %collective-permute-start.17 = (bf16[464,128]{1,0:T(8,128)(2,1)S(1)}, bf16[464,128]{1,0:T(8,128)(2,1)S(1)}, u32[]{:S(2)}, u32[]{:S(2)}) collective-permute-start(bf16[464,128]{1,0:T(8,128)(2,1)S(1)} %select_convert_fusion.1), channel_id=1, source_target_pairs={{0,4},{1,5},{2,6},{3,7},{4,0},{5,1},{6,2},{7,3},{8,12},{9,13},{10,... | collective-permute-start | bytes 356360 | tf_op jit(solution)/shard_map/ppermute | solution.py:705
  48.4 6.5 %collective-permute-start.29 = (bf16[2,80,512]{2,1,0:T(8,128)(2,1)S(1)}, bf16[2,80,512]{2,1,0:T(8,128)(2,1)S(1)}, u32[]{:S(2)}, u32[]{:S(2)}) collective-permute-start(bf16[2,80,512]{2,1,0:T(8,128)(2,1)S(1)} %get-tuple-element.134), channel_id=1, source_target_pairs={{0,124},{1,125},{2,126},{3,127},{4,8},{5,9},{6,10},{7,11},{8,4},{9... | collective-permute-start | bytes 491528 | tf_op jit(solution)/shard_map/ppermute | solution.py:701
  55.4 4.3 %collective-permute-done.18 = bf16[464,128]{1,0:T(8,128)(2,1)S(1)} collective-permute-done((bf16[464,128]{1,0:T(8,128)(2,1)S(1)}, bf16[464,128]{1,0:T(8,128)(2,1)S(1)}, u32[]{:S(2)}, u32[]{:S(2)}) %collective-permute-start.18) | collective-permute-done | bytes 118816 | tf_op jit(solution)/shard_map/ppermute | solution.py:705
  59.9 1.2 %collective-permute-start.12 = (bf16[464,128]{1,0:T(8,128)(2,1)S(1)}, bf16[464,128]{1,0:T(8,128)(2,1)S(1)}, u32[]{:S(2)}, u32[]{:S(2)}) collective-permute-start(bf16[464,128]{1,0:T(8,128)(2,1)S(1)} %add_convert_fusion.12), channel_id=1, source_target_pairs={{0,66},{1,67},{2,64},{3,65},{4,70},{5,71},{6,68},{7,69},{8,74},{9,... | collective-permute-start | bytes 356360 | tf_op jit(solution)/shard_map/ppermute | solution.py:705
  61.1 2.9 %collective-permute-start.26 = (bf16[512,128]{1,0:T(8,128)(2,1)S(1)}, bf16[512,128]{1,0:T(8,128)(2,1)S(1)}, u32[]{:S(2)}, u32[]{:S(2)}) collective-permute-start(bf16[512,128]{1,0:T(8,128)(2,1)S(1)} %add_convert_fusion.2), channel_id=1, source_target_pairs={{0,12},{1,13},{2,14},{3,15},{4,8},{5,9},{6,10},{7,11},{8,4},{9,5},... | collective-permute-start | bytes 393224 | tf_op jit(solution)/shard_map/ppermute | solution.py:705
  65.1 2.8 %collective-permute-start.13 = (bf16[464,128]{1,0:T(8,128)(2,1)S(1)}, bf16[464,128]{1,0:T(8,128)(2,1)S(1)}, u32[]{:S(2)}, u32[]{:S(2)}) collective-permute-start(bf16[464,128]{1,0:T(8,128)(2,1)S(1)} %add_convert_fusion.11), channel_id=1, source_target_pairs={{0,48},{1,49},{2,50},{3,51},{4,52},{5,53},{6,54},{7,55},{8,56},{9,... | collective-permute-start | bytes 356360 | tf_op jit(solution)/shard_map/ppermute | solution.py:705
  67.9 1.2 %collective-permute-start.27 = (bf16[512,128]{1,0:T(8,128)(2,1)S(1)}, bf16[512,128]{1,0:T(8,128)(2,1)S(1)}, u32[]{:S(2)}, u32[]{:S(2)}) collective-permute-start(bf16[512,128]{1,0:T(8,128)(2,1)S(1)} %add_convert_fusion.1), channel_id=1, source_target_pairs={{0,66},{1,67},{2,64},{3,65},{4,70},{5,71},{6,68},{7,69},{8,74},{9,... | collective-permute-start | bytes 393224 | tf_op jit(solution)/shard_map/ppermute | solution.py:705
  69.2 2.1 %collective-permute-done.20 = bf16[464,128]{1,0:T(8,128)(2,1)S(1)} collective-permute-done((bf16[464,128]{1,0:T(8,128)(2,1)S(1)}, bf16[464,128]{1,0:T(8,128)(2,1)S(1)}, u32[]{:S(2)}, u32[]{:S(2)}) %collective-permute-start.20) | collective-permute-done | bytes 118816 | tf_op jit(solution)/shard_map/ppermute | solution.py:705
  72.2 0.9 collective-permute-start.14
  73.4 1.9 %collective-permute-start.30 = (bf16[512,128]{1,0:T(8,128)(2,1)S(1)}, bf16[512,128]{1,0:T(8,128)(2,1)S(1)}, u32[]{:S(2)}, u32[]{:S(2)}) collective-permute-start(bf16[512,128]{1,0:T(8,128)(2,1)S(1)} %convert_add_fusion.3), channel_id=1, source_target_pairs={{0,48},{1,49},{2,50},{3,51},{4,52},{5,53},{6,54},{7,55},{8,56},{9,... | collective-permute-start | bytes 393224 | tf_op jit(solution)/shard_map/ppermute | solution.py:705
  75.3 1.0 collective-permute-done.21
  76.4 1.1 %collective-permute-done.14 = bf16[464,128]{1,0:T(8,128)(2,1)S(1)} collective-permute-done((bf16[464,128]{1,0:T(8,128)(2,1)S(1)}, bf16[464,128]{1,0:T(8,128)(2,1)S(1)}, u32[]{:S(2)}, u32[]{:S(2)}) %collective-permute-start.14) | collective-permute-done | bytes 118816 | tf_op jit(solution)/shard_map/ppermute | solution.py:705
  78.6 1.5 %collective-permute-start.31 = (bf16[512,128]{1,0:T(8,128)(2,1)S(1)}, bf16[512,128]{1,0:T(8,128)(2,1)S(1)}, u32[]{:S(2)}, u32[]{:S(2)}) collective-permute-start(bf16[512,128]{1,0:T(8,128)(2,1)S(1)} %add_convert_fusion), channel_id=1, source_target_pairs={{0,2},{1,3},{2,0},{3,1},{4,6},{5,7},{6,4},{7,5},{8,10},{9,11},{10,... | collective-permute-start | bytes 393224 | tf_op jit(solution)/shard_map/ppermute | solution.py:705
  80.5 1.0 %collective-permute-done.15 = bf16[464,128]{1,0:T(8,128)(2,1)S(1)} collective-permute-done((bf16[464,128]{1,0:T(8,128)(2,1)S(1)}, bf16[464,128]{1,0:T(8,128)(2,1)S(1)}, u32[]{:S(2)}, u32[]{:S(2)}) %collective-permute-start.15) | collective-permute-done | bytes 118816 | tf_op jit(solution)/shard_map/ppermute | solution.py:705
  82.6 5.7 %back_first.1 = (bf16[2,16,16,400]{3,2,1,0:T(8,128)(2,1)}, f32[2,4,704,128]{3,2,1,0:T(8,128)S(1)}) custom-call(s32[2,8]{1,0:T(2,128)} %beside_ref.5, bf16[2,16,16,400]{3,2,1,0:T(8,128)(2,1)S(1)} %get-tuple-element.124.refs_0_.cg_ref, f32[512,400]{1,0:T(8,128)S(1)} %get-tuple-element.87.refs_1_.mask_ref, bf16[512,512]{1,0:T(8,128)(2,1)S(1)} %get-tuple-element.100.gated_ref, ...), custom_call_target="tpu_custom_call" | custom-call | flops 1000000000 | bytes 16000000 | tf_op jit(solution)/shard_map/back_first/pallas_call | solution.py:969
  88.9 7.8 %collective-permute-start.33 = (bf16[5488,128]{1,0:T(8,128)(2,1)S(1)}, bf16[5488,128]{1,0:T(8,128)(2,1)S(1)}, u32[]{:S(2)}, u32[]{:S(2)}) collective-permute-start(bf16[5488,128]{1,0:T(8,128)(2,1)S(1)} %fusion.mine_ref), channel_id=1, source_target_pairs={{0,1},{1,0},{2,3},{3,2},{4,5},{5,4},{6,7},{7,6},{8,9},{9,8},{10,11... | collective-permute-start | bytes 4214792 | tf_op jit(solution)/shard_map/ppermute | solution.py:705
  96.7 3.3 %back_second.1 = bf16[2,16,16,400]{3,2,1,0:T(8,128)(2,1)} custom-call(f32[2,4,704,128]{3,2,1,0:T(8,128)S(1)} %get-tuple-element.143.p_ref, f32[512,400]{1,0:T(8,128)S(1)} %get-tuple-element.87.refs_1_.mask_ref, bf16[512,512]{1,0:T(8,128)(2,1)S(1)} %get-tuple-element.100.gated_ref, ...), custom_call_target="tpu_custom_call", output_to_operand_aliasing={{}: (4, {})} | custom-call | flops 1000000000 | bytes 16000000 | tf_op jit(solution)/shard_map/back_second/pallas_call | solution.py:993
  100.0 2.8 %unpack.1 = (f32[400,1600]{1,0:T(8,128)}, f32[400,1600]{1,0:T(8,128)}, f32[49,400]{1,0:T(8,128)}, f32[400]{0:T(512)}, f32[400]{0:T(512)}, /*index=5*/f32[400]{0:T(512)}, f32[1600]{0:T(1024)}, f32[400]{0:T(512)}) custom-call(bf16[5488,128]{1,0:T(8,128)(2,1)S(1)} %fusion.mine_ref, bf16[5488,128]{1,0:T(8,128)(2,1)S(1)} %collective-permute-done.33.theirs_ref), custom_call_target="tpu_custom_call" | custom-call | tf_op jit(solution)/shard_map/unpack/pallas_call | solution.py:1005
  (83 shorter events, 9.8 us)
Async XLA Ops:
  1.8 4.8 %collective-permute-start = (bf16[2,48,512]{2,1,0:T(8,128)(2,1)S(1)}, bf16[2,48,512]{2,1,0:T(8,128)(2,1)S(1)}, u32[]{:S(2)}, u32[]{:S(2)}) collective-permute-start(bf16[2,48,512]{2,1,0:T(8,128)(2,1)S(1)} %get-tuple-element.88), channel_id=1, source_target_pairs={{0,1},{1,0},{2,3},{3,2},{4,5},{5,4},{6,7},{7,6},{8,9},{9,8},{10,11... | collective-permute-start | bytes 294920 | tf_op jit(solution)/shard_map/ppermute | solution.py:701
  3.3 4.5 %collective-permute-start.1 = (bf16[2,48,512]{2,1,0:T(8,128)(2,1)S(1)}, bf16[2,48,512]{2,1,0:T(8,128)(2,1)S(1)}, u32[]{:S(2)}, u32[]{:S(2)}) collective-permute-start(bf16[2,48,512]{2,1,0:T(8,128)(2,1)S(1)} %get-tuple-element.89), channel_id=1, source_target_pairs={{0,3},{1,2},{2,1},{3,0},{4,7},{5,6},{6,5},{7,4},{8,11},{9,10},{10,... | collective-permute-start | bytes 294920 | tf_op jit(solution)/shard_map/ppermute | solution.py:701
  8.3 14.7 %collective-permute-start.2 = (bf16[2,80,512]{2,1,0:T(8,128)(2,1)S(1)}, bf16[2,80,512]{2,1,0:T(8,128)(2,1)S(1)}, u32[]{:S(2)}, u32[]{:S(2)}) collective-permute-start(bf16[2,80,512]{2,1,0:T(8,128)(2,1)S(1)} %get-tuple-element.94), channel_id=1, source_target_pairs={{0,4},{1,5},{2,6},{3,7},{4,0},{5,1},{6,2},{7,3},{8,12},{9,13},{10,... | collective-permute-start | bytes 491528 | tf_op jit(solution)/shard_map/ppermute | solution.py:701
  10.1 12.9 %collective-permute-start.3 = (bf16[2,80,512]{2,1,0:T(8,128)(2,1)S(1)}, bf16[2,80,512]{2,1,0:T(8,128)(2,1)S(1)}, u32[]{:S(2)}, u32[]{:S(2)}) collective-permute-start(bf16[2,80,512]{2,1,0:T(8,128)(2,1)S(1)} %get-tuple-element.95), channel_id=1, source_target_pairs={{0,124},{1,125},{2,126},{3,127},{4,8},{5,9},{6,10},{7,11},{8,4},{9... | collective-permute-start | bytes 491528 | tf_op jit(solution)/shard_map/ppermute | solution.py:701
  36.2 6.5 %collective-permute-start.7 = (bf16[752,128]{1,0:T(8,128)(2,1)S(1)}, bf16[752,128]{1,0:T(8,128)(2,1)S(1)}, u32[]{:S(2)}, u32[]{:S(2)}) collective-permute-start(bf16[752,128]{1,0:T(8,128)(2,1)S(1)} %get-tuple-element.115), channel_id=1, source_target_pairs={{0,4},{1,5},{2,6},{3,7},{4,0},{5,1},{6,2},{7,3},{8,12},{9,13},{10,... | collective-permute-start | bytes 577544 | tf_op jit(solution)/shard_map/ppermute | solution.py:705
  36.3 6.5 %collective-permute-start.8 = (bf16[2,48,512]{2,1,0:T(8,128)(2,1)S(1)}, bf16[2,48,512]{2,1,0:T(8,128)(2,1)S(1)}, u32[]{:S(2)}, u32[]{:S(2)}) collective-permute-start(bf16[2,48,512]{2,1,0:T(8,128)(2,1)S(1)} %get-tuple-element.121), channel_id=1, source_target_pairs={{0,1},{1,0},{2,3},{3,2},{4,5},{5,4},{6,7},{7,6},{8,9},{9,8},{10,11... | collective-permute-start | bytes 294920 | tf_op jit(solution)/shard_map/ppermute | solution.py:701
  36.7 6.1 %collective-permute-start.9 = (bf16[2,48,512]{2,1,0:T(8,128)(2,1)S(1)}, bf16[2,48,512]{2,1,0:T(8,128)(2,1)S(1)}, u32[]{:S(2)}, u32[]{:S(2)}) collective-permute-start(bf16[2,48,512]{2,1,0:T(8,128)(2,1)S(1)} %get-tuple-element.122), channel_id=1, source_target_pairs={{0,3},{1,2},{2,1},{3,0},{4,7},{5,6},{6,5},{7,4},{8,11},{9,10},{10,... | collective-permute-start | bytes 294920 | tf_op jit(solution)/shard_map/ppermute | solution.py:701
  37.1 9.1 %collective-permute-start.5 = (bf16[928,128]{1,0:T(8,128)(2,1)S(1)}, bf16[928,128]{1,0:T(8,128)(2,1)S(1)}, u32[]{:S(2)}, u32[]{:S(2)}) collective-permute-start(bf16[928,128]{1,0:T(8,128)(2,1)S(1)} %get-tuple-element.111), channel_id=1, source_target_pairs={{0,2},{1,3},{2,0},{3,1},{4,6},{5,7},{6,4},{7,5},{8,10},{9,11},{10,... | collective-permute-start | bytes 712712 | tf_op jit(solution)/shard_map/ppermute | solution.py:705
  38.2 8.0 %collective-permute-start.6 = (bf16[928,128]{1,0:T(8,128)(2,1)S(1)}, bf16[928,128]{1,0:T(8,128)(2,1)S(1)}, u32[]{:S(2)}, u32[]{:S(2)}) collective-permute-start(bf16[928,128]{1,0:T(8,128)(2,1)S(1)} %get-tuple-element.113), channel_id=1, source_target_pairs={{0,16},{1,17},{2,18},{3,19},{4,20},{5,21},{6,22},{7,23},{8,24},{9,... | collective-permute-start | bytes 712712 | tf_op jit(solution)/shard_map/ppermute | solution.py:705
  46.4 8.6 %collective-permute-start.17 = (bf16[464,128]{1,0:T(8,128)(2,1)S(1)}, bf16[464,128]{1,0:T(8,128)(2,1)S(1)}, u32[]{:S(2)}, u32[]{:S(2)}) collective-permute-start(bf16[464,128]{1,0:T(8,128)(2,1)S(1)} %select_convert_fusion.1), channel_id=1, source_target_pairs={{0,4},{1,5},{2,6},{3,7},{4,0},{5,1},{6,2},{7,3},{8,12},{9,13},{10,... | collective-permute-start | bytes 356360 | tf_op jit(solution)/shard_map/ppermute | solution.py:705
  47.8 7.3 %collective-permute-start.10 = (bf16[464,128]{1,0:T(8,128)(2,1)S(1)}, bf16[464,128]{1,0:T(8,128)(2,1)S(1)}, u32[]{:S(2)}, u32[]{:S(2)}) collective-permute-start(bf16[464,128]{1,0:T(8,128)(2,1)S(1)} %select_convert_fusion.2), channel_id=1, source_target_pairs={{0,16},{1,17},{2,18},{3,19},{4,20},{5,21},{6,22},{7,23},{8,24},{9,... | collective-permute-start | bytes 356360 | tf_op jit(solution)/shard_map/ppermute | solution.py:705
  47.9 7.3 %collective-permute-start.24 = (bf16[512,128]{1,0:T(8,128)(2,1)S(1)}, bf16[512,128]{1,0:T(8,128)(2,1)S(1)}, u32[]{:S(2)}, u32[]{:S(2)}) collective-permute-start(bf16[512,128]{1,0:T(8,128)(2,1)S(1)} %select_convert_fusion), channel_id=1, source_target_pairs={{0,2},{1,3},{2,0},{3,1},{4,6},{5,7},{6,4},{7,5},{8,10},{9,11},{10,... | collective-permute-start | bytes 393224 | tf_op jit(solution)/shard_map/ppermute | solution.py:705
  48.3 25.1 %collective-permute-start.28 = (bf16[2,80,512]{2,1,0:T(8,128)(2,1)S(1)}, bf16[2,80,512]{2,1,0:T(8,128)(2,1)S(1)}, u32[]{:S(2)}, u32[]{:S(2)}) collective-permute-start(bf16[2,80,512]{2,1,0:T(8,128)(2,1)S(1)} %get-tuple-element.133), channel_id=1, source_target_pairs={{0,4},{1,5},{2,6},{3,7},{4,0},{5,1},{6,2},{7,3},{8,12},{9,13},{10,... | collective-permute-start | bytes 491528 | tf_op jit(solution)/shard_map/ppermute | solution.py:701
  48.4 24.9 %collective-permute-start.29 = (bf16[2,80,512]{2,1,0:T(8,128)(2,1)S(1)}, bf16[2,80,512]{2,1,0:T(8,128)(2,1)S(1)}, u32[]{:S(2)}, u32[]{:S(2)}) collective-permute-start(bf16[2,80,512]{2,1,0:T(8,128)(2,1)S(1)} %get-tuple-element.134), channel_id=1, source_target_pairs={{0,124},{1,125},{2,126},{3,127},{4,8},{5,9},{6,10},{7,11},{8,4},{9... | collective-permute-start | bytes 491528 | tf_op jit(solution)/shard_map/ppermute | solution.py:701
  55.0 4.7 %collective-permute-start.18 = (bf16[464,128]{1,0:T(8,128)(2,1)S(1)}, bf16[464,128]{1,0:T(8,128)(2,1)S(1)}, u32[]{:S(2)}, u32[]{:S(2)}) collective-permute-start(bf16[464,128]{1,0:T(8,128)(2,1)S(1)} %add_convert_fusion.8), channel_id=1, source_target_pairs={{0,2},{1,3},{2,0},{3,1},{4,6},{5,7},{6,4},{7,5},{8,10},{9,11},{10,... | collective-permute-start | bytes 356360 | tf_op jit(solution)/shard_map/ppermute | solution.py:705
  55.1 4.7 %collective-permute-start.11 = (bf16[464,128]{1,0:T(8,128)(2,1)S(1)}, bf16[464,128]{1,0:T(8,128)(2,1)S(1)}, u32[]{:S(2)}, u32[]{:S(2)}) collective-permute-start(bf16[464,128]{1,0:T(8,128)(2,1)S(1)} %add_convert_fusion.13), channel_id=1, source_target_pairs={{0,4},{1,5},{2,6},{3,7},{4,0},{5,1},{6,2},{7,3},{8,12},{9,13},{10,... | collective-permute-start | bytes 356360 | tf_op jit(solution)/shard_map/ppermute | solution.py:705
  55.3 5.8 %collective-permute-start.25 = (bf16[512,128]{1,0:T(8,128)(2,1)S(1)}, bf16[512,128]{1,0:T(8,128)(2,1)S(1)}, u32[]{:S(2)}, u32[]{:S(2)}) collective-permute-start(bf16[512,128]{1,0:T(8,128)(2,1)S(1)} %add_convert_fusion.3), channel_id=1, source_target_pairs={{0,16},{1,17},{2,18},{3,19},{4,20},{5,21},{6,22},{7,23},{8,24},{9,... | collective-permute-start | bytes 393224 | tf_op jit(solution)/shard_map/ppermute | solution.py:705
  59.7 5.0 %collective-permute-start.19 = (bf16[464,128]{1,0:T(8,128)(2,1)S(1)}, bf16[464,128]{1,0:T(8,128)(2,1)S(1)}, u32[]{:S(2)}, u32[]{:S(2)}) collective-permute-start(bf16[464,128]{1,0:T(8,128)(2,1)S(1)} %add_convert_fusion.7), channel_id=1, source_target_pairs={{0,48},{1,49},{2,50},{3,51},{4,52},{5,53},{6,54},{7,55},{8,56},{9,... | collective-permute-start | bytes 356360 | tf_op jit(solution)/shard_map/ppermute | solution.py:705
  59.9 5.2 %collective-permute-start.12 = (bf16[464,128]{1,0:T(8,128)(2,1)S(1)}, bf16[464,128]{1,0:T(8,128)(2,1)S(1)}, u32[]{:S(2)}, u32[]{:S(2)}) collective-permute-start(bf16[464,128]{1,0:T(8,128)(2,1)S(1)} %add_convert_fusion.12), channel_id=1, source_target_pairs={{0,66},{1,67},{2,64},{3,65},{4,70},{5,71},{6,68},{7,69},{8,74},{9,... | collective-permute-start | bytes 356360 | tf_op jit(solution)/shard_map/ppermute | solution.py:705
  61.1 6.8 %collective-permute-start.26 = (bf16[512,128]{1,0:T(8,128)(2,1)S(1)}, bf16[512,128]{1,0:T(8,128)(2,1)S(1)}, u32[]{:S(2)}, u32[]{:S(2)}) collective-permute-start(bf16[512,128]{1,0:T(8,128)(2,1)S(1)} %add_convert_fusion.2), channel_id=1, source_target_pairs={{0,12},{1,13},{2,14},{3,15},{4,8},{5,9},{6,10},{7,11},{8,4},{9,5},... | collective-permute-start | bytes 393224 | tf_op jit(solution)/shard_map/ppermute | solution.py:705
  64.7 6.5 %collective-permute-start.20 = (bf16[464,128]{1,0:T(8,128)(2,1)S(1)}, bf16[464,128]{1,0:T(8,128)(2,1)S(1)}, u32[]{:S(2)}, u32[]{:S(2)}) collective-permute-start(bf16[464,128]{1,0:T(8,128)(2,1)S(1)} %add_convert_fusion.6), channel_id=1, source_target_pairs={{0,12},{1,13},{2,14},{3,15},{4,8},{5,9},{6,10},{7,11},{8,4},{9,5},... | collective-permute-start | bytes 356360 | tf_op jit(solution)/shard_map/ppermute | solution.py:705
  65.1 7.1 %collective-permute-start.13 = (bf16[464,128]{1,0:T(8,128)(2,1)S(1)}, bf16[464,128]{1,0:T(8,128)(2,1)S(1)}, u32[]{:S(2)}, u32[]{:S(2)}) collective-permute-start(bf16[464,128]{1,0:T(8,128)(2,1)S(1)} %add_convert_fusion.11), channel_id=1, source_target_pairs={{0,48},{1,49},{2,50},{3,51},{4,52},{5,53},{6,54},{7,55},{8,56},{9,... | collective-permute-start | bytes 356360 | tf_op jit(solution)/shard_map/ppermute | solution.py:705
  67.9 5.4 %collective-permute-start.27 = (bf16[512,128]{1,0:T(8,128)(2,1)S(1)}, bf16[512,128]{1,0:T(8,128)(2,1)S(1)}, u32[]{:S(2)}, u32[]{:S(2)}) collective-permute-start(bf16[512,128]{1,0:T(8,128)(2,1)S(1)} %add_convert_fusion.1), channel_id=1, source_target_pairs={{0,66},{1,67},{2,64},{3,65},{4,70},{5,71},{6,68},{7,69},{8,74},{9,... | collective-permute-start | bytes 393224 | tf_op jit(solution)/shard_map/ppermute | solution.py:705
  71.3 5.0 %collective-permute-start.21 = (bf16[464,128]{1,0:T(8,128)(2,1)S(1)}, bf16[464,128]{1,0:T(8,128)(2,1)S(1)}, u32[]{:S(2)}, u32[]{:S(2)}) collective-permute-start(bf16[464,128]{1,0:T(8,128)(2,1)S(1)} %add_convert_fusion.5), channel_id=1, source_target_pairs={{0,66},{1,67},{2,64},{3,65},{4,70},{5,71},{6,68},{7,69},{8,74},{9,... | collective-permute-start | bytes 356360 | tf_op jit(solution)/shard_map/ppermute | solution.py:705
  72.2 5.3 %collective-permute-start.14 = (bf16[464,128]{1,0:T(8,128)(2,1)S(1)}, bf16[464,128]{1,0:T(8,128)(2,1)S(1)}, u32[]{:S(2)}, u32[]{:S(2)}) collective-permute-start(bf16[464,128]{1,0:T(8,128)(2,1)S(1)} %add_convert_fusion.10), channel_id=1, source_target_pairs={{0,12},{1,13},{2,14},{3,15},{4,8},{5,9},{6,10},{7,11},{8,4},{9,5},... | collective-permute-start | bytes 356360 | tf_op jit(solution)/shard_map/ppermute | solution.py:705
  73.4 5.1 %collective-permute-start.30 = (bf16[512,128]{1,0:T(8,128)(2,1)S(1)}, bf16[512,128]{1,0:T(8,128)(2,1)S(1)}, u32[]{:S(2)}, u32[]{:S(2)}) collective-permute-start(bf16[512,128]{1,0:T(8,128)(2,1)S(1)} %convert_add_fusion.3), channel_id=1, source_target_pairs={{0,48},{1,49},{2,50},{3,51},{4,52},{5,53},{6,54},{7,55},{8,56},{9,... | collective-permute-start | bytes 393224 | tf_op jit(solution)/shard_map/ppermute | solution.py:705
  76.3 4.1 %collective-permute-start.22 = (bf16[464,128]{1,0:T(8,128)(2,1)S(1)}, bf16[464,128]{1,0:T(8,128)(2,1)S(1)}, u32[]{:S(2)}, u32[]{:S(2)}) collective-permute-start(bf16[464,128]{1,0:T(8,128)(2,1)S(1)} %add_convert_fusion.4), channel_id=1, source_target_pairs={{0,4},{1,5},{2,6},{3,7},{4,0},{5,1},{6,2},{7,3},{8,12},{9,13},{10,... | collective-permute-start | bytes 356360 | tf_op jit(solution)/shard_map/ppermute | solution.py:705
  77.5 4.1 %collective-permute-start.15 = (bf16[464,128]{1,0:T(8,128)(2,1)S(1)}, bf16[464,128]{1,0:T(8,128)(2,1)S(1)}, u32[]{:S(2)}, u32[]{:S(2)}) collective-permute-start(bf16[464,128]{1,0:T(8,128)(2,1)S(1)} %add_convert_fusion.9), channel_id=1, source_target_pairs={{0,16},{1,17},{2,18},{3,19},{4,20},{5,21},{6,22},{7,23},{8,24},{9,... | collective-permute-start | bytes 356360 | tf_op jit(solution)/shard_map/ppermute | solution.py:705
  80.4 8.1 %collective-permute-start.23 = (bf16[928,128]{1,0:T(8,128)(2,1)S(1)}, bf16[928,128]{1,0:T(8,128)(2,1)S(1)}, u32[]{:S(2)}, u32[]{:S(2)}) collective-permute-start(bf16[928,128]{1,0:T(8,128)(2,1)S(1)} %pad_maximum_fusion.3), channel_id=1, source_target_pairs={{0,16},{1,17},{2,18},{3,19},{4,20},{5,21},{6,22},{7,23},{8,24},{9,... | collective-permute-start | bytes 712712 | tf_op jit(solution)/shard_map/ppermute | solution.py:705
  81.6 6.7 %collective-permute-start.16 = (bf16[928,128]{1,0:T(8,128)(2,1)S(1)}, bf16[928,128]{1,0:T(8,128)(2,1)S(1)}, u32[]{:S(2)}, u32[]{:S(2)}) collective-permute-start(bf16[928,128]{1,0:T(8,128)(2,1)S(1)} %pad_maximum_fusion.2), channel_id=1, source_target_pairs={{0,2},{1,3},{2,0},{3,1},{4,6},{5,7},{6,4},{7,5},{8,10},{9,11},{10,... | collective-permute-start | bytes 712712 | tf_op jit(solution)/shard_map/ppermute | solution.py:705
  82.5 6.2 %collective-permute-start.32 = (bf16[1024,128]{1,0:T(8,128)(2,1)S(1)}, bf16[1024,128]{1,0:T(8,128)(2,1)S(1)}, u32[]{:S(2)}, u32[]{:S(2)}) collective-permute-start(bf16[1024,128]{1,0:T(8,128)(2,1)S(1)} %pad_maximum_fusion.1), channel_id=1, source_target_pairs={{0,4},{1,5},{2,6},{3,7},{4,0},{5,1},{6,2},{7,3},{8,12},{9,13},{10,... | collective-permute-start | bytes 786440 | tf_op jit(solution)/shard_map/ppermute | solution.py:705
  88.9 11.1 %collective-permute-start.33 = (bf16[5488,128]{1,0:T(8,128)(2,1)S(1)}, bf16[5488,128]{1,0:T(8,128)(2,1)S(1)}, u32[]{:S(2)}, u32[]{:S(2)}) collective-permute-start(bf16[5488,128]{1,0:T(8,128)(2,1)S(1)} %fusion.mine_ref), channel_id=1, source_target_pairs={{0,1},{1,0},{2,3},{3,2},{4,5},{5,4},{6,7},{7,6},{8,9},{9,8},{10,11... | collective-permute-start | bytes 4214792 | tf_op jit(solution)/shard_map/ppermute | solution.py:705
  (2 other events, 7.4 us)

commit v4 on v3

--- a/solution.py
+++ b/solution.py
@@ -20,9 +20,12 @@
 HT = 13
 PITCH = 32
 ROWS = HT * C + 16
+PIECES = ((0, 1024, 8 * C), (1024, 576, 5 * C + 16))
 EXTRA = 272
 SIZES = (1856, 1856, 1504)
 AXES = ("wide", "narrow")
+SLOT_ROWS = 3 * 72 + 16
+SIDE_ROWS = 2 * SLOT_ROWS
 f32 = jnp.float32
 bf16 = jnp.bfloat16
 VMEM = pl.BlockSpec(memory_space=pltpu.VMEM)
@@ -77,9 +80,9 @@
 
 def wide_kernel(masked, *refs):
     if masked:
-        tiles_ref, mask_ref, n1_ref, n2_ref, first_ref, second_ref, m_ref, r_ref, o_ref = refs
+        tiles_ref, mask_ref, n1_ref, n2_ref, first_ref, second_ref, m_ref, r_ref, o_ref, q_ref = refs
     else:
-        tiles_ref, n1_ref, n2_ref, first_ref, second_ref, m_ref, r_ref, o_ref = refs
+        tiles_ref, n1_ref, n2_ref, first_ref, second_ref, m_ref, r_ref, o_ref, q_ref = refs
     n_even = lax.axis_index("narrow") % 2 == 0
     w_even = lax.axis_index("wide") % 2 == 0
     zero_lanes(o_ref)
@@ -105,10 +108,20 @@
                     o_ref[side, s, g, at : at + 3, :] = r_ref[0, s, g, pl.ds(col, 3, stride=TE), :]
                     o_ref[side, s, g, at + 3 : at + 19, 0:w] = m_ref[s, g, pl.ds(col, TE, stride=TE), 0:w]
                     o_ref[side, s, g, at + 19 : at + 22, :] = r_ref[1, s, g, pl.ds(col, 3, stride=TE), :]
-            west = o_ref[0, s, g]
-            east = o_ref[1, s, g]
-            first_ref[s, :, 128 * g : 128 * g + 128] = jnp.where(w_even, east, west).astype(bf16)
-            second_ref[s, :, 128 * g : 128 * g + 128] = jnp.where(w_even, west, east).astype(bf16)
+            west = o_ref[0, s, g, 0:72, :]
+            east = o_ref[1, s, g, 0:72, :]
+            at = s * SLOT_ROWS + g * 72
+            for k, value in enumerate((jnp.where(w_even, east, west), jnp.where(w_even, west, east))):
+                if g < GROUPS - 1:
+                    q_ref[k, at : at + 72, :] = value
+                else:
+                    blocks = [value[8 * j : 8 * j + 8, 0:16] for j in range(9)]
+                    q_ref[k, at : at + 8, :] = jnp.concatenate(blocks[0:8], axis=1)
+                    q_ref[k, at + 8 : at + 16, :] = jnp.concatenate(
+                        [blocks[8], jnp.zeros((8, 112), f32)], axis=1
+                    )
+    first_ref[...] = q_ref[0].astype(bf16)
+    second_ref[...] = q_ref[1].astype(bf16)
 
 
 def place_centre(cells, s, p_ref):
@@ -137,15 +150,22 @@
 
 def place_columns(w1_ref, w2_ref, rw_ref):
     w_even = lax.axis_index("wide") % 2 == 0
-    for s in range(2):
-        one = w1_ref[s].astype(f32)
-        two = w2_ref[s].astype(f32)
-        west = jnp.where(w_even, two, one)
-        east = jnp.where(w_even, one, two)
-        for g in range(GROUPS):
-            at = slice(128 * g, 128 * g + 128)
-            rw_ref[0, s, g] = west[:, at]
-            rw_ref[1, s, g] = east[:, at]
+    one = w1_ref[...].astype(f32)
+    two = w2_ref[...].astype(f32)
+    for side, value in enumerate((jnp.where(w_even, two, one), jnp.where(w_even, one, two))):
+        for s in range(2):
+            for g in range(GROUPS):
+                at = s * SLOT_ROWS + g * 72
+                if g < GROUPS - 1:
+                    rw_ref[side, s, g, 0:72, :] = value[at : at + 72]
+                else:
+                    for j in range(9):
+                        rows = value[at : at + 8] if j < 8 else value[at + 8 : at + 16]
+                        lane = 16 * j % 128
+                        block = jnp.concatenate(
+                            [rows[:, lane : lane + 16], jnp.zeros((8, 112), f32)], axis=1
+                        )
+                        rw_ref[side, s, g, 8 * j : 8 * j + 8, :] = block
 
 
 def entry_of(neighbours_ref, t, d):
@@ -369,20 +389,19 @@
     keep_ref,
     send_ref,
     ng_ref,
+    up_bias_sum_ref,
     z_ref,
     r_ref,
-    up_bias_sum_ref,
     border_ref,
+    normed_ref,
+    normed_t_ref,
     rn_ref,
     rw_ref,
     weight_ref,
     y_ref,
-    normed_ref,
-    normed_t_ref,
     neighbours_ref,
     sem,
 ):
-    core0 = lax.axis_index("narrow") % 2 == 0
     copy = pltpu.make_async_copy(beside_ref, neighbours_ref, sem)
     copy.start()
     place_rows(n1_ref, n2_ref, rn_ref)
@@ -412,12 +431,12 @@
     each_group(sides)
 
     normed_ref[...] = jnp.zeros(normed_ref.shape, bf16)
-    step_rows = 64
+    step_rows = 128
 
     def norm(i, _):
         at = pl.ds(pl.multiple_of(i * step_rows, step_rows), step_rows)
-        inside = pl.ds(pl.multiple_of((i % 4) * step_rows, step_rows), step_rows)
-        conv = jnp.concatenate([y_ref[i // 4, g, inside, :] for g in range(GROUPS)], axis=1)[:, 0:C]
+        inside = pl.ds(pl.multiple_of((i % 2) * step_rows, step_rows), step_rows)
+        conv = jnp.concatenate([y_ref[i // 2, g, inside, :] for g in range(GROUPS)], axis=1)[:, 0:C]
         mean = jnp.sum(conv, axis=1, keepdims=True) * (1.0 / C)
         dev = conv - mean
         var = jnp.sum(dev * dev, axis=1, keepdims=True) * (1.0 / C)
@@ -431,14 +450,51 @@
     lax.fori_loop(0, CELLS // step_rows, norm, 0)
     normed_t_ref[...] = normed_ref[...].T
 
+    hidden(
+        0,
+        normed_ref,
+        normed_t_ref,
+        gated_ref,
+        gated_t_ref,
+        small_ref,
+        up_ref,
+        down_ref,
+        keep_ref,
+        send_ref,
+        ng_ref,
+        up_bias_sum_ref,
+    )
+
+
+def hidden(
+    piece,
+    normed_ref,
+    normed_t_ref,
+    gated_ref,
+    gated_t_ref,
+    small_ref,
+    up_ref,
+    down_ref,
+    keep_ref,
+    send_ref,
+    ng_ref,
+    up_bias_sum_ref,
+):
+    core0 = lax.axis_index("narrow") % 2 == 0
+    first, count, rows = PIECES[piece]
+    used = (count + 127) // 128 * C
+    if used < rows:
+        keep_ref[used:, :] = jnp.zeros((rows - used, 128), f32)
+        send_ref[used:, :] = jnp.zeros((rows - used, 128), bf16)
+
     def products(lo, width):
-        at = slice(lo, lo + width)
+        at = slice(first + lo, first + lo + width)
         h = jnp.dot(normed_ref[:, 0:C], up_ref[:, at], preferred_element_type=f32) + small_ref[3:4, at]
         ag = jnp.dot(gated_ref[:, 0:C], down_ref[:, at], preferred_element_type=f32)
         return h, ag
 
-    def hidden_chunk(lo, width, h, ag):
-        at = slice(lo, lo + width)
+    def gradients(lo, width, h, ag):
+        at = slice(first + lo, first + lo + width)
         act, slope = gelu_pair(h)
         hg = ag * slope
         hgb = hg.astype(bf16)
@@ -449,31 +505,31 @@
             ng_ref[...] = ng
         else:
             ng_ref[...] += ng
-        up_bias_sum_ref[:, at] = jnp.sum(hgb.astype(f32), axis=0, keepdims=True)
+        up_bias_sum_ref[:, lo : lo + width] = jnp.sum(hgb.astype(f32), axis=0, keepdims=True)
         keep = jnp.where(core0, ug, dg)
         send = jnp.where(core0, dg, ug).astype(bf16)
         for k in range((width + 127) // 128):
             w = min(128, width - 128 * k)
-            rows = slice((lo // 128 + k) * C, (lo // 128 + k + 1) * C)
+            at = slice((lo // 128 + k) * C, (lo // 128 + k + 1) * C)
             if w < 128:
-                keep_ref[rows, :] = jnp.zeros((C, 128), f32)
-                send_ref[rows, :] = jnp.zeros((C, 128), bf16)
-            keep_ref[rows, 0:w] = keep[:, 128 * k : 128 * k + w]
-            send_ref[rows, 0:w] = send[:, 128 * k : 128 * k + w]
-
-    keep_ref[HT * C :, :] = jnp.zeros((16, 128), f32)
-    send_ref[HT * C :, :] = jnp.zeros((16, 128), bf16)
-    chunks = ((0, 512), (512, 512), (1024, 576))
+                keep_ref[at, :] = jnp.zeros((C, 128), f32)
+                send_ref[at, :] = jnp.zeros((C, 128), bf16)
+            keep_ref[at, 0:w] = keep[:, 128 * k : 128 * k + w]
+            send_ref[at, 0:w] = send[:, 128 * k : 128 * k + w]
+
+    cut = 512 if piece == 0 else 256
+    chunks = ((0, cut), (cut, count - cut))
     ready = products(*chunks[0])
     for i, chunk in enumerate(chunks):
         current = ready
         if i + 1 < len(chunks):
             ready = products(*chunks[i + 1])
-        hidden_chunk(*chunk, *current)
+        gradients(*chunk, *current)
 
 
 def grad_kernel(
-    ng_ref,
+    ng0_ref,
+    ng1_ref,
     z_ref,
     r_ref,
     small_ref,
@@ -488,7 +544,7 @@
 
     def back(i, sums):
         at = pl.ds(pl.multiple_of(i * step_rows, step_rows), step_rows)
-        ng = ng_ref[at, :]
+        ng = ng0_ref[at, :] + ng1_ref[at, :]
         zhat = z_ref[at, :]
         rstd = r_ref[at, 0:1]
         q = ng * small_ref[1:2, 0:C]
@@ -517,7 +573,7 @@
     pack_narrow(tile_rows, lax.axis_index("narrow") % 2 == 0, g1_ref, g2_ref)
 
 def taps_kernel(
-    after_ref, y_ref, p_in_ref, border_ref, sums_ref, up_bias_sum_ref, down_bias_ref, extra_ref, p_ref, dw_ref
+    after_ref, y_ref, p_in_ref, border_ref, sums_ref, ub0_ref, ub1_ref, down_bias_ref, extra_ref, p_ref, dw_ref
 ):
     p_ref[...] = p_in_ref[...]
     dw_ref[...] = jnp.zeros(dw_ref.shape, f32)
@@ -557,24 +613,34 @@
         extra_ref[g * 64 + 50 : g * 64 + 51, 0:w] = sums_ref[1:2, lanes(g)]
         extra_ref[g * 64 + 51 : g * 64 + 52, 0:w] = sums_ref[2:3, lanes(g)]
         extra_ref[g * 64 + 52 : g * 64 + 53, 0:w] = down_bias_ref[:, lanes(g)]
-    for l in range(HT):
-        w = min(128, HID - 128 * l)
-        extra_ref[256 + l : 257 + l, 0:w] = up_bias_sum_ref[:, 128 * l : 128 * l + w]
-
-
-def split_kernel(keep_ref, got_ref, after_ref, *refs):
+    for (first, count, _), ref in zip(PIECES, (ub0_ref, ub1_ref)):
+        for lo in range(0, count, 128):
+            w = min(128, count - lo)
+            at = 256 + (first + lo) // 128
+            extra_ref[at : at + 1, 0:w] = ref[:, lo : lo + w]
+
+
+def split_kernel(keep0_ref, got0_ref, keep1_ref, got1_ref, after_ref, *refs):
     me = here()
     refs[-1][...] = jnp.zeros((8, 128), f32)
     lo = 0
     for i, size in enumerate(SIZES):
         send_ref, mine_ref = refs[i], refs[len(SIZES) + i]
-        high = parity(me, STAGES[ORDERS[i][0]][1])
+        high = jnp.where(keeps_high(me, ORDERS[i], 0), 1, 0)
         half = size // 2
         for j in range(2):
 
             def store(ref, lo=lo):
-                total = keep_ref[lo : lo + half, :] + got_ref[lo : lo + half, :].astype(f32)
-                ref[...] = total.astype(ref.dtype)
+                first = 0
+                for (_, _, rows), keep_ref, got_ref in zip(
+                    PIECES, (keep0_ref, keep1_ref), (got0_ref, got1_ref)
+                ):
+                    at = slice(max(lo - first, 0), min(lo + half - first, rows))
+                    if at.start < at.stop:
+                        total = keep_ref[at, :] + got_ref[at, :].astype(f32)
+                        to = slice(at.start + first - lo, at.stop + first - lo)
+                        ref[to, :] = total.astype(ref.dtype)
+                    first += rows
 
             pl.when(high == j)(functools.partial(store, mine_ref))
             pl.when(high != j)(functools.partial(store, send_ref))
@@ -725,21 +791,31 @@
     return sum((me >> bit) & 1 for bit in bits) & 1
 
 
-def halved(part, step, high):
+def exchange(x, order, stage):
+    masks = [STAGES[order[(stage + 3 * core) % 6]][0] for core in range(2)]
+    return lax.ppermute(x, AXES, [(i, i ^ masks[i & 1]) for i in range(128)])
+
+
+def keeps_high(me, order, stage):
+    zero, one = (parity(me, STAGES[order[(stage + 3 * core) % 6]][1]) for core in range(2))
+    return jnp.where(me % 2 == 0, zero, one) == 1
+
+
+def halved(part, order, stage, high):
     half = part.shape[0] // 2
     low_rows, high_rows = part[0:half], part[half:]
     send = jnp.where(high, low_rows, high_rows).astype(bf16)
     keep = jnp.where(high, high_rows, low_rows)
-    return keep + flip(send, STAGES[step][0]).astype(f32)
-
-
-def doubled(part, step):
+    return keep + exchange(send, order, stage).astype(f32)
+
+
+def doubled(part, order, stage):
     mine = part.astype(bf16)
-    return mine.astype(f32) + flip(mine, STAGES[step][0]).astype(f32)
-
-
-def joined(part, step, high):
-    got = flip(part, STAGES[step][0])
+    return mine.astype(f32) + exchange(mine, order, stage).astype(f32)
+
+
+def joined(part, order, stage, high):
+    got = exchange(part, order, stage)
     return jnp.concatenate([jnp.where(high, got, part), jnp.where(high, part, got)], axis=0)
 
 
@@ -763,17 +839,16 @@
     me = here()
     shape = jax.ShapeDtypeStruct
     stay = lambda v: pltpu.with_memory_space_constraint(v, pltpu.HBM)
-    steps = sorted({order[stage] for order in ORDERS for stage in range(DEPTH)})
-    highs = [parity(me, STAGES[step][1]) == 1 for step in steps]
-    highs, field = together(highs, field)
-    high = dict(zip(steps, highs))
+    high = [[keeps_high(me, order, stage) for stage in range(DEPTH)] for order in ORDERS]
+    high, field = together(high, field)
     neighbours = stay(neighbours)
     narrow_shape = shape((2, 48, CP), bf16)
-    wide_shape = shape((2, 80, CP), bf16)
+    wide_shape = shape((SIDE_ROWS, 128), bf16)
     wide_scratch = [
         pltpu.VMEM((2, GROUPS, TE * TE, 128), f32),
         RN_SCRATCH,
         RW_SCRATCH,
+        pltpu.VMEM((2, SIDE_ROWS, 128), f32),
     ]
     p_shape = shape((2, GROUPS, 22 * PITCH, 128), f32)
 
@@ -850,26 +925,32 @@
         name="prep",
     )(neighbours, field, mask, n1, n2, taps, small)
 
-    keep, send, ng, z, r, up_bias_sum, border = pl.pallas_call(
+    def piece_shapes(piece):
+        _, count, rows = PIECES[piece]
+        return (
+            shape((rows, 128), f32),
+            shape((rows, 128), bf16),
+            shape((CELLS, C), f32),
+            shape((1, count), f32),
+        )
+
+    keep0, send0, ng0, ub0, z, r, border, normed, normed_t = pl.pallas_call(
         front_kernel,
-        out_shape=(
-            shape((ROWS, 128), f32),
-            shape((ROWS, 128), bf16),
-            shape((CELLS, C), f32),
+        out_shape=piece_shapes(0)
+        + (
             shape((CELLS, C), f32),
             shape((CELLS, 128), f32),
-            shape((1, HID), f32),
             shape((2, GROUPS, 6 * 24, 128), f32),
+            shape((CELLS, CP), bf16),
+            shape((CP, CELLS), bf16),
         ),
         in_specs=[HBM] + [VMEM] * 12,
-        out_specs=(VMEM,) * 7,
+        out_specs=(VMEM,) * 9,
         scratch_shapes=[
             RN_SCRATCH,
             RW_SCRATCH,
             W_SCRATCH,
             pltpu.VMEM((2, GROUPS, TE * TE, 128), f32),
-            pltpu.VMEM((CELLS, CP), bf16),
-            pltpu.VMEM((CP, CELLS), bf16),
             NEIGHBOURS,
             pltpu.SemaphoreType.DMA,
         ],
@@ -890,8 +971,17 @@
         up_held,
         down_held,
     )
-
-    got = flip(send, 1)
+    got0 = flip(send0, 1)
+    keep1, send1, ng1, ub1 = pl.pallas_call(
+        functools.partial(hidden, 1),
+        out_shape=piece_shapes(1),
+        in_specs=[VMEM] * 7,
+        out_specs=(VMEM,) * 4,
+        compiler_params=params(12),
+        cost_estimate=estimate(),
+        name="hidden",
+    )(normed, normed_t, gated, gated_t, small, up_held, down_held)
+    got1 = flip(send1, 1)
     cg, g1, g2, cg_wide, sums = pl.pallas_call(
         grad_kernel,
         out_shape=(
@@ -901,12 +991,12 @@
             shape((CELLS, CP), f32),
             shape((3, C), f32),
         ),
-        in_specs=[VMEM] * 4,
+        in_specs=[VMEM] * 5,
         out_specs=(VMEM,) * 5,
         compiler_params=params(4),
         cost_estimate=estimate(),
         name="grad",
-    )(ng, z, r, small)
+    )(ng0, ng1, z, r, small)
 
     halves = [size // 2 for size in SIZES]
     pieces = pl.pallas_call(
@@ -914,19 +1004,19 @@
         out_shape=tuple(shape((half, 128), bf16) for half in halves)
         + tuple(shape((half, 128), f32) for half in halves)
         + (shape((8, 128), f32),),
-        in_specs=[VMEM] * 3,
+        in_specs=[VMEM] * 5,
         out_specs=(VMEM,) * (2 * len(SIZES) + 1),
         compiler_params=params(4),
         name="split",
-    )(keep, got, sums)
+    )(keep0, got0, keep1, got1, sums)
 
     orders = list(enumerate(ORDERS))
-    got = [flip(pieces[i], STAGES[order[0]][0]) for i, order in orders]
+    got = [exchange(pieces[i], order, 0) for i, order in orders]
     n1, n2 = swap(g1, ("narrow", 0)), swap(g2, ("narrow", 1))
     extra = pl.pallas_call(
         taps_kernel,
         out_shape=shape((EXTRA, 128), f32),
-        in_specs=[VMEM] * 7,
+        in_specs=[VMEM] * 8,
         out_specs=VMEM,
         scratch_shapes=[
             pltpu.VMEM(p_shape.shape, f32),
@@ -935,7 +1025,7 @@
         compiler_params=params(8),
         cost_estimate=estimate(),
         name="taps",
-    )(pieces[-1], cg_wide, p, border, sums, up_bias_sum, down_bias_sum)
+    )(pieces[-1], cg_wide, p, border, sums, ub0, ub1, down_bias_sum)
     parts = [pieces[len(SIZES) + i] + got[i].astype(f32) for i, order in orders]
     parts[-1] = jnp.concatenate([parts[-1], extra], axis=0)
     parts[-1], n1, n2 = together(parts[-1], n1, n2)
@@ -951,14 +1041,14 @@
     parts, s1, s2 = together(parts, s1, s2)
     w2, w1 = swap(s2, ("wide", 1)), swap(s1, ("wide", 0))
     for stage in range(1, DEPTH):
-        parts = [halved(parts[i], order[stage], high[order[stage]]) for i, order in orders]
+        parts = [halved(parts[i], order, stage, high[i][stage]) for i, order in orders]
     for stage in range(DEPTH, 6):
-        parts = [doubled(parts[i], order[stage]) for i, order in orders]
+        parts = [doubled(parts[i], order, stage) for i, order in orders]
         if stage == 4:
             parts[-1], w1, w2 = together(parts[-1], w1, w2)
     parts = [part.astype(bf16) for part in parts]
     for stage in reversed(range(1, DEPTH)):
-        parts = [joined(parts[i], order[stage], high[order[stage]]) for i, order in orders]
+        parts = [joined(parts[i], order, stage, high[i][stage]) for i, order in orders]
     parts[-1], w1, w2 = together(parts[-1], w1, w2)
 
     tile_scratch = [
@@ -978,12 +1068,12 @@
         cost_estimate=estimate(),
         name="back_first",
     )(neighbours, cg, mask, gated, n1, n2, w1, w2, taps)
-    matrix = [joined(parts[i], order[0], high[order[0]]) for i, order in orders[:-1]]
+    matrix = [joined(parts[i], order, 0, high[i][0]) for i, order in orders[:-1]]
     last = parts[-1]
     order = ORDERS[-1]
-    got = flip(last, STAGES[order[0]][0])
+    got = exchange(last, order, 0)
     one, two = last[0 : halves[-1]], got[0 : halves[-1]]
-    upper = high[order[0]]
+    upper = high[-1][0]
     extra = (last[halves[-1] :].astype(f32) + got[halves[-1] :].astype(f32)).astype(bf16)
     mine = jnp.concatenate(
         matrix + [jnp.where(upper, two, one), jnp.where(upper, one, two), extra], axis=0

time: 103 us -> 101 us (0.981)
  waiting for transfers between devices: 17.9 us -> 15.7 us
  starting transfers between devices: 45.2 us -> 46.8 us
  Pallas kernels: 37.1 us -> 35.6 us
    ppermute x0 -> x24, starting transfers between devices: none -> 25.4 us  [exchange(): return lax.ppermute(x, AXES, [(i, i ^ masks[i & 1]) for i in range(128)])]
    ppermute x26 -> x3, starting transfers between devices: 26.1 us -> 4.72 us  [flip(): return lax.ppermute(x, AXES, [(i, i ^ mask) for i in range(128)])]
    ppermute x26 -> x3, waiting for transfers between devices: 16.8 us -> 0.51 us  [flip(): return lax.ppermute(x, AXES, [(i, i ^ mask) for i in range(128)])]
    ppermute x0 -> x24, waiting for transfers between devices: none -> 14 us  [exchange(): return lax.ppermute(x, AXES, [(i, i ^ masks[i & 1]) for i in range(128)])]
    ppermute x8, starting transfers between devices: 19.1 us -> 16.7 us  [swap(): return lax.ppermute(x, AXES, swap_pairs(kind))]
    pallas_call x1 -> x2, Pallas kernels: 9.45 us -> 8.97 us  [the longest x1 6.49 us: local(): pl.pallas_call(front_kernel, out_shape=piece_shapes(0) + (shape((CELLS, C...]
  transfers between devices with their start and end apart: 34 -> 35, of which waited for: 13 -> 12; matrix products, arithmetic and copies ran while one was open for 1% -> 1% of each run, Pallas kernels for 22% -> 24%
where the time goes in v4:
time: 101 us
  starting transfers between devices  46.8 us (46%)
  Pallas kernels  35.6 us (35%)
  waiting for transfers between devices  15.7 us (16%)
  other arithmetic  1.5 us (1%)
  between operations  1.07 us (1%)
    ppermute x24, starting transfers between devices, exchange(): return lax.ppermute(x, AXES, [(i, i ^ masks[i & 1]) for i in range(128)])  25.4 us
    ppermute x8, starting transfers between devices, swap(): return lax.ppermute(x, AXES, swap_pairs(kind))  16.7 us
    ppermute x24, waiting for transfers between devices, exchange(): return lax.ppermute(x, AXES, [(i, i ^ masks[i & 1]) for i in range(128)])  14 us
    pallas_call x1, Pallas kernels, local(): pl.pallas_call(front_kernel, out_shape=piece_shapes(0) + (shape((CELLS, C...  6.49 us
    pallas_call x1, Pallas kernels, local(): pl.pallas_call(back_first_kernel, out_shape=(shape((2, TE, TE, C), bf16),...  5.44 us
    pallas_call x1, Pallas kernels, local(): pl.pallas_call(prep_kernel, out_shape=(p_shape, shape((2, GROUPS, TE * TE...  5.17 us
    ppermute x3, starting transfers between devices, flip(): return lax.ppermute(x, AXES, [(i, i ^ mask) for i in range(128)])  4.72 us
    pallas_call x1, Pallas kernels, local(): pl.pallas_call(taps_kernel, out_shape=shape((EXTRA, 128), f32), in_specs=...  4.44 us
  transfers between devices with their start and end apart: 35, of which 12 were waited for; matrix products, arithmetic and copies ran while one was open for 1% of the time, Pallas kernels for 24%

profile of v4, /device:TPU:1, one launch (start us, length us, event | category | flops | bytes accessed | tf_op | source)
XLA Modules:
  0.0 100.7 jit_solution(5727114780102980272)
XLA Ops:
  0.7 1.2 %pack_rows.1 = (bf16[2,48,512]{2,1,0:T(8,128)(2,1)S(1)}, bf16[2,48,512]{2,1,0:T(8,128)(2,1)S(1)}, bf16[2,16,16,400]{3,2,1,0:T(8,128)(2,1)S(1)}, s32[2,16,16]{2,1,0:T(8,128)S(1)}) custom-call(bf16[2,16,16,400]{3,2,1,0:T(8,128)(2,1)} %field_ref, s32[2,16,16]{2,1,0:T(8,128)} %land_ref.1), custom_call_target="tpu_custom_call" | custom-call | tf_op jit(solution)/shard_map/pack_rows/pallas_call | solution.py:855
  1.9 1.5 %collective-permute-start = (bf16[2,48,512]{2,1,0:T(8,128)(2,1)S(1)}, bf16[2,48,512]{2,1,0:T(8,128)(2,1)S(1)}, u32[]{:S(2)}, u32[]{:S(2)}) collective-permute-start(bf16[2,48,512]{2,1,0:T(8,128)(2,1)S(1)} %get-tuple-element.97), channel_id=1, source_target_pairs={{0,1},{1,0},{2,3},{3,2},{4,5},{5,4},{6,7},{7,6},{8,9},{9,8},{10,11... | collective-permute-start | bytes 294920 | tf_op jit(solution)/shard_map/ppermute | solution.py:767
  3.4 1.3 %collective-permute-start.1 = (bf16[2,48,512]{2,1,0:T(8,128)(2,1)S(1)}, bf16[2,48,512]{2,1,0:T(8,128)(2,1)S(1)}, u32[]{:S(2)}, u32[]{:S(2)}) collective-permute-start(bf16[2,48,512]{2,1,0:T(8,128)(2,1)S(1)} %get-tuple-element.98), channel_id=1, source_target_pairs={{0,3},{1,2},{2,1},{3,0},{4,7},{5,6},{6,5},{7,4},{8,11},{9,10},{10,... | collective-permute-start | bytes 294920 | tf_op jit(solution)/shard_map/ppermute | solution.py:767
  4.6 2.1 %hold.1 = (f32[512,400]{1,0:T(8,128)S(1)}, bf16[512,512]{1,0:T(8,128)(2,1)S(1)}, bf16[512,512]{1,0:T(8,128)(2,1)S(1)}, f32[1,400]{1,0:T(1,128)S(1)}, bf16[400,16...) custom-call(s32[2,16,16]{2,1,0:T(8,128)S(1)} %get-tuple-element.95.land_ref, ...), custom_call_target="tpu_custom_call" | custom-call | flops 1000000000 | bytes 16000000 | tf_op jit(solution)/shard_map/hold/pallas_call | solution.py:870
  6.7 1.1 %collective-permute-done.1.refs_3_.n2_ref = bf16[2,48,512]{2,1,0:T(8,128)(2,1)S(1)} collective-permute-done((bf16[2,48,512]{2,1,0:T(8,128)(2,1)S(1)}, bf16[2,48,512]{2,1,0:T(8,128)(2,1)S(1)}, u32[]{:S(2)}, u32[]{:S(2)}) %collective-permute-start.1) | collective-permute-done | bytes 98336 | tf_op jit(solution)/shard_map/ppermute | solution.py:767
  8.3 1.8 %collective-permute-start.2 = (bf16[464,128]{1,0:T(8,128)(2,1)S(1)}, bf16[464,128]{1,0:T(8,128)(2,1)S(1)}, u32[]{:S(2)}, u32[]{:S(2)}) collective-permute-start(bf16[464,128]{1,0:T(8,128)(2,1)S(1)} %get-tuple-element.103), channel_id=1, source_target_pairs={{0,4},{1,5},{2,6},{3,7},{4,0},{5,1},{6,2},{7,3},{8,12},{9,13},{10,... | collective-permute-start | bytes 356360 | tf_op jit(solution)/shard_map/ppermute | solution.py:767
  10.1 7.2 %collective-permute-start.3 = (bf16[464,128]{1,0:T(8,128)(2,1)S(1)}, bf16[464,128]{1,0:T(8,128)(2,1)S(1)}, u32[]{:S(2)}, u32[]{:S(2)}) collective-permute-start(bf16[464,128]{1,0:T(8,128)(2,1)S(1)} %get-tuple-element.104), channel_id=1, source_target_pairs={{0,124},{1,125},{2,126},{3,127},{4,8},{5,9},{6,10},{7,11},{8,4},{9... | collective-permute-start | bytes 356360 | tf_op jit(solution)/shard_map/ppermute | solution.py:767
  17.3 5.2 %prep.1 = (f32[2,4,704,128]{3,2,1,0:T(8,128)S(1)}, f32[2,4,256,128]{3,2,1,0:T(8,128)S(1)}) custom-call(s32[2,8]{1,0:T(2,128)} %beside_ref.5, bf16[2,16,16,400]{3,2,1,0:T(8,128)(2,1)S(1)} %get-tuple-element.94.refs_0_.field_ref, f32[512,400]{1,0:T(8,128)S(1)} %get-tuple-element.96.refs_1_.mask_ref, ...), custom_call_target="tpu_custom_call" | custom-call | flops 1000000000 | bytes 16000000 | tf_op jit(solution)/shard_map/prep/pallas_call | solution.py:917
  22.5 6.5 %front.1 = (f32[3200,128]{1,0:T(8,128)S(1)}, bf16[3200,128]{1,0:T(8,128)(2,1)S(1)}, f32[512,400]{1,0:T(8,128)S(1)}, f32[1,1024]{1,0:T(1,128)S(1)}, f32[512,400]{...) custom-call(s32[2,8]{1,0:T(2,128)} %beside_ref.5, ...), custom_call_target="tpu_custom_call" | custom-call | tf_op jit(solution)/shard_map/front/pallas_call | solution.py:937
  29.7 2.5 %hidden.1 = (f32[2016,128]{1,0:T(8,128)S(1)}, bf16[2016,128]{1,0:T(8,128)(2,1)S(1)}, f32[512,400]{1,0:T(8,128)S(1)}, f32[1,576]{1,0:T(1,128)S(1)}) custom-call(bf16[512,512]{1,0:T(8,128)(2,1)S(1)} %get-tuple-element.115.normed_ref, bf16[512,512]{1,0:T(8,128)(2,1)S(1)} %get-tuple-element.116.normed_t_ref, bf16[512,512]{1,0:T(8,128)(2,1)S(1)} %get-tuple-element.109.gated_ref, ...), custom_call_target="tpu_custom_call" | custom-call | flops 1000000000 | bytes 16000000 | tf_op jit(solution)/shard_map/hidden/pallas_call | solution.py:975
  32.3 1.4 %grad.1 = (bf16[2,16,16,400]{3,2,1,0:T(8,128)(2,1)S(1)}, bf16[2,48,512]{2,1,0:T(8,128)(2,1)S(1)}, bf16[2,48,512]{2,1,0:T(8,128)(2,1)S(1)}, f32[512,512]{1,0:T(8,128)S(1)}, f32[3,400]{1,0:T(4,128)S(1)}) custom-call(f32[512,400]{1,0:T(8,128)S(1)} %get-tuple-element.119.ng0_ref, f32[512,400]{1,0:T(8,128)S(1)} %get-tuple-element.120.ng1_ref, ...), custom_call_target="tpu_custom_call" | custom-call | flops 1000000000 | bytes 16000000 | tf_op jit(solution)/shard_map/grad/pallas_call | solution.py:985
  35.5 1.0 collective-permute-start.6
  36.5 4.9 %collective-permute-start.7 = (bf16[928,128]{1,0:T(8,128)(2,1)S(1)}, bf16[928,128]{1,0:T(8,128)(2,1)S(1)}, u32[]{:S(2)}, u32[]{:S(2)}) collective-permute-start(bf16[928,128]{1,0:T(8,128)(2,1)S(1)} %get-tuple-element.127), channel_id=1, source_target_pairs={{0,16},{1,49},{2,18},{3,51},{4,20},{5,53},{6,22},{7,55},{8,24},{9,... | collective-permute-start | bytes 712712 | tf_op jit(solution)/shard_map/ppermute | solution.py:796
  41.3 4.4 %taps.1 = f32[272,128]{1,0:T(8,128)S(1)} custom-call(f32[8,128]{1,0:T(8,128)S(1)} %get-tuple-element.130.after_ref, f32[512,512]{1,0:T(8,128)S(1)} %get-tuple-element.131.y_ref, f32[2,4,704,128]{3,2,1,0:T(8,128)S(1)} %get-tuple-element.107.p_ref.p_in_ref, f32[2,4,144,128]{3,2,1,0:T(8,128)S(1)} %get-tuple-element.132.border_ref, ...), custom_call_target="tpu_custom_call" | custom-call | flops 1000000000 | bytes 16000000 | tf_op jit(solution)/shard_map/taps/pallas_call | solution.py:1016
  46.7 1.2 %collective-permute-start.11 = (bf16[464,128]{1,0:T(8,128)(2,1)S(1)}, bf16[464,128]{1,0:T(8,128)(2,1)S(1)}, u32[]{:S(2)}, u32[]{:S(2)}) collective-permute-start(bf16[464,128]{1,0:T(8,128)(2,1)S(1)} %select_convert_fusion.2), channel_id=1, source_target_pairs={{0,16},{1,49},{2,18},{3,51},{4,20},{5,53},{6,22},{7,55},{8,24},{9,... | collective-permute-start | bytes 356360 | tf_op jit(solution)/shard_map/ppermute | solution.py:796
  48.6 3.5 %collective-permute-start.30 = (bf16[464,128]{1,0:T(8,128)(2,1)S(1)}, bf16[464,128]{1,0:T(8,128)(2,1)S(1)}, u32[]{:S(2)}, u32[]{:S(2)}) collective-permute-start(bf16[464,128]{1,0:T(8,128)(2,1)S(1)} %get-tuple-element.152), channel_id=1, source_target_pairs={{0,124},{1,125},{2,126},{3,127},{4,8},{5,9},{6,10},{7,11},{8,4},{9... | collective-permute-start | bytes 356360 | tf_op jit(solution)/shard_map/ppermute | solution.py:767
  52.1 2.1 %collective-permute-start.25 = (bf16[512,128]{1,0:T(8,128)(2,1)S(1)}, bf16[512,128]{1,0:T(8,128)(2,1)S(1)}, u32[]{:S(2)}, u32[]{:S(2)}) collective-permute-start(bf16[512,128]{1,0:T(8,128)(2,1)S(1)} %select_convert_fusion), channel_id=1, source_target_pairs={{0,2},{1,67},{2,0},{3,65},{4,6},{5,71},{6,4},{7,69},{8,10},{9,75},... | collective-permute-start | bytes 393224 | tf_op jit(solution)/shard_map/ppermute | solution.py:796
  55.1 3.0 %collective-permute-done.25 = bf16[512,128]{1,0:T(8,128)(2,1)S(1)} collective-permute-done((bf16[512,128]{1,0:T(8,128)(2,1)S(1)}, bf16[512,128]{1,0:T(8,128)(2,1)S(1)}, u32[]{:S(2)}, u32[]{:S(2)}) %collective-permute-start.25) | collective-permute-done | bytes 131104 | tf_op jit(solution)/shard_map/ppermute | solution.py:796
  58.2 1.1 %collective-permute-done.19 = bf16[464,128]{1,0:T(8,128)(2,1)S(1)} collective-permute-done((bf16[464,128]{1,0:T(8,128)(2,1)S(1)}, bf16[464,128]{1,0:T(8,128)(2,1)S(1)}, u32[]{:S(2)}, u32[]{:S(2)}) %collective-permute-start.19) | collective-permute-done | bytes 118816 | tf_op jit(solution)/shard_map/ppermute | solution.py:796
  60.4 2.9 %collective-permute-done.26 = bf16[512,128]{1,0:T(8,128)(2,1)S(1)} collective-permute-done((bf16[512,128]{1,0:T(8,128)(2,1)S(1)}, bf16[512,128]{1,0:T(8,128)(2,1)S(1)}, u32[]{:S(2)}, u32[]{:S(2)}) %collective-permute-start.26) | collective-permute-done | bytes 131104 | tf_op jit(solution)/shard_map/ppermute | solution.py:796
  65.2 2.0 %collective-permute-done.27 = bf16[512,128]{1,0:T(8,128)(2,1)S(1)} collective-permute-done((bf16[512,128]{1,0:T(8,128)(2,1)S(1)}, bf16[512,128]{1,0:T(8,128)(2,1)S(1)}, u32[]{:S(2)}, u32[]{:S(2)}) %collective-permute-start.27) | collective-permute-done | bytes 131104 | tf_op jit(solution)/shard_map/ppermute | solution.py:796
  70.0 1.4 %collective-permute-done.28 = bf16[512,128]{1,0:T(8,128)(2,1)S(1)} collective-permute-done((bf16[512,128]{1,0:T(8,128)(2,1)S(1)}, bf16[512,128]{1,0:T(8,128)(2,1)S(1)}, u32[]{:S(2)}, u32[]{:S(2)}) %collective-permute-start.28) | collective-permute-done | bytes 131104 | tf_op jit(solution)/shard_map/ppermute | solution.py:796
  71.6 1.3 %collective-permute-done.22 = bf16[464,128]{1,0:T(8,128)(2,1)S(1)} collective-permute-done((bf16[464,128]{1,0:T(8,128)(2,1)S(1)}, bf16[464,128]{1,0:T(8,128)(2,1)S(1)}, u32[]{:S(2)}, u32[]{:S(2)}) %collective-permute-start.22) | collective-permute-done | bytes 118816 | tf_op jit(solution)/shard_map/ppermute | solution.py:796
  72.9 1.3 %collective-permute-start.23 = (bf16[464,128]{1,0:T(8,128)(2,1)S(1)}, bf16[464,128]{1,0:T(8,128)(2,1)S(1)}, u32[]{:S(2)}, u32[]{:S(2)}) collective-permute-start(bf16[464,128]{1,0:T(8,128)(2,1)S(1)} %add_convert_fusion.4), channel_id=1, source_target_pairs={{0,4},{1,13},{2,6},{3,15},{4,0},{5,9},{6,2},{7,11},{8,12},{9,5},{1... | collective-permute-start | bytes 356360 | tf_op jit(solution)/shard_map/ppermute | solution.py:796
  74.2 2.0 %collective-permute-start.16 = (bf16[464,128]{1,0:T(8,128)(2,1)S(1)}, bf16[464,128]{1,0:T(8,128)(2,1)S(1)}, u32[]{:S(2)}, u32[]{:S(2)}) collective-permute-start(bf16[464,128]{1,0:T(8,128)(2,1)S(1)} %add_convert_fusion.9), channel_id=1, source_target_pairs={{0,16},{1,49},{2,18},{3,51},{4,20},{5,53},{6,22},{7,55},{8,24},{9,... | collective-permute-start | bytes 356360 | tf_op jit(solution)/shard_map/ppermute | solution.py:796
  76.2 2.2 %collective-permute-start.32 = (bf16[512,128]{1,0:T(8,128)(2,1)S(1)}, bf16[512,128]{1,0:T(8,128)(2,1)S(1)}, u32[]{:S(2)}, u32[]{:S(2)}) collective-permute-start(bf16[512,128]{1,0:T(8,128)(2,1)S(1)} %add_convert_fusion), channel_id=1, source_target_pairs={{0,2},{1,67},{2,0},{3,65},{4,6},{5,71},{6,4},{7,69},{8,10},{9,75},... | collective-permute-start | bytes 393224 | tf_op jit(solution)/shard_map/ppermute | solution.py:796
  79.5 2.7 %collective-permute-start.17 = (bf16[928,128]{1,0:T(8,128)(2,1)S(1)}, bf16[928,128]{1,0:T(8,128)(2,1)S(1)}, u32[]{:S(2)}, u32[]{:S(2)}) collective-permute-start(bf16[928,128]{1,0:T(8,128)(2,1)S(1)} %pad_maximum_fusion.2), channel_id=1, source_target_pairs={{0,2},{1,67},{2,0},{3,65},{4,6},{5,71},{6,4},{7,69},{8,10},{9,75},... | collective-permute-start | bytes 712712 | tf_op jit(solution)/shard_map/ppermute | solution.py:796
  82.3 2.7 %collective-permute-start.33 = (bf16[1024,128]{1,0:T(8,128)(2,1)S(1)}, bf16[1024,128]{1,0:T(8,128)(2,1)S(1)}, u32[]{:S(2)}, u32[]{:S(2)}) collective-permute-start(bf16[1024,128]{1,0:T(8,128)(2,1)S(1)} %pad_maximum_fusion.1), channel_id=1, source_target_pairs={{0,4},{1,13},{2,6},{3,15},{4,0},{5,9},{6,2},{7,11},{8,12},{9,5},{1... | collective-permute-start | bytes 786440 | tf_op jit(solution)/shard_map/ppermute | solution.py:796
  85.0 5.4 %back_first.1 = (bf16[2,16,16,400]{3,2,1,0:T(8,128)(2,1)}, f32[2,4,704,128]{3,2,1,0:T(8,128)S(1)}) custom-call(s32[2,8]{1,0:T(2,128)} %beside_ref.5, bf16[2,16,16,400]{3,2,1,0:T(8,128)(2,1)S(1)} %get-tuple-element.139.refs_0_.cg_ref, f32[512,400]{1,0:T(8,128)S(1)} %get-tuple-element.96.refs_1_.mask_ref, bf16[512,512]{1,0:T(8,128)(2,1)S(1)} %get-tuple-element.109.gated_ref, ...), custom_call_target="tpu_custom_call" | custom-call | flops 1000000000 | bytes 16000000 | tf_op jit(solution)/shard_map/back_first/pallas_call | solution.py:1059
  91.0 3.8 %collective-permute-start.34 = (bf16[5488,128]{1,0:T(8,128)(2,1)S(1)}, bf16[5488,128]{1,0:T(8,128)(2,1)S(1)}, u32[]{:S(2)}, u32[]{:S(2)}) collective-permute-start(bf16[5488,128]{1,0:T(8,128)(2,1)S(1)} %fusion.mine_ref), channel_id=1, source_target_pairs={{0,1},{1,0},{2,3},{3,2},{4,5},{5,4},{6,7},{7,6},{8,9},{9,8},{10,11... | collective-permute-start | bytes 4214792 | tf_op jit(solution)/shard_map/ppermute | solution.py:771
  94.9 3.0 %back_second.1 = bf16[2,16,16,400]{3,2,1,0:T(8,128)(2,1)} custom-call(f32[2,4,704,128]{3,2,1,0:T(8,128)S(1)} %get-tuple-element.161.p_ref, f32[512,400]{1,0:T(8,128)S(1)} %get-tuple-element.96.refs_1_.mask_ref, bf16[512,512]{1,0:T(8,128)(2,1)S(1)} %get-tuple-element.109.gated_ref, ...), custom_call_target="tpu_custom_call", output_to_operand_aliasing={{}: (4, {})} | custom-call | flops 1000000000 | bytes 16000000 | tf_op jit(solution)/shard_map/back_second/pallas_call | solution.py:1083
  97.9 2.8 %unpack.1 = (f32[400,1600]{1,0:T(8,128)}, f32[400,1600]{1,0:T(8,128)}, f32[49,400]{1,0:T(8,128)}, f32[400]{0:T(512)}, f32[400]{0:T(512)}, /*index=5*/f32[400]{0:T(512)}, f32[1600]{0:T(1024)}, f32[400]{0:T(512)}) custom-call(bf16[5488,128]{1,0:T(8,128)(2,1)S(1)} %fusion.mine_ref, bf16[5488,128]{1,0:T(8,128)(2,1)S(1)} %collective-permute-done.34.theirs_ref), custom_call_target="tpu_custom_call" | custom-call | tf_op jit(solution)/shard_map/unpack/pallas_call | solution.py:1095
  (86 shorter events, 13.2 us)
Async XLA Ops:
  1.9 4.8 %collective-permute-start = (bf16[2,48,512]{2,1,0:T(8,128)(2,1)S(1)}, bf16[2,48,512]{2,1,0:T(8,128)(2,1)S(1)}, u32[]{:S(2)}, u32[]{:S(2)}) collective-permute-start(bf16[2,48,512]{2,1,0:T(8,128)(2,1)S(1)} %get-tuple-element.97), channel_id=1, source_target_pairs={{0,1},{1,0},{2,3},{3,2},{4,5},{5,4},{6,7},{7,6},{8,9},{9,8},{10,11... | collective-permute-start | bytes 294920 | tf_op jit(solution)/shard_map/ppermute | solution.py:767
  3.4 4.5 %collective-permute-start.1 = (bf16[2,48,512]{2,1,0:T(8,128)(2,1)S(1)}, bf16[2,48,512]{2,1,0:T(8,128)(2,1)S(1)}, u32[]{:S(2)}, u32[]{:S(2)}) collective-permute-start(bf16[2,48,512]{2,1,0:T(8,128)(2,1)S(1)} %get-tuple-element.98), channel_id=1, source_target_pairs={{0,3},{1,2},{2,1},{3,0},{4,7},{5,6},{6,5},{7,4},{8,11},{9,10},{10,... | collective-permute-start | bytes 294920 | tf_op jit(solution)/shard_map/ppermute | solution.py:767
  8.3 14.1 %collective-permute-start.2 = (bf16[464,128]{1,0:T(8,128)(2,1)S(1)}, bf16[464,128]{1,0:T(8,128)(2,1)S(1)}, u32[]{:S(2)}, u32[]{:S(2)}) collective-permute-start(bf16[464,128]{1,0:T(8,128)(2,1)S(1)} %get-tuple-element.103), channel_id=1, source_target_pairs={{0,4},{1,5},{2,6},{3,7},{4,0},{5,1},{6,2},{7,3},{8,12},{9,13},{10,... | collective-permute-start | bytes 356360 | tf_op jit(solution)/shard_map/ppermute | solution.py:767
  10.1 12.3 %collective-permute-start.3 = (bf16[464,128]{1,0:T(8,128)(2,1)S(1)}, bf16[464,128]{1,0:T(8,128)(2,1)S(1)}, u32[]{:S(2)}, u32[]{:S(2)}) collective-permute-start(bf16[464,128]{1,0:T(8,128)(2,1)S(1)} %get-tuple-element.104), channel_id=1, source_target_pairs={{0,124},{1,125},{2,126},{3,127},{4,8},{5,9},{6,10},{7,11},{8,4},{9... | collective-permute-start | bytes 356360 | tf_op jit(solution)/shard_map/ppermute | solution.py:767
  29.0 5.3 %collective-permute-start.4 = (bf16[3200,128]{1,0:T(8,128)(2,1)S(1)}, bf16[3200,128]{1,0:T(8,128)(2,1)S(1)}, u32[]{:S(2)}, u32[]{:S(2)}) collective-permute-start(bf16[3200,128]{1,0:T(8,128)(2,1)S(1)} %get-tuple-element.114), channel_id=1, source_target_pairs={{0,1},{1,0},{2,3},{3,2},{4,5},{5,4},{6,7},{7,6},{8,9},{9,8},{10,11... | collective-permute-start | bytes 2457608 | tf_op jit(solution)/shard_map/ppermute | solution.py:771
  34.6 11.2 %collective-permute-start.8 = (bf16[752,128]{1,0:T(8,128)(2,1)S(1)}, bf16[752,128]{1,0:T(8,128)(2,1)S(1)}, u32[]{:S(2)}, u32[]{:S(2)}) collective-permute-start(bf16[752,128]{1,0:T(8,128)(2,1)S(1)} %get-tuple-element.129), channel_id=1, source_target_pairs={{0,4},{1,13},{2,6},{3,15},{4,0},{5,9},{6,2},{7,11},{8,12},{9,5},{1... | collective-permute-start | bytes 577544 | tf_op jit(solution)/shard_map/ppermute | solution.py:796
  34.7 11.2 %collective-permute-start.9 = (bf16[2,48,512]{2,1,0:T(8,128)(2,1)S(1)}, bf16[2,48,512]{2,1,0:T(8,128)(2,1)S(1)}, u32[]{:S(2)}, u32[]{:S(2)}) collective-permute-start(bf16[2,48,512]{2,1,0:T(8,128)(2,1)S(1)} %get-tuple-element.136), channel_id=1, source_target_pairs={{0,1},{1,0},{2,3},{3,2},{4,5},{5,4},{6,7},{7,6},{8,9},{9,8},{10,11... | collective-permute-start | bytes 294920 | tf_op jit(solution)/shard_map/ppermute | solution.py:767
  34.9 11.0 %collective-permute-start.10 = (bf16[2,48,512]{2,1,0:T(8,128)(2,1)S(1)}, bf16[2,48,512]{2,1,0:T(8,128)(2,1)S(1)}, u32[]{:S(2)}, u32[]{:S(2)}) collective-permute-start(bf16[2,48,512]{2,1,0:T(8,128)(2,1)S(1)} %get-tuple-element.137), channel_id=1, source_target_pairs={{0,3},{1,2},{2,1},{3,0},{4,7},{5,6},{6,5},{7,4},{8,11},{9,10},{10,... | collective-permute-start | bytes 294920 | tf_op jit(solution)/shard_map/ppermute | solution.py:767
  35.5 10.8 %collective-permute-start.6 = (bf16[928,128]{1,0:T(8,128)(2,1)S(1)}, bf16[928,128]{1,0:T(8,128)(2,1)S(1)}, u32[]{:S(2)}, u32[]{:S(2)}) collective-permute-start(bf16[928,128]{1,0:T(8,128)(2,1)S(1)} %get-tuple-element.125), channel_id=1, source_target_pairs={{0,2},{1,67},{2,0},{3,65},{4,6},{5,71},{6,4},{7,69},{8,10},{9,75},... | collective-permute-start | bytes 712712 | tf_op jit(solution)/shard_map/ppermute | solution.py:796
  36.5 9.9 %collective-permute-start.7 = (bf16[928,128]{1,0:T(8,128)(2,1)S(1)}, bf16[928,128]{1,0:T(8,128)(2,1)S(1)}, u32[]{:S(2)}, u32[]{:S(2)}) collective-permute-start(bf16[928,128]{1,0:T(8,128)(2,1)S(1)} %get-tuple-element.127), channel_id=1, source_target_pairs={{0,16},{1,49},{2,18},{3,51},{4,20},{5,53},{6,22},{7,55},{8,24},{9,... | collective-permute-start | bytes 712712 | tf_op jit(solution)/shard_map/ppermute | solution.py:796
  46.5 7.8 %collective-permute-start.18 = (bf16[464,128]{1,0:T(8,128)(2,1)S(1)}, bf16[464,128]{1,0:T(8,128)(2,1)S(1)}, u32[]{:S(2)}, u32[]{:S(2)}) collective-permute-start(bf16[464,128]{1,0:T(8,128)(2,1)S(1)} %select_convert_fusion.1), channel_id=1, source_target_pairs={{0,4},{1,13},{2,6},{3,15},{4,0},{5,9},{6,2},{7,11},{8,12},{9,5},{1... | collective-permute-start | bytes 356360 | tf_op jit(solution)/shard_map/ppermute | solution.py:796
  46.7 8.3 %collective-permute-start.11 = (bf16[464,128]{1,0:T(8,128)(2,1)S(1)}, bf16[464,128]{1,0:T(8,128)(2,1)S(1)}, u32[]{:S(2)}, u32[]{:S(2)}) collective-permute-start(bf16[464,128]{1,0:T(8,128)(2,1)S(1)} %select_convert_fusion.2), channel_id=1, source_target_pairs={{0,16},{1,49},{2,18},{3,51},{4,20},{5,53},{6,22},{7,55},{8,24},{9,... | collective-permute-start | bytes 356360 | tf_op jit(solution)/shard_map/ppermute | solution.py:796
  47.9 23.6 %collective-permute-start.29 = (bf16[464,128]{1,0:T(8,128)(2,1)S(1)}, bf16[464,128]{1,0:T(8,128)(2,1)S(1)}, u32[]{:S(2)}, u32[]{:S(2)}) collective-permute-start(bf16[464,128]{1,0:T(8,128)(2,1)S(1)} %get-tuple-element.151), channel_id=1, source_target_pairs={{0,4},{1,5},{2,6},{3,7},{4,0},{5,1},{6,2},{7,3},{8,12},{9,13},{10,... | collective-permute-start | bytes 356360 | tf_op jit(solution)/shard_map/ppermute | solution.py:767
  48.6 22.9 %collective-permute-start.30 = (bf16[464,128]{1,0:T(8,128)(2,1)S(1)}, bf16[464,128]{1,0:T(8,128)(2,1)S(1)}, u32[]{:S(2)}, u32[]{:S(2)}) collective-permute-start(bf16[464,128]{1,0:T(8,128)(2,1)S(1)} %get-tuple-element.152), channel_id=1, source_target_pairs={{0,124},{1,125},{2,126},{3,127},{4,8},{5,9},{6,10},{7,11},{8,4},{9... | collective-permute-start | bytes 356360 | tf_op jit(solution)/shard_map/ppermute | solution.py:767
  52.1 6.0 %collective-permute-start.25 = (bf16[512,128]{1,0:T(8,128)(2,1)S(1)}, bf16[512,128]{1,0:T(8,128)(2,1)S(1)}, u32[]{:S(2)}, u32[]{:S(2)}) collective-permute-start(bf16[512,128]{1,0:T(8,128)(2,1)S(1)} %select_convert_fusion), channel_id=1, source_target_pairs={{0,2},{1,67},{2,0},{3,65},{4,6},{5,71},{6,4},{7,69},{8,10},{9,75},... | collective-permute-start | bytes 393224 | tf_op jit(solution)/shard_map/ppermute | solution.py:796
  54.3 5.1 %collective-permute-start.19 = (bf16[464,128]{1,0:T(8,128)(2,1)S(1)}, bf16[464,128]{1,0:T(8,128)(2,1)S(1)}, u32[]{:S(2)}, u32[]{:S(2)}) collective-permute-start(bf16[464,128]{1,0:T(8,128)(2,1)S(1)} %add_convert_fusion.8), channel_id=1, source_target_pairs={{0,2},{1,67},{2,0},{3,65},{4,6},{5,71},{6,4},{7,69},{8,10},{9,75},... | collective-permute-start | bytes 356360 | tf_op jit(solution)/shard_map/ppermute | solution.py:796
  55.0 5.2 %collective-permute-start.12 = (bf16[464,128]{1,0:T(8,128)(2,1)S(1)}, bf16[464,128]{1,0:T(8,128)(2,1)S(1)}, u32[]{:S(2)}, u32[]{:S(2)}) collective-permute-start(bf16[464,128]{1,0:T(8,128)(2,1)S(1)} %add_convert_fusion.13), channel_id=1, source_target_pairs={{0,4},{1,13},{2,6},{3,15},{4,0},{5,9},{6,2},{7,11},{8,12},{9,5},{1... | collective-permute-start | bytes 356360 | tf_op jit(solution)/shard_map/ppermute | solution.py:796
  58.1 5.1 %collective-permute-start.26 = (bf16[512,128]{1,0:T(8,128)(2,1)S(1)}, bf16[512,128]{1,0:T(8,128)(2,1)S(1)}, u32[]{:S(2)}, u32[]{:S(2)}) collective-permute-start(bf16[512,128]{1,0:T(8,128)(2,1)S(1)} %add_convert_fusion.3), channel_id=1, source_target_pairs={{0,16},{1,49},{2,18},{3,51},{4,20},{5,53},{6,22},{7,55},{8,24},{9,... | collective-permute-start | bytes 393224 | tf_op jit(solution)/shard_map/ppermute | solution.py:796
  59.4 4.8 %collective-permute-start.20 = (bf16[464,128]{1,0:T(8,128)(2,1)S(1)}, bf16[464,128]{1,0:T(8,128)(2,1)S(1)}, u32[]{:S(2)}, u32[]{:S(2)}) collective-permute-start(bf16[464,128]{1,0:T(8,128)(2,1)S(1)} %add_convert_fusion.7), channel_id=1, source_target_pairs={{0,48},{1,17},{2,50},{3,19},{4,52},{5,21},{6,54},{7,23},{8,56},{9,... | collective-permute-start | bytes 356360 | tf_op jit(solution)/shard_map/ppermute | solution.py:796
  60.3 4.7 %collective-permute-start.13 = (bf16[464,128]{1,0:T(8,128)(2,1)S(1)}, bf16[464,128]{1,0:T(8,128)(2,1)S(1)}, u32[]{:S(2)}, u32[]{:S(2)}) collective-permute-start(bf16[464,128]{1,0:T(8,128)(2,1)S(1)} %add_convert_fusion.12), channel_id=1, source_target_pairs={{0,66},{1,3},{2,64},{3,1},{4,70},{5,7},{6,68},{7,5},{8,74},{9,11},... | collective-permute-start | bytes 356360 | tf_op jit(solution)/shard_map/ppermute | solution.py:796
  64.2 4.5 %collective-permute-start.21 = (bf16[464,128]{1,0:T(8,128)(2,1)S(1)}, bf16[464,128]{1,0:T(8,128)(2,1)S(1)}, u32[]{:S(2)}, u32[]{:S(2)}) collective-permute-start(bf16[464,128]{1,0:T(8,128)(2,1)S(1)} %add_convert_fusion.6), channel_id=1, source_target_pairs={{0,12},{1,5},{2,14},{3,7},{4,8},{5,1},{6,10},{7,3},{8,4},{9,13},{1... | collective-permute-start | bytes 356360 | tf_op jit(solution)/shard_map/ppermute | solution.py:796
  65.0 4.4 %collective-permute-start.14 = (bf16[464,128]{1,0:T(8,128)(2,1)S(1)}, bf16[464,128]{1,0:T(8,128)(2,1)S(1)}, u32[]{:S(2)}, u32[]{:S(2)}) collective-permute-start(bf16[464,128]{1,0:T(8,128)(2,1)S(1)} %add_convert_fusion.11), channel_id=1, source_target_pairs={{0,48},{1,17},{2,50},{3,19},{4,52},{5,21},{6,54},{7,23},{8,56},{9,... | collective-permute-start | bytes 356360 | tf_op jit(solution)/shard_map/ppermute | solution.py:796
  67.2 4.2 %collective-permute-start.28 = (bf16[512,128]{1,0:T(8,128)(2,1)S(1)}, bf16[512,128]{1,0:T(8,128)(2,1)S(1)}, u32[]{:S(2)}, u32[]{:S(2)}) collective-permute-start(bf16[512,128]{1,0:T(8,128)(2,1)S(1)} %add_convert_fusion.1), channel_id=1, source_target_pairs={{0,66},{1,3},{2,64},{3,1},{4,70},{5,7},{6,68},{7,5},{8,74},{9,11},... | collective-permute-start | bytes 393224 | tf_op jit(solution)/shard_map/ppermute | solution.py:796
  69.5 4.7 %collective-permute-start.15 = (bf16[464,128]{1,0:T(8,128)(2,1)S(1)}, bf16[464,128]{1,0:T(8,128)(2,1)S(1)}, u32[]{:S(2)}, u32[]{:S(2)}) collective-permute-start(bf16[464,128]{1,0:T(8,128)(2,1)S(1)} %add_convert_fusion.10), channel_id=1, source_target_pairs={{0,12},{1,5},{2,14},{3,7},{4,8},{5,1},{6,10},{7,3},{8,4},{9,13},{1... | collective-permute-start | bytes 356360 | tf_op jit(solution)/shard_map/ppermute | solution.py:796
  71.5 4.7 %collective-permute-start.31 = (bf16[512,128]{1,0:T(8,128)(2,1)S(1)}, bf16[512,128]{1,0:T(8,128)(2,1)S(1)}, u32[]{:S(2)}, u32[]{:S(2)}) collective-permute-start(bf16[512,128]{1,0:T(8,128)(2,1)S(1)} %convert_add_fusion.3), channel_id=1, source_target_pairs={{0,48},{1,17},{2,50},{3,19},{4,52},{5,21},{6,54},{7,23},{8,56},{9,... | collective-permute-start | bytes 393224 | tf_op jit(solution)/shard_map/ppermute | solution.py:796
  72.9 5.6 %collective-permute-start.23 = (bf16[464,128]{1,0:T(8,128)(2,1)S(1)}, bf16[464,128]{1,0:T(8,128)(2,1)S(1)}, u32[]{:S(2)}, u32[]{:S(2)}) collective-permute-start(bf16[464,128]{1,0:T(8,128)(2,1)S(1)} %add_convert_fusion.4), channel_id=1, source_target_pairs={{0,4},{1,13},{2,6},{3,15},{4,0},{5,9},{6,2},{7,11},{8,12},{9,5},{1... | collective-permute-start | bytes 356360 | tf_op jit(solution)/shard_map/ppermute | solution.py:796
  74.2 5.3 %collective-permute-start.16 = (bf16[464,128]{1,0:T(8,128)(2,1)S(1)}, bf16[464,128]{1,0:T(8,128)(2,1)S(1)}, u32[]{:S(2)}, u32[]{:S(2)}) collective-permute-start(bf16[464,128]{1,0:T(8,128)(2,1)S(1)} %add_convert_fusion.9), channel_id=1, source_target_pairs={{0,16},{1,49},{2,18},{3,51},{4,20},{5,53},{6,22},{7,55},{8,24},{9,... | collective-permute-start | bytes 356360 | tf_op jit(solution)/shard_map/ppermute | solution.py:796
  76.2 6.1 %collective-permute-start.32 = (bf16[512,128]{1,0:T(8,128)(2,1)S(1)}, bf16[512,128]{1,0:T(8,128)(2,1)S(1)}, u32[]{:S(2)}, u32[]{:S(2)}) collective-permute-start(bf16[512,128]{1,0:T(8,128)(2,1)S(1)} %add_convert_fusion), channel_id=1, source_target_pairs={{0,2},{1,67},{2,0},{3,65},{4,6},{5,71},{6,4},{7,69},{8,10},{9,75},... | collective-permute-start | bytes 393224 | tf_op jit(solution)/shard_map/ppermute | solution.py:796
  78.5 12.1 %collective-permute-start.24 = (bf16[928,128]{1,0:T(8,128)(2,1)S(1)}, bf16[928,128]{1,0:T(8,128)(2,1)S(1)}, u32[]{:S(2)}, u32[]{:S(2)}) collective-permute-start(bf16[928,128]{1,0:T(8,128)(2,1)S(1)} %pad_maximum_fusion.3), channel_id=1, source_target_pairs={{0,16},{1,49},{2,18},{3,51},{4,20},{5,53},{6,22},{7,55},{8,24},{9,... | collective-permute-start | bytes 712712 | tf_op jit(solution)/shard_map/ppermute | solution.py:796
  79.5 10.9 %collective-permute-start.17 = (bf16[928,128]{1,0:T(8,128)(2,1)S(1)}, bf16[928,128]{1,0:T(8,128)(2,1)S(1)}, u32[]{:S(2)}, u32[]{:S(2)}) collective-permute-start(bf16[928,128]{1,0:T(8,128)(2,1)S(1)} %pad_maximum_fusion.2), channel_id=1, source_target_pairs={{0,2},{1,67},{2,0},{3,65},{4,6},{5,71},{6,4},{7,69},{8,10},{9,75},... | collective-permute-start | bytes 712712 | tf_op jit(solution)/shard_map/ppermute | solution.py:796
  82.3 8.5 %collective-permute-start.33 = (bf16[1024,128]{1,0:T(8,128)(2,1)S(1)}, bf16[1024,128]{1,0:T(8,128)(2,1)S(1)}, u32[]{:S(2)}, u32[]{:S(2)}) collective-permute-start(bf16[1024,128]{1,0:T(8,128)(2,1)S(1)} %pad_maximum_fusion.1), channel_id=1, source_target_pairs={{0,4},{1,13},{2,6},{3,15},{4,0},{5,9},{6,2},{7,11},{8,12},{9,5},{1... | collective-permute-start | bytes 786440 | tf_op jit(solution)/shard_map/ppermute | solution.py:796
  91.0 6.8 %collective-permute-start.34 = (bf16[5488,128]{1,0:T(8,128)(2,1)S(1)}, bf16[5488,128]{1,0:T(8,128)(2,1)S(1)}, u32[]{:S(2)}, u32[]{:S(2)}) collective-permute-start(bf16[5488,128]{1,0:T(8,128)(2,1)S(1)} %fusion.mine_ref), channel_id=1, source_target_pairs={{0,1},{1,0},{2,3},{3,2},{4,5},{5,4},{6,7},{7,6},{8,9},{9,8},{10,11... | collective-permute-start | bytes 4214792 | tf_op jit(solution)/shard_map/ppermute | solution.py:771
  (3 other events, 9.9 us)

commit v5 on v4

--- a/solution.py
+++ b/solution.py
@@ -540,7 +540,7 @@
     sums_ref,
 ):
     y_ref[...] = jnp.zeros(y_ref.shape, f32)
-    step_rows = 64
+    step_rows = 128
 
     def back(i, sums):
         at = pl.ds(pl.multiple_of(i * step_rows, step_rows), step_rows)
@@ -551,7 +551,7 @@
         a = jnp.sum(q, axis=1, keepdims=True) * (1.0 / C)
         b = jnp.sum(q * zhat, axis=1, keepdims=True) * (1.0 / C)
         cg = (rstd * (q - a - zhat * b)).astype(bf16)
-        cg_ref[i // 4, pl.ds((i % 4) * 4, 4)] = cg.reshape(4, TE, C)
+        cg_ref[i // 2, pl.ds((i % 2) * 8, 8)] = cg.reshape(8, TE, C)
         wide = cg.astype(f32)
         y_ref[at, 0:C] = wide
         return (
@@ -1028,7 +1028,7 @@
     )(pieces[-1], cg_wide, p, border, sums, ub0, ub1, down_bias_sum)
     parts = [pieces[len(SIZES) + i] + got[i].astype(f32) for i, order in orders]
     parts[-1] = jnp.concatenate([parts[-1], extra], axis=0)
-    parts[-1], n1, n2 = together(parts[-1], n1, n2)
+    parts, n1, n2 = together(parts, n1, n2)
     s1, s2 = pl.pallas_call(
         functools.partial(wide_kernel, False),
         out_shape=(wide_shape, wide_shape),
@@ -1038,10 +1038,9 @@
         compiler_params=params(8),
         name="pack_columns_back",
     )(cg, n1, n2)
-    parts, s1, s2 = together(parts, s1, s2)
-    w2, w1 = swap(s2, ("wide", 1)), swap(s1, ("wide", 0))
     for stage in range(1, DEPTH):
         parts = [halved(parts[i], order, stage, high[i][stage]) for i, order in orders]
+    w1, w2 = swap(s1, ("wide", 0)), swap(s2, ("wide", 1))
     for stage in range(DEPTH, 6):
         parts = [doubled(parts[i], order, stage) for i, order in orders]
         if stage == 4:

time: 101 us -> 100 us (0.990)
  waiting for transfers between devices: 15.7 us -> 11.9 us
  starting transfers between devices: 46.8 us -> 50.2 us
    ppermute x24, waiting for transfers between devices: 14 us -> 9.88 us  [exchange(): return lax.ppermute(x, AXES, [(i, i ^ masks[i & 1]) for i in range(128)])]
    ppermute x24, starting transfers between devices: 25.4 us -> 27.2 us  [exchange(): return lax.ppermute(x, AXES, [(i, i ^ masks[i & 1]) for i in range(128)])]
    ppermute x3, starting transfers between devices: 4.72 us -> 6 us  [flip(): return lax.ppermute(x, AXES, [(i, i ^ mask) for i in range(128)])]
  transfers between devices with their start and end apart: 35 -> 35, of which waited for: 12 -> 10; matrix products, arithmetic and copies ran while one was open for 1% -> 1% of each run, Pallas kernels for 24% -> 24%
where the time goes in v5:
time: 100 us
  starting transfers between devices  50.2 us (50%)
  Pallas kernels  35.3 us (35%)
  waiting for transfers between devices  11.9 us (12%)
  other arithmetic  1.5 us (2%)
  between operations  1.07 us (1%)
    ppermute x24, starting transfers between devices, exchange(): return lax.ppermute(x, AXES, [(i, i ^ masks[i & 1]) for i in range(128)])  27.2 us
    ppermute x8, starting transfers between devices, swap(): return lax.ppermute(x, AXES, swap_pairs(kind))  17.1 us
    ppermute x24, waiting for transfers between devices, exchange(): return lax.ppermute(x, AXES, [(i, i ^ masks[i & 1]) for i in range(128)])  9.88 us
    pallas_call x1, Pallas kernels, local(): pl.pallas_call(front_kernel, out_shape=piece_shapes(0) + (shape((CELLS, C...  6.49 us
    ppermute x3, starting transfers between devices, flip(): return lax.ppermute(x, AXES, [(i, i ^ mask) for i in range(128)])  6 us
    pallas_call x1, Pallas kernels, local(): pl.pallas_call(back_first_kernel, out_shape=(shape((2, TE, TE, C), bf16),...  5.44 us
    pallas_call x1, Pallas kernels, local(): pl.pallas_call(prep_kernel, out_shape=(p_shape, shape((2, GROUPS, TE * TE...  5.17 us
    pallas_call x1, Pallas kernels, local(): pl.pallas_call(taps_kernel, out_shape=shape((EXTRA, 128), f32), in_specs=...  4.44 us
  transfers between devices with their start and end apart: 35, of which 10 were waited for; matrix products, arithmetic and copies ran while one was open for 1% of the time, Pallas kernels for 24%

profile of v5, /device:TPU:1, one launch (start us, length us, event | category | flops | bytes accessed | tf_op | source)
XLA Modules:
  0.0 100.0 jit_solution(8794466725885885446)
XLA Ops:
  0.7 1.2 %pack_rows.1 = (bf16[2,48,512]{2,1,0:T(8,128)(2,1)S(1)}, bf16[2,48,512]{2,1,0:T(8,128)(2,1)S(1)}, bf16[2,16,16,400]{3,2,1,0:T(8,128)(2,1)S(1)}, s32[2,16,16]{2,1,0:T(8,128)S(1)}) custom-call(bf16[2,16,16,400]{3,2,1,0:T(8,128)(2,1)} %field_ref, s32[2,16,16]{2,1,0:T(8,128)} %land_ref.1), custom_call_target="tpu_custom_call" | custom-call | tf_op jit(solution)/shard_map/pack_rows/pallas_call | solution.py:855
  1.9 1.5 %collective-permute-start = (bf16[2,48,512]{2,1,0:T(8,128)(2,1)S(1)}, bf16[2,48,512]{2,1,0:T(8,128)(2,1)S(1)}, u32[]{:S(2)}, u32[]{:S(2)}) collective-permute-start(bf16[2,48,512]{2,1,0:T(8,128)(2,1)S(1)} %get-tuple-element.94), channel_id=1, source_target_pairs={{0,1},{1,0},{2,3},{3,2},{4,5},{5,4},{6,7},{7,6},{8,9},{9,8},{10,11... | collective-permute-start | bytes 294920 | tf_op jit(solution)/shard_map/ppermute | solution.py:767
  3.4 1.3 %collective-permute-start.1 = (bf16[2,48,512]{2,1,0:T(8,128)(2,1)S(1)}, bf16[2,48,512]{2,1,0:T(8,128)(2,1)S(1)}, u32[]{:S(2)}, u32[]{:S(2)}) collective-permute-start(bf16[2,48,512]{2,1,0:T(8,128)(2,1)S(1)} %get-tuple-element.95), channel_id=1, source_target_pairs={{0,3},{1,2},{2,1},{3,0},{4,7},{5,6},{6,5},{7,4},{8,11},{9,10},{10,... | collective-permute-start | bytes 294920 | tf_op jit(solution)/shard_map/ppermute | solution.py:767
  4.6 2.1 %hold.1 = (f32[512,400]{1,0:T(8,128)S(1)}, bf16[512,512]{1,0:T(8,128)(2,1)S(1)}, bf16[512,512]{1,0:T(8,128)(2,1)S(1)}, f32[1,400]{1,0:T(1,128)S(1)}, bf16[400,16...) custom-call(s32[2,16,16]{2,1,0:T(8,128)S(1)} %get-tuple-element.92.land_ref, ...), custom_call_target="tpu_custom_call" | custom-call | flops 1000000000 | bytes 16000000 | tf_op jit(solution)/shard_map/hold/pallas_call | solution.py:870
  6.7 1.1 %collective-permute-done.1.refs_3_.n2_ref = bf16[2,48,512]{2,1,0:T(8,128)(2,1)S(1)} collective-permute-done((bf16[2,48,512]{2,1,0:T(8,128)(2,1)S(1)}, bf16[2,48,512]{2,1,0:T(8,128)(2,1)S(1)}, u32[]{:S(2)}, u32[]{:S(2)}) %collective-permute-start.1) | collective-permute-done | bytes 98336 | tf_op jit(solution)/shard_map/ppermute | solution.py:767
  8.3 1.8 %collective-permute-start.2 = (bf16[464,128]{1,0:T(8,128)(2,1)S(1)}, bf16[464,128]{1,0:T(8,128)(2,1)S(1)}, u32[]{:S(2)}, u32[]{:S(2)}) collective-permute-start(bf16[464,128]{1,0:T(8,128)(2,1)S(1)} %get-tuple-element.100), channel_id=1, source_target_pairs={{0,4},{1,5},{2,6},{3,7},{4,0},{5,1},{6,2},{7,3},{8,12},{9,13},{10,... | collective-permute-start | bytes 356360 | tf_op jit(solution)/shard_map/ppermute | solution.py:767
  10.1 7.2 %collective-permute-start.3 = (bf16[464,128]{1,0:T(8,128)(2,1)S(1)}, bf16[464,128]{1,0:T(8,128)(2,1)S(1)}, u32[]{:S(2)}, u32[]{:S(2)}) collective-permute-start(bf16[464,128]{1,0:T(8,128)(2,1)S(1)} %get-tuple-element.101), channel_id=1, source_target_pairs={{0,124},{1,125},{2,126},{3,127},{4,8},{5,9},{6,10},{7,11},{8,4},{9... | collective-permute-start | bytes 356360 | tf_op jit(solution)/shard_map/ppermute | solution.py:767
  17.3 5.2 %prep.1 = (f32[2,4,704,128]{3,2,1,0:T(8,128)S(1)}, f32[2,4,256,128]{3,2,1,0:T(8,128)S(1)}) custom-call(s32[2,8]{1,0:T(2,128)} %beside_ref.5, bf16[2,16,16,400]{3,2,1,0:T(8,128)(2,1)S(1)} %get-tuple-element.91.refs_0_.field_ref, f32[512,400]{1,0:T(8,128)S(1)} %get-tuple-element.93.refs_1_.mask_ref, ...), custom_call_target="tpu_custom_call" | custom-call | flops 1000000000 | bytes 16000000 | tf_op jit(solution)/shard_map/prep/pallas_call | solution.py:917
  22.5 6.5 %front.1 = (f32[3200,128]{1,0:T(8,128)S(1)}, bf16[3200,128]{1,0:T(8,128)(2,1)S(1)}, f32[512,400]{1,0:T(8,128)S(1)}, f32[1,1024]{1,0:T(1,128)S(1)}, f32[512,400]{...) custom-call(s32[2,8]{1,0:T(2,128)} %beside_ref.5, ...), custom_call_target="tpu_custom_call" | custom-call | tf_op jit(solution)/shard_map/front/pallas_call | solution.py:937
  29.7 2.5 %hidden.1 = (f32[2016,128]{1,0:T(8,128)S(1)}, bf16[2016,128]{1,0:T(8,128)(2,1)S(1)}, f32[512,400]{1,0:T(8,128)S(1)}, f32[1,576]{1,0:T(1,128)S(1)}) custom-call(bf16[512,512]{1,0:T(8,128)(2,1)S(1)} %get-tuple-element.112.normed_ref, bf16[512,512]{1,0:T(8,128)(2,1)S(1)} %get-tuple-element.113.normed_t_ref, bf16[512,512]{1,0:T(8,128)(2,1)S(1)} %get-tuple-element.106.gated_ref, ...), custom_call_target="tpu_custom_call" | custom-call | flops 1000000000 | bytes 16000000 | tf_op jit(solution)/shard_map/hidden/pallas_call | solution.py:975
  32.3 1.0 grad.1
  35.5 1.0 %collective-permute-start.6 = (bf16[928,128]{1,0:T(8,128)(2,1)S(1)}, bf16[928,128]{1,0:T(8,128)(2,1)S(1)}, u32[]{:S(2)}, u32[]{:S(2)}) collective-permute-start(bf16[928,128]{1,0:T(8,128)(2,1)S(1)} %get-tuple-element.122), channel_id=1, source_target_pairs={{0,2},{1,67},{2,0},{3,65},{4,6},{5,71},{6,4},{7,69},{8,10},{9,75},... | collective-permute-start | bytes 712712 | tf_op jit(solution)/shard_map/ppermute | solution.py:796
  36.5 4.9 %collective-permute-start.7 = (bf16[928,128]{1,0:T(8,128)(2,1)S(1)}, bf16[928,128]{1,0:T(8,128)(2,1)S(1)}, u32[]{:S(2)}, u32[]{:S(2)}) collective-permute-start(bf16[928,128]{1,0:T(8,128)(2,1)S(1)} %get-tuple-element.124), channel_id=1, source_target_pairs={{0,16},{1,49},{2,18},{3,51},{4,20},{5,53},{6,22},{7,55},{8,24},{9,... | collective-permute-start | bytes 712712 | tf_op jit(solution)/shard_map/ppermute | solution.py:796
  41.3 4.4 %taps.1 = f32[272,128]{1,0:T(8,128)S(1)} custom-call(f32[8,128]{1,0:T(8,128)S(1)} %get-tuple-element.127.after_ref, f32[512,512]{1,0:T(8,128)S(1)} %get-tuple-element.128.y_ref, f32[2,4,704,128]{3,2,1,0:T(8,128)S(1)} %get-tuple-element.104.p_ref.p_in_ref, f32[2,4,144,128]{3,2,1,0:T(8,128)S(1)} %get-tuple-element.129.border_ref, ...), custom_call_target="tpu_custom_call" | custom-call | flops 1000000000 | bytes 16000000 | tf_op jit(solution)/shard_map/taps/pallas_call | solution.py:1016
  46.3 1.6 %collective-permute-start.11 = (bf16[464,128]{1,0:T(8,128)(2,1)S(1)}, bf16[464,128]{1,0:T(8,128)(2,1)S(1)}, u32[]{:S(2)}, u32[]{:S(2)}) collective-permute-start(bf16[464,128]{1,0:T(8,128)(2,1)S(1)} %select_convert_fusion.2), channel_id=1, source_target_pairs={{0,16},{1,49},{2,18},{3,51},{4,20},{5,53},{6,22},{7,55},{8,24},{9,... | collective-permute-start | bytes 356360 | tf_op jit(solution)/shard_map/ppermute | solution.py:796
  50.0 3.8 %collective-permute-start.30 = (bf16[464,128]{1,0:T(8,128)(2,1)S(1)}, bf16[464,128]{1,0:T(8,128)(2,1)S(1)}, u32[]{:S(2)}, u32[]{:S(2)}) collective-permute-start(bf16[464,128]{1,0:T(8,128)(2,1)S(1)} %get-tuple-element.146), channel_id=1, source_target_pairs={{0,124},{1,125},{2,126},{3,127},{4,8},{5,9},{6,10},{7,11},{8,4},{9... | collective-permute-start | bytes 356360 | tf_op jit(solution)/shard_map/ppermute | solution.py:767
  54.8 2.3 %collective-permute-start.26 = (bf16[512,128]{1,0:T(8,128)(2,1)S(1)}, bf16[512,128]{1,0:T(8,128)(2,1)S(1)}, u32[]{:S(2)}, u32[]{:S(2)}) collective-permute-start(bf16[512,128]{1,0:T(8,128)(2,1)S(1)} %add_convert_fusion.3), channel_id=1, source_target_pairs={{0,16},{1,49},{2,18},{3,51},{4,20},{5,53},{6,22},{7,55},{8,24},{9,... | collective-permute-start | bytes 393224 | tf_op jit(solution)/shard_map/ppermute | solution.py:796
  57.1 2.5 %collective-permute-done.19 = bf16[464,128]{1,0:T(8,128)(2,1)S(1)} collective-permute-done((bf16[464,128]{1,0:T(8,128)(2,1)S(1)}, bf16[464,128]{1,0:T(8,128)(2,1)S(1)}, u32[]{:S(2)}, u32[]{:S(2)}) %collective-permute-start.19) | collective-permute-done | bytes 118816 | tf_op jit(solution)/shard_map/ppermute | solution.py:796
  59.7 1.1 %collective-permute-done.12 = bf16[464,128]{1,0:T(8,128)(2,1)S(1)} collective-permute-done((bf16[464,128]{1,0:T(8,128)(2,1)S(1)}, bf16[464,128]{1,0:T(8,128)(2,1)S(1)}, u32[]{:S(2)}, u32[]{:S(2)}) %collective-permute-start.12) | collective-permute-done | bytes 118816 | tf_op jit(solution)/shard_map/ppermute | solution.py:796
  61.2 2.5 %collective-permute-done.20 = bf16[464,128]{1,0:T(8,128)(2,1)S(1)} collective-permute-done((bf16[464,128]{1,0:T(8,128)(2,1)S(1)}, bf16[464,128]{1,0:T(8,128)(2,1)S(1)}, u32[]{:S(2)}, u32[]{:S(2)}) %collective-permute-start.20) | collective-permute-done | bytes 118816 | tf_op jit(solution)/shard_map/ppermute | solution.py:796
  63.8 1.1 %collective-permute-done.13 = bf16[464,128]{1,0:T(8,128)(2,1)S(1)} collective-permute-done((bf16[464,128]{1,0:T(8,128)(2,1)S(1)}, bf16[464,128]{1,0:T(8,128)(2,1)S(1)}, u32[]{:S(2)}, u32[]{:S(2)}) %collective-permute-start.13) | collective-permute-done | bytes 118816 | tf_op jit(solution)/shard_map/ppermute | solution.py:796
  65.4 1.3 %collective-permute-start.28 = (bf16[512,128]{1,0:T(8,128)(2,1)S(1)}, bf16[512,128]{1,0:T(8,128)(2,1)S(1)}, u32[]{:S(2)}, u32[]{:S(2)}) collective-permute-start(bf16[512,128]{1,0:T(8,128)(2,1)S(1)} %add_convert_fusion.1), channel_id=1, source_target_pairs={{0,66},{1,3},{2,64},{3,1},{4,70},{5,7},{6,68},{7,5},{8,74},{9,11},... | collective-permute-start | bytes 393224 | tf_op jit(solution)/shard_map/ppermute | solution.py:796
  69.6 1.0 collective-permute-start.31
  71.3 1.8 %collective-permute-start.23 = (bf16[464,128]{1,0:T(8,128)(2,1)S(1)}, bf16[464,128]{1,0:T(8,128)(2,1)S(1)}, u32[]{:S(2)}, u32[]{:S(2)}) collective-permute-start(bf16[464,128]{1,0:T(8,128)(2,1)S(1)} %add_convert_fusion.4), channel_id=1, source_target_pairs={{0,4},{1,13},{2,6},{3,15},{4,0},{5,9},{6,2},{7,11},{8,12},{9,5},{1... | collective-permute-start | bytes 356360 | tf_op jit(solution)/shard_map/ppermute | solution.py:796
  74.2 2.3 %collective-permute-start.32 = (bf16[512,128]{1,0:T(8,128)(2,1)S(1)}, bf16[512,128]{1,0:T(8,128)(2,1)S(1)}, u32[]{:S(2)}, u32[]{:S(2)}) collective-permute-start(bf16[512,128]{1,0:T(8,128)(2,1)S(1)} %add_convert_fusion), channel_id=1, source_target_pairs={{0,2},{1,67},{2,0},{3,65},{4,6},{5,71},{6,4},{7,69},{8,10},{9,75},... | collective-permute-start | bytes 393224 | tf_op jit(solution)/shard_map/ppermute | solution.py:796
  76.7 1.9 %collective-permute-start.24 = (bf16[928,128]{1,0:T(8,128)(2,1)S(1)}, bf16[928,128]{1,0:T(8,128)(2,1)S(1)}, u32[]{:S(2)}, u32[]{:S(2)}) collective-permute-start(bf16[928,128]{1,0:T(8,128)(2,1)S(1)} %pad_maximum_fusion.3), channel_id=1, source_target_pairs={{0,16},{1,49},{2,18},{3,51},{4,20},{5,53},{6,22},{7,55},{8,24},{9,... | collective-permute-start | bytes 712712 | tf_op jit(solution)/shard_map/ppermute | solution.py:796
  78.6 2.9 %collective-permute-start.17 = (bf16[928,128]{1,0:T(8,128)(2,1)S(1)}, bf16[928,128]{1,0:T(8,128)(2,1)S(1)}, u32[]{:S(2)}, u32[]{:S(2)}) collective-permute-start(bf16[928,128]{1,0:T(8,128)(2,1)S(1)} %pad_maximum_fusion.2), channel_id=1, source_target_pairs={{0,2},{1,67},{2,0},{3,65},{4,6},{5,71},{6,4},{7,69},{8,10},{9,75},... | collective-permute-start | bytes 712712 | tf_op jit(solution)/shard_map/ppermute | solution.py:796
  81.5 1.5 %collective-permute-start.33 = (bf16[1024,128]{1,0:T(8,128)(2,1)S(1)}, bf16[1024,128]{1,0:T(8,128)(2,1)S(1)}, u32[]{:S(2)}, u32[]{:S(2)}) collective-permute-start(bf16[1024,128]{1,0:T(8,128)(2,1)S(1)} %pad_maximum_fusion.1), channel_id=1, source_target_pairs={{0,4},{1,13},{2,6},{3,15},{4,0},{5,9},{6,2},{7,11},{8,12},{9,5},{1... | collective-permute-start | bytes 786440 | tf_op jit(solution)/shard_map/ppermute | solution.py:796
  83.0 5.4 %back_first.1 = (bf16[2,16,16,400]{3,2,1,0:T(8,128)(2,1)}, f32[2,4,704,128]{3,2,1,0:T(8,128)S(1)}) custom-call(s32[2,8]{1,0:T(2,128)} %beside_ref.5, bf16[2,16,16,400]{3,2,1,0:T(8,128)(2,1)S(1)} %get-tuple-element.142.refs_0_.cg_ref, f32[512,400]{1,0:T(8,128)S(1)} %get-tuple-element.93.refs_1_.mask_ref, bf16[512,512]{1,0:T(8,128)(2,1)S(1)} %get-tuple-element.106.gated_ref, ...), custom_call_target="tpu_custom_call" | custom-call | flops 1000000000 | bytes 16000000 | tf_op jit(solution)/shard_map/back_first/pallas_call | solution.py:1058
  89.0 5.1 %collective-permute-start.34 = (bf16[5488,128]{1,0:T(8,128)(2,1)S(1)}, bf16[5488,128]{1,0:T(8,128)(2,1)S(1)}, u32[]{:S(2)}, u32[]{:S(2)}) collective-permute-start(bf16[5488,128]{1,0:T(8,128)(2,1)S(1)} %fusion.mine_ref), channel_id=1, source_target_pairs={{0,1},{1,0},{2,3},{3,2},{4,5},{5,4},{6,7},{7,6},{8,9},{9,8},{10,11... | collective-permute-start | bytes 4214792 | tf_op jit(solution)/shard_map/ppermute | solution.py:771
  94.1 3.0 %back_second.1 = bf16[2,16,16,400]{3,2,1,0:T(8,128)(2,1)} custom-call(f32[2,4,704,128]{3,2,1,0:T(8,128)S(1)} %get-tuple-element.155.p_ref, f32[512,400]{1,0:T(8,128)S(1)} %get-tuple-element.93.refs_1_.mask_ref, bf16[512,512]{1,0:T(8,128)(2,1)S(1)} %get-tuple-element.106.gated_ref, ...), custom_call_target="tpu_custom_call", output_to_operand_aliasing={{}: (4, {})} | custom-call | flops 1000000000 | bytes 16000000 | tf_op jit(solution)/shard_map/back_second/pallas_call | solution.py:1082
  97.2 2.8 %unpack.1 = (f32[400,1600]{1,0:T(8,128)}, f32[400,1600]{1,0:T(8,128)}, f32[49,400]{1,0:T(8,128)}, f32[400]{0:T(512)}, f32[400]{0:T(512)}, /*index=5*/f32[400]{0:T(512)}, f32[1600]{0:T(1024)}, f32[400]{0:T(512)}) custom-call(bf16[5488,128]{1,0:T(8,128)(2,1)S(1)} %fusion.mine_ref, bf16[5488,128]{1,0:T(8,128)(2,1)S(1)} %collective-permute-done.34.theirs_ref), custom_call_target="tpu_custom_call" | custom-call | tf_op jit(solution)/shard_map/unpack/pallas_call | solution.py:1094
  (86 shorter events, 13.5 us)
Async XLA Ops:
  1.9 4.8 %collective-permute-start = (bf16[2,48,512]{2,1,0:T(8,128)(2,1)S(1)}, bf16[2,48,512]{2,1,0:T(8,128)(2,1)S(1)}, u32[]{:S(2)}, u32[]{:S(2)}) collective-permute-start(bf16[2,48,512]{2,1,0:T(8,128)(2,1)S(1)} %get-tuple-element.94), channel_id=1, source_target_pairs={{0,1},{1,0},{2,3},{3,2},{4,5},{5,4},{6,7},{7,6},{8,9},{9,8},{10,11... | collective-permute-start | bytes 294920 | tf_op jit(solution)/shard_map/ppermute | solution.py:767
  3.4 4.5 %collective-permute-start.1 = (bf16[2,48,512]{2,1,0:T(8,128)(2,1)S(1)}, bf16[2,48,512]{2,1,0:T(8,128)(2,1)S(1)}, u32[]{:S(2)}, u32[]{:S(2)}) collective-permute-start(bf16[2,48,512]{2,1,0:T(8,128)(2,1)S(1)} %get-tuple-element.95), channel_id=1, source_target_pairs={{0,3},{1,2},{2,1},{3,0},{4,7},{5,6},{6,5},{7,4},{8,11},{9,10},{10,... | collective-permute-start | bytes 294920 | tf_op jit(solution)/shard_map/ppermute | solution.py:767
  8.3 14.1 %collective-permute-start.2 = (bf16[464,128]{1,0:T(8,128)(2,1)S(1)}, bf16[464,128]{1,0:T(8,128)(2,1)S(1)}, u32[]{:S(2)}, u32[]{:S(2)}) collective-permute-start(bf16[464,128]{1,0:T(8,128)(2,1)S(1)} %get-tuple-element.100), channel_id=1, source_target_pairs={{0,4},{1,5},{2,6},{3,7},{4,0},{5,1},{6,2},{7,3},{8,12},{9,13},{10,... | collective-permute-start | bytes 356360 | tf_op jit(solution)/shard_map/ppermute | solution.py:767
  10.1 12.3 %collective-permute-start.3 = (bf16[464,128]{1,0:T(8,128)(2,1)S(1)}, bf16[464,128]{1,0:T(8,128)(2,1)S(1)}, u32[]{:S(2)}, u32[]{:S(2)}) collective-permute-start(bf16[464,128]{1,0:T(8,128)(2,1)S(1)} %get-tuple-element.101), channel_id=1, source_target_pairs={{0,124},{1,125},{2,126},{3,127},{4,8},{5,9},{6,10},{7,11},{8,4},{9... | collective-permute-start | bytes 356360 | tf_op jit(solution)/shard_map/ppermute | solution.py:767
  29.0 5.3 %collective-permute-start.4 = (bf16[3200,128]{1,0:T(8,128)(2,1)S(1)}, bf16[3200,128]{1,0:T(8,128)(2,1)S(1)}, u32[]{:S(2)}, u32[]{:S(2)}) collective-permute-start(bf16[3200,128]{1,0:T(8,128)(2,1)S(1)} %get-tuple-element.111), channel_id=1, source_target_pairs={{0,1},{1,0},{2,3},{3,2},{4,5},{5,4},{6,7},{7,6},{8,9},{9,8},{10,11... | collective-permute-start | bytes 2457608 | tf_op jit(solution)/shard_map/ppermute | solution.py:771
  34.6 11.2 %collective-permute-start.8 = (bf16[752,128]{1,0:T(8,128)(2,1)S(1)}, bf16[752,128]{1,0:T(8,128)(2,1)S(1)}, u32[]{:S(2)}, u32[]{:S(2)}) collective-permute-start(bf16[752,128]{1,0:T(8,128)(2,1)S(1)} %get-tuple-element.126), channel_id=1, source_target_pairs={{0,4},{1,13},{2,6},{3,15},{4,0},{5,9},{6,2},{7,11},{8,12},{9,5},{1... | collective-permute-start | bytes 577544 | tf_op jit(solution)/shard_map/ppermute | solution.py:796
  34.7 11.4 %collective-permute-start.9 = (bf16[2,48,512]{2,1,0:T(8,128)(2,1)S(1)}, bf16[2,48,512]{2,1,0:T(8,128)(2,1)S(1)}, u32[]{:S(2)}, u32[]{:S(2)}) collective-permute-start(bf16[2,48,512]{2,1,0:T(8,128)(2,1)S(1)} %get-tuple-element.133), channel_id=1, source_target_pairs={{0,1},{1,0},{2,3},{3,2},{4,5},{5,4},{6,7},{7,6},{8,9},{9,8},{10,11... | collective-permute-start | bytes 294920 | tf_op jit(solution)/shard_map/ppermute | solution.py:767
  34.9 11.2 %collective-permute-start.10 = (bf16[2,48,512]{2,1,0:T(8,128)(2,1)S(1)}, bf16[2,48,512]{2,1,0:T(8,128)(2,1)S(1)}, u32[]{:S(2)}, u32[]{:S(2)}) collective-permute-start(bf16[2,48,512]{2,1,0:T(8,128)(2,1)S(1)} %get-tuple-element.134), channel_id=1, source_target_pairs={{0,3},{1,2},{2,1},{3,0},{4,7},{5,6},{6,5},{7,4},{8,11},{9,10},{10,... | collective-permute-start | bytes 294920 | tf_op jit(solution)/shard_map/ppermute | solution.py:767
  35.5 10.4 %collective-permute-start.6 = (bf16[928,128]{1,0:T(8,128)(2,1)S(1)}, bf16[928,128]{1,0:T(8,128)(2,1)S(1)}, u32[]{:S(2)}, u32[]{:S(2)}) collective-permute-start(bf16[928,128]{1,0:T(8,128)(2,1)S(1)} %get-tuple-element.122), channel_id=1, source_target_pairs={{0,2},{1,67},{2,0},{3,65},{4,6},{5,71},{6,4},{7,69},{8,10},{9,75},... | collective-permute-start | bytes 712712 | tf_op jit(solution)/shard_map/ppermute | solution.py:796
  36.5 9.5 %collective-permute-start.7 = (bf16[928,128]{1,0:T(8,128)(2,1)S(1)}, bf16[928,128]{1,0:T(8,128)(2,1)S(1)}, u32[]{:S(2)}, u32[]{:S(2)}) collective-permute-start(bf16[928,128]{1,0:T(8,128)(2,1)S(1)} %get-tuple-element.124), channel_id=1, source_target_pairs={{0,16},{1,49},{2,18},{3,51},{4,20},{5,53},{6,22},{7,55},{8,24},{9,... | collective-permute-start | bytes 712712 | tf_op jit(solution)/shard_map/ppermute | solution.py:796
  46.1 7.7 %collective-permute-start.18 = (bf16[464,128]{1,0:T(8,128)(2,1)S(1)}, bf16[464,128]{1,0:T(8,128)(2,1)S(1)}, u32[]{:S(2)}, u32[]{:S(2)}) collective-permute-start(bf16[464,128]{1,0:T(8,128)(2,1)S(1)} %select_convert_fusion.1), channel_id=1, source_target_pairs={{0,4},{1,13},{2,6},{3,15},{4,0},{5,9},{6,2},{7,11},{8,12},{9,5},{1... | collective-permute-start | bytes 356360 | tf_op jit(solution)/shard_map/ppermute | solution.py:796
  46.3 8.3 %collective-permute-start.11 = (bf16[464,128]{1,0:T(8,128)(2,1)S(1)}, bf16[464,128]{1,0:T(8,128)(2,1)S(1)}, u32[]{:S(2)}, u32[]{:S(2)}) collective-permute-start(bf16[464,128]{1,0:T(8,128)(2,1)S(1)} %select_convert_fusion.2), channel_id=1, source_target_pairs={{0,16},{1,49},{2,18},{3,51},{4,20},{5,53},{6,22},{7,55},{8,24},{9,... | collective-permute-start | bytes 356360 | tf_op jit(solution)/shard_map/ppermute | solution.py:796
  47.9 6.8 %collective-permute-start.25 = (bf16[512,128]{1,0:T(8,128)(2,1)S(1)}, bf16[512,128]{1,0:T(8,128)(2,1)S(1)}, u32[]{:S(2)}, u32[]{:S(2)}) collective-permute-start(bf16[512,128]{1,0:T(8,128)(2,1)S(1)} %select_convert_fusion), channel_id=1, source_target_pairs={{0,2},{1,67},{2,0},{3,65},{4,6},{5,71},{6,4},{7,69},{8,10},{9,75},... | collective-permute-start | bytes 393224 | tf_op jit(solution)/shard_map/ppermute | solution.py:796
  49.3 20.3 %collective-permute-start.29 = (bf16[464,128]{1,0:T(8,128)(2,1)S(1)}, bf16[464,128]{1,0:T(8,128)(2,1)S(1)}, u32[]{:S(2)}, u32[]{:S(2)}) collective-permute-start(bf16[464,128]{1,0:T(8,128)(2,1)S(1)} %get-tuple-element.145), channel_id=1, source_target_pairs={{0,4},{1,5},{2,6},{3,7},{4,0},{5,1},{6,2},{7,3},{8,12},{9,13},{10,... | collective-permute-start | bytes 356360 | tf_op jit(solution)/shard_map/ppermute | solution.py:767
  50.0 19.5 %collective-permute-start.30 = (bf16[464,128]{1,0:T(8,128)(2,1)S(1)}, bf16[464,128]{1,0:T(8,128)(2,1)S(1)}, u32[]{:S(2)}, u32[]{:S(2)}) collective-permute-start(bf16[464,128]{1,0:T(8,128)(2,1)S(1)} %get-tuple-element.146), channel_id=1, source_target_pairs={{0,124},{1,125},{2,126},{3,127},{4,8},{5,9},{6,10},{7,11},{8,4},{9... | collective-permute-start | bytes 356360 | tf_op jit(solution)/shard_map/ppermute | solution.py:767
  53.9 5.7 %collective-permute-start.19 = (bf16[464,128]{1,0:T(8,128)(2,1)S(1)}, bf16[464,128]{1,0:T(8,128)(2,1)S(1)}, u32[]{:S(2)}, u32[]{:S(2)}) collective-permute-start(bf16[464,128]{1,0:T(8,128)(2,1)S(1)} %add_convert_fusion.8), channel_id=1, source_target_pairs={{0,2},{1,67},{2,0},{3,65},{4,6},{5,71},{6,4},{7,69},{8,10},{9,75},... | collective-permute-start | bytes 356360 | tf_op jit(solution)/shard_map/ppermute | solution.py:796
  54.6 6.2 %collective-permute-start.12 = (bf16[464,128]{1,0:T(8,128)(2,1)S(1)}, bf16[464,128]{1,0:T(8,128)(2,1)S(1)}, u32[]{:S(2)}, u32[]{:S(2)}) collective-permute-start(bf16[464,128]{1,0:T(8,128)(2,1)S(1)} %add_convert_fusion.13), channel_id=1, source_target_pairs={{0,4},{1,13},{2,6},{3,15},{4,0},{5,9},{6,2},{7,11},{8,12},{9,5},{1... | collective-permute-start | bytes 356360 | tf_op jit(solution)/shard_map/ppermute | solution.py:796
  54.8 6.3 %collective-permute-start.26 = (bf16[512,128]{1,0:T(8,128)(2,1)S(1)}, bf16[512,128]{1,0:T(8,128)(2,1)S(1)}, u32[]{:S(2)}, u32[]{:S(2)}) collective-permute-start(bf16[512,128]{1,0:T(8,128)(2,1)S(1)} %add_convert_fusion.3), channel_id=1, source_target_pairs={{0,16},{1,49},{2,18},{3,51},{4,20},{5,53},{6,22},{7,55},{8,24},{9,... | collective-permute-start | bytes 393224 | tf_op jit(solution)/shard_map/ppermute | solution.py:796
  59.6 4.1 %collective-permute-start.20 = (bf16[464,128]{1,0:T(8,128)(2,1)S(1)}, bf16[464,128]{1,0:T(8,128)(2,1)S(1)}, u32[]{:S(2)}, u32[]{:S(2)}) collective-permute-start(bf16[464,128]{1,0:T(8,128)(2,1)S(1)} %add_convert_fusion.7), channel_id=1, source_target_pairs={{0,48},{1,17},{2,50},{3,19},{4,52},{5,21},{6,54},{7,23},{8,56},{9,... | collective-permute-start | bytes 356360 | tf_op jit(solution)/shard_map/ppermute | solution.py:796
  60.8 4.1 %collective-permute-start.13 = (bf16[464,128]{1,0:T(8,128)(2,1)S(1)}, bf16[464,128]{1,0:T(8,128)(2,1)S(1)}, u32[]{:S(2)}, u32[]{:S(2)}) collective-permute-start(bf16[464,128]{1,0:T(8,128)(2,1)S(1)} %add_convert_fusion.12), channel_id=1, source_target_pairs={{0,66},{1,3},{2,64},{3,1},{4,70},{5,7},{6,68},{7,5},{8,74},{9,11},... | collective-permute-start | bytes 356360 | tf_op jit(solution)/shard_map/ppermute | solution.py:796
  61.1 4.3 %collective-permute-start.27 = (bf16[512,128]{1,0:T(8,128)(2,1)S(1)}, bf16[512,128]{1,0:T(8,128)(2,1)S(1)}, u32[]{:S(2)}, u32[]{:S(2)}) collective-permute-start(bf16[512,128]{1,0:T(8,128)(2,1)S(1)} %add_convert_fusion.2), channel_id=1, source_target_pairs={{0,12},{1,5},{2,14},{3,7},{4,8},{5,1},{6,10},{7,3},{8,4},{9,13},{1... | collective-permute-start | bytes 393224 | tf_op jit(solution)/shard_map/ppermute | solution.py:796
  63.7 3.8 %collective-permute-start.21 = (bf16[464,128]{1,0:T(8,128)(2,1)S(1)}, bf16[464,128]{1,0:T(8,128)(2,1)S(1)}, u32[]{:S(2)}, u32[]{:S(2)}) collective-permute-start(bf16[464,128]{1,0:T(8,128)(2,1)S(1)} %add_convert_fusion.6), channel_id=1, source_target_pairs={{0,12},{1,5},{2,14},{3,7},{4,8},{5,1},{6,10},{7,3},{8,4},{9,13},{1... | collective-permute-start | bytes 356360 | tf_op jit(solution)/shard_map/ppermute | solution.py:796
  65.4 4.1 %collective-permute-start.28 = (bf16[512,128]{1,0:T(8,128)(2,1)S(1)}, bf16[512,128]{1,0:T(8,128)(2,1)S(1)}, u32[]{:S(2)}, u32[]{:S(2)}) collective-permute-start(bf16[512,128]{1,0:T(8,128)(2,1)S(1)} %add_convert_fusion.1), channel_id=1, source_target_pairs={{0,66},{1,3},{2,64},{3,1},{4,70},{5,7},{6,68},{7,5},{8,74},{9,11},... | collective-permute-start | bytes 393224 | tf_op jit(solution)/shard_map/ppermute | solution.py:796
  68.7 4.4 %collective-permute-start.15 = (bf16[464,128]{1,0:T(8,128)(2,1)S(1)}, bf16[464,128]{1,0:T(8,128)(2,1)S(1)}, u32[]{:S(2)}, u32[]{:S(2)}) collective-permute-start(bf16[464,128]{1,0:T(8,128)(2,1)S(1)} %add_convert_fusion.10), channel_id=1, source_target_pairs={{0,12},{1,5},{2,14},{3,7},{4,8},{5,1},{6,10},{7,3},{8,4},{9,13},{1... | collective-permute-start | bytes 356360 | tf_op jit(solution)/shard_map/ppermute | solution.py:796
  69.6 4.6 %collective-permute-start.31 = (bf16[512,128]{1,0:T(8,128)(2,1)S(1)}, bf16[512,128]{1,0:T(8,128)(2,1)S(1)}, u32[]{:S(2)}, u32[]{:S(2)}) collective-permute-start(bf16[512,128]{1,0:T(8,128)(2,1)S(1)} %convert_add_fusion.3), channel_id=1, source_target_pairs={{0,48},{1,17},{2,50},{3,19},{4,52},{5,21},{6,54},{7,23},{8,56},{9,... | collective-permute-start | bytes 393224 | tf_op jit(solution)/shard_map/ppermute | solution.py:796
  71.3 5.3 %collective-permute-start.23 = (bf16[464,128]{1,0:T(8,128)(2,1)S(1)}, bf16[464,128]{1,0:T(8,128)(2,1)S(1)}, u32[]{:S(2)}, u32[]{:S(2)}) collective-permute-start(bf16[464,128]{1,0:T(8,128)(2,1)S(1)} %add_convert_fusion.4), channel_id=1, source_target_pairs={{0,4},{1,13},{2,6},{3,15},{4,0},{5,9},{6,2},{7,11},{8,12},{9,5},{1... | collective-permute-start | bytes 356360 | tf_op jit(solution)/shard_map/ppermute | solution.py:796
  73.2 5.4 %collective-permute-start.16 = (bf16[464,128]{1,0:T(8,128)(2,1)S(1)}, bf16[464,128]{1,0:T(8,128)(2,1)S(1)}, u32[]{:S(2)}, u32[]{:S(2)}) collective-permute-start(bf16[464,128]{1,0:T(8,128)(2,1)S(1)} %add_convert_fusion.9), channel_id=1, source_target_pairs={{0,16},{1,49},{2,18},{3,51},{4,20},{5,53},{6,22},{7,55},{8,24},{9,... | collective-permute-start | bytes 356360 | tf_op jit(solution)/shard_map/ppermute | solution.py:796
  74.2 7.3 %collective-permute-start.32 = (bf16[512,128]{1,0:T(8,128)(2,1)S(1)}, bf16[512,128]{1,0:T(8,128)(2,1)S(1)}, u32[]{:S(2)}, u32[]{:S(2)}) collective-permute-start(bf16[512,128]{1,0:T(8,128)(2,1)S(1)} %add_convert_fusion), channel_id=1, source_target_pairs={{0,2},{1,67},{2,0},{3,65},{4,6},{5,71},{6,4},{7,69},{8,10},{9,75},... | collective-permute-start | bytes 393224 | tf_op jit(solution)/shard_map/ppermute | solution.py:796
  76.7 12.0 %collective-permute-start.24 = (bf16[928,128]{1,0:T(8,128)(2,1)S(1)}, bf16[928,128]{1,0:T(8,128)(2,1)S(1)}, u32[]{:S(2)}, u32[]{:S(2)}) collective-permute-start(bf16[928,128]{1,0:T(8,128)(2,1)S(1)} %pad_maximum_fusion.3), channel_id=1, source_target_pairs={{0,16},{1,49},{2,18},{3,51},{4,20},{5,53},{6,22},{7,55},{8,24},{9,... | collective-permute-start | bytes 712712 | tf_op jit(solution)/shard_map/ppermute | solution.py:796
  78.6 9.8 %collective-permute-start.17 = (bf16[928,128]{1,0:T(8,128)(2,1)S(1)}, bf16[928,128]{1,0:T(8,128)(2,1)S(1)}, u32[]{:S(2)}, u32[]{:S(2)}) collective-permute-start(bf16[928,128]{1,0:T(8,128)(2,1)S(1)} %pad_maximum_fusion.2), channel_id=1, source_target_pairs={{0,2},{1,67},{2,0},{3,65},{4,6},{5,71},{6,4},{7,69},{8,10},{9,75},... | collective-permute-start | bytes 712712 | tf_op jit(solution)/shard_map/ppermute | solution.py:796
  81.5 7.3 %collective-permute-start.33 = (bf16[1024,128]{1,0:T(8,128)(2,1)S(1)}, bf16[1024,128]{1,0:T(8,128)(2,1)S(1)}, u32[]{:S(2)}, u32[]{:S(2)}) collective-permute-start(bf16[1024,128]{1,0:T(8,128)(2,1)S(1)} %pad_maximum_fusion.1), channel_id=1, source_target_pairs={{0,4},{1,13},{2,6},{3,15},{4,0},{5,9},{6,2},{7,11},{8,12},{9,5},{1... | collective-permute-start | bytes 786440 | tf_op jit(solution)/shard_map/ppermute | solution.py:796
  89.0 8.1 %collective-permute-start.34 = (bf16[5488,128]{1,0:T(8,128)(2,1)S(1)}, bf16[5488,128]{1,0:T(8,128)(2,1)S(1)}, u32[]{:S(2)}, u32[]{:S(2)}) collective-permute-start(bf16[5488,128]{1,0:T(8,128)(2,1)S(1)} %fusion.mine_ref), channel_id=1, source_target_pairs={{0,1},{1,0},{2,3},{3,2},{4,5},{5,4},{6,7},{7,6},{8,9},{9,8},{10,11... | collective-permute-start | bytes 4214792 | tf_op jit(solution)/shard_map/ppermute | solution.py:771
  (3 other events, 9.5 us)

commit v6 on v5

--- a/solution.py
+++ b/solution.py
@@ -95,9 +95,9 @@
         from_north = jnp.where(n_even, two, one)
         from_south = jnp.where(n_even, one, two)
         for g in range(GROUPS):
-            m_ref[s, g, :, 0 : group_width(g)] = cells[:, lanes(g)]
-            r_ref[0, s, g] = from_north[:, 128 * g : 128 * g + 128]
-            r_ref[1, s, g] = from_south[:, 128 * g : 128 * g + 128]
+            m_ref[s, g, 0 : TE * TE, 0 : group_width(g)] = cells[:, lanes(g)]
+            r_ref[0, s, g, 0:48, :] = from_north[:, 128 * g : 128 * g + 128]
+            r_ref[1, s, g, 0:48, :] = from_south[:, 128 * g : 128 * g + 128]
     for s in range(2):
         for g in range(GROUPS):
             w = group_width(g)
@@ -144,8 +144,8 @@
         south = jnp.where(n_even, one, two)
         for g in range(GROUPS):
             at = slice(128 * g, 128 * g + 128)
-            rn_ref[0, s, g] = north[:, at]
-            rn_ref[1, s, g] = south[:, at]
+            rn_ref[0, s, g, 0:48, :] = north[:, at]
+            rn_ref[1, s, g, 0:48, :] = south[:, at]
 
 
 def place_columns(w1_ref, w2_ref, rw_ref):
@@ -407,7 +407,7 @@
     place_rows(n1_ref, n2_ref, rn_ref)
     place_columns(w1_ref, w2_ref, rw_ref)
     take_weights(weight_ref, depth_weight_ref)
-    y_ref[...] = y_in_ref[...]
+    y_ref[:, :, 0 : TE * TE, :] = y_in_ref[...]
     copy.wait()
 
     def sides(t, g):
@@ -741,8 +741,8 @@
 
 
 NEIGHBOURS = pltpu.SMEM((2, 8), jnp.int32)
-P_SCRATCH = pltpu.VMEM((2, GROUPS, 22 * PITCH, 128), f32)
-RN_SCRATCH = pltpu.VMEM((2, 2, GROUPS, 48, 128), f32)
+P_SCRATCH = pltpu.VMEM((2, GROUPS, 23 * PITCH, 128), f32)
+RN_SCRATCH = pltpu.VMEM((2, 2, GROUPS, 64, 128), f32)
 RW_SCRATCH = pltpu.VMEM((2, 2, GROUPS, 80, 128), f32)
 W_SCRATCH = pltpu.VMEM((56, CP), f32)
 Y_SCRATCH = pltpu.VMEM((CELLS, CP), f32)
@@ -845,12 +845,12 @@
     narrow_shape = shape((2, 48, CP), bf16)
     wide_shape = shape((SIDE_ROWS, 128), bf16)
     wide_scratch = [
-        pltpu.VMEM((2, GROUPS, TE * TE, 128), f32),
+        pltpu.VMEM((2, GROUPS, TE * TE + TE, 128), f32),
         RN_SCRATCH,
         RW_SCRATCH,
         pltpu.VMEM((2, SIDE_ROWS, 128), f32),
     ]
-    p_shape = shape((2, GROUPS, 22 * PITCH, 128), f32)
+    p_shape = shape((2, GROUPS, 23 * PITCH, 128), f32)
 
     s1, s2, field, land = pl.pallas_call(
         narrow_kernel,
@@ -950,7 +950,7 @@
             RN_SCRATCH,
             RW_SCRATCH,
             W_SCRATCH,
-            pltpu.VMEM((2, GROUPS, TE * TE, 128), f32),
+            pltpu.VMEM((2, GROUPS, TE * TE + TE, 128), f32),
             NEIGHBOURS,
             pltpu.SemaphoreType.DMA,
         ],

time: 100 us -> 100 us (level)
  no operation moved by 1% of the time
where the time goes in v6:
time: 100 us; the launch traced here: 99.9 us
  starting transfers between devices  50.2 us (50%)
  Pallas kernels  35.2 us (35%)
  waiting for transfers between devices  11.9 us (12%)
  other arithmetic  1.47 us (1%)
  between operations  1.08 us (1%)
    ppermute x24, starting transfers between devices, exchange(): return lax.ppermute(x, AXES, [(i, i ^ masks[i & 1]) for i in range(128)])  27.1 us
    ppermute x8, starting transfers between devices, swap(): return lax.ppermute(x, AXES, swap_pairs(kind))  17.1 us
    ppermute x24, waiting for transfers between devices, exchange(): return lax.ppermute(x, AXES, [(i, i ^ masks[i & 1]) for i in range(128)])  9.89 us
    pallas_call x1, Pallas kernels, local(): pl.pallas_call(front_kernel, out_shape=piece_shapes(0) + (shape((CELLS, C...  6.49 us
    ppermute x3, starting transfers between devices, flip(): return lax.ppermute(x, AXES, [(i, i ^ mask) for i in range(128)])  6.03 us
    pallas_call x1, Pallas kernels, local(): pl.pallas_call(back_first_kernel, out_shape=(shape((2, TE, TE, C), bf16),...  5.41 us
    pallas_call x1, Pallas kernels, local(): pl.pallas_call(prep_kernel, out_shape=(p_shape, shape((2, GROUPS, TE * TE...  5.17 us
    pallas_call x1, Pallas kernels, local(): pl.pallas_call(taps_kernel, out_shape=shape((EXTRA, 128), f32), in_specs=...  4.45 us
  transfers between devices with their start and end apart: 35, of which 10 were waited for; matrix products, arithmetic and copies ran while one was open for 1% of the time, Pallas kernels for 24%

profile of v6, /device:TPU:1, one launch (start us, length us, event | category | flops | bytes accessed | tf_op | source)
XLA Modules:
  0.0 99.9 jit_solution(2751669286260333341)
XLA Ops:
  0.7 1.2 %pack_rows.1 = (bf16[2,48,512]{2,1,0:T(8,128)(2,1)S(1)}, bf16[2,48,512]{2,1,0:T(8,128)(2,1)S(1)}, bf16[2,16,16,400]{3,2,1,0:T(8,128)(2,1)S(1)}, s32[2,16,16]{2,1,0:T(8,128)S(1)}) custom-call(bf16[2,16,16,400]{3,2,1,0:T(8,128)(2,1)} %field_ref, s32[2,16,16]{2,1,0:T(8,128)} %land_ref.1), custom_call_target="tpu_custom_call" | custom-call | tf_op jit(solution)/shard_map/pack_rows/pallas_call | solution.py:855
  1.9 1.5 %collective-permute-start = (bf16[2,48,512]{2,1,0:T(8,128)(2,1)S(1)}, bf16[2,48,512]{2,1,0:T(8,128)(2,1)S(1)}, u32[]{:S(2)}, u32[]{:S(2)}) collective-permute-start(bf16[2,48,512]{2,1,0:T(8,128)(2,1)S(1)} %get-tuple-element.94), channel_id=1, source_target_pairs={{0,1},{1,0},{2,3},{3,2},{4,5},{5,4},{6,7},{7,6},{8,9},{9,8},{10,11... | collective-permute-start | bytes 294920 | tf_op jit(solution)/shard_map/ppermute | solution.py:767
  3.4 1.3 %collective-permute-start.1 = (bf16[2,48,512]{2,1,0:T(8,128)(2,1)S(1)}, bf16[2,48,512]{2,1,0:T(8,128)(2,1)S(1)}, u32[]{:S(2)}, u32[]{:S(2)}) collective-permute-start(bf16[2,48,512]{2,1,0:T(8,128)(2,1)S(1)} %get-tuple-element.95), channel_id=1, source_target_pairs={{0,3},{1,2},{2,1},{3,0},{4,7},{5,6},{6,5},{7,4},{8,11},{9,10},{10,... | collective-permute-start | bytes 294920 | tf_op jit(solution)/shard_map/ppermute | solution.py:767
  4.6 2.1 %hold.1 = (f32[512,400]{1,0:T(8,128)S(1)}, bf16[512,512]{1,0:T(8,128)(2,1)S(1)}, bf16[512,512]{1,0:T(8,128)(2,1)S(1)}, f32[1,400]{1,0:T(1,128)S(1)}, bf16[400,16...) custom-call(s32[2,16,16]{2,1,0:T(8,128)S(1)} %get-tuple-element.92.land_ref, ...), custom_call_target="tpu_custom_call" | custom-call | flops 1000000000 | bytes 16000000 | tf_op jit(solution)/shard_map/hold/pallas_call | solution.py:870
  6.7 1.1 %collective-permute-done.1.refs_3_.n2_ref = bf16[2,48,512]{2,1,0:T(8,128)(2,1)S(1)} collective-permute-done((bf16[2,48,512]{2,1,0:T(8,128)(2,1)S(1)}, bf16[2,48,512]{2,1,0:T(8,128)(2,1)S(1)}, u32[]{:S(2)}, u32[]{:S(2)}) %collective-permute-start.1) | collective-permute-done | bytes 98336 | tf_op jit(solution)/shard_map/ppermute | solution.py:767
  8.3 1.8 %collective-permute-start.2 = (bf16[464,128]{1,0:T(8,128)(2,1)S(1)}, bf16[464,128]{1,0:T(8,128)(2,1)S(1)}, u32[]{:S(2)}, u32[]{:S(2)}) collective-permute-start(bf16[464,128]{1,0:T(8,128)(2,1)S(1)} %get-tuple-element.100), channel_id=1, source_target_pairs={{0,4},{1,5},{2,6},{3,7},{4,0},{5,1},{6,2},{7,3},{8,12},{9,13},{10,... | collective-permute-start | bytes 356360 | tf_op jit(solution)/shard_map/ppermute | solution.py:767
  10.1 7.2 %collective-permute-start.3 = (bf16[464,128]{1,0:T(8,128)(2,1)S(1)}, bf16[464,128]{1,0:T(8,128)(2,1)S(1)}, u32[]{:S(2)}, u32[]{:S(2)}) collective-permute-start(bf16[464,128]{1,0:T(8,128)(2,1)S(1)} %get-tuple-element.101), channel_id=1, source_target_pairs={{0,124},{1,125},{2,126},{3,127},{4,8},{5,9},{6,10},{7,11},{8,4},{9... | collective-permute-start | bytes 356360 | tf_op jit(solution)/shard_map/ppermute | solution.py:767
  17.3 5.2 %prep.1 = (f32[2,4,736,128]{3,2,1,0:T(8,128)S(1)}, f32[2,4,256,128]{3,2,1,0:T(8,128)S(1)}) custom-call(s32[2,8]{1,0:T(2,128)} %beside_ref.5, bf16[2,16,16,400]{3,2,1,0:T(8,128)(2,1)S(1)} %get-tuple-element.91.refs_0_.field_ref, f32[512,400]{1,0:T(8,128)S(1)} %get-tuple-element.93.refs_1_.mask_ref, ...), custom_call_target="tpu_custom_call" | custom-call | flops 1000000000 | bytes 16000000 | tf_op jit(solution)/shard_map/prep/pallas_call | solution.py:917
  22.5 6.5 %front.1 = (f32[3200,128]{1,0:T(8,128)S(1)}, bf16[3200,128]{1,0:T(8,128)(2,1)S(1)}, f32[512,400]{1,0:T(8,128)S(1)}, f32[1,1024]{1,0:T(1,128)S(1)}, f32[512,400]{...) custom-call(s32[2,8]{1,0:T(2,128)} %beside_ref.5, ...), custom_call_target="tpu_custom_call" | custom-call | tf_op jit(solution)/shard_map/front/pallas_call | solution.py:937
  29.7 2.5 %hidden.1 = (f32[2016,128]{1,0:T(8,128)S(1)}, bf16[2016,128]{1,0:T(8,128)(2,1)S(1)}, f32[512,400]{1,0:T(8,128)S(1)}, f32[1,576]{1,0:T(1,128)S(1)}) custom-call(bf16[512,512]{1,0:T(8,128)(2,1)S(1)} %get-tuple-element.112.normed_ref, bf16[512,512]{1,0:T(8,128)(2,1)S(1)} %get-tuple-element.113.normed_t_ref, bf16[512,512]{1,0:T(8,128)(2,1)S(1)} %get-tuple-element.106.gated_ref, ...), custom_call_target="tpu_custom_call" | custom-call | flops 1000000000 | bytes 16000000 | tf_op jit(solution)/shard_map/hidden/pallas_call | solution.py:975
  35.4 1.0 %collective-permute-start.6 = (bf16[928,128]{1,0:T(8,128)(2,1)S(1)}, bf16[928,128]{1,0:T(8,128)(2,1)S(1)}, u32[]{:S(2)}, u32[]{:S(2)}) collective-permute-start(bf16[928,128]{1,0:T(8,128)(2,1)S(1)} %get-tuple-element.122), channel_id=1, source_target_pairs={{0,2},{1,67},{2,0},{3,65},{4,6},{5,71},{6,4},{7,69},{8,10},{9,75},... | collective-permute-start | bytes 712712 | tf_op jit(solution)/shard_map/ppermute | solution.py:796
  36.4 4.9 %collective-permute-start.7 = (bf16[928,128]{1,0:T(8,128)(2,1)S(1)}, bf16[928,128]{1,0:T(8,128)(2,1)S(1)}, u32[]{:S(2)}, u32[]{:S(2)}) collective-permute-start(bf16[928,128]{1,0:T(8,128)(2,1)S(1)} %get-tuple-element.124), channel_id=1, source_target_pairs={{0,16},{1,49},{2,18},{3,51},{4,20},{5,53},{6,22},{7,55},{8,24},{9,... | collective-permute-start | bytes 712712 | tf_op jit(solution)/shard_map/ppermute | solution.py:796
  41.3 4.4 %taps.1 = f32[272,128]{1,0:T(8,128)S(1)} custom-call(f32[8,128]{1,0:T(8,128)S(1)} %get-tuple-element.127.after_ref, f32[512,512]{1,0:T(8,128)S(1)} %get-tuple-element.128.y_ref, f32[2,4,736,128]{3,2,1,0:T(8,128)S(1)} %get-tuple-element.104.p_ref.p_in_ref, f32[2,4,144,128]{3,2,1,0:T(8,128)S(1)} %get-tuple-element.129.border_ref, ...), custom_call_target="tpu_custom_call" | custom-call | flops 1000000000 | bytes 16000000 | tf_op jit(solution)/shard_map/taps/pallas_call | solution.py:1016
  46.2 1.6 %collective-permute-start.11 = (bf16[464,128]{1,0:T(8,128)(2,1)S(1)}, bf16[464,128]{1,0:T(8,128)(2,1)S(1)}, u32[]{:S(2)}, u32[]{:S(2)}) collective-permute-start(bf16[464,128]{1,0:T(8,128)(2,1)S(1)} %select_convert_fusion.2), channel_id=1, source_target_pairs={{0,16},{1,49},{2,18},{3,51},{4,20},{5,53},{6,22},{7,55},{8,24},{9,... | collective-permute-start | bytes 356360 | tf_op jit(solution)/shard_map/ppermute | solution.py:796
  49.9 3.8 %collective-permute-start.30 = (bf16[464,128]{1,0:T(8,128)(2,1)S(1)}, bf16[464,128]{1,0:T(8,128)(2,1)S(1)}, u32[]{:S(2)}, u32[]{:S(2)}) collective-permute-start(bf16[464,128]{1,0:T(8,128)(2,1)S(1)} %get-tuple-element.146), channel_id=1, source_target_pairs={{0,124},{1,125},{2,126},{3,127},{4,8},{5,9},{6,10},{7,11},{8,4},{9... | collective-permute-start | bytes 356360 | tf_op jit(solution)/shard_map/ppermute | solution.py:767
  54.7 2.3 %collective-permute-start.26 = (bf16[512,128]{1,0:T(8,128)(2,1)S(1)}, bf16[512,128]{1,0:T(8,128)(2,1)S(1)}, u32[]{:S(2)}, u32[]{:S(2)}) collective-permute-start(bf16[512,128]{1,0:T(8,128)(2,1)S(1)} %add_convert_fusion.3), channel_id=1, source_target_pairs={{0,16},{1,49},{2,18},{3,51},{4,20},{5,53},{6,22},{7,55},{8,24},{9,... | collective-permute-start | bytes 393224 | tf_op jit(solution)/shard_map/ppermute | solution.py:796
  57.0 2.5 %collective-permute-done.19 = bf16[464,128]{1,0:T(8,128)(2,1)S(1)} collective-permute-done((bf16[464,128]{1,0:T(8,128)(2,1)S(1)}, bf16[464,128]{1,0:T(8,128)(2,1)S(1)}, u32[]{:S(2)}, u32[]{:S(2)}) %collective-permute-start.19) | collective-permute-done | bytes 118816 | tf_op jit(solution)/shard_map/ppermute | solution.py:796
  59.6 1.1 %collective-permute-done.12 = bf16[464,128]{1,0:T(8,128)(2,1)S(1)} collective-permute-done((bf16[464,128]{1,0:T(8,128)(2,1)S(1)}, bf16[464,128]{1,0:T(8,128)(2,1)S(1)}, u32[]{:S(2)}, u32[]{:S(2)}) %collective-permute-start.12) | collective-permute-done | bytes 118816 | tf_op jit(solution)/shard_map/ppermute | solution.py:796
  61.1 2.5 %collective-permute-done.20 = bf16[464,128]{1,0:T(8,128)(2,1)S(1)} collective-permute-done((bf16[464,128]{1,0:T(8,128)(2,1)S(1)}, bf16[464,128]{1,0:T(8,128)(2,1)S(1)}, u32[]{:S(2)}, u32[]{:S(2)}) %collective-permute-start.20) | collective-permute-done | bytes 118816 | tf_op jit(solution)/shard_map/ppermute | solution.py:796
  63.7 1.1 %collective-permute-done.13 = bf16[464,128]{1,0:T(8,128)(2,1)S(1)} collective-permute-done((bf16[464,128]{1,0:T(8,128)(2,1)S(1)}, bf16[464,128]{1,0:T(8,128)(2,1)S(1)}, u32[]{:S(2)}, u32[]{:S(2)}) %collective-permute-start.13) | collective-permute-done | bytes 118816 | tf_op jit(solution)/shard_map/ppermute | solution.py:796
  65.4 1.3 %collective-permute-start.28 = (bf16[512,128]{1,0:T(8,128)(2,1)S(1)}, bf16[512,128]{1,0:T(8,128)(2,1)S(1)}, u32[]{:S(2)}, u32[]{:S(2)}) collective-permute-start(bf16[512,128]{1,0:T(8,128)(2,1)S(1)} %add_convert_fusion.1), channel_id=1, source_target_pairs={{0,66},{1,3},{2,64},{3,1},{4,70},{5,7},{6,68},{7,5},{8,74},{9,11},... | collective-permute-start | bytes 393224 | tf_op jit(solution)/shard_map/ppermute | solution.py:796
  67.6 1.0 collective-permute-done.14
  69.5 1.0 collective-permute-start.31
  71.3 1.8 %collective-permute-start.23 = (bf16[464,128]{1,0:T(8,128)(2,1)S(1)}, bf16[464,128]{1,0:T(8,128)(2,1)S(1)}, u32[]{:S(2)}, u32[]{:S(2)}) collective-permute-start(bf16[464,128]{1,0:T(8,128)(2,1)S(1)} %add_convert_fusion.4), channel_id=1, source_target_pairs={{0,4},{1,13},{2,6},{3,15},{4,0},{5,9},{6,2},{7,11},{8,12},{9,5},{1... | collective-permute-start | bytes 356360 | tf_op jit(solution)/shard_map/ppermute | solution.py:796
  74.1 2.3 %collective-permute-start.32 = (bf16[512,128]{1,0:T(8,128)(2,1)S(1)}, bf16[512,128]{1,0:T(8,128)(2,1)S(1)}, u32[]{:S(2)}, u32[]{:S(2)}) collective-permute-start(bf16[512,128]{1,0:T(8,128)(2,1)S(1)} %add_convert_fusion), channel_id=1, source_target_pairs={{0,2},{1,67},{2,0},{3,65},{4,6},{5,71},{6,4},{7,69},{8,10},{9,75},... | collective-permute-start | bytes 393224 | tf_op jit(solution)/shard_map/ppermute | solution.py:796
  76.6 1.9 %collective-permute-start.24 = (bf16[928,128]{1,0:T(8,128)(2,1)S(1)}, bf16[928,128]{1,0:T(8,128)(2,1)S(1)}, u32[]{:S(2)}, u32[]{:S(2)}) collective-permute-start(bf16[928,128]{1,0:T(8,128)(2,1)S(1)} %pad_maximum_fusion.3), channel_id=1, source_target_pairs={{0,16},{1,49},{2,18},{3,51},{4,20},{5,53},{6,22},{7,55},{8,24},{9,... | collective-permute-start | bytes 712712 | tf_op jit(solution)/shard_map/ppermute | solution.py:796
  78.5 2.8 %collective-permute-start.17 = (bf16[928,128]{1,0:T(8,128)(2,1)S(1)}, bf16[928,128]{1,0:T(8,128)(2,1)S(1)}, u32[]{:S(2)}, u32[]{:S(2)}) collective-permute-start(bf16[928,128]{1,0:T(8,128)(2,1)S(1)} %pad_maximum_fusion.2), channel_id=1, source_target_pairs={{0,2},{1,67},{2,0},{3,65},{4,6},{5,71},{6,4},{7,69},{8,10},{9,75},... | collective-permute-start | bytes 712712 | tf_op jit(solution)/shard_map/ppermute | solution.py:796
  81.4 1.5 %collective-permute-start.33 = (bf16[1024,128]{1,0:T(8,128)(2,1)S(1)}, bf16[1024,128]{1,0:T(8,128)(2,1)S(1)}, u32[]{:S(2)}, u32[]{:S(2)}) collective-permute-start(bf16[1024,128]{1,0:T(8,128)(2,1)S(1)} %pad_maximum_fusion.1), channel_id=1, source_target_pairs={{0,4},{1,13},{2,6},{3,15},{4,0},{5,9},{6,2},{7,11},{8,12},{9,5},{1... | collective-permute-start | bytes 786440 | tf_op jit(solution)/shard_map/ppermute | solution.py:796
  82.9 5.4 %back_first.1 = (bf16[2,16,16,400]{3,2,1,0:T(8,128)(2,1)}, f32[2,4,736,128]{3,2,1,0:T(8,128)S(1)}) custom-call(s32[2,8]{1,0:T(2,128)} %beside_ref.5, bf16[2,16,16,400]{3,2,1,0:T(8,128)(2,1)S(1)} %get-tuple-element.142.refs_0_.cg_ref, f32[512,400]{1,0:T(8,128)S(1)} %get-tuple-element.93.refs_1_.mask_ref, bf16[512,512]{1,0:T(8,128)(2,1)S(1)} %get-tuple-element.106.gated_ref, ...), custom_call_target="tpu_custom_call" | custom-call | flops 1000000000 | bytes 16000000 | tf_op jit(solution)/shard_map/back_first/pallas_call | solution.py:1058
  88.9 5.1 %collective-permute-start.34 = (bf16[5488,128]{1,0:T(8,128)(2,1)S(1)}, bf16[5488,128]{1,0:T(8,128)(2,1)S(1)}, u32[]{:S(2)}, u32[]{:S(2)}) collective-permute-start(bf16[5488,128]{1,0:T(8,128)(2,1)S(1)} %fusion.mine_ref), channel_id=1, source_target_pairs={{0,1},{1,0},{2,3},{3,2},{4,5},{5,4},{6,7},{7,6},{8,9},{9,8},{10,11... | collective-permute-start | bytes 4214792 | tf_op jit(solution)/shard_map/ppermute | solution.py:771
  94.1 3.0 %back_second.1 = bf16[2,16,16,400]{3,2,1,0:T(8,128)(2,1)} custom-call(f32[2,4,736,128]{3,2,1,0:T(8,128)S(1)} %get-tuple-element.155.p_ref, f32[512,400]{1,0:T(8,128)S(1)} %get-tuple-element.93.refs_1_.mask_ref, bf16[512,512]{1,0:T(8,128)(2,1)S(1)} %get-tuple-element.106.gated_ref, ...), custom_call_target="tpu_custom_call", output_to_operand_aliasing={{}: (4, {})} | custom-call | flops 1000000000 | bytes 16000000 | tf_op jit(solution)/shard_map/back_second/pallas_call | solution.py:1082
  97.1 2.8 %unpack.1 = (f32[400,1600]{1,0:T(8,128)}, f32[400,1600]{1,0:T(8,128)}, f32[49,400]{1,0:T(8,128)}, f32[400]{0:T(512)}, f32[400]{0:T(512)}, /*index=5*/f32[400]{0:T(512)}, f32[1600]{0:T(1024)}, f32[400]{0:T(512)}) custom-call(bf16[5488,128]{1,0:T(8,128)(2,1)S(1)} %fusion.mine_ref, bf16[5488,128]{1,0:T(8,128)(2,1)S(1)} %collective-permute-done.34.theirs_ref), custom_call_target="tpu_custom_call" | custom-call | tf_op jit(solution)/shard_map/unpack/pallas_call | solution.py:1094
  (86 shorter events, 13.4 us)
Async XLA Ops:
  1.9 4.8 %collective-permute-start = (bf16[2,48,512]{2,1,0:T(8,128)(2,1)S(1)}, bf16[2,48,512]{2,1,0:T(8,128)(2,1)S(1)}, u32[]{:S(2)}, u32[]{:S(2)}) collective-permute-start(bf16[2,48,512]{2,1,0:T(8,128)(2,1)S(1)} %get-tuple-element.94), channel_id=1, source_target_pairs={{0,1},{1,0},{2,3},{3,2},{4,5},{5,4},{6,7},{7,6},{8,9},{9,8},{10,11... | collective-permute-start | bytes 294920 | tf_op jit(solution)/shard_map/ppermute | solution.py:767
  3.4 4.5 %collective-permute-start.1 = (bf16[2,48,512]{2,1,0:T(8,128)(2,1)S(1)}, bf16[2,48,512]{2,1,0:T(8,128)(2,1)S(1)}, u32[]{:S(2)}, u32[]{:S(2)}) collective-permute-start(bf16[2,48,512]{2,1,0:T(8,128)(2,1)S(1)} %get-tuple-element.95), channel_id=1, source_target_pairs={{0,3},{1,2},{2,1},{3,0},{4,7},{5,6},{6,5},{7,4},{8,11},{9,10},{10,... | collective-permute-start | bytes 294920 | tf_op jit(solution)/shard_map/ppermute | solution.py:767
  8.3 14.1 %collective-permute-start.2 = (bf16[464,128]{1,0:T(8,128)(2,1)S(1)}, bf16[464,128]{1,0:T(8,128)(2,1)S(1)}, u32[]{:S(2)}, u32[]{:S(2)}) collective-permute-start(bf16[464,128]{1,0:T(8,128)(2,1)S(1)} %get-tuple-element.100), channel_id=1, source_target_pairs={{0,4},{1,5},{2,6},{3,7},{4,0},{5,1},{6,2},{7,3},{8,12},{9,13},{10,... | collective-permute-start | bytes 356360 | tf_op jit(solution)/shard_map/ppermute | solution.py:767
  10.1 12.3 %collective-permute-start.3 = (bf16[464,128]{1,0:T(8,128)(2,1)S(1)}, bf16[464,128]{1,0:T(8,128)(2,1)S(1)}, u32[]{:S(2)}, u32[]{:S(2)}) collective-permute-start(bf16[464,128]{1,0:T(8,128)(2,1)S(1)} %get-tuple-element.101), channel_id=1, source_target_pairs={{0,124},{1,125},{2,126},{3,127},{4,8},{5,9},{6,10},{7,11},{8,4},{9... | collective-permute-start | bytes 356360 | tf_op jit(solution)/shard_map/ppermute | solution.py:767
  29.0 5.3 %collective-permute-start.4 = (bf16[3200,128]{1,0:T(8,128)(2,1)S(1)}, bf16[3200,128]{1,0:T(8,128)(2,1)S(1)}, u32[]{:S(2)}, u32[]{:S(2)}) collective-permute-start(bf16[3200,128]{1,0:T(8,128)(2,1)S(1)} %get-tuple-element.111), channel_id=1, source_target_pairs={{0,1},{1,0},{2,3},{3,2},{4,5},{5,4},{6,7},{7,6},{8,9},{9,8},{10,11... | collective-permute-start | bytes 2457608 | tf_op jit(solution)/shard_map/ppermute | solution.py:771
  34.5 11.2 %collective-permute-start.8 = (bf16[752,128]{1,0:T(8,128)(2,1)S(1)}, bf16[752,128]{1,0:T(8,128)(2,1)S(1)}, u32[]{:S(2)}, u32[]{:S(2)}) collective-permute-start(bf16[752,128]{1,0:T(8,128)(2,1)S(1)} %get-tuple-element.126), channel_id=1, source_target_pairs={{0,4},{1,13},{2,6},{3,15},{4,0},{5,9},{6,2},{7,11},{8,12},{9,5},{1... | collective-permute-start | bytes 577544 | tf_op jit(solution)/shard_map/ppermute | solution.py:796
  34.6 11.4 %collective-permute-start.9 = (bf16[2,48,512]{2,1,0:T(8,128)(2,1)S(1)}, bf16[2,48,512]{2,1,0:T(8,128)(2,1)S(1)}, u32[]{:S(2)}, u32[]{:S(2)}) collective-permute-start(bf16[2,48,512]{2,1,0:T(8,128)(2,1)S(1)} %get-tuple-element.133), channel_id=1, source_target_pairs={{0,1},{1,0},{2,3},{3,2},{4,5},{5,4},{6,7},{7,6},{8,9},{9,8},{10,11... | collective-permute-start | bytes 294920 | tf_op jit(solution)/shard_map/ppermute | solution.py:767
  34.8 11.1 %collective-permute-start.10 = (bf16[2,48,512]{2,1,0:T(8,128)(2,1)S(1)}, bf16[2,48,512]{2,1,0:T(8,128)(2,1)S(1)}, u32[]{:S(2)}, u32[]{:S(2)}) collective-permute-start(bf16[2,48,512]{2,1,0:T(8,128)(2,1)S(1)} %get-tuple-element.134), channel_id=1, source_target_pairs={{0,3},{1,2},{2,1},{3,0},{4,7},{5,6},{6,5},{7,4},{8,11},{9,10},{10,... | collective-permute-start | bytes 294920 | tf_op jit(solution)/shard_map/ppermute | solution.py:767
  35.4 10.4 %collective-permute-start.6 = (bf16[928,128]{1,0:T(8,128)(2,1)S(1)}, bf16[928,128]{1,0:T(8,128)(2,1)S(1)}, u32[]{:S(2)}, u32[]{:S(2)}) collective-permute-start(bf16[928,128]{1,0:T(8,128)(2,1)S(1)} %get-tuple-element.122), channel_id=1, source_target_pairs={{0,2},{1,67},{2,0},{3,65},{4,6},{5,71},{6,4},{7,69},{8,10},{9,75},... | collective-permute-start | bytes 712712 | tf_op jit(solution)/shard_map/ppermute | solution.py:796
  36.4 9.5 %collective-permute-start.7 = (bf16[928,128]{1,0:T(8,128)(2,1)S(1)}, bf16[928,128]{1,0:T(8,128)(2,1)S(1)}, u32[]{:S(2)}, u32[]{:S(2)}) collective-permute-start(bf16[928,128]{1,0:T(8,128)(2,1)S(1)} %get-tuple-element.124), channel_id=1, source_target_pairs={{0,16},{1,49},{2,18},{3,51},{4,20},{5,53},{6,22},{7,55},{8,24},{9,... | collective-permute-start | bytes 712712 | tf_op jit(solution)/shard_map/ppermute | solution.py:796
  46.0 7.7 %collective-permute-start.18 = (bf16[464,128]{1,0:T(8,128)(2,1)S(1)}, bf16[464,128]{1,0:T(8,128)(2,1)S(1)}, u32[]{:S(2)}, u32[]{:S(2)}) collective-permute-start(bf16[464,128]{1,0:T(8,128)(2,1)S(1)} %select_convert_fusion.1), channel_id=1, source_target_pairs={{0,4},{1,13},{2,6},{3,15},{4,0},{5,9},{6,2},{7,11},{8,12},{9,5},{1... | collective-permute-start | bytes 356360 | tf_op jit(solution)/shard_map/ppermute | solution.py:796
  46.2 8.3 %collective-permute-start.11 = (bf16[464,128]{1,0:T(8,128)(2,1)S(1)}, bf16[464,128]{1,0:T(8,128)(2,1)S(1)}, u32[]{:S(2)}, u32[]{:S(2)}) collective-permute-start(bf16[464,128]{1,0:T(8,128)(2,1)S(1)} %select_convert_fusion.2), channel_id=1, source_target_pairs={{0,16},{1,49},{2,18},{3,51},{4,20},{5,53},{6,22},{7,55},{8,24},{9,... | collective-permute-start | bytes 356360 | tf_op jit(solution)/shard_map/ppermute | solution.py:796
  47.9 6.8 %collective-permute-start.25 = (bf16[512,128]{1,0:T(8,128)(2,1)S(1)}, bf16[512,128]{1,0:T(8,128)(2,1)S(1)}, u32[]{:S(2)}, u32[]{:S(2)}) collective-permute-start(bf16[512,128]{1,0:T(8,128)(2,1)S(1)} %select_convert_fusion), channel_id=1, source_target_pairs={{0,2},{1,67},{2,0},{3,65},{4,6},{5,71},{6,4},{7,69},{8,10},{9,75},... | collective-permute-start | bytes 393224 | tf_op jit(solution)/shard_map/ppermute | solution.py:796
  49.2 20.3 %collective-permute-start.29 = (bf16[464,128]{1,0:T(8,128)(2,1)S(1)}, bf16[464,128]{1,0:T(8,128)(2,1)S(1)}, u32[]{:S(2)}, u32[]{:S(2)}) collective-permute-start(bf16[464,128]{1,0:T(8,128)(2,1)S(1)} %get-tuple-element.145), channel_id=1, source_target_pairs={{0,4},{1,5},{2,6},{3,7},{4,0},{5,1},{6,2},{7,3},{8,12},{9,13},{10,... | collective-permute-start | bytes 356360 | tf_op jit(solution)/shard_map/ppermute | solution.py:767
  49.9 19.5 %collective-permute-start.30 = (bf16[464,128]{1,0:T(8,128)(2,1)S(1)}, bf16[464,128]{1,0:T(8,128)(2,1)S(1)}, u32[]{:S(2)}, u32[]{:S(2)}) collective-permute-start(bf16[464,128]{1,0:T(8,128)(2,1)S(1)} %get-tuple-element.146), channel_id=1, source_target_pairs={{0,124},{1,125},{2,126},{3,127},{4,8},{5,9},{6,10},{7,11},{8,4},{9... | collective-permute-start | bytes 356360 | tf_op jit(solution)/shard_map/ppermute | solution.py:767
  53.8 5.7 %collective-permute-start.19 = (bf16[464,128]{1,0:T(8,128)(2,1)S(1)}, bf16[464,128]{1,0:T(8,128)(2,1)S(1)}, u32[]{:S(2)}, u32[]{:S(2)}) collective-permute-start(bf16[464,128]{1,0:T(8,128)(2,1)S(1)} %add_convert_fusion.8), channel_id=1, source_target_pairs={{0,2},{1,67},{2,0},{3,65},{4,6},{5,71},{6,4},{7,69},{8,10},{9,75},... | collective-permute-start | bytes 356360 | tf_op jit(solution)/shard_map/ppermute | solution.py:796
  54.6 6.2 %collective-permute-start.12 = (bf16[464,128]{1,0:T(8,128)(2,1)S(1)}, bf16[464,128]{1,0:T(8,128)(2,1)S(1)}, u32[]{:S(2)}, u32[]{:S(2)}) collective-permute-start(bf16[464,128]{1,0:T(8,128)(2,1)S(1)} %add_convert_fusion.13), channel_id=1, source_target_pairs={{0,4},{1,13},{2,6},{3,15},{4,0},{5,9},{6,2},{7,11},{8,12},{9,5},{1... | collective-permute-start | bytes 356360 | tf_op jit(solution)/shard_map/ppermute | solution.py:796
  54.7 6.2 %collective-permute-start.26 = (bf16[512,128]{1,0:T(8,128)(2,1)S(1)}, bf16[512,128]{1,0:T(8,128)(2,1)S(1)}, u32[]{:S(2)}, u32[]{:S(2)}) collective-permute-start(bf16[512,128]{1,0:T(8,128)(2,1)S(1)} %add_convert_fusion.3), channel_id=1, source_target_pairs={{0,16},{1,49},{2,18},{3,51},{4,20},{5,53},{6,22},{7,55},{8,24},{9,... | collective-permute-start | bytes 393224 | tf_op jit(solution)/shard_map/ppermute | solution.py:796
  59.6 4.1 %collective-permute-start.20 = (bf16[464,128]{1,0:T(8,128)(2,1)S(1)}, bf16[464,128]{1,0:T(8,128)(2,1)S(1)}, u32[]{:S(2)}, u32[]{:S(2)}) collective-permute-start(bf16[464,128]{1,0:T(8,128)(2,1)S(1)} %add_convert_fusion.7), channel_id=1, source_target_pairs={{0,48},{1,17},{2,50},{3,19},{4,52},{5,21},{6,54},{7,23},{8,56},{9,... | collective-permute-start | bytes 356360 | tf_op jit(solution)/shard_map/ppermute | solution.py:796
  60.8 4.1 %collective-permute-start.13 = (bf16[464,128]{1,0:T(8,128)(2,1)S(1)}, bf16[464,128]{1,0:T(8,128)(2,1)S(1)}, u32[]{:S(2)}, u32[]{:S(2)}) collective-permute-start(bf16[464,128]{1,0:T(8,128)(2,1)S(1)} %add_convert_fusion.12), channel_id=1, source_target_pairs={{0,66},{1,3},{2,64},{3,1},{4,70},{5,7},{6,68},{7,5},{8,74},{9,11},... | collective-permute-start | bytes 356360 | tf_op jit(solution)/shard_map/ppermute | solution.py:796
  61.0 4.3 %collective-permute-start.27 = (bf16[512,128]{1,0:T(8,128)(2,1)S(1)}, bf16[512,128]{1,0:T(8,128)(2,1)S(1)}, u32[]{:S(2)}, u32[]{:S(2)}) collective-permute-start(bf16[512,128]{1,0:T(8,128)(2,1)S(1)} %add_convert_fusion.2), channel_id=1, source_target_pairs={{0,12},{1,5},{2,14},{3,7},{4,8},{5,1},{6,10},{7,3},{8,4},{9,13},{1... | collective-permute-start | bytes 393224 | tf_op jit(solution)/shard_map/ppermute | solution.py:796
  63.7 3.8 %collective-permute-start.21 = (bf16[464,128]{1,0:T(8,128)(2,1)S(1)}, bf16[464,128]{1,0:T(8,128)(2,1)S(1)}, u32[]{:S(2)}, u32[]{:S(2)}) collective-permute-start(bf16[464,128]{1,0:T(8,128)(2,1)S(1)} %add_convert_fusion.6), channel_id=1, source_target_pairs={{0,12},{1,5},{2,14},{3,7},{4,8},{5,1},{6,10},{7,3},{8,4},{9,13},{1... | collective-permute-start | bytes 356360 | tf_op jit(solution)/shard_map/ppermute | solution.py:796
  65.4 4.1 %collective-permute-start.28 = (bf16[512,128]{1,0:T(8,128)(2,1)S(1)}, bf16[512,128]{1,0:T(8,128)(2,1)S(1)}, u32[]{:S(2)}, u32[]{:S(2)}) collective-permute-start(bf16[512,128]{1,0:T(8,128)(2,1)S(1)} %add_convert_fusion.1), channel_id=1, source_target_pairs={{0,66},{1,3},{2,64},{3,1},{4,70},{5,7},{6,68},{7,5},{8,74},{9,11},... | collective-permute-start | bytes 393224 | tf_op jit(solution)/shard_map/ppermute | solution.py:796
  68.7 4.4 %collective-permute-start.15 = (bf16[464,128]{1,0:T(8,128)(2,1)S(1)}, bf16[464,128]{1,0:T(8,128)(2,1)S(1)}, u32[]{:S(2)}, u32[]{:S(2)}) collective-permute-start(bf16[464,128]{1,0:T(8,128)(2,1)S(1)} %add_convert_fusion.10), channel_id=1, source_target_pairs={{0,12},{1,5},{2,14},{3,7},{4,8},{5,1},{6,10},{7,3},{8,4},{9,13},{1... | collective-permute-start | bytes 356360 | tf_op jit(solution)/shard_map/ppermute | solution.py:796
  69.5 4.6 %collective-permute-start.31 = (bf16[512,128]{1,0:T(8,128)(2,1)S(1)}, bf16[512,128]{1,0:T(8,128)(2,1)S(1)}, u32[]{:S(2)}, u32[]{:S(2)}) collective-permute-start(bf16[512,128]{1,0:T(8,128)(2,1)S(1)} %convert_add_fusion.3), channel_id=1, source_target_pairs={{0,48},{1,17},{2,50},{3,19},{4,52},{5,21},{6,54},{7,23},{8,56},{9,... | collective-permute-start | bytes 393224 | tf_op jit(solution)/shard_map/ppermute | solution.py:796
  71.3 5.3 %collective-permute-start.23 = (bf16[464,128]{1,0:T(8,128)(2,1)S(1)}, bf16[464,128]{1,0:T(8,128)(2,1)S(1)}, u32[]{:S(2)}, u32[]{:S(2)}) collective-permute-start(bf16[464,128]{1,0:T(8,128)(2,1)S(1)} %add_convert_fusion.4), channel_id=1, source_target_pairs={{0,4},{1,13},{2,6},{3,15},{4,0},{5,9},{6,2},{7,11},{8,12},{9,5},{1... | collective-permute-start | bytes 356360 | tf_op jit(solution)/shard_map/ppermute | solution.py:796
  73.1 5.4 %collective-permute-start.16 = (bf16[464,128]{1,0:T(8,128)(2,1)S(1)}, bf16[464,128]{1,0:T(8,128)(2,1)S(1)}, u32[]{:S(2)}, u32[]{:S(2)}) collective-permute-start(bf16[464,128]{1,0:T(8,128)(2,1)S(1)} %add_convert_fusion.9), channel_id=1, source_target_pairs={{0,16},{1,49},{2,18},{3,51},{4,20},{5,53},{6,22},{7,55},{8,24},{9,... | collective-permute-start | bytes 356360 | tf_op jit(solution)/shard_map/ppermute | solution.py:796
  74.1 7.3 %collective-permute-start.32 = (bf16[512,128]{1,0:T(8,128)(2,1)S(1)}, bf16[512,128]{1,0:T(8,128)(2,1)S(1)}, u32[]{:S(2)}, u32[]{:S(2)}) collective-permute-start(bf16[512,128]{1,0:T(8,128)(2,1)S(1)} %add_convert_fusion), channel_id=1, source_target_pairs={{0,2},{1,67},{2,0},{3,65},{4,6},{5,71},{6,4},{7,69},{8,10},{9,75},... | collective-permute-start | bytes 393224 | tf_op jit(solution)/shard_map/ppermute | solution.py:796
  76.6 11.9 %collective-permute-start.24 = (bf16[928,128]{1,0:T(8,128)(2,1)S(1)}, bf16[928,128]{1,0:T(8,128)(2,1)S(1)}, u32[]{:S(2)}, u32[]{:S(2)}) collective-permute-start(bf16[928,128]{1,0:T(8,128)(2,1)S(1)} %pad_maximum_fusion.3), channel_id=1, source_target_pairs={{0,16},{1,49},{2,18},{3,51},{4,20},{5,53},{6,22},{7,55},{8,24},{9,... | collective-permute-start | bytes 712712 | tf_op jit(solution)/shard_map/ppermute | solution.py:796
  78.5 9.8 %collective-permute-start.17 = (bf16[928,128]{1,0:T(8,128)(2,1)S(1)}, bf16[928,128]{1,0:T(8,128)(2,1)S(1)}, u32[]{:S(2)}, u32[]{:S(2)}) collective-permute-start(bf16[928,128]{1,0:T(8,128)(2,1)S(1)} %pad_maximum_fusion.2), channel_id=1, source_target_pairs={{0,2},{1,67},{2,0},{3,65},{4,6},{5,71},{6,4},{7,69},{8,10},{9,75},... | collective-permute-start | bytes 712712 | tf_op jit(solution)/shard_map/ppermute | solution.py:796
  81.4 7.3 %collective-permute-start.33 = (bf16[1024,128]{1,0:T(8,128)(2,1)S(1)}, bf16[1024,128]{1,0:T(8,128)(2,1)S(1)}, u32[]{:S(2)}, u32[]{:S(2)}) collective-permute-start(bf16[1024,128]{1,0:T(8,128)(2,1)S(1)} %pad_maximum_fusion.1), channel_id=1, source_target_pairs={{0,4},{1,13},{2,6},{3,15},{4,0},{5,9},{6,2},{7,11},{8,12},{9,5},{1... | collective-permute-start | bytes 786440 | tf_op jit(solution)/shard_map/ppermute | solution.py:796
  88.9 8.1 %collective-permute-start.34 = (bf16[5488,128]{1,0:T(8,128)(2,1)S(1)}, bf16[5488,128]{1,0:T(8,128)(2,1)S(1)}, u32[]{:S(2)}, u32[]{:S(2)}) collective-permute-start(bf16[5488,128]{1,0:T(8,128)(2,1)S(1)} %fusion.mine_ref), channel_id=1, source_target_pairs={{0,1},{1,0},{2,3},{3,2},{4,5},{5,4},{6,7},{7,6},{8,9},{9,8},{10,11... | collective-permute-start | bytes 4214792 | tf_op jit(solution)/shard_map/ppermute | solution.py:771
  (3 other events, 9.5 us)
